TPU v7x, 256 devices: a whole 4x4x8 slice. The times are simulated.
256 devices in a mesh: az: 8 (over x, y_lo), rng: 32 (over z, y_hi, core).
Axes of the slice: x: 4, y: 4 (y_hi: 2, y_lo: 2; y = y_hi * 2 + y_lo), z: 8, core: 2. Of those that a mesh axis runs over, the one named last changes fastest.
Arguments:
- echoes: bfloat16 [2, 256, 32, 4096], P(None, 'az', None, 'rng'), may hold values from -12 to 12
- arc_start: int32 [64], replicated, may hold values from 0 to 255, as said below
- arc_offsets: int32 [64, 16], replicated, may hold values from 0 to 63, as said below
- doppler_bins: int32 [64, 16], replicated, may hold values from 0 to 31
- steer_angles: float32 [64, 16], replicated, may hold values from -3.140625 to 3.140625
- train_mask: int32 [64, 32], P('az', 'rng'), may hold values from 0 to 1, as said below
Outputs:
- smoothed: float32 [64, 16, 4096], P('az', None, 'rng')
Inputs may be any that keep to these rules, and one draw needn't show every extreme that they name: `arc_start`: beam b's arc begins at column (b * 4 - 64 / 2 + j) mod 256 for some j with 0 <= j < 4. `arc_offsets`: each row holds 16 distinct offsets, ascending. `train_mask`: the last block of every beam is a training block.
All inputs are finite; a program needn't handle non-finite values.
Results may differ from a plain program's by a relative error of at most 0.0035.
Values may be sent and summed in bfloat16 or wider, within the bound.
No kernel may reach another device: no remote copies, remote signals or barrier semaphores. Data moves between devices by JAX's collectives and lax.ppermute only.
A program may use at most 64 MiB of HBM per device.

v0:
```python
import jax
import jax.numpy as jnp
from jax import lax
from jax.sharding import PartitionSpec as P

COLS = 256
ARC = 64
BINS = 3
BEAMS = 64
BLK = 128


LOADING = 0.1


def with_halo(block, sides, width, periodic):
    for axis, dim in sides:
        count = lax.axis_size(axis)
        forward = [(i, i + 1) for i in range(count - 1)]
        if periodic:
            forward.append((count - 1, 0))
        backward = [(target, source) for source, target in forward]
        low = lax.ppermute(
            lax.slice_in_dim(block, block.shape[dim] - width, None, axis=dim), axis, forward
        )
        high = lax.ppermute(lax.slice_in_dim(block, 0, width, axis=dim), axis, backward)
        block = jnp.concatenate([low, block, high], axis=dim)
    return block


def in_order(tiles, dim):
    tiles = jnp.moveaxis(tiles, 0, dim)
    dims = tiles.shape
    return tiles.reshape(*dims[:dim], dims[dim] * dims[dim + 1], *dims[dim + 2 :])


def copy_for_each(value, axis):
    length = lax.axis_size(axis)
    return lax.all_to_all(
        jnp.broadcast_to(value[None], (length, *value.shape)), axis, 0, 0, tiled=True
    )


def gathered_copies(value, axis, dim):
    return in_order(copy_for_each(value, axis), dim)


def doppler_table(num_pulses):
    freq_ids = jnp.arange(num_pulses, dtype=jnp.int32)
    phase_steps = freq_ids[:, None] * freq_ids[None, :] % num_pulses
    phase_angle = -2.0 * jnp.pi / num_pulses * phase_steps.astype(jnp.float32)
    return (jnp.cos(phase_angle).astype(jnp.bfloat16), jnp.sin(phase_angle).astype(jnp.bfloat16))


def snapshot(beam_cols, centers, beam_angle, table_re, table_im):
    num_sel = beam_cols.shape[1]
    num_pulses = beam_cols.shape[2]
    num_cells = beam_cols.shape[3]
    num_chan = centers.shape[0]
    bin_ids = (
        (centers[:, None] + jnp.arange(BINS, dtype=jnp.int32)[None, :] - BINS // 2) % num_pulses
    ).reshape(-1)
    bin_pick = (jnp.arange(num_pulses, dtype=jnp.int32)[None, :] == bin_ids[:, None]).astype(
        jnp.bfloat16
    )
    wt_real = jnp.dot(bin_pick, table_re, preferred_element_type=jnp.float32).astype(jnp.bfloat16)
    wt_imag = jnp.dot(bin_pick, table_im, preferred_element_type=jnp.float32).astype(jnp.bfloat16)
    stacked_table = jnp.concatenate(
        [jnp.concatenate([wt_real, -wt_imag], 1), jnp.concatenate([wt_imag, wt_real], 1)], 0
    )
    flat_cols = jnp.transpose(beam_cols, (0, 2, 1, 3)).reshape(2 * num_pulses, num_sel * num_cells)
    spectrum = jnp.dot(stacked_table, flat_cols, preferred_element_type=jnp.float32).reshape(
        2, num_chan, BINS, num_sel, num_cells
    )
    cosine = jnp.cos(beam_angle)[None, None, :, None]
    sine_part = jnp.sin(beam_angle)[None, None, :, None]
    part_real = cosine * spectrum[0] - sine_part * spectrum[1]
    part_imag = sine_part * spectrum[0] + cosine * spectrum[1]
    joined = jnp.concatenate(
        [
            part_real.reshape(num_chan, BINS * num_sel, num_cells),
            part_imag.reshape(num_chan, BINS * num_sel, num_cells),
        ],
        1,
    )
    return joined.astype(jnp.bfloat16)


def beam_snapshots(column_block, col_index, centers, angles_all, table_re, table_im):

    def per_beam(packed):
        index_row, center_row, beam_angle = packed
        beam_cols = jnp.take(column_block, index_row, axis=1)
        return snapshot(beam_cols, center_row, beam_angle, table_re, table_im)

    return lax.map(per_beam, (col_index, centers, angles_all))


def weights_from_blocks(block_a, block_b, train_count):
    dof_size = block_a.shape[0]
    embedded = (
        jnp.concatenate(
            [jnp.concatenate([block_a, -block_b], 1), jnp.concatenate([block_b, block_a], 1)], 0
        )
        / train_count
    )
    loading_level = LOADING * jnp.trace(block_a) / (train_count * dof_size)
    embedded = embedded + loading_level * jnp.eye(2 * dof_size, dtype=jnp.float32)
    factor = jnp.linalg.cholesky(embedded)
    steering = (
        jnp.arange(2 * dof_size, dtype=jnp.int32)[:, None] // dof_size
        == jnp.arange(2, dtype=jnp.int32)[None, :]
    ).astype(jnp.float32)
    solved = jax.scipy.linalg.cho_solve((factor, True), steering)
    quiescent = jnp.sum(solved[:dof_size, 0])
    return (solved.T, quiescent)


def body(echoes, arc_start, arc_offsets, doppler_bins, steer_angles, train_mask):
    columns = echoes.shape[1]
    num_pulses = echoes.shape[2]
    cycle_size = lax.axis_size("az")
    cycle_pos = lax.axis_index("az")
    beam_count = BEAMS // cycle_size
    chan_count = doppler_bins.shape[1]
    item_count = beam_count * chan_count
    table_re, table_im = doppler_table(num_pulses)
    own_beams = cycle_pos * beam_count + jnp.arange(beam_count, dtype=jnp.int32)
    extended = with_halo(echoes, (("az", 1),), ARC // 2, True)
    arc_first = (arc_start[own_beams] - cycle_pos * columns + ARC // 2) % COLS
    col_index = arc_first[:, None] + arc_offsets[own_beams]
    snapshots = beam_snapshots(
        extended, col_index, doppler_bins[own_beams], steer_angles[own_beams], table_re, table_im
    )
    block_count = train_mask.shape[1]
    cell_mask = (
        jnp.broadcast_to(train_mask[:, :, None], (beam_count, block_count, BLK))
        .reshape(beam_count, block_count * BLK)
        .astype(jnp.bfloat16)
    )
    gram_local = jnp.einsum(
        "bkdr,bker->bkde",
        snapshots * cell_mask[:, None, None, :],
        snapshots,
        preferred_element_type=jnp.float32,
    )
    count_beam = (BLK * jnp.sum(train_mask, axis=1)).astype(jnp.float32)
    count_local = jnp.broadcast_to(count_beam[:, None], (beam_count, chan_count)).reshape(
        item_count
    )
    dof_size = gram_local.shape[2] // 2
    gram_items = gram_local.reshape(item_count, 2 * dof_size, 2 * dof_size)
    gram_part, count_part = (
        lax.psum_scatter(gram_items, "rng", scatter_dimension=0, tiled=True),
        lax.psum_scatter(count_local, "rng", scatter_dimension=0, tiled=True),
    )
    block_a = gram_part[:, :dof_size, :dof_size] + gram_part[:, dof_size:, dof_size:]
    block_b = gram_part[:, dof_size:, :dof_size] - gram_part[:, :dof_size, dof_size:]
    solved_part, quiet_part = jax.vmap(weights_from_blocks)(block_a, block_b, count_part)
    solved_all, quiet_all = (
        gathered_copies(solved_part, "rng", 0),
        gathered_copies(quiet_part, "rng", 0),
    )
    adapted = solved_all.reshape(beam_count, chan_count, 2, 2 * dof_size).astype(jnp.bfloat16)
    quiescent = quiet_all.reshape(beam_count, chan_count)
    projected = jnp.einsum(
        "bkcd,bkdr->bkcr", adapted, snapshots, preferred_element_type=jnp.float32
    )
    power_map = (
        projected[:, :, 0] * projected[:, :, 0] + projected[:, :, 1] * projected[:, :, 1]
    ) / quiescent[:, :, None]
    beam_ext = with_halo(power_map, (("az", 0),), 1, True)
    full_ext = with_halo(beam_ext, (("rng", 2),), 1, False)
    row_sums = full_ext[:, :, :-2] + full_ext[:, :, 1:-1] + full_ext[:, :, 2:]
    smoothed = (row_sums[:-2] + row_sums[1:-1] + row_sums[2:]) / 9.0
    return smoothed


def solution(mesh):
    return jax.shard_map(
        body,
        mesh=mesh,
        in_specs=(P(None, "az", None, "rng"), P(), P(), P(), P(), P("az", "rng")),
        out_specs=P("az", None, "rng"),
        check_vma=False,
    )
```

profile of v0, /device:TPU:1, one launch (start us, length us, event | category | flops | bytes accessed | tf_op | source)
XLA Modules:
  0.0 335.5 jit_solution(12063443060458211406)
XLA Ops:
  6.5 2.1 collective-permute-start
  8.7 2.2 collective-permute-start.1
  10.9 0.6 gather_fusion.3
  11.6 0.8 copy.34
  12.9 0.8 copy.32
  14.2 0.8 copy.33
  15.6 0.7 convert_bitcast_fusion
  16.4 14.2 %collective-permute-done = bf16[2,32,32,128]{3,2,1,0:T(8,128)(2,1)S(1)} collective-permute-done((bf16[2,32,32,128]{3,2,1,0:T(8,128)(2,1)}, bf16[2,32,32,128]{3,2,1,0:T(8,128)(2,1)S(1)}, u32[]{:S(2)}, u32[]{:S(2)}) %collective-permute-start) | collective-permute-done | bytes 524320 | tf_op jit(solution)/shard_map/ppermute | solution.py:23
  30.6 2.5 collective-permute-done.1
  33.2 1.2 pad_maximum_fusion
  34.4 27.6 %while.13 = (s32[]{:T(128)}, bf16[8,16,96,128]{3,2,1,0:T(8,128)(2,1)}, f32[8,16]{1,0:T(8,128)S(1)}, s32[8,16]{1,0:T(8,128)S(1)}, s32[8,16]{1,0:T(8,128)S(1)}, /*index=5*/bf16[2,96,32,128]{3,2,1,0:T(8,128)(2,1)S(1)}, s32[]{:T(128)}) while((s32[]{:T(128)}, bf16[8,16,96,128]{3,2,1,0:T(8,128)(2,1)}, f32[8,16]{1,0:T(8,128)S(1)}, ...), condition=%wide.region_1.2_spmd.clone, body=%wide.region_0.1_spmd.clone.sunk | while | flops 27155712 | bytes 7760125 | solution.py:96
  34.4 0.6 gather_fusion
  37.1 0.8 maximum_dynamic-update-slice_fusion.2
  40.5 0.8 maximum_dynamic-update-slice_fusion.2
  43.9 0.8 maximum_dynamic-update-slice_fusion.2
  44.7 0.6 gather_fusion
  47.4 0.8 maximum_dynamic-update-slice_fusion.2
  48.1 0.6 gather_fusion
  50.8 0.8 maximum_dynamic-update-slice_fusion.2
  51.6 0.6 gather_fusion
  54.2 0.8 maximum_dynamic-update-slice_fusion.2
  55.1 0.6 gather_fusion
  57.7 0.8 maximum_dynamic-update-slice_fusion.2
  58.5 0.6 gather_fusion
  61.2 0.8 maximum_dynamic-update-slice_fusion.2
  62.0 7.8 %fusion.38 = f32[8,16,96,96]{2,3,1,0:T(8,128)} fusion(bf16[8,16,96,128]{3,2,1,0:T(8,128)(2,1)} %get-tuple-element.108, bf16[8]{0:T(256)(128)(2,1)S(1)} %get-tuple-element.157), kind=kOutput, calls=%fused_computation.64 | convolution fusion | flops 303562752 | bytes 7864336 | tf_op jit(solution)/shard_map/bkdr,bker->bkde/dot_general | solution.py:141
  71.6 68.9 %all-reduce = f32[128]{0:T(128)S(1)} all-reduce(f32[128]{0:T(128)S(1)} %reshape.294), channel_id=3, replica_groups=mesh['az'=8,'rng'=32] {'rng'}, use_global_device_ids=true, to_apply=%region_3.4.clone | all-reduce | flops 128 | bytes 1024
  140.6 0.6 iota_compare_fusion.3
  141.8 64.1 %reduce-scatter.2.cloned.1.call-done = f32[4,96,96]{1,2,0:T(8,128)} async-done(((f32[128,96,96]{1,2,0:T(8,128)}), f32[4,96,96]{1,2,0:T(8,128)}) %reduce-scatter.2.cloned.1.call-update) | async-done | bytes 147472 | tf_op jit(solution)/shard_map/reduce_scatter | solution.py:154
  205.9 1.2 fusion.57
  207.5 0.7 fusion.46
  208.2 35.9 %custom-call.11 = f32[4,96,96]{2,1,0:T(8,128)S(1)} custom-call(f32[4,96,96]{2,1,0:T(8,128)} %fusion.46), custom_call_target="Cholesky" | custom-call | tf_op jit(solution)/shard_map/vmap(jit(cholesky))/cholesky | solution.py:109
  244.1 0.7 select_reduce_fusion
  245.1 29.5 %custom-call.12 = f32[4,1,96,96]{2,3,1,0:T(8,128)S(1)} custom-call(f32[4,1,96,96]{3,2,1,0:T(8,128)S(1)} %select_bitcast_fusion.1), custom_call_target="InvertDiagBlocksLowerTriangular" | custom-call | tf_op jit(solution)/shard_map/vmap(jit(_cho_solve))/triangular_solve | solution.py:114
  274.6 1.0 fusion.44
  276.1 19.4 %all_to_all.11 = f32[32,1,4]{2,1,0:T(1,128)S(1)} all-to-all(f32[32,1,4]{2,1,0:T(1,128)S(1)} %broadcast_in_dim.54), channel_id=1, replica_groups=mesh['az'=8,'rng'=32] {'rng'}, dimensions={0} | all-to-all | bytes 1024 | tf_op jit(solution)/shard_map/all_to_all | solution.py:39
  295.6 0.7 broadcast_in_dim.53
  296.2 4.1 %all-to-all-start = ((bf16[32,4,2,96]{3,2,1,0:T(2,128)(2,1)}), bf16[32,4,2,96]{3,2,1,0:T(2,128)(2,1)S(1)}, u32[]{:S(2)}, u32[]{:S(2)}) async-start(bf16[32,4,2,96]{3,2,1,0:T(2,128)(2,1)} %broadcast_in_dim.53), calls=%async_computation.1 | async-start | bytes 131072 | tf_op jit(solution)/shard_map/all_to_all | solution.py:39
  300.9 0.6 reduce.10
  301.6 8.7 %all-to-all-done = bf16[32,4,2,96]{3,2,1,0:T(2,128)(2,1)S(1)} async-done(((bf16[32,4,2,96]{3,2,1,0:T(2,128)(2,1)}), bf16[32,4,2,96]{3,2,1,0:T(2,128)(2,1)S(1)}, u32[]{:S(2)}, u32[]{:S(2)}) %all-to-all-start) | async-done | bytes 49184 | tf_op jit(solution)/shard_map/all_to_all | solution.py:39
  310.3 0.9 fusion.51
  311.5 1.3 collective-permute-start.2
  312.7 2.4 collective-permute-start.3
  315.1 1.0 collective-permute-done.2
  316.2 4.3 %collective-permute-start.4 = (f32[10,16,1]{2,1,0:T(8,128)S(1)}, f32[10,16,1]{2,1,0:T(8,128)S(1)}, u32[]{:S(2)}, u32[]{:S(2)}) collective-permute-start(f32[10,16,1]{2,1,0:T(8,128)S(1)} %get-tuple-element.152), channel_id=1, source_target_pairs={{0,1},{1,2},{2,3},{3,4},{4,5},{5,6},{6,7},{7,8},{8,9},{9,10},{10,1... | collective-permute-start | bytes 1928 | tf_op jit(solution)/shard_map/ppermute | solution.py:23
  320.6 1.9 collective-permute-start.5
  322.5 5.3 %collective-permute-done.5 = f32[10,16,1]{2,1,0:T(8,128)S(1)} collective-permute-done((f32[10,16,1]{2,1,0:T(8,128)S(1)}, f32[10,16,1]{2,1,0:T(8,128)S(1)}, u32[]{:S(2)}, u32[]{:S(2)}) %collective-permute-start.5) | collective-permute-done | bytes 672 | tf_op jit(solution)/shard_map/ppermute | solution.py:26
  328.0 0.6 fusion.49
  (213 shorter events, 22.7 us)
Async XLA Ops:
  6.5 4.3 %copy-start = (s32[64]{0:T(128)S(1)}, s32[64]{0:T(128)}, u32[]{:S(2)}) copy-start(s32[64]{0:T(128)} %param.9) | copy-start | bytes 772
  6.5 199.4 %reduce-scatter.2.cloned.1.call-start = ((), (), s32[]{:S(2)}) async-start(), calls=%async_computation.3 | async-start | bytes 6488064 | tf_op jit(solution)/shard_map/reduce_scatter | solution.py:154
  6.5 24.1 %collective-permute-start = (bf16[2,32,32,128]{3,2,1,0:T(8,128)(2,1)}, bf16[2,32,32,128]{3,2,1,0:T(8,128)(2,1)S(1)}, u32[]{:S(2)}, u32[]{:S(2)}) collective-permute-start(bf16[2,32,32,128]{3,2,1,0:T(8,128)(2,1)} %param.8), channel_id=1, source_target_pairs={{0,32},{32,64},{64,96},{96,128},{128,160},{160,192},{192,224},{224... | collective-permute-start | bytes 1572872 | tf_op jit(solution)/shard_map/ppermute | solution.py:23
  8.7 24.5 %collective-permute-start.1 = (bf16[2,32,32,128]{3,2,1,0:T(8,128)(2,1)}, bf16[2,32,32,128]{3,2,1,0:T(8,128)(2,1)S(1)}, u32[]{:S(2)}, u32[]{:S(2)}) collective-permute-start(bf16[2,32,32,128]{3,2,1,0:T(8,128)(2,1)} %param.8), channel_id=1, source_target_pairs={{32,0},{64,32},{96,64},{128,96},{160,128},{192,160},{224,192},{0,2... | collective-permute-start | bytes 1572872 | tf_op jit(solution)/shard_map/ppermute | solution.py:26
  69.7 0.7 copy-start.2
  69.7 240.5 %copy-start.1 = (bf16[8,16,96,128]{3,2,1,0:T(8,128)(2,1)S(1)}, bf16[8,16,96,128]{3,2,1,0:T(8,128)(2,1)}, u32[]{:S(2)}) copy-start(bf16[8,16,96,128]{3,2,1,0:T(8,128)(2,1)} %get-tuple-element.108) | copy-start | bytes 9437188
  296.2 14.1 %all-to-all-start = ((bf16[32,4,2,96]{3,2,1,0:T(2,128)(2,1)}), bf16[32,4,2,96]{3,2,1,0:T(2,128)(2,1)S(1)}, u32[]{:S(2)}, u32[]{:S(2)}) async-start(bf16[32,4,2,96]{3,2,1,0:T(2,128)(2,1)} %broadcast_in_dim.53), calls=%async_computation.1 | async-start | bytes 131072 | tf_op jit(solution)/shard_map/all_to_all | solution.py:39
  311.5 4.7 %collective-permute-start.2 = (f32[1,16,128]{2,1,0:T(8,128)S(1)}, f32[1,16,128]{2,1,0:T(8,128)S(1)}, u32[]{:S(2)}, u32[]{:S(2)}) collective-permute-start(f32[1,16,128]{2,1,0:T(8,128)S(1)} %get-tuple-element.154), channel_id=1, source_target_pairs={{0,32},{32,64},{64,96},{96,128},{128,160},{160,192},{192,224},{224... | collective-permute-start | bytes 24584 | tf_op jit(solution)/shard_map/ppermute | solution.py:23
  312.7 3.4 %collective-permute-start.3 = (f32[1,16,128]{2,1,0:T(8,128)S(1)}, f32[1,16,128]{2,1,0:T(8,128)S(1)}, u32[]{:S(2)}, u32[]{:S(2)}) collective-permute-start(f32[1,16,128]{2,1,0:T(8,128)S(1)} %get-tuple-element.155), channel_id=1, source_target_pairs={{32,0},{64,32},{96,64},{128,96},{160,128},{192,160},{224,192},{0,2... | collective-permute-start | bytes 24584 | tf_op jit(solution)/shard_map/ppermute | solution.py:26
  316.2 6.3 %collective-permute-start.4 = (f32[10,16,1]{2,1,0:T(8,128)S(1)}, f32[10,16,1]{2,1,0:T(8,128)S(1)}, u32[]{:S(2)}, u32[]{:S(2)}) collective-permute-start(f32[10,16,1]{2,1,0:T(8,128)S(1)} %get-tuple-element.152), channel_id=1, source_target_pairs={{0,1},{1,2},{2,3},{3,4},{4,5},{5,6},{6,7},{7,8},{8,9},{9,10},{10,1... | collective-permute-start | bytes 1928 | tf_op jit(solution)/shard_map/ppermute | solution.py:23
  320.6 7.3 %collective-permute-start.5 = (f32[10,16,1]{2,1,0:T(8,128)S(1)}, f32[10,16,1]{2,1,0:T(8,128)S(1)}, u32[]{:S(2)}, u32[]{:S(2)}) collective-permute-start(f32[10,16,1]{2,1,0:T(8,128)S(1)} %get-tuple-element.153), channel_id=1, source_target_pairs={{1,0},{2,1},{3,2},{4,3},{5,4},{6,5},{7,6},{8,7},{9,8},{10,9},{11,1... | collective-permute-start | bytes 1928 | tf_op jit(solution)/shard_map/ppermute | solution.py:26
Sparse Core Ops, SparseCore 0:
  69.9 135.9 reduce-scatter.1
where the time goes:
time: 337 us; the launch traced here: 335 us
  waiting for transfers between devices  95.9 us (28%)
  blocking collectives  88.4 us (26%)
  other arithmetic  83 us (25%)
  starting transfers between devices  18.4 us (5%)
  local copies, waits for them, and re-layouts  17.6 us (5%)
  matrix products  17.3 us (5%)
  between operations  14.2 us (4%)
    unnamed x1, blocking collectives  68.9 us
    reduce_scatter x1, waiting for transfers between devices, body(): lax.psum_scatter(gram_items, 'rng', scatter_dimension=0, tiled=True)  64.1 us
    another operation x4, other arithmetic, weights_from_blocks(): factor = jnp.linalg.cholesky(embedded)  37.4 us
    another operation x3, other arithmetic, weights_from_blocks(): solved = jax.scipy.linalg.cho_solve((factor, True), steering)  29.6 us
    all_to_all x1, blocking collectives, copy_for_each(): lax.all_to_all(jnp.broadcast_to(value[None], (length, *value.shape)), axi...  19.4 us
    ppermute x3, waiting for transfers between devices, with_halo(): lax.ppermute(lax.slice_in_dim(block, block.shape[dim] - width, None, axis...  15.3 us
    all_to_all x1, waiting for transfers between devices, copy_for_each(): lax.all_to_all(jnp.broadcast_to(value[None], (length, *value.shape)), axi...  8.66 us
    ppermute x3, waiting for transfers between devices, with_halo(): lax.ppermute(lax.slice_in_dim(block, 0, width, axis=dim), axis, backward)  7.86 us
  transfers between devices with their start and end apart: 8, of which 6 were waited for; matrix products, arithmetic and copies ran while one was open for 3% of the time, Pallas kernels for 0%

commit v1 on v0

v1 whole, which is shorter than its diff:
```python
import functools

import jax
import jax.numpy as jnp
import numpy as np
from jax import lax
from jax.experimental import pallas as pl
from jax.experimental.pallas import tpu as pltpu
from jax.sharding import PartitionSpec as P

COLS = 256
ARC = 64
BINS = 3
BEAMS = 64
BLK = 128
PULSES = 32
SEL = 16
DBINS = 16
DOF = BINS * SEL
OWN_COLS = 32
OWN_BEAMS = 8
CELLS = 128
GROUPS = 16
LANES = 128
SLOTS = PULSES + 3
LOADING = 0.1
F32 = jnp.float32
BF16 = jnp.bfloat16
TRANSPOSED = (((1,), (1,)), ((), ()))


def table_array():
    ids = np.arange(PULSES)
    steps = (ids[:, None] * ids[None, :] % PULSES).astype(np.float32)
    angle = np.float32(-2.0 * np.pi / PULSES) * steps
    real, imag = np.cos(angle), np.sin(angle)
    return np.concatenate(
        [np.concatenate([real, -imag], 1), np.concatenate([imag, real], 1)], 0
    ).astype(jnp.bfloat16)


def lane_ids(rows):
    return lax.broadcasted_iota(jnp.int32, (rows, LANES), 1)


def own_group():
    place = lax.axis_index("rng")
    bits = [lax.rem(lax.div(place, 1 << bit), 2) for bit in range(4)]
    return bits[0] * 8 + bits[1] * 4 + bits[2] * 2 + bits[3]


def exclusive(left, right):
    return lax.bitwise_xor(left, right)


def gram_kernel(
    start_ref, offset_ref, bins_ref, mask_ref, cos_ref, sin_ref,
    table_ref, low_ref, own_ref, high_ref,
    snap_ref, keep_ref, send_ref,
    spec_ref, wide_ref, minus_ref,
):
    az = lax.axis_index("az")
    mine = own_group()
    table = table_ref[...]

    def transform(pair, carry):
        for part, ref in enumerate((low_ref, own_ref, high_ref)):
            blocks = [
                jnp.concatenate([ref[0, 2 * pair + one], ref[1, 2 * pair + one]], 0)
                for one in range(2)
            ]
            both = jnp.dot(
                table, jnp.concatenate(blocks, 1), preferred_element_type=F32
            )
            spec_ref[part * OWN_COLS + 2 * pair] = both[:, :CELLS]
            spec_ref[part * OWN_COLS + 2 * pair + 1] = both[:, CELLS:]
        return carry

    lax.fori_loop(0, OWN_COLS // 2, transform, 0)

    lane = lane_ids(DOF)
    row = lax.broadcasted_iota(jnp.int32, (DOF, LANES), 0)
    blank = jnp.zeros((LANES - 2 * DOF, 2 * CELLS), BF16)

    def one_beam(beam, carry):
        glob = az * OWN_BEAMS + beam
        first = lax.bitwise_and(start_ref[glob] - az * OWN_COLS + ARC // 2, COLS - 1)
        for sel in range(SEL):
            column = first + offset_ref[glob, sel]
            real = spec_ref[column, :PULSES]
            imag = spec_ref[column, PULSES:]
            cosine = cos_ref[glob, sel]
            sine = sin_ref[glob, sel]
            rows = pl.ds(SEL + sel, PULSES, stride=SEL)
            wide_ref[0, rows, :] = cosine * real - sine * imag
            wide_ref[1, rows, :] = sine * real + cosine * imag
        last = PULSES * SEL
        for part in range(2):
            for low, high, place in (
                (SEL, SEL + last, SEL),
                (last, last + SEL, 0),
                (SEL, 3 * SEL, SEL + last),
            ):
                value = wide_ref[part, low:high, :]
                snap_ref[beam, part, place : place + high - low, :] = value.astype(BF16)
                if part == 0:
                    minus_ref[place : place + high - low, :] = (-value).astype(BF16)
        weight = mask_ref[beam, 0].astype(F32)
        for half in range(2):
            out = [None, None, None]
            for pair in range(4):
                same, turned = [], []
                for one in range(2):
                    centre = bins_ref[glob, half * 8 + pair * 2 + one]
                    rows = pl.ds(pl.multiple_of(centre * SEL, SEL), DOF)
                    real = snap_ref[beam, 0, rows, :]
                    imag = snap_ref[beam, 1, rows, :]
                    minus = minus_ref[rows, :]
                    same.append(jnp.concatenate([real, imag], 1))
                    turned.append(jnp.concatenate([imag, minus], 1))
                left = jnp.concatenate([same[0], turned[0], same[1], turned[1]], 0)
                right = jnp.concatenate([same[0], same[1], blank], 0)
                gram = lax.dot_general(
                    left, right, TRANSPOSED, preferred_element_type=F32
                )
                packed = jnp.where(
                    lane < DOF,
                    jnp.where(row >= lane, gram[:DOF], gram[DOF : 2 * DOF]),
                    jnp.where(
                        row >= lane - DOF, gram[2 * DOF : 3 * DOF], gram[3 * DOF :]
                    ),
                )
                shift = 2 * DOF * pair % LANES
                if shift:
                    packed = pltpu.roll(packed, shift, 1)
                if pair == 0:
                    out[0] = packed
                elif pair == 1:
                    out[0] = jnp.where(lane >= 96, packed, out[0])
                    out[1] = packed
                elif pair == 2:
                    out[1] = jnp.where(lane >= 64, packed, out[1])
                    out[2] = packed
                else:
                    out[2] = jnp.where(lane >= 32, packed, out[2])
            place = exclusive(beam * 2 + half, mine)
            whole = jnp.concatenate(out, 1) * weight

            @pl.when(place < 8)
            def _():
                keep_ref[lax.rem(place, 8)] = whole

            @pl.when(place >= 8)
            def _():
                send_ref[lax.rem(place, 8)] = whole

        return carry

    lax.fori_loop(0, OWN_BEAMS, one_beam, 0)


def spread(value, index):
    return jnp.take_along_axis(
        value, jnp.full(value.shape, index, jnp.int32), axis=1
    )


def solve_kernel(first_ref, second_ref, marks_ref, out_ref, rows_ref):
    lane = lane_ids(DOF)
    row = lax.broadcasted_iota(jnp.int32, (DOF, LANES), 0)
    total = first_ref[...] + second_ref[...]
    parts = [total[:, LANES * i : LANES * (i + 1)] for i in range(3)]
    for pair in range(4):
        if pair == 0:
            packed = parts[0]
        elif pair == 1:
            packed = jnp.where(
                lane < 32, pltpu.roll(parts[0], 32, 1), pltpu.roll(parts[1], 32, 1)
            )
        elif pair == 2:
            packed = jnp.where(
                lane < 64, pltpu.roll(parts[1], 64, 1), pltpu.roll(parts[2], 64, 1)
            )
        else:
            packed = pltpu.roll(parts[2], 96, 1)
        square = jnp.concatenate([packed, jnp.zeros((LANES - DOF, LANES), F32)], 0)
        turned = jnp.transpose(square)
        for one in range(2):
            here = packed if one == 0 else pltpu.roll(packed, LANES - DOF, 1)
            there = turned[one * DOF : (one + 1) * DOF]
            block_a = jnp.where(row >= lane, here, there)
            block_b = jnp.where(
                row < lane, here, jnp.where(row == lane, 0.0, -there)
            )
            block_b = pltpu.roll(block_b, 64, 1)
            joined = jnp.where(
                lane < DOF,
                block_a,
                jnp.where(
                    lane == DOF,
                    1.0,
                    jnp.where(
                        jnp.logical_and(lane >= 64, lane < 64 + DOF), block_b, 0.0
                    ),
                ),
            )
            rows_ref[pl.ds(pair * 2 + one, DOF, stride=8), :] = joined
    small = lane_ids(8)
    lines = [rows_ref[8 * i : 8 * i + 8, :] for i in range(DOF)]
    diagonal = jnp.zeros((8, LANES), F32)
    for i in range(DOF):
        diagonal = jnp.where(small == i, lines[i], diagonal)
    level = LOADING / DOF * jnp.sum(diagonal, axis=1, keepdims=True)
    level = jnp.broadcast_to(level, (8, LANES))
    for i in range(DOF):
        lines[i] = jnp.where(small == i, lines[i] + level, lines[i])
    for k in range(DOF):
        pivot = lines[k]
        pivot = pivot / spread(pivot, k)
        swapped = pltpu.roll(pivot, 64, 1)
        swapped = jnp.where(small < 64, -swapped, swapped)
        for i in range(DOF):
            if i != k:
                lines[i] = (
                    lines[i]
                    - spread(lines[i], k) * pivot
                    - spread(lines[i], 64 + k) * swapped
                )
        lines[k] = pivot
    found = jnp.zeros((8, LANES), F32)
    for i in range(DOF):
        found = jnp.where(small == i, spread(lines[i], DOF), found)
        found = jnp.where(small == 64 + i, spread(lines[i], 64 + DOF), found)
    quiet = jnp.sum(jnp.where(small < DOF, found, 0.0), axis=1, keepdims=True)
    found = jnp.where(small == 56, jnp.broadcast_to(quiet, (8, LANES)), found)
    out_ref[...] = jnp.where(small == 120, marks_ref[...], found)


def power_kernel(bins_ref, weights_ref, snap_ref, power_ref):
    az = lax.axis_index("az")
    mine = own_group()
    small = lane_ids(8)
    counts = jnp.zeros((8, LANES), F32)
    for place in range(GROUPS):
        counts = counts + weights_ref[place]
    counts = spread(counts, 120) * BLK
    used = jnp.logical_or(
        small < DOF, jnp.logical_and(small >= 64, small < 64 + DOF)
    )
    row = lax.broadcasted_iota(jnp.int32, (2 * 8, LANES), 0)
    for group in range(GROUPS):
        beam = group // 2
        scaled = weights_ref[exclusive(mine, group)] * counts[beam : beam + 1, :]
        quiet = spread(scaled, 56)
        direct = jnp.where(used, scaled, 0.0)
        turned = pltpu.roll(direct, 64, 1)
        turned = jnp.where(small < 64, -turned, turned)
        left = jnp.concatenate([direct, turned], 0).astype(BF16)
        found = jnp.zeros((16, LANES), F32)
        for one in range(8):
            centre = bins_ref[az * OWN_BEAMS + beam, (group % 2) * 8 + one]
            rows = pl.ds(pl.multiple_of(centre * SEL, SEL), 64)
            right = jnp.concatenate(
                [snap_ref[beam, 0, rows, :], snap_ref[beam, 1, rows, :]], 0
            )
            product = jnp.dot(left, right, preferred_element_type=F32)
            found = jnp.where(lax.rem(row, 8) == one, product, found)
        power_ref[group] = (found[:8] * found[:8] + found[8:] * found[8:]) / quiet


def with_halo(block, sides, width, periodic):
    for axis, dim in sides:
        count = lax.axis_size(axis)
        forward = [(i, i + 1) for i in range(count - 1)]
        if periodic:
            forward.append((count - 1, 0))
        backward = [(target, source) for source, target in forward]
        low = lax.ppermute(
            lax.slice_in_dim(block, block.shape[dim] - width, None, axis=dim), axis, forward
        )
        high = lax.ppermute(lax.slice_in_dim(block, 0, width, axis=dim), axis, backward)
        block = jnp.concatenate([low, block, high], axis=dim)
    return block


def swap(value, bit):
    return lax.ppermute(value, "rng", [(i, i ^ (1 << bit)) for i in range(32)])


def halo_columns(echoes):
    ring = [(i, (i + 1) % 8) for i in range(8)]
    low = lax.ppermute(echoes, "az", ring)
    high = lax.ppermute(echoes, "az", [(b, a) for a, b in ring])
    return low, high


SMEM = pl.BlockSpec(memory_space=pltpu.SMEM)
VMEM = pl.BlockSpec(memory_space=pltpu.VMEM)


def body(echoes, arc_start, arc_offsets, doppler_bins, steer_angles, train_mask):
    low, high = halo_columns(echoes)
    marks = jnp.broadcast_to(train_mask.astype(F32), (OWN_BEAMS, LANES))
    marks = marks + swap(marks, 4)
    half = jax.ShapeDtypeStruct((8, DOF, 8 * DOF), F32)
    snaps, keep, send = pl.pallas_call(
        gram_kernel,
        out_shape=(
            jax.ShapeDtypeStruct((OWN_BEAMS, 2, SLOTS * SEL, CELLS), BF16),
            half,
            half,
        ),
        in_specs=[SMEM] * 6 + [VMEM] * 4,
        out_specs=(VMEM, VMEM, VMEM),
        scratch_shapes=[
            pltpu.VMEM((3 * OWN_COLS, 2 * PULSES, CELLS), F32),
            pltpu.VMEM((2, SLOTS * SEL, CELLS), F32),
            pltpu.VMEM((SLOTS * SEL, CELLS), BF16),
        ],
        compiler_params=pltpu.CompilerParams(vmem_limit_bytes=40 * 2**20),
        name="grams",
    )(
        arc_start, arc_offsets, doppler_bins, train_mask,
        jnp.cos(steer_angles), jnp.sin(steer_angles),
        jnp.asarray(table_array()), low, echoes, high,
    )
    part = keep + swap(send, 0)
    for bit, size in ((1, 4), (2, 2), (3, 1)):
        part = part[:size] + swap(part[size:], bit)
    part = part.reshape(DOF, 8 * DOF)
    other = swap(part, 4)
    weights = pl.pallas_call(
        solve_kernel,
        out_shape=jax.ShapeDtypeStruct((8, LANES), F32),
        in_specs=[VMEM] * 3,
        out_specs=VMEM,
        scratch_shapes=[pltpu.VMEM((DOF * 8, LANES), F32)],
        compiler_params=pltpu.CompilerParams(vmem_limit_bytes=32 * 2**20),
        name="solve",
    )(part, other, marks)
    weights = weights[None]
    for bit in (3, 2, 1, 0):
        weights = jnp.concatenate([weights, swap(weights, bit)], 0)
    power = pl.pallas_call(
        power_kernel,
        out_shape=jax.ShapeDtypeStruct((GROUPS, 8, CELLS), F32),
        in_specs=[SMEM, VMEM, VMEM],
        out_specs=VMEM,
        compiler_params=pltpu.CompilerParams(vmem_limit_bytes=32 * 2**20),
        name="power",
    )(doppler_bins, weights, snaps)
    power_map = power.reshape(OWN_BEAMS, DBINS, CELLS)
    beam_ext = with_halo(power_map, (("az", 0),), 1, True)
    full_ext = with_halo(beam_ext, (("rng", 2),), 1, False)
    row_sums = full_ext[:, :, :-2] + full_ext[:, :, 1:-1] + full_ext[:, :, 2:]
    return (row_sums[:-2] + row_sums[1:-1] + row_sums[2:]) / 9.0


def solution(mesh):
    return jax.shard_map(
        body,
        mesh=mesh,
        in_specs=(P(None, "az", None, "rng"), P(), P(), P(), P(), P("az", "rng")),
        out_specs=P("az", None, "rng"),
        check_vma=False,
    )
```

time: 337 us -> 127 us (0.38)
  blocking collectives: 88.4 us -> 0 us
  other arithmetic: 83 us -> 0.99 us
  waiting for transfers between devices: 95.9 us -> 46.5 us
  Pallas kernels: 0 us -> 27.2 us
  starting transfers between devices: 18.4 us -> 45.5 us
  matrix products: 17.3 us -> 0 us
  between operations: 14.2 us -> 0.13 us
  local copies, waits for them, and re-layouts: 17.6 us -> 5.83 us
    unnamed x1 -> x0, blocking collectives: 68.9 us -> none
    another operation x7 -> x0, other arithmetic: 67 us -> none  [the longest x4 37.4 us: weights_from_blocks(): factor = jnp.linalg.cholesky(embedded)]
    reduce_scatter x1 -> x0, waiting for transfers between devices: 64.1 us -> none  [body(): lax.psum_scatter(gram_items, 'rng', scatter_dimension=0, tiled=True)]
    ppermute x0 -> x12, waiting for transfers between devices: none -> 40.1 us  [the longest x10 21 us: swap(): return lax.ppermute(value, 'rng', [(i, i ^ 1 << bit) for i in range(32)])]
    ppermute x0 -> x12, starting transfers between devices: none -> 34 us  [the longest x10 29.7 us: swap(): return lax.ppermute(value, 'rng', [(i, i ^ 1 << bit) for i in range(32)])]
    pallas_call x0 -> x3, Pallas kernels: none -> 27.2 us  [the longest x1 13.3 us: body(): pl.pallas_call(gram_kernel, out_shape=(jax.ShapeDtypeStruct((OWN_BEAMS, 2...]
    all_to_all x1 -> x0, blocking collectives: 19.4 us -> none  [copy_for_each(): lax.all_to_all(jnp.broadcast_to(value[None], (length, *value.shape)), axi...]
    dot_general x26 -> x0, matrix products: 16 us -> none  [the longest x1 7.75 us: body(): jnp.einsum('bkdr,bker->bkde', snapshots * cell_mask[:, None, None, :], sn...]
  transfers between devices with their start and end apart: 8 -> 16, of which waited for: 6 -> 12; matrix products, arithmetic and copies ran while one was open for 3% -> 3% of each run, Pallas kernels for 0% -> 0%
where the time goes in v1:
time: 127 us; the launch traced here: 126 us
  waiting for transfers between devices  46.5 us (37%)
  starting transfers between devices  45.5 us (36%)
  Pallas kernels  27.2 us (21%)
  local copies, waits for them, and re-layouts  5.83 us (5%)
    ppermute x10, starting transfers between devices, swap(): return lax.ppermute(value, 'rng', [(i, i ^ 1 << bit) for i in range(32)])  29.7 us
    ppermute x10, waiting for transfers between devices, swap(): return lax.ppermute(value, 'rng', [(i, i ^ 1 << bit) for i in range(32)])  21 us
    ppermute x1, waiting for transfers between devices, halo_columns(): low = lax.ppermute(echoes, 'az', ring)  16.6 us
    pallas_call x1, Pallas kernels, body(): pl.pallas_call(gram_kernel, out_shape=(jax.ShapeDtypeStruct((OWN_BEAMS, 2...  13.3 us
    pallas_call x1, Pallas kernels, body(): pl.pallas_call(solve_kernel, out_shape=jax.ShapeDtypeStruct((8, LANES), F...  11.5 us
    ppermute x2, starting transfers between devices, with_halo(): lax.ppermute(lax.slice_in_dim(block, block.shape[dim] - width, None, axis...  6 us
    ppermute x2, starting transfers between devices, with_halo(): lax.ppermute(lax.slice_in_dim(block, 0, width, axis=dim), axis, backward)  5.48 us
    ppermute x2, waiting for transfers between devices, with_halo(): lax.ppermute(lax.slice_in_dim(block, 0, width, axis=dim), axis, backward)  5.33 us
  transfers between devices with their start and end apart: 16, of which 12 were waited for; matrix products, arithmetic and copies ran while one was open for 3% of the time, Pallas kernels for 0%

profile of v1, /device:TPU:1, one launch (start us, length us, event | category | flops | bytes accessed | tf_op | source)
XLA Modules:
  0.0 126.1 jit_solution(11444834477156214878)
XLA Ops:
  0.0 2.1 %collective-permute-start = (bf16[2,32,32,128]{3,2,1,0:T(8,128)(2,1)}, bf16[2,32,32,128]{3,2,1,0:T(8,128)(2,1)S(1)}, u32[]{:S(2)}, u32[]{:S(2)}) collective-permute-start(bf16[2,32,32,128]{3,2,1,0:T(8,128)(2,1)} %own_ref.1), channel_id=1, source_target_pairs={{0,32},{32,64},{64,96},{96,128},{128,160},{160,192},{192,224},{224... | collective-permute-start | bytes 1572872 | tf_op jit(solution)/shard_map/ppermute | solution.py:292
  2.1 2.2 %collective-permute-start.1 = (bf16[2,32,32,128]{3,2,1,0:T(8,128)(2,1)}, bf16[2,32,32,128]{3,2,1,0:T(8,128)(2,1)S(1)}, u32[]{:S(2)}, u32[]{:S(2)}) collective-permute-start(bf16[2,32,32,128]{3,2,1,0:T(8,128)(2,1)} %own_ref.1), channel_id=1, source_target_pairs={{32,0},{64,32},{96,64},{128,96},{160,128},{192,160},{224,192},{0,2... | collective-permute-start | bytes 1572872 | tf_op jit(solution)/shard_map/ppermute | solution.py:293
  4.3 0.7 fusion.5
  5.1 0.1 copy.17.cos_ref
  5.2 0.1 copy.18.sin_ref
  5.2 0.8 copy.19.bins_ref
  6.0 0.8 copy.14.offset_ref
  6.8 0.7 copy.16.mask_ref
  7.5 16.6 %collective-permute-done.low_ref = bf16[2,32,32,128]{3,2,1,0:T(8,128)(2,1)S(1)} collective-permute-done((bf16[2,32,32,128]{3,2,1,0:T(8,128)(2,1)}, bf16[2,32,32,128]{3,2,1,0:T(8,128)(2,1)S(1)}, u32[]{:S(2)}, u32[]{:S(2)}) %collective-permute-start) | collective-permute-done | bytes 524320 | tf_op jit(solution)/shard_map/ppermute | solution.py:292
  24.1 2.5 %collective-permute-done.1.high_ref = bf16[2,32,32,128]{3,2,1,0:T(8,128)(2,1)S(1)} collective-permute-done((bf16[2,32,32,128]{3,2,1,0:T(8,128)(2,1)}, bf16[2,32,32,128]{3,2,1,0:T(8,128)(2,1)S(1)}, u32[]{:S(2)}, u32[]{:S(2)}) %collective-permute-start.1) | collective-permute-done | bytes 524320 | tf_op jit(solution)/shard_map/ppermute | solution.py:293
  26.6 1.0 copy-done
  27.7 0.7 copy-done.1
  28.4 0.7 copy-done.2
  29.0 13.3 %grams.1 = (bf16[8,2,560,128]{3,2,1,0:T(8,128)(2,1)S(1)}, f32[8,48,384]{2,1,0:T(8,128)S(1)}, f32[8,48,384]{2,1,0:T(8,128)S(1)}) custom-call(s32[64]{0:T(128)S(1)} %copy-done.2, s32[64,16]{1,0:T(8,128)S(1)} %copy.14.offset_ref, s32[64,16]{1,0:T(8,128)S(1)} %copy.19.bins_ref, s32[8,1]{1,0:T(8,128)S(1)} %copy.16.mask_ref, f32[64,16]{1,0:T(8,128)S(1)} %copy.17.cos_ref, ...), custom_call_target="tpu_custom_call" | custom-call | tf_op jit(solution)/shard_map/grams/pallas_call | solution.py:306
  42.3 0.0 copy-start.3
  42.3 1.4 %collective-permute-start.2 = (f32[8,48,384]{2,1,0:T(8,128)S(1)}, f32[8,48,384]{2,1,0:T(8,128)S(1)}, u32[]{:S(2)}, u32[]{:S(2)}) collective-permute-start(f32[8,48,384]{2,1,0:T(8,128)S(1)} %get-tuple-element.9), channel_id=1, source_target_pairs={{0,1},{1,0},{2,3},{3,2},{4,5},{5,4},{6,7},{7,6},{8,9},{9,8},{10,11... | collective-permute-start | bytes 1769480 | tf_op jit(solution)/shard_map/ppermute | solution.py:287
  43.7 1.6 %collective-permute-done.2 = f32[8,48,384]{2,1,0:T(8,128)S(1)} collective-permute-done((f32[8,48,384]{2,1,0:T(8,128)S(1)}, f32[8,48,384]{2,1,0:T(8,128)S(1)}, u32[]{:S(2)}, u32[]{:S(2)}) %collective-permute-start.2) | collective-permute-done | bytes 589856 | tf_op jit(solution)/shard_map/ppermute | solution.py:287
  45.3 0.1 add.27
  45.4 2.7 %collective-permute-start.3 = (f32[4,48,384]{2,1,0:T(8,128)S(1)}, f32[4,48,384]{2,1,0:T(8,128)S(1)}, u32[]{:S(2)}, u32[]{:S(2)}) collective-permute-start(f32[4,48,384]{2,1,0:T(8,128)S(1)} %slice.71), channel_id=1, source_target_pairs={{0,2},{1,3},{2,0},{3,1},{4,6},{5,7},{6,4},{7,5},{8,10},{9,11},{10,... | collective-permute-start | bytes 884744 | tf_op jit(solution)/shard_map/ppermute | solution.py:287
  48.1 7.1 %collective-permute-done.3 = f32[4,48,384]{2,1,0:T(8,128)S(1)} collective-permute-done((f32[4,48,384]{2,1,0:T(8,128)S(1)}, f32[4,48,384]{2,1,0:T(8,128)S(1)}, u32[]{:S(2)}, u32[]{:S(2)}) %collective-permute-start.3) | collective-permute-done | bytes 294944 | tf_op jit(solution)/shard_map/ppermute | solution.py:287
  55.3 1.7 %collective-permute-start.4 = (f32[2,48,384]{2,1,0:T(8,128)S(1)}, f32[2,48,384]{2,1,0:T(8,128)S(1)}, u32[]{:S(2)}, u32[]{:S(2)}) collective-permute-start(f32[2,48,384]{2,1,0:T(8,128)S(1)} %slice.73), channel_id=1, source_target_pairs={{0,4},{1,5},{2,6},{3,7},{4,0},{5,1},{6,2},{7,3},{8,12},{9,13},{10,... | collective-permute-start | bytes 442376 | tf_op jit(solution)/shard_map/ppermute | solution.py:287
  57.0 2.8 %collective-permute-done.4 = f32[2,48,384]{2,1,0:T(8,128)S(1)} collective-permute-done((f32[2,48,384]{2,1,0:T(8,128)S(1)}, f32[2,48,384]{2,1,0:T(8,128)S(1)}, u32[]{:S(2)}, u32[]{:S(2)}) %collective-permute-start.4) | collective-permute-done | bytes 147488 | tf_op jit(solution)/shard_map/ppermute | solution.py:287
  59.9 3.1 %collective-permute-start.5 = (f32[1,48,384]{2,1,0:T(8,128)S(1)}, f32[1,48,384]{2,1,0:T(8,128)S(1)}, u32[]{:S(2)}, u32[]{:S(2)}) collective-permute-start(f32[1,48,384]{2,1,0:T(8,128)S(1)} %slice.75), channel_id=1, source_target_pairs={{0,8},{1,9},{2,10},{3,11},{4,12},{5,13},{6,14},{7,15},{8,0},{9,1},... | collective-permute-start | bytes 221192 | tf_op jit(solution)/shard_map/ppermute | solution.py:287
  63.0 0.1 broadcast_in_dim.11
  63.1 4.6 %collective-permute-start.7 = (f32[8,128]{1,0:T(8,128)S(1)}, f32[8,128]{1,0:T(8,128)S(1)}, u32[]{:S(2)}, u32[]{:S(2)}) collective-permute-start(f32[8,128]{1,0:T(8,128)S(1)} %broadcast_in_dim.11), channel_id=1, source_target_pairs={{0,16},{1,17},{2,18},{3,19},{4,20},{5,21},{6,22},{7,23},{8,24},{9,... | collective-permute-start | bytes 12296 | tf_op jit(solution)/shard_map/ppermute | solution.py:287
  67.7 3.9 %collective-permute-start.6 = (f32[48,384]{1,0:T(8,128)S(1)}, f32[48,384]{1,0:T(8,128)S(1)}, u32[]{:S(2)}, u32[]{:S(2)}) collective-permute-start(f32[48,384]{1,0:T(8,128)S(1)} %fusion.2.first_ref), channel_id=1, source_target_pairs={{0,16},{1,17},{2,18},{3,19},{4,20},{5,21},{6,22},{7,23},{8,24},{9,... | collective-permute-start | bytes 221192 | tf_op jit(solution)/shard_map/ppermute | solution.py:287
  71.6 0.0 collective-permute-done.7
  71.6 0.1 broadcast_add_fusion.marks_ref
  71.7 3.4 %collective-permute-done.6.second_ref = f32[48,384]{1,0:T(8,128)S(1)} collective-permute-done((f32[48,384]{1,0:T(8,128)S(1)}, f32[48,384]{1,0:T(8,128)S(1)}, u32[]{:S(2)}, u32[]{:S(2)}) %collective-permute-start.6) | collective-permute-done | bytes 73760 | tf_op jit(solution)/shard_map/ppermute | solution.py:287
  75.1 11.5 %solve.1 = f32[8,128]{1,0:T(8,128)S(1)} custom-call(f32[48,384]{1,0:T(8,128)S(1)} %fusion.2.first_ref, f32[48,384]{1,0:T(8,128)S(1)} %collective-permute-done.6.second_ref, f32[8,128]{1,0:T(8,128)S(1)} %broadcast_add_fusion.marks_ref), custom_call_target="tpu_custom_call" | custom-call | tf_op jit(solution)/shard_map/solve/pallas_call | solution.py:332
  86.6 1.3 %collective-permute-start.8 = (f32[1,8,128]{2,1,0:T(8,128)S(1)}, f32[1,8,128]{2,1,0:T(8,128)S(1)}, u32[]{:S(2)}, u32[]{:S(2)}) collective-permute-start(f32[1,8,128]{2,1,0:T(8,128)S(1)} %bitcast.13), channel_id=1, source_target_pairs={{0,8},{1,9},{2,10},{3,11},{4,12},{5,13},{6,14},{7,15},{8,0},{9,1},... | collective-permute-start | bytes 12296 | tf_op jit(solution)/shard_map/ppermute | solution.py:287
  87.9 2.1 %collective-permute-done.8 = f32[1,8,128]{2,1,0:T(8,128)S(1)} collective-permute-done((f32[1,8,128]{2,1,0:T(8,128)S(1)}, f32[1,8,128]{2,1,0:T(8,128)S(1)}, u32[]{:S(2)}, u32[]{:S(2)}) %collective-permute-start.8) | collective-permute-done | bytes 4128 | tf_op jit(solution)/shard_map/ppermute | solution.py:287
  89.9 0.8 collective-permute-start.9
  90.8 1.7 %collective-permute-done.9 = f32[2,8,128]{2,1,0:T(8,128)S(1)} collective-permute-done((f32[2,8,128]{2,1,0:T(8,128)S(1)}, f32[2,8,128]{2,1,0:T(8,128)S(1)}, u32[]{:S(2)}, u32[]{:S(2)}) %collective-permute-start.9) | collective-permute-done | bytes 8224 | tf_op jit(solution)/shard_map/ppermute | solution.py:287
  92.5 2.6 %collective-permute-start.10 = (f32[4,8,128]{2,1,0:T(8,128)S(1)}, f32[4,8,128]{2,1,0:T(8,128)S(1)}, u32[]{:S(2)}, u32[]{:S(2)}) collective-permute-start(f32[4,8,128]{2,1,0:T(8,128)S(1)} %pad_maximum_fusion.8), channel_id=1, source_target_pairs={{0,2},{1,3},{2,0},{3,1},{4,6},{5,7},{6,4},{7,5},{8,10},{9,11},{10,... | collective-permute-start | bytes 49160 | tf_op jit(solution)/shard_map/ppermute | solution.py:287
  95.1 1.5 %collective-permute-done.10 = f32[4,8,128]{2,1,0:T(8,128)S(1)} collective-permute-done((f32[4,8,128]{2,1,0:T(8,128)S(1)}, f32[4,8,128]{2,1,0:T(8,128)S(1)}, u32[]{:S(2)}, u32[]{:S(2)}) %collective-permute-start.10) | collective-permute-done | bytes 16416 | tf_op jit(solution)/shard_map/ppermute | solution.py:287
  96.5 7.5 %collective-permute-start.11 = (f32[8,8,128]{2,1,0:T(8,128)S(1)}, f32[8,8,128]{2,1,0:T(8,128)S(1)}, u32[]{:S(2)}, u32[]{:S(2)}) collective-permute-start(f32[8,8,128]{2,1,0:T(8,128)S(1)} %pad_maximum_fusion.7), channel_id=1, source_target_pairs={{0,1},{1,0},{2,3},{3,2},{4,5},{5,4},{6,7},{7,6},{8,9},{9,8},{10,11... | collective-permute-start | bytes 98312 | tf_op jit(solution)/shard_map/ppermute | solution.py:287
  104.1 0.9 collective-permute-done.11
  104.9 2.4 %power.1 = f32[16,8,128]{2,1,0:T(8,128)S(1)} custom-call(s32[64,16]{1,0:T(8,128)S(1)} %copy.19.bins_ref, f32[16,8,128]{2,1,0:T(8,128)S(1)} %constant_dynamic-update-slice_fusion.weights_ref, bf16[8,2,560,128]{3,2,1,0:T(8,128)(2,1)S(1)} %get-tuple-element.10.snap_ref), custom_call_target="tpu_custom_call" | custom-call | tf_op jit(solution)/shard_map/power/pallas_call | solution.py:344
  107.3 0.1 collective-permute-start.12
  107.4 3.6 %collective-permute-start.13 = (f32[1,16,128]{2,1,0:T(8,128)S(1)}, f32[1,16,128]{2,1,0:T(8,128)S(1)}, u32[]{:S(2)}, u32[]{:S(2)}) collective-permute-start(f32[1,16,128]{2,1,0:T(8,128)S(1)} %get-tuple-element.14), channel_id=1, source_target_pairs={{32,0},{64,32},{96,64},{128,96},{160,128},{192,160},{224,192},{0,2... | collective-permute-start | bytes 24584 | tf_op jit(solution)/shard_map/ppermute | solution.py:281
  111.0 1.0 collective-permute-done.12
  112.0 0.1 fusion.4
  112.1 5.9 %collective-permute-start.14 = (f32[10,16,1]{2,1,0:T(8,128)S(1)}, f32[10,16,1]{2,1,0:T(8,128)S(1)}, u32[]{:S(2)}, u32[]{:S(2)}) collective-permute-start(f32[10,16,1]{2,1,0:T(8,128)S(1)} %get-tuple-element.11), channel_id=1, source_target_pairs={{0,1},{1,2},{2,3},{3,4},{4,5},{5,6},{6,7},{7,8},{8,9},{9,10},{10,1... | collective-permute-start | bytes 1928 | tf_op jit(solution)/shard_map/ppermute | solution.py:278
  118.1 1.9 %collective-permute-start.15 = (f32[10,16,1]{2,1,0:T(8,128)S(1)}, f32[10,16,1]{2,1,0:T(8,128)S(1)}, u32[]{:S(2)}, u32[]{:S(2)}) collective-permute-start(f32[10,16,1]{2,1,0:T(8,128)S(1)} %get-tuple-element.12), channel_id=1, source_target_pairs={{1,0},{2,1},{3,2},{4,3},{5,4},{6,5},{7,6},{8,7},{9,8},{10,9},{11,1... | collective-permute-start | bytes 1928 | tf_op jit(solution)/shard_map/ppermute | solution.py:281
  120.0 5.3 %collective-permute-done.15 = f32[10,16,1]{2,1,0:T(8,128)S(1)} collective-permute-done((f32[10,16,1]{2,1,0:T(8,128)S(1)}, f32[10,16,1]{2,1,0:T(8,128)S(1)}, u32[]{:S(2)}, u32[]{:S(2)}) %collective-permute-start.15) | collective-permute-done | bytes 672 | tf_op jit(solution)/shard_map/ppermute | solution.py:281
  125.3 0.1 fusion
  125.5 0.6 fusion.3
  (24 shorter events, 0.1 us)
Async XLA Ops:
  0.0 24.1 %collective-permute-start = (bf16[2,32,32,128]{3,2,1,0:T(8,128)(2,1)}, bf16[2,32,32,128]{3,2,1,0:T(8,128)(2,1)S(1)}, u32[]{:S(2)}, u32[]{:S(2)}) collective-permute-start(bf16[2,32,32,128]{3,2,1,0:T(8,128)(2,1)} %own_ref.1), channel_id=1, source_target_pairs={{0,32},{32,64},{64,96},{96,128},{128,160},{160,192},{192,224},{224... | collective-permute-start | bytes 1572872 | tf_op jit(solution)/shard_map/ppermute | solution.py:292
  2.1 24.5 %collective-permute-start.1 = (bf16[2,32,32,128]{3,2,1,0:T(8,128)(2,1)}, bf16[2,32,32,128]{3,2,1,0:T(8,128)(2,1)S(1)}, u32[]{:S(2)}, u32[]{:S(2)}) collective-permute-start(bf16[2,32,32,128]{3,2,1,0:T(8,128)(2,1)} %own_ref.1), channel_id=1, source_target_pairs={{32,0},{64,32},{96,64},{128,96},{160,128},{192,160},{224,192},{0,2... | collective-permute-start | bytes 1572872 | tf_op jit(solution)/shard_map/ppermute | solution.py:293
  26.6 1.0 copy-start
  27.7 0.7 copy-start.1
  28.4 0.7 copy-start.2
  42.3 20.7 %copy-start.3 = (s32[8,1]{0,1:T(1,128)S(1)}, s32[8,1]{0,1:T(1,128)}, u32[]{:S(2)}) copy-start(s32[8,1]{0,1:T(1,128)} %param.12) | copy-start | bytes 100
  42.3 3.0 %collective-permute-start.2 = (f32[8,48,384]{2,1,0:T(8,128)S(1)}, f32[8,48,384]{2,1,0:T(8,128)S(1)}, u32[]{:S(2)}, u32[]{:S(2)}) collective-permute-start(f32[8,48,384]{2,1,0:T(8,128)S(1)} %get-tuple-element.9), channel_id=1, source_target_pairs={{0,1},{1,0},{2,3},{3,2},{4,5},{5,4},{6,7},{7,6},{8,9},{9,8},{10,11... | collective-permute-start | bytes 1769480 | tf_op jit(solution)/shard_map/ppermute | solution.py:287
  45.4 9.8 %collective-permute-start.3 = (f32[4,48,384]{2,1,0:T(8,128)S(1)}, f32[4,48,384]{2,1,0:T(8,128)S(1)}, u32[]{:S(2)}, u32[]{:S(2)}) collective-permute-start(f32[4,48,384]{2,1,0:T(8,128)S(1)} %slice.71), channel_id=1, source_target_pairs={{0,2},{1,3},{2,0},{3,1},{4,6},{5,7},{6,4},{7,5},{8,10},{9,11},{10,... | collective-permute-start | bytes 884744 | tf_op jit(solution)/shard_map/ppermute | solution.py:287
  55.3 4.6 %collective-permute-start.4 = (f32[2,48,384]{2,1,0:T(8,128)S(1)}, f32[2,48,384]{2,1,0:T(8,128)S(1)}, u32[]{:S(2)}, u32[]{:S(2)}) collective-permute-start(f32[2,48,384]{2,1,0:T(8,128)S(1)} %slice.73), channel_id=1, source_target_pairs={{0,4},{1,5},{2,6},{3,7},{4,0},{5,1},{6,2},{7,3},{8,12},{9,13},{10,... | collective-permute-start | bytes 442376 | tf_op jit(solution)/shard_map/ppermute | solution.py:287
  59.9 7.8 %collective-permute-start.5 = (f32[1,48,384]{2,1,0:T(8,128)S(1)}, f32[1,48,384]{2,1,0:T(8,128)S(1)}, u32[]{:S(2)}, u32[]{:S(2)}) collective-permute-start(f32[1,48,384]{2,1,0:T(8,128)S(1)} %slice.75), channel_id=1, source_target_pairs={{0,8},{1,9},{2,10},{3,11},{4,12},{5,13},{6,14},{7,15},{8,0},{9,1},... | collective-permute-start | bytes 221192 | tf_op jit(solution)/shard_map/ppermute | solution.py:287
  63.1 8.6 %collective-permute-start.7 = (f32[8,128]{1,0:T(8,128)S(1)}, f32[8,128]{1,0:T(8,128)S(1)}, u32[]{:S(2)}, u32[]{:S(2)}) collective-permute-start(f32[8,128]{1,0:T(8,128)S(1)} %broadcast_in_dim.11), channel_id=1, source_target_pairs={{0,16},{1,17},{2,18},{3,19},{4,20},{5,21},{6,22},{7,23},{8,24},{9,... | collective-permute-start | bytes 12296 | tf_op jit(solution)/shard_map/ppermute | solution.py:287
  67.7 7.4 %collective-permute-start.6 = (f32[48,384]{1,0:T(8,128)S(1)}, f32[48,384]{1,0:T(8,128)S(1)}, u32[]{:S(2)}, u32[]{:S(2)}) collective-permute-start(f32[48,384]{1,0:T(8,128)S(1)} %fusion.2.first_ref), channel_id=1, source_target_pairs={{0,16},{1,17},{2,18},{3,19},{4,20},{5,21},{6,22},{7,23},{8,24},{9,... | collective-permute-start | bytes 221192 | tf_op jit(solution)/shard_map/ppermute | solution.py:287
  86.6 3.4 %collective-permute-start.8 = (f32[1,8,128]{2,1,0:T(8,128)S(1)}, f32[1,8,128]{2,1,0:T(8,128)S(1)}, u32[]{:S(2)}, u32[]{:S(2)}) collective-permute-start(f32[1,8,128]{2,1,0:T(8,128)S(1)} %bitcast.13), channel_id=1, source_target_pairs={{0,8},{1,9},{2,10},{3,11},{4,12},{5,13},{6,14},{7,15},{8,0},{9,1},... | collective-permute-start | bytes 12296 | tf_op jit(solution)/shard_map/ppermute | solution.py:287
  89.9 2.5 %collective-permute-start.9 = (f32[2,8,128]{2,1,0:T(8,128)S(1)}, f32[2,8,128]{2,1,0:T(8,128)S(1)}, u32[]{:S(2)}, u32[]{:S(2)}) collective-permute-start(f32[2,8,128]{2,1,0:T(8,128)S(1)} %pad_maximum_fusion.9), channel_id=1, source_target_pairs={{0,4},{1,5},{2,6},{3,7},{4,0},{5,1},{6,2},{7,3},{8,12},{9,13},{10,... | collective-permute-start | bytes 24584 | tf_op jit(solution)/shard_map/ppermute | solution.py:287
  92.5 4.1 %collective-permute-start.10 = (f32[4,8,128]{2,1,0:T(8,128)S(1)}, f32[4,8,128]{2,1,0:T(8,128)S(1)}, u32[]{:S(2)}, u32[]{:S(2)}) collective-permute-start(f32[4,8,128]{2,1,0:T(8,128)S(1)} %pad_maximum_fusion.8), channel_id=1, source_target_pairs={{0,2},{1,3},{2,0},{3,1},{4,6},{5,7},{6,4},{7,5},{8,10},{9,11},{10,... | collective-permute-start | bytes 49160 | tf_op jit(solution)/shard_map/ppermute | solution.py:287
  96.5 8.4 %collective-permute-start.11 = (f32[8,8,128]{2,1,0:T(8,128)S(1)}, f32[8,8,128]{2,1,0:T(8,128)S(1)}, u32[]{:S(2)}, u32[]{:S(2)}) collective-permute-start(f32[8,8,128]{2,1,0:T(8,128)S(1)} %pad_maximum_fusion.7), channel_id=1, source_target_pairs={{0,1},{1,0},{2,3},{3,2},{4,5},{5,4},{6,7},{7,6},{8,9},{9,8},{10,11... | collective-permute-start | bytes 98312 | tf_op jit(solution)/shard_map/ppermute | solution.py:287
  107.3 4.7 %collective-permute-start.12 = (f32[1,16,128]{2,1,0:T(8,128)S(1)}, f32[1,16,128]{2,1,0:T(8,128)S(1)}, u32[]{:S(2)}, u32[]{:S(2)}) collective-permute-start(f32[1,16,128]{2,1,0:T(8,128)S(1)} %get-tuple-element.13), channel_id=1, source_target_pairs={{0,32},{32,64},{64,96},{96,128},{128,160},{160,192},{192,224},{224... | collective-permute-start | bytes 24584 | tf_op jit(solution)/shard_map/ppermute | solution.py:278
  107.4 4.6 %collective-permute-start.13 = (f32[1,16,128]{2,1,0:T(8,128)S(1)}, f32[1,16,128]{2,1,0:T(8,128)S(1)}, u32[]{:S(2)}, u32[]{:S(2)}) collective-permute-start(f32[1,16,128]{2,1,0:T(8,128)S(1)} %get-tuple-element.14), channel_id=1, source_target_pairs={{32,0},{64,32},{96,64},{128,96},{160,128},{192,160},{224,192},{0,2... | collective-permute-start | bytes 24584 | tf_op jit(solution)/shard_map/ppermute | solution.py:281
  112.1 7.9 %collective-permute-start.14 = (f32[10,16,1]{2,1,0:T(8,128)S(1)}, f32[10,16,1]{2,1,0:T(8,128)S(1)}, u32[]{:S(2)}, u32[]{:S(2)}) collective-permute-start(f32[10,16,1]{2,1,0:T(8,128)S(1)} %get-tuple-element.11), channel_id=1, source_target_pairs={{0,1},{1,2},{2,3},{3,4},{4,5},{5,6},{6,7},{7,8},{8,9},{9,10},{10,1... | collective-permute-start | bytes 1928 | tf_op jit(solution)/shard_map/ppermute | solution.py:278
  118.1 7.3 %collective-permute-start.15 = (f32[10,16,1]{2,1,0:T(8,128)S(1)}, f32[10,16,1]{2,1,0:T(8,128)S(1)}, u32[]{:S(2)}, u32[]{:S(2)}) collective-permute-start(f32[10,16,1]{2,1,0:T(8,128)S(1)} %get-tuple-element.12), channel_id=1, source_target_pairs={{1,0},{2,1},{3,2},{4,3},{5,4},{6,5},{7,6},{8,7},{9,8},{10,9},{11,1... | collective-permute-start | bytes 1928 | tf_op jit(solution)/shard_map/ppermute | solution.py:281

commit v2 on v1

--- a/solution.py
+++ b/solution.py
@@ -53,30 +53,48 @@
     return lax.bitwise_xor(left, right)
 
 
+def spectra(table, ref, pair, out_ref, base):
+    blocks = [
+        jnp.concatenate([ref[0, 2 * pair + one], ref[1, 2 * pair + one]], 0)
+        for one in range(2)
+    ]
+    both = jnp.dot(table, jnp.concatenate(blocks, 1), preferred_element_type=F32)
+    out_ref[base + 2 * pair] = both[:, :CELLS]
+    out_ref[base + 2 * pair + 1] = both[:, CELLS:]
+
+
+def own_kernel(table_ref, own_ref, spec_ref, passed_ref):
+    table = table_ref[...]
+    passed_ref[...] = table
+
+    def step(index, carry):
+        for one in range(4):
+            spectra(table, own_ref, 4 * index + one, spec_ref, 0)
+        return carry
+
+    lax.fori_loop(0, OWN_COLS // 8, step, 0)
+
+
 def gram_kernel(
-    start_ref, offset_ref, bins_ref, mask_ref, cos_ref, sin_ref,
-    table_ref, low_ref, own_ref, high_ref,
-    snap_ref, keep_ref, send_ref,
+    column_ref, bins_ref, mask_ref, cos_ref, sin_ref,
+    table_ref, low_ref, own_ref, high_ref, marks_ref,
+    snap_ref, keep_ref, send_ref, passed_ref,
     spec_ref, wide_ref, minus_ref,
 ):
     az = lax.axis_index("az")
     mine = own_group()
     table = table_ref[...]
-
-    def transform(pair, carry):
-        for part, ref in enumerate((low_ref, own_ref, high_ref)):
-            blocks = [
-                jnp.concatenate([ref[0, 2 * pair + one], ref[1, 2 * pair + one]], 0)
-                for one in range(2)
-            ]
-            both = jnp.dot(
-                table, jnp.concatenate(blocks, 1), preferred_element_type=F32
-            )
-            spec_ref[part * OWN_COLS + 2 * pair] = both[:, :CELLS]
-            spec_ref[part * OWN_COLS + 2 * pair + 1] = both[:, CELLS:]
+    passed_ref[...] = marks_ref[...]
+
+    def transform(index, carry):
+        for one in range(2):
+            spectra(table, low_ref, 2 * index + one, spec_ref, 0)
+            spectra(table, high_ref, 2 * index + one, spec_ref, 2 * OWN_COLS)
+        for one in range(4):
+            spec_ref[OWN_COLS + 4 * index + one] = own_ref[4 * index + one]
         return carry
 
-    lax.fori_loop(0, OWN_COLS // 2, transform, 0)
+    lax.fori_loop(0, OWN_COLS // 4, transform, 0)
 
     lane = lane_ids(DOF)
     row = lax.broadcasted_iota(jnp.int32, (DOF, LANES), 0)
@@ -84,9 +102,8 @@
 
     def one_beam(beam, carry):
         glob = az * OWN_BEAMS + beam
-        first = lax.bitwise_and(start_ref[glob] - az * OWN_COLS + ARC // 2, COLS - 1)
         for sel in range(SEL):
-            column = first + offset_ref[glob, sel]
+            column = column_ref[glob, sel]
             real = spec_ref[column, :PULSES]
             imag = spec_ref[column, PULSES:]
             cosine = cos_ref[glob, sel]
@@ -165,11 +182,16 @@
     )
 
 
-def solve_kernel(first_ref, second_ref, marks_ref, out_ref, rows_ref):
+def solve_kernel(first_ref, second_ref, marks_ref, out_ref, turn_ref):
     lane = lane_ids(DOF)
     row = lax.broadcasted_iota(jnp.int32, (DOF, LANES), 0)
+    slot = lax.div(lane, SEL)
+    lower = row >= lane
+    same = row == lane
     total = first_ref[...] + second_ref[...]
     parts = [total[:, LANES * i : LANES * (i + 1)] for i in range(3)]
+    block_a = [None] * BINS
+    block_b = [None] * BINS
     for pair in range(4):
         if pair == 0:
             packed = parts[0]
@@ -186,53 +208,90 @@
         square = jnp.concatenate([packed, jnp.zeros((LANES - DOF, LANES), F32)], 0)
         turned = jnp.transpose(square)
         for one in range(2):
+            item = pair * 2 + one
             here = packed if one == 0 else pltpu.roll(packed, LANES - DOF, 1)
             there = turned[one * DOF : (one + 1) * DOF]
-            block_a = jnp.where(row >= lane, here, there)
-            block_b = jnp.where(
-                row < lane, here, jnp.where(row == lane, 0.0, -there)
+            value_a = jnp.where(lower, here, there)
+            value_b = jnp.where(lower, jnp.where(same, 0.0, -there), here)
+            if item:
+                value_a = pltpu.roll(value_a, SEL * item, 1)
+                value_b = pltpu.roll(value_b, SEL * item, 1)
+            for part in range(BINS):
+                if item == 0:
+                    block_a[part] = value_a
+                    block_b[part] = value_b
+                else:
+                    chosen = slot == (item + part) % 8
+                    block_a[part] = jnp.where(chosen, value_a, block_a[part])
+                    block_b[part] = jnp.where(chosen, value_b, block_b[part])
+    for part in range(1, BINS):
+        block_a[part] = pltpu.roll(block_a[part], LANES - SEL * part, 1)
+        block_b[part] = pltpu.roll(block_b[part], LANES - SEL * part, 1)
+    small = lane_ids(8)
+    line = lax.broadcasted_iota(jnp.int32, (8, LANES), 0)
+    place = lax.rem(small, SEL)
+    base = small - place
+    diagonal = jnp.zeros((8, LANES), F32)
+    masks = []
+    for group in range(DOF // 8):
+        masks.append(place == line + group % 2 * 8)
+        diagonal = diagonal + jnp.where(
+            masks[group], block_a[group // 2][8 * group : 8 * group + 8], 0.0
+        )
+    level = jnp.sum(diagonal, axis=0, keepdims=True)
+    level = jnp.broadcast_to(level, (8, LANES))
+    for step in (1, 2, 4, 8):
+        partner = base + lax.rem(place + step, SEL)
+        level = level + jnp.take_along_axis(level, partner, axis=1)
+    level = LOADING / DOF * level
+    real = [[None] * 4 for _ in range(6)]
+    imag = [[None] * 4 for _ in range(6)]
+    for group in range(6):
+        for part in range(BINS):
+            real[group][part] = block_a[part][8 * group : 8 * group + 8]
+            imag[group][part] = block_b[part][8 * group : 8 * group + 8]
+        real[group][group // 2] = jnp.where(
+            masks[group], real[group][group // 2] + level, real[group][group // 2]
+        )
+        real[group][3] = jnp.ones((8, LANES), F32)
+        imag[group][3] = jnp.zeros((8, LANES), F32)
+    inverse = [jnp.ones((8, LANES), F32)] * 6
+    for k in range(DOF):
+        group, inner, part = k // 8, k % 8, k // SEL
+        index = base + k % SEL
+        mult_re = [jnp.take_along_axis(real[i][part], index, axis=1) for i in range(6)]
+        mult_im = [jnp.take_along_axis(imag[i][part], index, axis=1) for i in range(6)]
+        pivot = jnp.broadcast_to(mult_re[group][inner : inner + 1], (8, LANES))
+        pivot = 1.0 / pivot
+        here = line == inner
+        mult_re[group] = jnp.where(here, 0.0, mult_re[group])
+        mult_im[group] = jnp.where(here, 0.0, mult_im[group])
+        inverse[group] = jnp.where(here, pivot, inverse[group])
+        for block in (*range(part, BINS), 3):
+            row_re = pivot * jnp.broadcast_to(
+                real[group][block][inner : inner + 1], (8, LANES)
             )
-            block_b = pltpu.roll(block_b, 64, 1)
-            joined = jnp.where(
-                lane < DOF,
-                block_a,
-                jnp.where(
-                    lane == DOF,
-                    1.0,
-                    jnp.where(
-                        jnp.logical_and(lane >= 64, lane < 64 + DOF), block_b, 0.0
-                    ),
-                ),
+            row_im = pivot * jnp.broadcast_to(
+                imag[group][block][inner : inner + 1], (8, LANES)
             )
-            rows_ref[pl.ds(pair * 2 + one, DOF, stride=8), :] = joined
-    small = lane_ids(8)
-    lines = [rows_ref[8 * i : 8 * i + 8, :] for i in range(DOF)]
-    diagonal = jnp.zeros((8, LANES), F32)
-    for i in range(DOF):
-        diagonal = jnp.where(small == i, lines[i], diagonal)
-    level = LOADING / DOF * jnp.sum(diagonal, axis=1, keepdims=True)
-    level = jnp.broadcast_to(level, (8, LANES))
-    for i in range(DOF):
-        lines[i] = jnp.where(small == i, lines[i] + level, lines[i])
-    for k in range(DOF):
-        pivot = lines[k]
-        pivot = pivot / spread(pivot, k)
-        swapped = pltpu.roll(pivot, 64, 1)
-        swapped = jnp.where(small < 64, -swapped, swapped)
-        for i in range(DOF):
-            if i != k:
-                lines[i] = (
-                    lines[i]
-                    - spread(lines[i], k) * pivot
-                    - spread(lines[i], 64 + k) * swapped
+            for i in range(6):
+                real[i][block] = (
+                    real[i][block] - mult_re[i] * row_re + mult_im[i] * row_im
                 )
-        lines[k] = pivot
-    found = jnp.zeros((8, LANES), F32)
-    for i in range(DOF):
-        found = jnp.where(small == i, spread(lines[i], DOF), found)
-        found = jnp.where(small == 64 + i, spread(lines[i], 64 + DOF), found)
-    quiet = jnp.sum(jnp.where(small < DOF, found, 0.0), axis=1, keepdims=True)
-    found = jnp.where(small == 56, jnp.broadcast_to(quiet, (8, LANES)), found)
+                imag[i][block] = (
+                    imag[i][block] - mult_re[i] * row_im - mult_im[i] * row_re
+                )
+    gap = jnp.zeros((SEL, LANES), F32)
+    found_re = [real[i][3] * inverse[i] for i in range(6)]
+    found_im = [imag[i][3] * inverse[i] for i in range(6)]
+    quiet = found_re[0]
+    for i in range(1, 6):
+        quiet = quiet + found_re[i]
+    quiet = jnp.broadcast_to(jnp.sum(quiet, axis=0, keepdims=True), (SEL, LANES))
+    turn_ref[...] = jnp.transpose(
+        jnp.concatenate([*found_re, quiet, *found_im, gap], 0)
+    )
+    found = turn_ref[pl.ds(0, 8, stride=SEL), :]
     out_ref[...] = jnp.where(small == 120, marks_ref[...], found)
 
 
@@ -283,8 +342,8 @@
     return block
 
 
-def swap(value, bit):
-    return lax.ppermute(value, "rng", [(i, i ^ (1 << bit)) for i in range(32)])
+def swap(value, turn):
+    return lax.ppermute(value, "rng", [(i, i ^ turn) for i in range(32)])
 
 
 def halo_columns(echoes):
@@ -301,17 +360,30 @@
 def body(echoes, arc_start, arc_offsets, doppler_bins, steer_angles, train_mask):
     low, high = halo_columns(echoes)
     marks = jnp.broadcast_to(train_mask.astype(F32), (OWN_BEAMS, LANES))
-    marks = marks + swap(marks, 4)
+    marks = marks + swap(marks, 16)
     half = jax.ShapeDtypeStruct((8, DOF, 8 * DOF), F32)
-    snaps, keep, send = pl.pallas_call(
+    first = (arc_start - lax.axis_index("az") * OWN_COLS + ARC // 2) % COLS
+    spec, table = pl.pallas_call(
+        own_kernel,
+        out_shape=(
+            jax.ShapeDtypeStruct((OWN_COLS, 2 * PULSES, CELLS), F32),
+            jax.ShapeDtypeStruct((2 * PULSES, 2 * PULSES), BF16),
+        ),
+        in_specs=[VMEM, VMEM],
+        out_specs=(VMEM, VMEM),
+        compiler_params=pltpu.CompilerParams(vmem_limit_bytes=32 * 2**20),
+        name="spectra",
+    )(jnp.asarray(table_array()), echoes)
+    snaps, keep, send, marks = pl.pallas_call(
         gram_kernel,
         out_shape=(
             jax.ShapeDtypeStruct((OWN_BEAMS, 2, SLOTS * SEL, CELLS), BF16),
             half,
             half,
+            jax.ShapeDtypeStruct((OWN_BEAMS, LANES), F32),
         ),
-        in_specs=[SMEM] * 6 + [VMEM] * 4,
-        out_specs=(VMEM, VMEM, VMEM),
+        in_specs=[SMEM] * 5 + [VMEM] * 5,
+        out_specs=(VMEM, VMEM, VMEM, VMEM),
         scratch_shapes=[
             pltpu.VMEM((3 * OWN_COLS, 2 * PULSES, CELLS), F32),
             pltpu.VMEM((2, SLOTS * SEL, CELLS), F32),
@@ -320,27 +392,26 @@
         compiler_params=pltpu.CompilerParams(vmem_limit_bytes=40 * 2**20),
         name="grams",
     )(
-        arc_start, arc_offsets, doppler_bins, train_mask,
+        first[:, None] + arc_offsets, doppler_bins, train_mask,
         jnp.cos(steer_angles), jnp.sin(steer_angles),
-        jnp.asarray(table_array()), low, echoes, high,
+        table, low, spec, high, marks,
     )
-    part = keep + swap(send, 0)
-    for bit, size in ((1, 4), (2, 2), (3, 1)):
-        part = part[:size] + swap(part[size:], bit)
-    part = part.reshape(DOF, 8 * DOF)
-    other = swap(part, 4)
+    part = keep + swap(send, 1)
+    part = part[:2] + swap(part[2:4], 4) + swap(part[4:6], 2) + swap(part[6:], 6)
+    part = part[0] + swap(part[1], 8)
+    other = swap(part, 16)
     weights = pl.pallas_call(
         solve_kernel,
         out_shape=jax.ShapeDtypeStruct((8, LANES), F32),
         in_specs=[VMEM] * 3,
         out_specs=VMEM,
-        scratch_shapes=[pltpu.VMEM((DOF * 8, LANES), F32)],
+        scratch_shapes=[pltpu.VMEM((LANES, LANES), F32)],
         compiler_params=pltpu.CompilerParams(vmem_limit_bytes=32 * 2**20),
         name="solve",
     )(part, other, marks)
     weights = weights[None]
-    for bit in (3, 2, 1, 0):
-        weights = jnp.concatenate([weights, swap(weights, bit)], 0)
+    for turn in (8, 4, 2, 1):
+        weights = jnp.concatenate([weights, swap(weights, turn)], 0)
     power = pl.pallas_call(
         power_kernel,
         out_shape=jax.ShapeDtypeStruct((GROUPS, 8, CELLS), F32),

time: 127 us -> 114 us (0.90)
  the two profiles are of different devices: /device:TPU:1 before, /device:TPU:127 now
where the time goes in v2:
time: 114 us; the launch traced here: 113 us
  waiting for transfers between devices  44.6 us (39%)
  starting transfers between devices  40.6 us (36%)
  Pallas kernels  20.2 us (18%)
  local copies, waits for them, and re-layouts  5.17 us (5%)
  other arithmetic  2.36 us (2%)
    ppermute x11, starting transfers between devices, swap(): return lax.ppermute(value, 'rng', [(i, i ^ turn) for i in range(32)])  25.6 us
    ppermute x11, waiting for transfers between devices, swap(): return lax.ppermute(value, 'rng', [(i, i ^ turn) for i in range(32)])  24.5 us
    pallas_call x1, Pallas kernels, body(): pl.pallas_call(gram_kernel, out_shape=(jax.ShapeDtypeStruct((OWN_BEAMS, 2...  12.1 us
    ppermute x2, waiting for transfers between devices, with_halo(): lax.ppermute(lax.slice_in_dim(block, 0, width, axis=dim), axis, backward)  9.63 us
    ppermute x2, starting transfers between devices, with_halo(): lax.ppermute(lax.slice_in_dim(block, block.shape[dim] - width, None, axis...  8.12 us
    ppermute x1, waiting for transfers between devices, halo_columns(): high = lax.ppermute(echoes, 'az', [(b, a) for a, b in ring])  7.62 us
    pallas_call x1, Pallas kernels, body(): pl.pallas_call(solve_kernel, out_shape=jax.ShapeDtypeStruct((8, LANES), F...  5.02 us
    unnamed x11, local copies, waits for them, and re-layouts  4.06 us
  transfers between devices with their start and end apart: 17, of which 15 were waited for; matrix products, arithmetic and copies ran while one was open for 4% of the time, Pallas kernels for 1%

profile of v2, /device:TPU:127, one launch (start us, length us, event | category | flops | bytes accessed | tf_op | source)
XLA Modules:
  0.0 113.1 jit_solution(18271930202747946245)
XLA Ops:
  0.0 0.5 collective-permute-start.1
  0.5 3.1 %collective-permute-start = (bf16[2,32,32,128]{3,2,1,0:T(8,128)(2,1)}, bf16[2,32,32,128]{3,2,1,0:T(8,128)(2,1)S(1)}, u32[]{:S(2)}, u32[]{:S(2)}) collective-permute-start(bf16[2,32,32,128]{3,2,1,0:T(8,128)(2,1)} %own_ref.1), channel_id=1, source_target_pairs={{0,32},{32,64},{64,96},{96,128},{128,160},{160,192},{192,224},{224... | collective-permute-start | bytes 1572872 | tf_op jit(solution)/shard_map/ppermute | solution.py:351
  3.6 0.7 convert_bitcast_fusion
  4.3 4.2 %collective-permute-start.2 = (f32[8,128]{1,0:T(8,128)S(1)}, f32[8,128]{1,0:T(8,128)S(1)}, u32[]{:S(2)}, u32[]{:S(2)}) collective-permute-start(f32[8,128]{1,0:T(8,128)S(1)} %broadcast_in_dim.12), channel_id=1, source_target_pairs={{0,16},{1,17},{2,18},{3,19},{4,20},{5,21},{6,22},{7,23},{8,24},{9,... | collective-permute-start | bytes 12296 | tf_op jit(solution)/shard_map/ppermute | solution.py:346
  8.5 0.8 copy.15
  9.3 0.7 and_select_fusion
  10.0 0.7 fusion.9
  10.8 0.7 copy.17.mask_ref
  11.5 0.1 copy.19.sin_ref
  11.6 0.8 copy.20.bins_ref
  12.4 0.1 copy.18.cos_ref
  12.5 1.0 copy-done
  13.5 0.7 copy-done.1
  14.2 0.7 spectra.1
  15.0 7.6 %collective-permute-done.1.high_ref = bf16[2,32,32,128]{3,2,1,0:T(8,128)(2,1)S(1)} collective-permute-done((bf16[2,32,32,128]{3,2,1,0:T(8,128)(2,1)}, bf16[2,32,32,128]{3,2,1,0:T(8,128)(2,1)S(1)}, u32[]{:S(2)}, u32[]{:S(2)}) %collective-permute-start.1) | collective-permute-done | bytes 524320 | tf_op jit(solution)/shard_map/ppermute | solution.py:352
  22.6 1.8 %collective-permute-done.low_ref = bf16[2,32,32,128]{3,2,1,0:T(8,128)(2,1)S(1)} collective-permute-done((bf16[2,32,32,128]{3,2,1,0:T(8,128)(2,1)}, bf16[2,32,32,128]{3,2,1,0:T(8,128)(2,1)S(1)}, u32[]{:S(2)}, u32[]{:S(2)}) %collective-permute-start) | collective-permute-done | bytes 524320 | tf_op jit(solution)/shard_map/ppermute | solution.py:351
  24.4 12.1 %grams.1 = (bf16[8,2,560,128]{3,2,1,0:T(8,128)(2,1)S(1)}, f32[8,48,384]{2,1,0:T(8,128)S(1)}, f32[8,48,384]{2,1,0:T(8,128)S(1)}, f32[8,128]{1,0:T(8,128)S(1)}) custom-call(s32[64,16]{1,0:T(8,128)S(1)} %broadcast_add_fusion.column_ref, s32[64,16]{1,0:T(8,128)S(1)} %copy.20.bins_ref, s32[8,1]{1,0:T(8,128)S(1)} %copy.17.mask_ref, f32[64,16]{1,0:T(8,128)S(1)} %copy.18.cos_ref, ...), custom_call_target="tpu_custom_call" | custom-call | tf_op jit(solution)/shard_map/grams/pallas_call | solution.py:377
  36.5 2.0 %collective-permute-start.3 = (f32[8,48,384]{2,1,0:T(8,128)S(1)}, f32[8,48,384]{2,1,0:T(8,128)S(1)}, u32[]{:S(2)}, u32[]{:S(2)}) collective-permute-start(f32[8,48,384]{2,1,0:T(8,128)S(1)} %get-tuple-element.14), channel_id=1, source_target_pairs={{0,1},{1,0},{2,3},{3,2},{4,5},{5,4},{6,7},{7,6},{8,9},{9,8},{10,11... | collective-permute-start | bytes 1769480 | tf_op jit(solution)/shard_map/ppermute | solution.py:346
  38.4 1.6 %collective-permute-done.3 = f32[8,48,384]{2,1,0:T(8,128)S(1)} collective-permute-done((f32[8,48,384]{2,1,0:T(8,128)S(1)}, f32[8,48,384]{2,1,0:T(8,128)S(1)}, u32[]{:S(2)}, u32[]{:S(2)}) %collective-permute-start.3) | collective-permute-done | bytes 589856 | tf_op jit(solution)/shard_map/ppermute | solution.py:346
  40.2 0.1 collective-permute-start.4
  40.3 2.0 %collective-permute-start.6 = (f32[2,48,384]{2,1,0:T(8,128)S(1)}, f32[2,48,384]{2,1,0:T(8,128)S(1)}, u32[]{:S(2)}, u32[]{:S(2)}) collective-permute-start(f32[2,48,384]{2,1,0:T(8,128)S(1)} %get-tuple-element.18), channel_id=1, source_target_pairs={{0,6},{1,7},{2,4},{3,5},{4,2},{5,3},{6,0},{7,1},{8,14},{9,15},{10,... | collective-permute-start | bytes 442376 | tf_op jit(solution)/shard_map/ppermute | solution.py:346
  42.2 2.2 %collective-permute-start.5 = (f32[2,48,384]{2,1,0:T(8,128)S(1)}, f32[2,48,384]{2,1,0:T(8,128)S(1)}, u32[]{:S(2)}, u32[]{:S(2)}) collective-permute-start(f32[2,48,384]{2,1,0:T(8,128)S(1)} %get-tuple-element.19), channel_id=1, source_target_pairs={{0,2},{1,3},{2,0},{3,1},{4,6},{5,7},{6,4},{7,5},{8,10},{9,11},{10,... | collective-permute-start | bytes 442376 | tf_op jit(solution)/shard_map/ppermute | solution.py:346
  44.4 0.9 collective-permute-done.4
  45.3 3.7 %collective-permute-done.6 = f32[2,48,384]{2,1,0:T(8,128)S(1)} collective-permute-done((f32[2,48,384]{2,1,0:T(8,128)S(1)}, f32[2,48,384]{2,1,0:T(8,128)S(1)}, u32[]{:S(2)}, u32[]{:S(2)}) %collective-permute-start.6) | collective-permute-done | bytes 147488 | tf_op jit(solution)/shard_map/ppermute | solution.py:346
  49.0 2.8 %collective-permute-done.5 = f32[2,48,384]{2,1,0:T(8,128)S(1)} collective-permute-done((f32[2,48,384]{2,1,0:T(8,128)S(1)}, f32[2,48,384]{2,1,0:T(8,128)S(1)}, u32[]{:S(2)}, u32[]{:S(2)}) %collective-permute-start.5) | collective-permute-done | bytes 147488 | tf_op jit(solution)/shard_map/ppermute | solution.py:346
  51.9 0.1 collective-permute-start.7
  52.0 5.2 %collective-permute-done.7 = f32[48,384]{1,0:T(8,128)S(1)} collective-permute-done((f32[48,384]{1,0:T(8,128)S(1)}, f32[48,384]{1,0:T(8,128)S(1)}, u32[]{:S(2)}, u32[]{:S(2)}) %collective-permute-start.7) | collective-permute-done | bytes 73760 | tf_op jit(solution)/shard_map/ppermute | solution.py:346
  57.2 4.8 %collective-permute-start.8 = (f32[48,384]{1,0:T(8,128)S(1)}, f32[48,384]{1,0:T(8,128)S(1)}, u32[]{:S(2)}, u32[]{:S(2)}) collective-permute-start(f32[48,384]{1,0:T(8,128)S(1)} %fusion.4.first_ref), channel_id=1, source_target_pairs={{0,16},{1,17},{2,18},{3,19},{4,20},{5,21},{6,22},{7,23},{8,24},{9,... | collective-permute-start | bytes 221192 | tf_op jit(solution)/shard_map/ppermute | solution.py:346
  62.0 2.5 %collective-permute-done.8.second_ref = f32[48,384]{1,0:T(8,128)S(1)} collective-permute-done((f32[48,384]{1,0:T(8,128)S(1)}, f32[48,384]{1,0:T(8,128)S(1)}, u32[]{:S(2)}, u32[]{:S(2)}) %collective-permute-start.8) | collective-permute-done | bytes 73760 | tf_op jit(solution)/shard_map/ppermute | solution.py:346
  64.4 5.0 %solve.1 = f32[8,128]{1,0:T(8,128)S(1)} custom-call(f32[48,384]{1,0:T(8,128)S(1)} %fusion.4.first_ref, f32[48,384]{1,0:T(8,128)S(1)} %collective-permute-done.8.second_ref, f32[8,128]{1,0:T(8,128)S(1)} %get-tuple-element.15.marks_ref), custom_call_target="tpu_custom_call" | custom-call | tf_op jit(solution)/shard_map/solve/pallas_call | solution.py:403
  69.5 0.1 collective-permute-start.9
  69.6 3.3 %collective-permute-done.9 = f32[1,8,128]{2,1,0:T(8,128)S(1)} collective-permute-done((f32[1,8,128]{2,1,0:T(8,128)S(1)}, f32[1,8,128]{2,1,0:T(8,128)S(1)}, u32[]{:S(2)}, u32[]{:S(2)}) %collective-permute-start.9) | collective-permute-done | bytes 4128 | tf_op jit(solution)/shard_map/ppermute | solution.py:346
  72.9 2.5 %collective-permute-done.10 = f32[2,8,128]{2,1,0:T(8,128)S(1)} collective-permute-done((f32[2,8,128]{2,1,0:T(8,128)S(1)}, f32[2,8,128]{2,1,0:T(8,128)S(1)}, u32[]{:S(2)}, u32[]{:S(2)}) %collective-permute-start.10) | collective-permute-done | bytes 8224 | tf_op jit(solution)/shard_map/ppermute | solution.py:346
  75.4 3.0 %collective-permute-start.11 = (f32[4,8,128]{2,1,0:T(8,128)S(1)}, f32[4,8,128]{2,1,0:T(8,128)S(1)}, u32[]{:S(2)}, u32[]{:S(2)}) collective-permute-start(f32[4,8,128]{2,1,0:T(8,128)S(1)} %pad_maximum_fusion.8), channel_id=1, source_target_pairs={{0,2},{1,3},{2,0},{3,1},{4,6},{5,7},{6,4},{7,5},{8,10},{9,11},{10,... | collective-permute-start | bytes 49160 | tf_op jit(solution)/shard_map/ppermute | solution.py:346
  78.4 1.1 collective-permute-done.11
  79.5 7.2 %collective-permute-start.12 = (f32[8,8,128]{2,1,0:T(8,128)S(1)}, f32[8,8,128]{2,1,0:T(8,128)S(1)}, u32[]{:S(2)}, u32[]{:S(2)}) collective-permute-start(f32[8,8,128]{2,1,0:T(8,128)S(1)} %pad_maximum_fusion.7), channel_id=1, source_target_pairs={{0,1},{1,0},{2,3},{3,2},{4,5},{5,4},{6,7},{7,6},{8,9},{9,8},{10,11... | collective-permute-start | bytes 98312 | tf_op jit(solution)/shard_map/ppermute | solution.py:346
  86.7 0.9 collective-permute-done.12
  87.6 2.4 %power.1 = f32[16,8,128]{2,1,0:T(8,128)S(1)} custom-call(s32[64,16]{1,0:T(8,128)S(1)} %copy.20.bins_ref, f32[16,8,128]{2,1,0:T(8,128)S(1)} %constant_dynamic-update-slice_fusion.weights_ref, bf16[8,2,560,128]{3,2,1,0:T(8,128)(2,1)S(1)} %get-tuple-element.16.snap_ref), custom_call_target="tpu_custom_call" | custom-call | tf_op jit(solution)/shard_map/power/pallas_call | solution.py:415
  90.0 0.1 collective-permute-start.13
  90.1 1.5 %collective-permute-start.14 = (f32[1,16,128]{2,1,0:T(8,128)S(1)}, f32[1,16,128]{2,1,0:T(8,128)S(1)}, u32[]{:S(2)}, u32[]{:S(2)}) collective-permute-start(f32[1,16,128]{2,1,0:T(8,128)S(1)} %get-tuple-element.23), channel_id=1, source_target_pairs={{32,0},{64,32},{96,64},{128,96},{160,128},{192,160},{224,192},{0,2... | collective-permute-start | bytes 24584 | tf_op jit(solution)/shard_map/ppermute | solution.py:340
  91.5 1.0 collective-permute-done.13
  92.6 2.2 %collective-permute-done.14 = f32[1,16,128]{2,1,0:T(8,128)S(1)} collective-permute-done((f32[1,16,128]{2,1,0:T(8,128)S(1)}, f32[1,16,128]{2,1,0:T(8,128)S(1)}, u32[]{:S(2)}, u32[]{:S(2)}) %collective-permute-start.14) | collective-permute-done | bytes 8224 | tf_op jit(solution)/shard_map/ppermute | solution.py:340
  94.8 0.1 fusion.8
  94.9 8.0 %collective-permute-start.15 = (f32[10,16,1]{2,1,0:T(8,128)S(1)}, f32[10,16,1]{2,1,0:T(8,128)S(1)}, u32[]{:S(2)}, u32[]{:S(2)}) collective-permute-start(f32[10,16,1]{2,1,0:T(8,128)S(1)} %get-tuple-element.20), channel_id=1, source_target_pairs={{0,1},{1,2},{2,3},{3,4},{4,5},{5,6},{6,7},{7,8},{8,9},{9,10},{10,1... | collective-permute-start | bytes 1928 | tf_op jit(solution)/shard_map/ppermute | solution.py:337
  102.9 1.9 %collective-permute-start.16 = (f32[10,16,1]{2,1,0:T(8,128)S(1)}, f32[10,16,1]{2,1,0:T(8,128)S(1)}, u32[]{:S(2)}, u32[]{:S(2)}) collective-permute-start(f32[10,16,1]{2,1,0:T(8,128)S(1)} %get-tuple-element.21), channel_id=1, source_target_pairs={{1,0},{2,1},{3,2},{4,3},{5,4},{6,5},{7,6},{8,7},{9,8},{10,9},{11,1... | collective-permute-start | bytes 1928 | tf_op jit(solution)/shard_map/ppermute | solution.py:340
  104.9 7.4 %collective-permute-done.16 = f32[10,16,1]{2,1,0:T(8,128)S(1)} collective-permute-done((f32[10,16,1]{2,1,0:T(8,128)S(1)}, f32[10,16,1]{2,1,0:T(8,128)S(1)}, u32[]{:S(2)}, u32[]{:S(2)}) %collective-permute-start.16) | collective-permute-done | bytes 672 | tf_op jit(solution)/shard_map/ppermute | solution.py:340
  112.3 0.1 fusion.2
  112.4 0.6 fusion.5
  (23 shorter events, 0.4 us)
Async XLA Ops:
  0.0 22.6 %collective-permute-start.1 = (bf16[2,32,32,128]{3,2,1,0:T(8,128)(2,1)}, bf16[2,32,32,128]{3,2,1,0:T(8,128)(2,1)S(1)}, u32[]{:S(2)}, u32[]{:S(2)}) collective-permute-start(bf16[2,32,32,128]{3,2,1,0:T(8,128)(2,1)} %own_ref.1), channel_id=1, source_target_pairs={{32,0},{64,32},{96,64},{128,96},{160,128},{192,160},{224,192},{0,2... | collective-permute-start | bytes 1572872 | tf_op jit(solution)/shard_map/ppermute | solution.py:352
  0.5 23.9 %collective-permute-start = (bf16[2,32,32,128]{3,2,1,0:T(8,128)(2,1)}, bf16[2,32,32,128]{3,2,1,0:T(8,128)(2,1)S(1)}, u32[]{:S(2)}, u32[]{:S(2)}) collective-permute-start(bf16[2,32,32,128]{3,2,1,0:T(8,128)(2,1)} %own_ref.1), channel_id=1, source_target_pairs={{0,32},{32,64},{64,96},{96,128},{128,160},{160,192},{192,224},{224... | collective-permute-start | bytes 1572872 | tf_op jit(solution)/shard_map/ppermute | solution.py:351
  4.3 10.6 %collective-permute-start.2 = (f32[8,128]{1,0:T(8,128)S(1)}, f32[8,128]{1,0:T(8,128)S(1)}, u32[]{:S(2)}, u32[]{:S(2)}) collective-permute-start(f32[8,128]{1,0:T(8,128)S(1)} %broadcast_in_dim.12), channel_id=1, source_target_pairs={{0,16},{1,17},{2,18},{3,19},{4,20},{5,21},{6,22},{7,23},{8,24},{9,... | collective-permute-start | bytes 12296 | tf_op jit(solution)/shard_map/ppermute | solution.py:346
  12.5 1.0 copy-start
  13.5 0.7 copy-start.1
  36.5 3.6 %collective-permute-start.3 = (f32[8,48,384]{2,1,0:T(8,128)S(1)}, f32[8,48,384]{2,1,0:T(8,128)S(1)}, u32[]{:S(2)}, u32[]{:S(2)}) collective-permute-start(f32[8,48,384]{2,1,0:T(8,128)S(1)} %get-tuple-element.14), channel_id=1, source_target_pairs={{0,1},{1,0},{2,3},{3,2},{4,5},{5,4},{6,7},{7,6},{8,9},{9,8},{10,11... | collective-permute-start | bytes 1769480 | tf_op jit(solution)/shard_map/ppermute | solution.py:346
  40.2 5.1 %collective-permute-start.4 = (f32[2,48,384]{2,1,0:T(8,128)S(1)}, f32[2,48,384]{2,1,0:T(8,128)S(1)}, u32[]{:S(2)}, u32[]{:S(2)}) collective-permute-start(f32[2,48,384]{2,1,0:T(8,128)S(1)} %get-tuple-element.17), channel_id=1, source_target_pairs={{0,4},{1,5},{2,6},{3,7},{4,0},{5,1},{6,2},{7,3},{8,12},{9,13},{10,... | collective-permute-start | bytes 442376 | tf_op jit(solution)/shard_map/ppermute | solution.py:346
  40.3 8.8 %collective-permute-start.6 = (f32[2,48,384]{2,1,0:T(8,128)S(1)}, f32[2,48,384]{2,1,0:T(8,128)S(1)}, u32[]{:S(2)}, u32[]{:S(2)}) collective-permute-start(f32[2,48,384]{2,1,0:T(8,128)S(1)} %get-tuple-element.18), channel_id=1, source_target_pairs={{0,6},{1,7},{2,4},{3,5},{4,2},{5,3},{6,0},{7,1},{8,14},{9,15},{10,... | collective-permute-start | bytes 442376 | tf_op jit(solution)/shard_map/ppermute | solution.py:346
  42.2 9.6 %collective-permute-start.5 = (f32[2,48,384]{2,1,0:T(8,128)S(1)}, f32[2,48,384]{2,1,0:T(8,128)S(1)}, u32[]{:S(2)}, u32[]{:S(2)}) collective-permute-start(f32[2,48,384]{2,1,0:T(8,128)S(1)} %get-tuple-element.19), channel_id=1, source_target_pairs={{0,2},{1,3},{2,0},{3,1},{4,6},{5,7},{6,4},{7,5},{8,10},{9,11},{10,... | collective-permute-start | bytes 442376 | tf_op jit(solution)/shard_map/ppermute | solution.py:346
  51.9 5.3 %collective-permute-start.7 = (f32[48,384]{1,0:T(8,128)S(1)}, f32[48,384]{1,0:T(8,128)S(1)}, u32[]{:S(2)}, u32[]{:S(2)}) collective-permute-start(f32[48,384]{1,0:T(8,128)S(1)} %slice_bitcast_fusion), channel_id=1, source_target_pairs={{0,8},{1,9},{2,10},{3,11},{4,12},{5,13},{6,14},{7,15},{8,0},{9,1},... | collective-permute-start | bytes 221192 | tf_op jit(solution)/shard_map/ppermute | solution.py:346
  57.2 7.3 %collective-permute-start.8 = (f32[48,384]{1,0:T(8,128)S(1)}, f32[48,384]{1,0:T(8,128)S(1)}, u32[]{:S(2)}, u32[]{:S(2)}) collective-permute-start(f32[48,384]{1,0:T(8,128)S(1)} %fusion.4.first_ref), channel_id=1, source_target_pairs={{0,16},{1,17},{2,18},{3,19},{4,20},{5,21},{6,22},{7,23},{8,24},{9,... | collective-permute-start | bytes 221192 | tf_op jit(solution)/shard_map/ppermute | solution.py:346
  69.5 3.4 %collective-permute-start.9 = (f32[1,8,128]{2,1,0:T(8,128)S(1)}, f32[1,8,128]{2,1,0:T(8,128)S(1)}, u32[]{:S(2)}, u32[]{:S(2)}) collective-permute-start(f32[1,8,128]{2,1,0:T(8,128)S(1)} %bitcast.17), channel_id=1, source_target_pairs={{0,8},{1,9},{2,10},{3,11},{4,12},{5,13},{6,14},{7,15},{8,0},{9,1},... | collective-permute-start | bytes 12296 | tf_op jit(solution)/shard_map/ppermute | solution.py:346
  72.9 2.5 %collective-permute-start.10 = (f32[2,8,128]{2,1,0:T(8,128)S(1)}, f32[2,8,128]{2,1,0:T(8,128)S(1)}, u32[]{:S(2)}, u32[]{:S(2)}) collective-permute-start(f32[2,8,128]{2,1,0:T(8,128)S(1)} %pad_maximum_fusion.9), channel_id=1, source_target_pairs={{0,4},{1,5},{2,6},{3,7},{4,0},{5,1},{6,2},{7,3},{8,12},{9,13},{10,... | collective-permute-start | bytes 24584 | tf_op jit(solution)/shard_map/ppermute | solution.py:346
  75.4 4.1 %collective-permute-start.11 = (f32[4,8,128]{2,1,0:T(8,128)S(1)}, f32[4,8,128]{2,1,0:T(8,128)S(1)}, u32[]{:S(2)}, u32[]{:S(2)}) collective-permute-start(f32[4,8,128]{2,1,0:T(8,128)S(1)} %pad_maximum_fusion.8), channel_id=1, source_target_pairs={{0,2},{1,3},{2,0},{3,1},{4,6},{5,7},{6,4},{7,5},{8,10},{9,11},{10,... | collective-permute-start | bytes 49160 | tf_op jit(solution)/shard_map/ppermute | solution.py:346
  79.5 8.0 %collective-permute-start.12 = (f32[8,8,128]{2,1,0:T(8,128)S(1)}, f32[8,8,128]{2,1,0:T(8,128)S(1)}, u32[]{:S(2)}, u32[]{:S(2)}) collective-permute-start(f32[8,8,128]{2,1,0:T(8,128)S(1)} %pad_maximum_fusion.7), channel_id=1, source_target_pairs={{0,1},{1,0},{2,3},{3,2},{4,5},{5,4},{6,7},{7,6},{8,9},{9,8},{10,11... | collective-permute-start | bytes 98312 | tf_op jit(solution)/shard_map/ppermute | solution.py:346
  90.0 2.6 %collective-permute-start.13 = (f32[1,16,128]{2,1,0:T(8,128)S(1)}, f32[1,16,128]{2,1,0:T(8,128)S(1)}, u32[]{:S(2)}, u32[]{:S(2)}) collective-permute-start(f32[1,16,128]{2,1,0:T(8,128)S(1)} %get-tuple-element.22), channel_id=1, source_target_pairs={{0,32},{32,64},{64,96},{96,128},{128,160},{160,192},{192,224},{224... | collective-permute-start | bytes 24584 | tf_op jit(solution)/shard_map/ppermute | solution.py:337
  90.1 4.7 %collective-permute-start.14 = (f32[1,16,128]{2,1,0:T(8,128)S(1)}, f32[1,16,128]{2,1,0:T(8,128)S(1)}, u32[]{:S(2)}, u32[]{:S(2)}) collective-permute-start(f32[1,16,128]{2,1,0:T(8,128)S(1)} %get-tuple-element.23), channel_id=1, source_target_pairs={{32,0},{64,32},{96,64},{128,96},{160,128},{192,160},{224,192},{0,2... | collective-permute-start | bytes 24584 | tf_op jit(solution)/shard_map/ppermute | solution.py:340
  94.9 10.0 %collective-permute-start.15 = (f32[10,16,1]{2,1,0:T(8,128)S(1)}, f32[10,16,1]{2,1,0:T(8,128)S(1)}, u32[]{:S(2)}, u32[]{:S(2)}) collective-permute-start(f32[10,16,1]{2,1,0:T(8,128)S(1)} %get-tuple-element.20), channel_id=1, source_target_pairs={{0,1},{1,2},{2,3},{3,4},{4,5},{5,6},{6,7},{7,8},{8,9},{9,10},{10,1... | collective-permute-start | bytes 1928 | tf_op jit(solution)/shard_map/ppermute | solution.py:337
  102.9 9.4 %collective-permute-start.16 = (f32[10,16,1]{2,1,0:T(8,128)S(1)}, f32[10,16,1]{2,1,0:T(8,128)S(1)}, u32[]{:S(2)}, u32[]{:S(2)}) collective-permute-start(f32[10,16,1]{2,1,0:T(8,128)S(1)} %get-tuple-element.21), channel_id=1, source_target_pairs={{1,0},{2,1},{3,2},{4,3},{5,4},{6,5},{7,6},{8,7},{9,8},{10,9},{11,1... | collective-permute-start | bytes 1928 | tf_op jit(solution)/shard_map/ppermute | solution.py:340

commit v3 on v2

--- a/solution.py
+++ b/solution.py
@@ -76,12 +76,11 @@
 
 
 def gram_kernel(
-    column_ref, bins_ref, mask_ref, cos_ref, sin_ref,
+    ints_ref, floats_ref,
     table_ref, low_ref, own_ref, high_ref, marks_ref,
     snap_ref, keep_ref, send_ref, passed_ref,
-    spec_ref, wide_ref, minus_ref,
+    spec_ref, wide_ref,
 ):
-    az = lax.axis_index("az")
     mine = own_group()
     table = table_ref[...]
     passed_ref[...] = marks_ref[...]
@@ -98,54 +97,59 @@
 
     lane = lane_ids(DOF)
     row = lax.broadcasted_iota(jnp.int32, (DOF, LANES), 0)
+    lower = row >= lane - jnp.where(lane < DOF, 0, DOF)
     blank = jnp.zeros((LANES - 2 * DOF, 2 * CELLS), BF16)
-
-    def one_beam(beam, carry):
-        glob = az * OWN_BEAMS + beam
+    last = PULSES * SEL
+
+    def first_group(step):
+        return exclusive(exclusive(2 * step, 8), mine)
+
+    def turn(step):
+        beam = lax.div(first_group(step), 2)
         for sel in range(SEL):
-            column = column_ref[glob, sel]
+            column = ints_ref[beam, sel]
             real = spec_ref[column, :PULSES]
             imag = spec_ref[column, PULSES:]
-            cosine = cos_ref[glob, sel]
-            sine = sin_ref[glob, sel]
+            cosine = floats_ref[beam, sel]
+            sine = floats_ref[beam, SEL + sel]
             rows = pl.ds(SEL + sel, PULSES, stride=SEL)
             wide_ref[0, rows, :] = cosine * real - sine * imag
             wide_ref[1, rows, :] = sine * real + cosine * imag
-        last = PULSES * SEL
         for part in range(2):
             for low, high, place in (
                 (SEL, SEL + last, SEL),
                 (last, last + SEL, 0),
                 (SEL, 3 * SEL, SEL + last),
             ):
-                value = wide_ref[part, low:high, :]
-                snap_ref[beam, part, place : place + high - low, :] = value.astype(BF16)
-                if part == 0:
-                    minus_ref[place : place + high - low, :] = (-value).astype(BF16)
-        weight = mask_ref[beam, 0].astype(F32)
+                snap_ref[beam, part, place : place + high - low, :] = wide_ref[
+                    part, low:high, :
+                ].astype(BF16)
+
+    def multiply(step, out_ref):
+        group = first_group(step)
+        beam = lax.div(group, 2)
+        weight = ints_ref[beam, 2 * SEL].astype(F32)
         for half in range(2):
+            base = exclusive(lax.rem(group, 2), half) * 8
             out = [None, None, None]
             for pair in range(4):
                 same, turned = [], []
                 for one in range(2):
-                    centre = bins_ref[glob, half * 8 + pair * 2 + one]
+                    centre = ints_ref[beam, SEL + base + pair * 2 + one]
                     rows = pl.ds(pl.multiple_of(centre * SEL, SEL), DOF)
                     real = snap_ref[beam, 0, rows, :]
                     imag = snap_ref[beam, 1, rows, :]
-                    minus = minus_ref[rows, :]
                     same.append(jnp.concatenate([real, imag], 1))
-                    turned.append(jnp.concatenate([imag, minus], 1))
+                    turned.append(jnp.concatenate([imag, -real], 1))
                 left = jnp.concatenate([same[0], turned[0], same[1], turned[1]], 0)
                 right = jnp.concatenate([same[0], same[1], blank], 0)
                 gram = lax.dot_general(
                     left, right, TRANSPOSED, preferred_element_type=F32
                 )
                 packed = jnp.where(
-                    lane < DOF,
-                    jnp.where(row >= lane, gram[:DOF], gram[DOF : 2 * DOF]),
-                    jnp.where(
-                        row >= lane - DOF, gram[2 * DOF : 3 * DOF], gram[3 * DOF :]
-                    ),
+                    lower,
+                    jnp.where(lane < DOF, gram[:DOF], gram[2 * DOF : 3 * DOF]),
+                    jnp.where(lane < DOF, gram[DOF : 2 * DOF], gram[3 * DOF :]),
                 )
                 shift = 2 * DOF * pair % LANES
                 if shift:
@@ -160,20 +164,68 @@
                     out[2] = packed
                 else:
                     out[2] = jnp.where(lane >= 32, packed, out[2])
-            place = exclusive(beam * 2 + half, mine)
-            whole = jnp.concatenate(out, 1) * weight
-
-            @pl.when(place < 8)
-            def _():
-                keep_ref[lax.rem(place, 8)] = whole
-
-            @pl.when(place >= 8)
-            def _():
-                send_ref[lax.rem(place, 8)] = whole
-
+            place = lax.rem(2 * step, 8) + half
+            for part in range(3):
+                out_ref[place, :, LANES * part : LANES * (part + 1)] = (
+                    out[part] * weight
+                )
+
+    def sending(step, carry):
+        turn(step + 1)
+        multiply(step, send_ref)
         return carry
 
-    lax.fori_loop(0, OWN_BEAMS, one_beam, 0)
+    def keeping(step, carry):
+        turn(step + 1)
+        multiply(step, keep_ref)
+        return carry
+
+    turn(0)
+    lax.fori_loop(0, 4, sending, 0)
+    lax.fori_loop(4, 7, keeping, 0)
+    multiply(7, keep_ref)
+
+
+def edge_out_kernel(snap_ref, first_ref, second_ref):
+    rows = 8 * 8
+    lane = lane_ids(rows)
+    ends = [jnp.zeros((rows, LANES), F32) for _ in range(2)]
+    for beam in range(OWN_BEAMS):
+        for part in range(2):
+            for block in range(8):
+                low = SEL + rows * block
+                value = snap_ref[beam, part, low : low + rows, :].astype(F32)
+                target = 16 * block + 8 * part + beam
+                here = lane == target
+                for end in range(2):
+                    shift = (target + end) % LANES
+                    moved = pltpu.roll(value, shift, 1) if shift else value
+                    ends[end] = jnp.where(here, moved, ends[end])
+    even = lax.rem(lax.axis_index("rng"), 2) == 0
+    first_ref[...] = jnp.where(even, ends[1], ends[0]).astype(BF16)
+    second_ref[...] = jnp.where(even, ends[0], ends[1]).astype(BF16)
+
+
+def edge_in_kernel(first_ref, second_ref, direct_ref, turned_ref):
+    rows = 8 * 8
+    lane = lane_ids(rows)
+    first = first_ref[...].astype(F32)
+    second = second_ref[...].astype(F32)
+
+    def rolled(value, shift):
+        return pltpu.roll(value, shift % LANES, 1) if shift % LANES else value
+
+    for block in range(8):
+        both = jnp.where(
+            lane < 16, rolled(first, -16 * block), rolled(second, 16 - 16 * block)
+        )
+        for ref, value in ((direct_ref, both), (turned_ref, rolled(both, -8))):
+            value = value.astype(BF16)
+            ref[SEL + rows * block : SEL + rows * (block + 1), :] = value
+            if block == 0:
+                ref[PULSES * SEL + SEL :, :] = value[: 2 * SEL]
+            if block == 7:
+                ref[:SEL, :] = value[rows - SEL :]
 
 
 def spread(value, index):
@@ -295,9 +347,12 @@
     out_ref[...] = jnp.where(small == 120, marks_ref[...], found)
 
 
-def power_kernel(bins_ref, weights_ref, snap_ref, power_ref):
-    az = lax.axis_index("az")
+def power_kernel(
+    ints_ref, weights_ref, snap_ref, direct_ref, turned_ref,
+    power_ref, first_ref, second_ref,
+):
     mine = own_group()
+    even = lax.rem(lax.axis_index("rng"), 2) == 0
     small = lane_ids(8)
     counts = jnp.zeros((8, LANES), F32)
     for place in range(GROUPS):
@@ -306,7 +361,8 @@
     used = jnp.logical_or(
         small < DOF, jnp.logical_and(small >= 64, small < 64 + DOF)
     )
-    row = lax.broadcasted_iota(jnp.int32, (2 * 8, LANES), 0)
+    row = lax.broadcasted_iota(jnp.int32, (2 * 8, 2 * LANES), 0)
+    low_lane = jnp.where(even, 16, 0)
     for group in range(GROUPS):
         beam = group // 2
         scaled = weights_ref[exclusive(mine, group)] * counts[beam : beam + 1, :]
@@ -315,31 +371,46 @@
         turned = pltpu.roll(direct, 64, 1)
         turned = jnp.where(small < 64, -turned, turned)
         left = jnp.concatenate([direct, turned], 0).astype(BF16)
-        found = jnp.zeros((16, LANES), F32)
+        found = jnp.zeros((16, 2 * LANES), F32)
         for one in range(8):
-            centre = bins_ref[az * OWN_BEAMS + beam, (group % 2) * 8 + one]
+            centre = ints_ref[beam, SEL + (group % 2) * 8 + one]
             rows = pl.ds(pl.multiple_of(centre * SEL, SEL), 64)
             right = jnp.concatenate(
-                [snap_ref[beam, 0, rows, :], snap_ref[beam, 1, rows, :]], 0
+                [
+                    jnp.concatenate([snap_ref[beam, 0, rows, :], direct_ref[rows, :]], 1),
+                    jnp.concatenate([snap_ref[beam, 1, rows, :], turned_ref[rows, :]], 1),
+                ],
+                0,
             )
             product = jnp.dot(left, right, preferred_element_type=F32)
             found = jnp.where(lax.rem(row, 8) == one, product, found)
-        power_ref[group] = (found[:8] * found[:8] + found[8:] * found[8:]) / quiet
-
-
-def with_halo(block, sides, width, periodic):
-    for axis, dim in sides:
-        count = lax.axis_size(axis)
-        forward = [(i, i + 1) for i in range(count - 1)]
-        if periodic:
-            forward.append((count - 1, 0))
-        backward = [(target, source) for source, target in forward]
-        low = lax.ppermute(
-            lax.slice_in_dim(block, block.shape[dim] - width, None, axis=dim), axis, forward
+        power = found[:8] * found[:8] + found[8:] * found[8:]
+        inner = power[:, :LANES] / quiet
+        outer = power[:, LANES:] / quiet
+        low = spread(outer, beam + low_lane)
+        high = spread(outer, beam + 16 - low_lane)
+        below = jnp.where(small == 0, low, pltpu.roll(inner, 1, 1))
+        above = jnp.where(small == LANES - 1, high, pltpu.roll(inner, LANES - 1, 1))
+        power_ref[group] = below + inner + above
+    even = lax.rem(lax.axis_index("az"), 2) == 0
+    for half in range(2):
+        bottom, top = power_ref[half], power_ref[GROUPS - 2 + half]
+        first_ref[half] = jnp.where(even, top, bottom)
+        second_ref[half] = jnp.where(even, bottom, top)
+
+
+def smooth_kernel(power_ref, first_ref, second_ref, out_ref):
+    even = lax.rem(lax.axis_index("az"), 2) == 0
+    first, second = first_ref[...], second_ref[...]
+    low = jnp.where(even, second, first)
+    high = jnp.where(even, first, second)
+    for beam in range(OWN_BEAMS):
+        below = low if beam == 0 else power_ref[2 * beam - 2 : 2 * beam]
+        above = (
+            high if beam == OWN_BEAMS - 1 else power_ref[2 * beam + 2 : 2 * beam + 4]
         )
-        high = lax.ppermute(lax.slice_in_dim(block, 0, width, axis=dim), axis, backward)
-        block = jnp.concatenate([low, block, high], axis=dim)
-    return block
+        here = power_ref[2 * beam : 2 * beam + 2]
+        out_ref[2 * beam : 2 * beam + 2] = (below + here + above) / 9.0
 
 
 def swap(value, turn):
@@ -357,74 +428,133 @@
 VMEM = pl.BlockSpec(memory_space=pltpu.VMEM)
 
 
+def limit(mebibytes):
+    return pltpu.CompilerParams(vmem_limit_bytes=mebibytes * 2**20)
+
+
+def shape(*dims, dtype=F32):
+    return jax.ShapeDtypeStruct(dims, dtype)
+
+
+def neighbours(count, closed):
+    nearest = [(i, i ^ 1) for i in range(count)]
+    across = [(i, i + 1) if i % 2 else (i, i - 1) for i in range(count)]
+    if closed:
+        across = [(a, b % count) for a, b in across]
+    else:
+        across = [(a, b) for a, b in across if 0 <= b < count]
+    return nearest, across
+
+
 def body(echoes, arc_start, arc_offsets, doppler_bins, steer_angles, train_mask):
     low, high = halo_columns(echoes)
+    az = lax.axis_index("az")
+
+    def own(value):
+        return lax.dynamic_slice_in_dim(value, az * OWN_BEAMS, OWN_BEAMS, 0)
+
     marks = jnp.broadcast_to(train_mask.astype(F32), (OWN_BEAMS, LANES))
     marks = marks + swap(marks, 16)
-    half = jax.ShapeDtypeStruct((8, DOF, 8 * DOF), F32)
-    first = (arc_start - lax.axis_index("az") * OWN_COLS + ARC // 2) % COLS
+    first = (own(arc_start) - az * OWN_COLS + ARC // 2) % COLS
+    ints = jnp.concatenate(
+        [first[:, None] + own(arc_offsets), own(doppler_bins), train_mask], 1
+    )
+    angles = own(steer_angles)
+    floats = jnp.concatenate([jnp.cos(angles), jnp.sin(angles)], 1)
     spec, table = pl.pallas_call(
         own_kernel,
         out_shape=(
-            jax.ShapeDtypeStruct((OWN_COLS, 2 * PULSES, CELLS), F32),
-            jax.ShapeDtypeStruct((2 * PULSES, 2 * PULSES), BF16),
+            shape(OWN_COLS, 2 * PULSES, CELLS),
+            shape(2 * PULSES, 2 * PULSES, dtype=BF16),
         ),
         in_specs=[VMEM, VMEM],
         out_specs=(VMEM, VMEM),
-        compiler_params=pltpu.CompilerParams(vmem_limit_bytes=32 * 2**20),
+        compiler_params=limit(8),
         name="spectra",
     )(jnp.asarray(table_array()), echoes)
+    half = shape(8, DOF, 8 * DOF)
     snaps, keep, send, marks = pl.pallas_call(
         gram_kernel,
         out_shape=(
-            jax.ShapeDtypeStruct((OWN_BEAMS, 2, SLOTS * SEL, CELLS), BF16),
+            shape(OWN_BEAMS, 2, SLOTS * SEL, CELLS, dtype=BF16),
             half,
             half,
-            jax.ShapeDtypeStruct((OWN_BEAMS, LANES), F32),
+            shape(OWN_BEAMS, LANES),
         ),
-        in_specs=[SMEM] * 5 + [VMEM] * 5,
-        out_specs=(VMEM, VMEM, VMEM, VMEM),
+        in_specs=[SMEM] * 2 + [VMEM] * 5,
+        out_specs=(VMEM,) * 4,
         scratch_shapes=[
             pltpu.VMEM((3 * OWN_COLS, 2 * PULSES, CELLS), F32),
             pltpu.VMEM((2, SLOTS * SEL, CELLS), F32),
-            pltpu.VMEM((SLOTS * SEL, CELLS), BF16),
         ],
-        compiler_params=pltpu.CompilerParams(vmem_limit_bytes=40 * 2**20),
+        compiler_params=limit(16),
         name="grams",
-    )(
-        first[:, None] + arc_offsets, doppler_bins, train_mask,
-        jnp.cos(steer_angles), jnp.sin(steer_angles),
-        table, low, spec, high, marks,
-    )
+    )(ints, floats, table, low, spec, high, marks)
+    edge = shape(64, LANES, dtype=BF16)
+    edges = pl.pallas_call(
+        edge_out_kernel,
+        out_shape=(edge, edge),
+        in_specs=[VMEM],
+        out_specs=(VMEM, VMEM),
+        compiler_params=limit(8),
+        name="edges_out",
+    )(snaps)
     part = keep + swap(send, 1)
-    part = part[:2] + swap(part[2:4], 4) + swap(part[4:6], 2) + swap(part[6:], 6)
-    part = part[0] + swap(part[1], 8)
+    moved = [swap(part[2:4], 4), swap(part[4:6], 2), swap(part[6:], 6)]
+    moved, edges = lax.optimization_barrier((moved, edges))
+    part = part[:2] + moved[0] + moved[1] + moved[2]
+    moved = swap(part[1], 8)
+    edges = [
+        lax.ppermute(value, "rng", pairs)
+        for value, pairs in zip(edges, neighbours(32, False))
+    ]
+    moved, edges = lax.optimization_barrier((moved, edges))
+    part = part[0] + moved
     other = swap(part, 16)
+    edge = shape(SLOTS * SEL, LANES, dtype=BF16)
+    edges = pl.pallas_call(
+        edge_in_kernel,
+        out_shape=(edge, edge),
+        in_specs=[VMEM, VMEM],
+        out_specs=(VMEM, VMEM),
+        compiler_params=limit(8),
+        name="edges_in",
+    )(*edges)
+    other, edges = lax.optimization_barrier((other, edges))
     weights = pl.pallas_call(
         solve_kernel,
-        out_shape=jax.ShapeDtypeStruct((8, LANES), F32),
+        out_shape=shape(8, LANES),
         in_specs=[VMEM] * 3,
         out_specs=VMEM,
         scratch_shapes=[pltpu.VMEM((LANES, LANES), F32)],
-        compiler_params=pltpu.CompilerParams(vmem_limit_bytes=32 * 2**20),
+        compiler_params=limit(8),
         name="solve",
     )(part, other, marks)
     weights = weights[None]
     for turn in (8, 4, 2, 1):
         weights = jnp.concatenate([weights, swap(weights, turn)], 0)
-    power = pl.pallas_call(
+    rim = shape(2, 8, CELLS)
+    power, *rims = pl.pallas_call(
         power_kernel,
-        out_shape=jax.ShapeDtypeStruct((GROUPS, 8, CELLS), F32),
-        in_specs=[SMEM, VMEM, VMEM],
+        out_shape=(shape(GROUPS, 8, CELLS), rim, rim),
+        in_specs=[SMEM] + [VMEM] * 4,
+        out_specs=(VMEM,) * 3,
+        compiler_params=limit(8),
+        name="power",
+    )(ints, weights, snaps, *edges)
+    rims = [
+        lax.ppermute(value, "az", pairs)
+        for value, pairs in zip(rims, neighbours(8, True))
+    ]
+    smoothed = pl.pallas_call(
+        smooth_kernel,
+        out_shape=shape(GROUPS, 8, CELLS),
+        in_specs=[VMEM] * 3,
         out_specs=VMEM,
-        compiler_params=pltpu.CompilerParams(vmem_limit_bytes=32 * 2**20),
-        name="power",
-    )(doppler_bins, weights, snaps)
-    power_map = power.reshape(OWN_BEAMS, DBINS, CELLS)
-    beam_ext = with_halo(power_map, (("az", 0),), 1, True)
-    full_ext = with_halo(beam_ext, (("rng", 2),), 1, False)
-    row_sums = full_ext[:, :, :-2] + full_ext[:, :, 1:-1] + full_ext[:, :, 2:]
-    return (row_sums[:-2] + row_sums[1:-1] + row_sums[2:]) / 9.0
+        compiler_params=limit(8),
+        name="smooth",
+    )(power, *rims)
+    return smoothed.reshape(OWN_BEAMS, DBINS, CELLS)
 
 
 def solution(mesh):

time: 114 us -> 98.5 us (0.86)
  the two profiles are of different devices: /device:TPU:127 before, /device:TPU:1 now
where the time goes in v3:
time: 98.5 us; the launch traced here: 97.8 us
  starting transfers between devices  45.9 us (47%)
  waiting for transfers between devices  28.4 us (29%)
  Pallas kernels  17.7 us (18%)
  local copies, waits for them, and re-layouts  3.73 us (4%)
  other arithmetic  1.83 us (2%)
    ppermute x11, starting transfers between devices, swap(): return lax.ppermute(value, 'rng', [(i, i ^ turn) for i in range(32)])  31.9 us
    ppermute x11, waiting for transfers between devices, swap(): return lax.ppermute(value, 'rng', [(i, i ^ turn) for i in range(32)])  14.4 us
    pallas_call x1, Pallas kernels, body(): pl.pallas_call(gram_kernel, out_shape=(shape(OWN_BEAMS, 2, SLOTS * SEL, C...  7.91 us
    ppermute x2, starting transfers between devices, body(): lax.ppermute(value, 'rng', pairs)  5.9 us
    ppermute x1, waiting for transfers between devices, halo_columns(): high = lax.ppermute(echoes, 'az', [(b, a) for a, b in ring])  5.65 us
    pallas_call x1, Pallas kernels, body(): pl.pallas_call(solve_kernel, out_shape=shape(8, LANES), in_specs=[VMEM] *...  5.01 us
    ppermute x1, starting transfers between devices, halo_columns(): high = lax.ppermute(echoes, 'az', [(b, a) for a, b in ring])  4.32 us
    ppermute x2, starting transfers between devices, body(): lax.ppermute(value, 'az', pairs)  3.75 us
  transfers between devices with their start and end apart: 17, of which 12 were waited for; matrix products, arithmetic and copies ran while one was open for 4% of the time, Pallas kernels for 2%

profile of v3, /device:TPU:1, one launch (start us, length us, event | category | flops | bytes accessed | tf_op | source)
XLA Modules:
  0.0 97.8 jit_solution(7409072341451784425)
XLA Ops:
  0.0 4.3 %collective-permute-start.1 = (bf16[2,32,32,128]{3,2,1,0:T(8,128)(2,1)}, bf16[2,32,32,128]{3,2,1,0:T(8,128)(2,1)S(1)}, u32[]{:S(2)}, u32[]{:S(2)}) collective-permute-start(bf16[2,32,32,128]{3,2,1,0:T(8,128)(2,1)} %own_ref.1), channel_id=1, source_target_pairs={{32,0},{64,32},{96,64},{128,96},{160,128},{192,160},{224,192},{0,2... | collective-permute-start | bytes 1572872 | tf_op jit(solution)/shard_map/ppermute | solution.py:423
  4.3 0.7 convert_bitcast_fusion
  5.0 0.1 broadcast_in_dim.12
  5.1 6.9 %collective-permute-start.2 = (f32[8,128]{1,0:T(8,128)S(1)}, f32[8,128]{1,0:T(8,128)S(1)}, u32[]{:S(2)}, u32[]{:S(2)}) collective-permute-start(f32[8,128]{1,0:T(8,128)S(1)} %broadcast_in_dim.12), channel_id=1, source_target_pairs={{0,16},{1,17},{2,18},{3,19},{4,20},{5,21},{6,22},{7,23},{8,24},{9,... | collective-permute-start | bytes 12296 | tf_op jit(solution)/shard_map/ppermute | solution.py:417
  12.0 0.7 copy.10
  12.7 0.1 constant_dynamic-slice_fusion
  12.8 0.1 copy.14
  12.9 0.8 constant_dynamic-slice_fusion.1
  13.8 0.7 and_select_fusion
  14.6 0.1 pad_maximum_fusion.3.floats_ref
  14.7 0.1 pad_add_fusion.ints_ref
  14.8 1.0 %copy-done.1 = bf16[2,32,32,128]{3,2,1,0:T(8,128)(2,1)S(1)} copy-done((bf16[2,32,32,128]{3,2,1,0:T(8,128)(2,1)S(1)}, bf16[2,32,32,128]{3,2,1,0:T(8,128)(2,1)}, u32[]{:S(2)}) %copy-start.1) | copy-done | bytes 524312
  15.8 0.7 copy-done.2
  16.5 0.7 spectra.1
  17.2 0.1 broadcast_add_fusion.marks_ref
  17.3 5.7 %collective-permute-done.1.high_ref = bf16[2,32,32,128]{3,2,1,0:T(8,128)(2,1)S(1)} collective-permute-done((bf16[2,32,32,128]{3,2,1,0:T(8,128)(2,1)}, bf16[2,32,32,128]{3,2,1,0:T(8,128)(2,1)S(1)}, u32[]{:S(2)}, u32[]{:S(2)}) %collective-permute-start.1) | collective-permute-done | bytes 524320 | tf_op jit(solution)/shard_map/ppermute | solution.py:423
  23.0 3.3 %collective-permute-done.low_ref = bf16[2,32,32,128]{3,2,1,0:T(8,128)(2,1)S(1)} collective-permute-done((bf16[2,32,32,128]{3,2,1,0:T(8,128)(2,1)}, bf16[2,32,32,128]{3,2,1,0:T(8,128)(2,1)S(1)}, u32[]{:S(2)}, u32[]{:S(2)}) %collective-permute-start) | collective-permute-done | bytes 524320 | tf_op jit(solution)/shard_map/ppermute | solution.py:422
  26.2 7.9 %grams.1 = (bf16[8,2,560,128]{3,2,1,0:T(8,128)(2,1)S(1)}, f32[8,48,384]{2,1,0:T(8,128)S(1)}, f32[8,48,384]{2,1,0:T(8,128)S(1)}, f32[8,128]{1,0:T(8,128)S(1)}) custom-call(s32[8,33]{1,0:T(8,128)S(1)} %pad_add_fusion.ints_ref, f32[8,32]{1,0:T(8,128)S(1)} %pad_maximum_fusion.3.floats_ref, bf16[64,64]{1,0:T(8,128)(2,1)S(1)} %get-tuple-element.29.table_ref, ...), custom_call_target="tpu_custom_call" | custom-call | tf_op jit(solution)/shard_map/grams/pallas_call | solution.py:476
  34.1 0.6 collective-permute-start.3
  34.7 1.6 %collective-permute-done.3 = f32[8,48,384]{2,1,0:T(8,128)S(1)} collective-permute-done((f32[8,48,384]{2,1,0:T(8,128)S(1)}, f32[8,48,384]{2,1,0:T(8,128)S(1)}, u32[]{:S(2)}, u32[]{:S(2)}) %collective-permute-start.3) | collective-permute-done | bytes 589856 | tf_op jit(solution)/shard_map/ppermute | solution.py:417
  36.4 0.1 add.47
  36.5 4.3 %collective-permute-start.6 = (f32[2,48,384]{2,1,0:T(8,128)S(1)}, f32[2,48,384]{2,1,0:T(8,128)S(1)}, u32[]{:S(2)}, u32[]{:S(2)}) collective-permute-start(f32[2,48,384]{2,1,0:T(8,128)S(1)} %get-tuple-element.53), channel_id=1, source_target_pairs={{0,6},{1,7},{2,4},{3,5},{4,2},{5,3},{6,0},{7,1},{8,14},{9,15},{10,... | collective-permute-start | bytes 442376 | tf_op jit(solution)/shard_map/ppermute | solution.py:417
  40.7 0.2 collective-permute-start.5
  40.9 0.2 collective-permute-start.4
  41.1 1.2 %edges_out.1 = (bf16[64,128]{1,0:T(8,128)(2,1)S(1)}, bf16[64,128]{1,0:T(8,128)(2,1)S(1)}) custom-call(bf16[8,2,560,128]{3,2,1,0:T(8,128)(2,1)S(1)} %get-tuple-element.33.snap_ref), custom_call_target="tpu_custom_call" | custom-call | tf_op jit(solution)/shard_map/edges_out/pallas_call | solution.py:494
  42.3 2.4 %collective-permute-done.6 = f32[2,48,384]{2,1,0:T(8,128)S(1)} collective-permute-done((f32[2,48,384]{2,1,0:T(8,128)S(1)}, f32[2,48,384]{2,1,0:T(8,128)S(1)}, u32[]{:S(2)}, u32[]{:S(2)}) %collective-permute-start.6) | collective-permute-done | bytes 147488 | tf_op jit(solution)/shard_map/ppermute | solution.py:417
  44.6 2.7 %collective-permute-done.5 = f32[2,48,384]{2,1,0:T(8,128)S(1)} collective-permute-done((f32[2,48,384]{2,1,0:T(8,128)S(1)}, f32[2,48,384]{2,1,0:T(8,128)S(1)}, u32[]{:S(2)}, u32[]{:S(2)}) %collective-permute-start.5) | collective-permute-done | bytes 147488 | tf_op jit(solution)/shard_map/ppermute | solution.py:417
  47.4 3.1 %collective-permute-start.7 = (f32[48,384]{1,0:T(8,128)S(1)}, f32[48,384]{1,0:T(8,128)S(1)}, u32[]{:S(2)}, u32[]{:S(2)}) collective-permute-start(f32[48,384]{1,0:T(8,128)S(1)} %slice_bitcast_fusion), channel_id=1, source_target_pairs={{0,8},{1,9},{2,10},{3,11},{4,12},{5,13},{6,14},{7,15},{8,0},{9,1},... | collective-permute-start | bytes 221192 | tf_op jit(solution)/shard_map/ppermute | solution.py:417
  50.5 1.6 %collective-permute-start.8 = (bf16[64,128]{1,0:T(8,128)(2,1)S(1)}, bf16[64,128]{1,0:T(8,128)(2,1)S(1)}, u32[]{:S(2)}, u32[]{:S(2)}) collective-permute-start(bf16[64,128]{1,0:T(8,128)(2,1)S(1)} %get-tuple-element.39), channel_id=1, source_target_pairs={{0,1},{1,0},{2,3},{3,2},{4,5},{5,4},{6,7},{7,6},{8,9},{9,8},{10,11... | collective-permute-start | bytes 49160 | tf_op jit(solution)/shard_map/ppermute | solution.py:508
  52.1 4.3 %collective-permute-start.9 = (bf16[64,128]{1,0:T(8,128)(2,1)S(1)}, bf16[64,128]{1,0:T(8,128)(2,1)S(1)}, u32[]{:S(2)}, u32[]{:S(2)}) collective-permute-start(bf16[64,128]{1,0:T(8,128)(2,1)S(1)} %get-tuple-element.40), channel_id=1, source_target_pairs={{1,2},{2,1},{3,4},{4,3},{5,6},{6,5},{7,8},{8,7},{9,10},{10,9},{11,... | collective-permute-start | bytes 49160 | tf_op jit(solution)/shard_map/ppermute | solution.py:508
  56.4 2.2 %collective-permute-done.9.second_ref = bf16[64,128]{1,0:T(8,128)(2,1)S(1)} collective-permute-done((bf16[64,128]{1,0:T(8,128)(2,1)S(1)}, bf16[64,128]{1,0:T(8,128)(2,1)S(1)}, u32[]{:S(2)}, u32[]{:S(2)}) %collective-permute-start.9) | collective-permute-done | bytes 16416 | tf_op jit(solution)/shard_map/ppermute | solution.py:508
  58.7 5.1 %collective-permute-start.10 = (f32[48,384]{1,0:T(8,128)S(1)}, f32[48,384]{1,0:T(8,128)S(1)}, u32[]{:S(2)}, u32[]{:S(2)}) collective-permute-start(f32[48,384]{1,0:T(8,128)S(1)} %fusion.2.first_ref), channel_id=1, source_target_pairs={{0,16},{1,17},{2,18},{3,19},{4,20},{5,21},{6,22},{7,23},{8,24},{9,... | collective-permute-start | bytes 221192 | tf_op jit(solution)/shard_map/ppermute | solution.py:417
  63.7 0.2 edges_in.1
  64.0 2.0 %collective-permute-done.10.second_ref = f32[48,384]{1,0:T(8,128)S(1)} collective-permute-done((f32[48,384]{1,0:T(8,128)S(1)}, f32[48,384]{1,0:T(8,128)S(1)}, u32[]{:S(2)}, u32[]{:S(2)}) %collective-permute-start.10) | collective-permute-done | bytes 73760 | tf_op jit(solution)/shard_map/ppermute | solution.py:417
  66.0 5.0 %solve.1 = f32[8,128]{1,0:T(8,128)S(1)} custom-call(f32[48,384]{1,0:T(8,128)S(1)} %fusion.2.first_ref, f32[48,384]{1,0:T(8,128)S(1)} %collective-permute-done.10.second_ref, f32[8,128]{1,0:T(8,128)S(1)} %get-tuple-element.47.marks_ref), custom_call_target="tpu_custom_call" | custom-call | tf_op jit(solution)/shard_map/solve/pallas_call | solution.py:524
  71.0 1.2 %collective-permute-start.11 = (f32[1,8,128]{2,1,0:T(8,128)S(1)}, f32[1,8,128]{2,1,0:T(8,128)S(1)}, u32[]{:S(2)}, u32[]{:S(2)}) collective-permute-start(f32[1,8,128]{2,1,0:T(8,128)S(1)} %bitcast.11), channel_id=1, source_target_pairs={{0,8},{1,9},{2,10},{3,11},{4,12},{5,13},{6,14},{7,15},{8,0},{9,1},... | collective-permute-start | bytes 12296 | tf_op jit(solution)/shard_map/ppermute | solution.py:417
  72.2 2.4 %collective-permute-done.11 = f32[1,8,128]{2,1,0:T(8,128)S(1)} collective-permute-done((f32[1,8,128]{2,1,0:T(8,128)S(1)}, f32[1,8,128]{2,1,0:T(8,128)S(1)}, u32[]{:S(2)}, u32[]{:S(2)}) %collective-permute-start.11) | collective-permute-done | bytes 4128 | tf_op jit(solution)/shard_map/ppermute | solution.py:417
  74.6 3.6 %collective-permute-start.12 = (f32[2,8,128]{2,1,0:T(8,128)S(1)}, f32[2,8,128]{2,1,0:T(8,128)S(1)}, u32[]{:S(2)}, u32[]{:S(2)}) collective-permute-start(f32[2,8,128]{2,1,0:T(8,128)S(1)} %pad_maximum_fusion.2), channel_id=1, source_target_pairs={{0,4},{1,5},{2,6},{3,7},{4,0},{5,1},{6,2},{7,3},{8,12},{9,13},{10,... | collective-permute-start | bytes 24584 | tf_op jit(solution)/shard_map/ppermute | solution.py:417
  78.2 1.0 %collective-permute-done.12 = f32[2,8,128]{2,1,0:T(8,128)S(1)} collective-permute-done((f32[2,8,128]{2,1,0:T(8,128)S(1)}, f32[2,8,128]{2,1,0:T(8,128)S(1)}, u32[]{:S(2)}, u32[]{:S(2)}) %collective-permute-start.12) | collective-permute-done | bytes 8224 | tf_op jit(solution)/shard_map/ppermute | solution.py:417
  79.3 2.7 %collective-permute-start.13 = (f32[4,8,128]{2,1,0:T(8,128)S(1)}, f32[4,8,128]{2,1,0:T(8,128)S(1)}, u32[]{:S(2)}, u32[]{:S(2)}) collective-permute-start(f32[4,8,128]{2,1,0:T(8,128)S(1)} %pad_maximum_fusion.1), channel_id=1, source_target_pairs={{0,2},{1,3},{2,0},{3,1},{4,6},{5,7},{6,4},{7,5},{8,10},{9,11},{10,... | collective-permute-start | bytes 49160 | tf_op jit(solution)/shard_map/ppermute | solution.py:417
  82.0 1.4 %collective-permute-done.13 = f32[4,8,128]{2,1,0:T(8,128)S(1)} collective-permute-done((f32[4,8,128]{2,1,0:T(8,128)S(1)}, f32[4,8,128]{2,1,0:T(8,128)S(1)}, u32[]{:S(2)}, u32[]{:S(2)}) %collective-permute-start.13) | collective-permute-done | bytes 16416 | tf_op jit(solution)/shard_map/ppermute | solution.py:417
  83.4 4.2 %collective-permute-start.14 = (f32[8,8,128]{2,1,0:T(8,128)S(1)}, f32[8,8,128]{2,1,0:T(8,128)S(1)}, u32[]{:S(2)}, u32[]{:S(2)}) collective-permute-start(f32[8,8,128]{2,1,0:T(8,128)S(1)} %pad_maximum_fusion), channel_id=1, source_target_pairs={{0,1},{1,0},{2,3},{3,2},{4,5},{5,4},{6,7},{7,6},{8,9},{9,8},{10,11... | collective-permute-start | bytes 98312 | tf_op jit(solution)/shard_map/ppermute | solution.py:417
  87.5 0.9 collective-permute-done.14
  88.4 2.1 %power.1 = (f32[16,8,128]{2,1,0:T(8,128)S(1)}, f32[2,8,128]{2,1,0:T(8,128)S(1)}, f32[2,8,128]{2,1,0:T(8,128)S(1)}) custom-call(s32[8,33]{1,0:T(8,128)S(1)} %pad_add_fusion.ints_ref, f32[16,8,128]{2,1,0:T(8,128)S(1)} %constant_dynamic-update-slice_fusion.weights_ref, bf16[8,2,560,128]{3,2,1,0:T(8,128)(2,1)S(1)} %get-tuple-element.33.snap_ref, ...), custom_call_target="tpu_custom_call" | custom-call | tf_op jit(solution)/shard_map/power/pallas_call | solution.py:537
  90.5 2.0 %collective-permute-start.15 = (f32[2,8,128]{2,1,0:T(8,128)S(1)}, f32[2,8,128]{2,1,0:T(8,128)S(1)}, u32[]{:S(2)}, u32[]{:S(2)}) collective-permute-start(f32[2,8,128]{2,1,0:T(8,128)S(1)} %get-tuple-element.51), channel_id=1, source_target_pairs={{0,32},{32,0},{64,96},{96,64},{128,160},{160,128},{192,224},{224,1... | collective-permute-start | bytes 24584 | tf_op jit(solution)/shard_map/ppermute | solution.py:546
  92.5 1.7 %collective-permute-start.16 = (f32[2,8,128]{2,1,0:T(8,128)S(1)}, f32[2,8,128]{2,1,0:T(8,128)S(1)}, u32[]{:S(2)}, u32[]{:S(2)}) collective-permute-start(f32[2,8,128]{2,1,0:T(8,128)S(1)} %get-tuple-element.52), channel_id=1, source_target_pairs={{0,224},{32,64},{64,32},{96,128},{128,96},{160,192},{192,160},{224... | collective-permute-start | bytes 24584 | tf_op jit(solution)/shard_map/ppermute | solution.py:546
  94.3 2.9 %collective-permute-done.16.second_ref = f32[2,8,128]{2,1,0:T(8,128)S(1)} collective-permute-done((f32[2,8,128]{2,1,0:T(8,128)S(1)}, f32[2,8,128]{2,1,0:T(8,128)S(1)}, u32[]{:S(2)}, u32[]{:S(2)}) %collective-permute-start.16) | collective-permute-done | bytes 8224 | tf_op jit(solution)/shard_map/ppermute | solution.py:546
  97.1 0.6 smooth.1
  (26 shorter events, 0.4 us)
Async XLA Ops:
  0.0 12.7 %copy-start = (f32[64,16]{0,1:T(8,128)S(1)}, f32[64,16]{0,1:T(8,128)}, u32[]{:S(2)}) copy-start(f32[64,16]{0,1:T(8,128)} %param.11) | copy-start | bytes 12292
  0.0 22.9 %collective-permute-start.1 = (bf16[2,32,32,128]{3,2,1,0:T(8,128)(2,1)}, bf16[2,32,32,128]{3,2,1,0:T(8,128)(2,1)S(1)}, u32[]{:S(2)}, u32[]{:S(2)}) collective-permute-start(bf16[2,32,32,128]{3,2,1,0:T(8,128)(2,1)} %own_ref.1), channel_id=1, source_target_pairs={{32,0},{64,32},{96,64},{128,96},{160,128},{192,160},{224,192},{0,2... | collective-permute-start | bytes 1572872 | tf_op jit(solution)/shard_map/ppermute | solution.py:423
  4.3 21.9 %collective-permute-start = (bf16[2,32,32,128]{3,2,1,0:T(8,128)(2,1)}, bf16[2,32,32,128]{3,2,1,0:T(8,128)(2,1)S(1)}, u32[]{:S(2)}, u32[]{:S(2)}) collective-permute-start(bf16[2,32,32,128]{3,2,1,0:T(8,128)(2,1)} %own_ref.1), channel_id=1, source_target_pairs={{0,32},{32,64},{64,96},{96,128},{128,160},{160,192},{192,224},{224... | collective-permute-start | bytes 1572872 | tf_op jit(solution)/shard_map/ppermute | solution.py:422
  5.1 12.2 %collective-permute-start.2 = (f32[8,128]{1,0:T(8,128)S(1)}, f32[8,128]{1,0:T(8,128)S(1)}, u32[]{:S(2)}, u32[]{:S(2)}) collective-permute-start(f32[8,128]{1,0:T(8,128)S(1)} %broadcast_in_dim.12), channel_id=1, source_target_pairs={{0,16},{1,17},{2,18},{3,19},{4,20},{5,21},{6,22},{7,23},{8,24},{9,... | collective-permute-start | bytes 12296 | tf_op jit(solution)/shard_map/ppermute | solution.py:417
  14.8 1.0 %copy-start.1 = (bf16[2,32,32,128]{3,2,1,0:T(8,128)(2,1)S(1)}, bf16[2,32,32,128]{3,2,1,0:T(8,128)(2,1)}, u32[]{:S(2)}) copy-start(bf16[2,32,32,128]{3,2,1,0:T(8,128)(2,1)} %own_ref.1) | copy-start | bytes 1572868
  15.8 0.7 copy-start.2
  34.1 2.2 %collective-permute-start.3 = (f32[8,48,384]{2,1,0:T(8,128)S(1)}, f32[8,48,384]{2,1,0:T(8,128)S(1)}, u32[]{:S(2)}, u32[]{:S(2)}) collective-permute-start(f32[8,48,384]{2,1,0:T(8,128)S(1)} %get-tuple-element.32), channel_id=1, source_target_pairs={{0,1},{1,0},{2,3},{3,2},{4,5},{5,4},{6,7},{7,6},{8,9},{9,8},{10,11... | collective-permute-start | bytes 1769480 | tf_op jit(solution)/shard_map/ppermute | solution.py:417
  36.5 8.2 %collective-permute-start.6 = (f32[2,48,384]{2,1,0:T(8,128)S(1)}, f32[2,48,384]{2,1,0:T(8,128)S(1)}, u32[]{:S(2)}, u32[]{:S(2)}) collective-permute-start(f32[2,48,384]{2,1,0:T(8,128)S(1)} %get-tuple-element.53), channel_id=1, source_target_pairs={{0,6},{1,7},{2,4},{3,5},{4,2},{5,3},{6,0},{7,1},{8,14},{9,15},{10,... | collective-permute-start | bytes 442376 | tf_op jit(solution)/shard_map/ppermute | solution.py:417
  40.7 6.6 %collective-permute-start.5 = (f32[2,48,384]{2,1,0:T(8,128)S(1)}, f32[2,48,384]{2,1,0:T(8,128)S(1)}, u32[]{:S(2)}, u32[]{:S(2)}) collective-permute-start(f32[2,48,384]{2,1,0:T(8,128)S(1)} %get-tuple-element.54), channel_id=1, source_target_pairs={{0,2},{1,3},{2,0},{3,1},{4,6},{5,7},{6,4},{7,5},{8,10},{9,11},{10,... | collective-permute-start | bytes 442376 | tf_op jit(solution)/shard_map/ppermute | solution.py:417
  40.9 6.5 %collective-permute-start.4 = (f32[2,48,384]{2,1,0:T(8,128)S(1)}, f32[2,48,384]{2,1,0:T(8,128)S(1)}, u32[]{:S(2)}, u32[]{:S(2)}) collective-permute-start(f32[2,48,384]{2,1,0:T(8,128)S(1)} %get-tuple-element.55), channel_id=1, source_target_pairs={{0,4},{1,5},{2,6},{3,7},{4,0},{5,1},{6,2},{7,3},{8,12},{9,13},{10,... | collective-permute-start | bytes 442376 | tf_op jit(solution)/shard_map/ppermute | solution.py:417
  47.4 11.2 %collective-permute-start.7 = (f32[48,384]{1,0:T(8,128)S(1)}, f32[48,384]{1,0:T(8,128)S(1)}, u32[]{:S(2)}, u32[]{:S(2)}) collective-permute-start(f32[48,384]{1,0:T(8,128)S(1)} %slice_bitcast_fusion), channel_id=1, source_target_pairs={{0,8},{1,9},{2,10},{3,11},{4,12},{5,13},{6,14},{7,15},{8,0},{9,1},... | collective-permute-start | bytes 221192 | tf_op jit(solution)/shard_map/ppermute | solution.py:417
  50.5 5.9 %collective-permute-start.8 = (bf16[64,128]{1,0:T(8,128)(2,1)S(1)}, bf16[64,128]{1,0:T(8,128)(2,1)S(1)}, u32[]{:S(2)}, u32[]{:S(2)}) collective-permute-start(bf16[64,128]{1,0:T(8,128)(2,1)S(1)} %get-tuple-element.39), channel_id=1, source_target_pairs={{0,1},{1,0},{2,3},{3,2},{4,5},{5,4},{6,7},{7,6},{8,9},{9,8},{10,11... | collective-permute-start | bytes 49160 | tf_op jit(solution)/shard_map/ppermute | solution.py:508
  52.1 6.5 %collective-permute-start.9 = (bf16[64,128]{1,0:T(8,128)(2,1)S(1)}, bf16[64,128]{1,0:T(8,128)(2,1)S(1)}, u32[]{:S(2)}, u32[]{:S(2)}) collective-permute-start(bf16[64,128]{1,0:T(8,128)(2,1)S(1)} %get-tuple-element.40), channel_id=1, source_target_pairs={{1,2},{2,1},{3,4},{4,3},{5,6},{6,5},{7,8},{8,7},{9,10},{10,9},{11,... | collective-permute-start | bytes 49160 | tf_op jit(solution)/shard_map/ppermute | solution.py:508
  58.7 7.3 %collective-permute-start.10 = (f32[48,384]{1,0:T(8,128)S(1)}, f32[48,384]{1,0:T(8,128)S(1)}, u32[]{:S(2)}, u32[]{:S(2)}) collective-permute-start(f32[48,384]{1,0:T(8,128)S(1)} %fusion.2.first_ref), channel_id=1, source_target_pairs={{0,16},{1,17},{2,18},{3,19},{4,20},{5,21},{6,22},{7,23},{8,24},{9,... | collective-permute-start | bytes 221192 | tf_op jit(solution)/shard_map/ppermute | solution.py:417
  71.0 3.6 %collective-permute-start.11 = (f32[1,8,128]{2,1,0:T(8,128)S(1)}, f32[1,8,128]{2,1,0:T(8,128)S(1)}, u32[]{:S(2)}, u32[]{:S(2)}) collective-permute-start(f32[1,8,128]{2,1,0:T(8,128)S(1)} %bitcast.11), channel_id=1, source_target_pairs={{0,8},{1,9},{2,10},{3,11},{4,12},{5,13},{6,14},{7,15},{8,0},{9,1},... | collective-permute-start | bytes 12296 | tf_op jit(solution)/shard_map/ppermute | solution.py:417
  74.6 4.6 %collective-permute-start.12 = (f32[2,8,128]{2,1,0:T(8,128)S(1)}, f32[2,8,128]{2,1,0:T(8,128)S(1)}, u32[]{:S(2)}, u32[]{:S(2)}) collective-permute-start(f32[2,8,128]{2,1,0:T(8,128)S(1)} %pad_maximum_fusion.2), channel_id=1, source_target_pairs={{0,4},{1,5},{2,6},{3,7},{4,0},{5,1},{6,2},{7,3},{8,12},{9,13},{10,... | collective-permute-start | bytes 24584 | tf_op jit(solution)/shard_map/ppermute | solution.py:417
  79.3 4.1 %collective-permute-start.13 = (f32[4,8,128]{2,1,0:T(8,128)S(1)}, f32[4,8,128]{2,1,0:T(8,128)S(1)}, u32[]{:S(2)}, u32[]{:S(2)}) collective-permute-start(f32[4,8,128]{2,1,0:T(8,128)S(1)} %pad_maximum_fusion.1), channel_id=1, source_target_pairs={{0,2},{1,3},{2,0},{3,1},{4,6},{5,7},{6,4},{7,5},{8,10},{9,11},{10,... | collective-permute-start | bytes 49160 | tf_op jit(solution)/shard_map/ppermute | solution.py:417
  83.4 5.0 %collective-permute-start.14 = (f32[8,8,128]{2,1,0:T(8,128)S(1)}, f32[8,8,128]{2,1,0:T(8,128)S(1)}, u32[]{:S(2)}, u32[]{:S(2)}) collective-permute-start(f32[8,8,128]{2,1,0:T(8,128)S(1)} %pad_maximum_fusion), channel_id=1, source_target_pairs={{0,1},{1,0},{2,3},{3,2},{4,5},{5,4},{6,7},{7,6},{8,9},{9,8},{10,11... | collective-permute-start | bytes 98312 | tf_op jit(solution)/shard_map/ppermute | solution.py:417
  90.5 3.8 %collective-permute-start.15 = (f32[2,8,128]{2,1,0:T(8,128)S(1)}, f32[2,8,128]{2,1,0:T(8,128)S(1)}, u32[]{:S(2)}, u32[]{:S(2)}) collective-permute-start(f32[2,8,128]{2,1,0:T(8,128)S(1)} %get-tuple-element.51), channel_id=1, source_target_pairs={{0,32},{32,0},{64,96},{96,64},{128,160},{160,128},{192,224},{224,1... | collective-permute-start | bytes 24584 | tf_op jit(solution)/shard_map/ppermute | solution.py:546
  92.5 4.6 %collective-permute-start.16 = (f32[2,8,128]{2,1,0:T(8,128)S(1)}, f32[2,8,128]{2,1,0:T(8,128)S(1)}, u32[]{:S(2)}, u32[]{:S(2)}) collective-permute-start(f32[2,8,128]{2,1,0:T(8,128)S(1)} %get-tuple-element.52), channel_id=1, source_target_pairs={{0,224},{32,64},{64,32},{96,128},{128,96},{160,192},{192,160},{224... | collective-permute-start | bytes 24584 | tf_op jit(solution)/shard_map/ppermute | solution.py:546

commit v4 on v3

--- a/solution.py
+++ b/solution.py
@@ -45,8 +45,9 @@
 
 def own_group():
     place = lax.axis_index("rng")
-    bits = [lax.rem(lax.div(place, 1 << bit), 2) for bit in range(4)]
-    return bits[0] * 8 + bits[1] * 4 + bits[2] * 2 + bits[3]
+    bits = [lax.rem(lax.div(place, 1 << bit), 2) for bit in range(5)]
+    along = exclusive(bits[2], bits[4]) * 2 + exclusive(bits[3], bits[4])
+    return bits[0] * 8 + bits[1] * 4 + along
 
 
 def exclusive(left, right):
@@ -454,7 +455,7 @@
         return lax.dynamic_slice_in_dim(value, az * OWN_BEAMS, OWN_BEAMS, 0)
 
     marks = jnp.broadcast_to(train_mask.astype(F32), (OWN_BEAMS, LANES))
-    marks = marks + swap(marks, 16)
+    marks = marks + swap(marks, 28)
     first = (own(arc_start) - az * OWN_COLS + ARC // 2) % COLS
     ints = jnp.concatenate(
         [first[:, None] + own(arc_offsets), own(doppler_bins), train_mask], 1
@@ -499,18 +500,17 @@
         compiler_params=limit(8),
         name="edges_out",
     )(snaps)
-    part = keep + swap(send, 1)
+    moved, edges = lax.optimization_barrier((swap(send, 1), edges))
+    part = keep + moved
     moved = [swap(part[2:4], 4), swap(part[4:6], 2), swap(part[6:], 6)]
-    moved, edges = lax.optimization_barrier((moved, edges))
-    part = part[:2] + moved[0] + moved[1] + moved[2]
-    moved = swap(part[1], 8)
     edges = [
         lax.ppermute(value, "rng", pairs)
         for value, pairs in zip(edges, neighbours(32, False))
     ]
     moved, edges = lax.optimization_barrier((moved, edges))
-    part = part[0] + moved
-    other = swap(part, 16)
+    part = part[:2] + moved[0] + moved[1] + moved[2]
+    part = part[0] + swap(part[1], 8)
+    other = swap(part, 28)
     edge = shape(SLOTS * SEL, LANES, dtype=BF16)
     edges = pl.pallas_call(
         edge_in_kernel,

time: 98.5 us -> 94.3 us (0.957)
  starting transfers between devices: 45.9 us -> 41 us
  waiting for transfers between devices: 28.4 us -> 29.5 us
    ppermute x11, starting transfers between devices: 31.9 us -> 27.4 us  [swap(): return lax.ppermute(value, 'rng', [(i, i ^ turn) for i in range(32)])]
    ppermute x1, waiting for transfers between devices: 5.65 us -> 6.98 us  [halo_columns(): high = lax.ppermute(echoes, 'az', [(b, a) for a, b in ring])]
  transfers between devices with their start and end apart: 17 -> 17, of which waited for: 12 -> 11; matrix products, arithmetic and copies ran while one was open for 4% -> 4% of each run, Pallas kernels for 2% -> 2%
where the time goes in v4:
time: 94.3 us; the launch traced here: 94 us
  starting transfers between devices  41 us (43%)
  waiting for transfers between devices  29.5 us (31%)
  Pallas kernels  17.7 us (19%)
  local copies, waits for them, and re-layouts  3.73 us (4%)
  other arithmetic  1.84 us (2%)
    ppermute x11, starting transfers between devices, swap(): return lax.ppermute(value, 'rng', [(i, i ^ turn) for i in range(32)])  27.4 us
    ppermute x11, waiting for transfers between devices, swap(): return lax.ppermute(value, 'rng', [(i, i ^ turn) for i in range(32)])  14.3 us
    pallas_call x1, Pallas kernels, body(): pl.pallas_call(gram_kernel, out_shape=(shape(OWN_BEAMS, 2, SLOTS * SEL, C...  7.9 us
    ppermute x1, waiting for transfers between devices, halo_columns(): high = lax.ppermute(echoes, 'az', [(b, a) for a, b in ring])  6.98 us
    ppermute x2, starting transfers between devices, body(): lax.ppermute(value, 'rng', pairs)  5.42 us
    pallas_call x1, Pallas kernels, body(): pl.pallas_call(solve_kernel, out_shape=shape(8, LANES), in_specs=[VMEM] *...  5.01 us
    ppermute x1, starting transfers between devices, halo_columns(): high = lax.ppermute(echoes, 'az', [(b, a) for a, b in ring])  4.32 us
    ppermute x2, starting transfers between devices, body(): lax.ppermute(value, 'az', pairs)  3.91 us
  transfers between devices with their start and end apart: 17, of which 11 were waited for; matrix products, arithmetic and copies ran while one was open for 4% of the time, Pallas kernels for 2%

profile of v4, /device:TPU:1, one launch (start us, length us, event | category | flops | bytes accessed | tf_op | source)
XLA Modules:
  0.0 94.0 jit_solution(710024022400199867)
XLA Ops:
  0.0 4.3 %collective-permute-start.1 = (bf16[2,32,32,128]{3,2,1,0:T(8,128)(2,1)}, bf16[2,32,32,128]{3,2,1,0:T(8,128)(2,1)S(1)}, u32[]{:S(2)}, u32[]{:S(2)}) collective-permute-start(bf16[2,32,32,128]{3,2,1,0:T(8,128)(2,1)} %own_ref.1), channel_id=1, source_target_pairs={{32,0},{64,32},{96,64},{128,96},{160,128},{192,160},{224,192},{0,2... | collective-permute-start | bytes 1572872 | tf_op jit(solution)/shard_map/ppermute | solution.py:424
  4.3 0.7 convert_bitcast_fusion
  5.0 0.1 broadcast_in_dim.12
  5.1 5.6 %collective-permute-start.2 = (f32[8,128]{1,0:T(8,128)S(1)}, f32[8,128]{1,0:T(8,128)S(1)}, u32[]{:S(2)}, u32[]{:S(2)}) collective-permute-start(f32[8,128]{1,0:T(8,128)S(1)} %broadcast_in_dim.12), channel_id=1, source_target_pairs={{0,28},{1,29},{2,30},{3,31},{4,24},{5,25},{6,26},{7,27},{8,20},{9,... | collective-permute-start | bytes 12296 | tf_op jit(solution)/shard_map/ppermute | solution.py:418
  10.6 0.7 copy.10
  11.4 0.1 constant_dynamic-slice_fusion
  11.4 0.1 copy.14
  11.6 0.8 constant_dynamic-slice_fusion.1
  12.4 0.1 copy.13
  12.5 0.7 and_select_fusion
  13.2 0.1 pad_maximum_fusion.3.floats_ref
  13.3 0.1 broadcast_add_fusion.1
  13.4 0.1 pad_add_fusion.ints_ref
  13.5 1.0 %copy-done.1 = bf16[2,32,32,128]{3,2,1,0:T(8,128)(2,1)S(1)} copy-done((bf16[2,32,32,128]{3,2,1,0:T(8,128)(2,1)S(1)}, bf16[2,32,32,128]{3,2,1,0:T(8,128)(2,1)}, u32[]{:S(2)}) %copy-start.1) | copy-done | bytes 524312
  14.5 0.7 copy-done.2
  15.2 0.7 spectra.1
  15.9 0.1 broadcast_add_fusion.marks_ref
  16.0 7.0 %collective-permute-done.1.high_ref = bf16[2,32,32,128]{3,2,1,0:T(8,128)(2,1)S(1)} collective-permute-done((bf16[2,32,32,128]{3,2,1,0:T(8,128)(2,1)}, bf16[2,32,32,128]{3,2,1,0:T(8,128)(2,1)S(1)}, u32[]{:S(2)}, u32[]{:S(2)}) %collective-permute-start.1) | collective-permute-done | bytes 524320 | tf_op jit(solution)/shard_map/ppermute | solution.py:424
  23.0 3.3 %collective-permute-done.low_ref = bf16[2,32,32,128]{3,2,1,0:T(8,128)(2,1)S(1)} collective-permute-done((bf16[2,32,32,128]{3,2,1,0:T(8,128)(2,1)}, bf16[2,32,32,128]{3,2,1,0:T(8,128)(2,1)S(1)}, u32[]{:S(2)}, u32[]{:S(2)}) %collective-permute-start) | collective-permute-done | bytes 524320 | tf_op jit(solution)/shard_map/ppermute | solution.py:423
  26.2 7.9 %grams.1 = (bf16[8,2,560,128]{3,2,1,0:T(8,128)(2,1)S(1)}, f32[8,48,384]{2,1,0:T(8,128)S(1)}, f32[8,48,384]{2,1,0:T(8,128)S(1)}, f32[8,128]{1,0:T(8,128)S(1)}) custom-call(s32[8,33]{1,0:T(8,128)S(1)} %pad_add_fusion.ints_ref, f32[8,32]{1,0:T(8,128)S(1)} %pad_maximum_fusion.3.floats_ref, bf16[64,64]{1,0:T(8,128)(2,1)S(1)} %get-tuple-element.29.table_ref, ...), custom_call_target="tpu_custom_call" | custom-call | tf_op jit(solution)/shard_map/grams/pallas_call | solution.py:477
  34.1 0.6 collective-permute-start.3
  34.7 1.2 %edges_out.1 = (bf16[64,128]{1,0:T(8,128)(2,1)S(1)}, bf16[64,128]{1,0:T(8,128)(2,1)S(1)}) custom-call(bf16[8,2,560,128]{3,2,1,0:T(8,128)(2,1)S(1)} %get-tuple-element.33.snap_ref), custom_call_target="tpu_custom_call" | custom-call | tf_op jit(solution)/shard_map/edges_out/pallas_call | solution.py:495
  35.9 0.5 collective-permute-done.3
  36.3 0.1 add.47
  36.5 4.3 %collective-permute-start.6 = (f32[2,48,384]{2,1,0:T(8,128)S(1)}, f32[2,48,384]{2,1,0:T(8,128)S(1)}, u32[]{:S(2)}, u32[]{:S(2)}) collective-permute-start(f32[2,48,384]{2,1,0:T(8,128)S(1)} %get-tuple-element.53), channel_id=1, source_target_pairs={{0,6},{1,7},{2,4},{3,5},{4,2},{5,3},{6,0},{7,1},{8,14},{9,15},{10,... | collective-permute-start | bytes 442376 | tf_op jit(solution)/shard_map/ppermute | solution.py:418
  40.7 0.2 collective-permute-start.5
  40.9 0.2 collective-permute-start.4
  41.1 0.9 collective-permute-start.7
  42.0 4.5 %collective-permute-start.8 = (bf16[64,128]{1,0:T(8,128)(2,1)S(1)}, bf16[64,128]{1,0:T(8,128)(2,1)S(1)}, u32[]{:S(2)}, u32[]{:S(2)}) collective-permute-start(bf16[64,128]{1,0:T(8,128)(2,1)S(1)} %get-tuple-element.38), channel_id=1, source_target_pairs={{1,2},{2,1},{3,4},{4,3},{5,6},{6,5},{7,8},{8,7},{9,10},{10,9},{11,... | collective-permute-start | bytes 49160 | tf_op jit(solution)/shard_map/ppermute | solution.py:507
  46.5 2.0 %collective-permute-done.8.second_ref = bf16[64,128]{1,0:T(8,128)(2,1)S(1)} collective-permute-done((bf16[64,128]{1,0:T(8,128)(2,1)S(1)}, bf16[64,128]{1,0:T(8,128)(2,1)S(1)}, u32[]{:S(2)}, u32[]{:S(2)}) %collective-permute-start.8) | collective-permute-done | bytes 16416 | tf_op jit(solution)/shard_map/ppermute | solution.py:507
  48.7 3.4 %collective-permute-start.9 = (f32[48,384]{1,0:T(8,128)S(1)}, f32[48,384]{1,0:T(8,128)S(1)}, u32[]{:S(2)}, u32[]{:S(2)}) collective-permute-start(f32[48,384]{1,0:T(8,128)S(1)} %slice_bitcast_fusion), channel_id=1, source_target_pairs={{0,8},{1,9},{2,10},{3,11},{4,12},{5,13},{6,14},{7,15},{8,0},{9,1},... | collective-permute-start | bytes 221192 | tf_op jit(solution)/shard_map/ppermute | solution.py:418
  52.0 1.7 %collective-permute-done.9 = f32[48,384]{1,0:T(8,128)S(1)} collective-permute-done((f32[48,384]{1,0:T(8,128)S(1)}, f32[48,384]{1,0:T(8,128)S(1)}, u32[]{:S(2)}, u32[]{:S(2)}) %collective-permute-start.9) | collective-permute-done | bytes 73760 | tf_op jit(solution)/shard_map/ppermute | solution.py:418
  53.8 7.0 %collective-permute-start.10 = (f32[48,384]{1,0:T(8,128)S(1)}, f32[48,384]{1,0:T(8,128)S(1)}, u32[]{:S(2)}, u32[]{:S(2)}) collective-permute-start(f32[48,384]{1,0:T(8,128)S(1)} %fusion.2.first_ref), channel_id=1, source_target_pairs={{0,28},{1,29},{2,30},{3,31},{4,24},{5,25},{6,26},{7,27},{8,20},{9,... | collective-permute-start | bytes 221192 | tf_op jit(solution)/shard_map/ppermute | solution.py:418
  60.8 0.2 edges_in.1
  61.1 2.9 %collective-permute-done.10.second_ref = f32[48,384]{1,0:T(8,128)S(1)} collective-permute-done((f32[48,384]{1,0:T(8,128)S(1)}, f32[48,384]{1,0:T(8,128)S(1)}, u32[]{:S(2)}, u32[]{:S(2)}) %collective-permute-start.10) | collective-permute-done | bytes 73760 | tf_op jit(solution)/shard_map/ppermute | solution.py:418
  64.0 5.0 %solve.1 = f32[8,128]{1,0:T(8,128)S(1)} custom-call(f32[48,384]{1,0:T(8,128)S(1)} %fusion.2.first_ref, f32[48,384]{1,0:T(8,128)S(1)} %collective-permute-done.10.second_ref, f32[8,128]{1,0:T(8,128)S(1)} %get-tuple-element.47.marks_ref), custom_call_target="tpu_custom_call" | custom-call | tf_op jit(solution)/shard_map/solve/pallas_call | solution.py:524
  69.0 0.3 collective-permute-start.11
  69.3 3.3 %collective-permute-done.11 = f32[1,8,128]{2,1,0:T(8,128)S(1)} collective-permute-done((f32[1,8,128]{2,1,0:T(8,128)S(1)}, f32[1,8,128]{2,1,0:T(8,128)S(1)}, u32[]{:S(2)}, u32[]{:S(2)}) %collective-permute-start.11) | collective-permute-done | bytes 4128 | tf_op jit(solution)/shard_map/ppermute | solution.py:418
  72.7 2.5 %collective-permute-done.12 = f32[2,8,128]{2,1,0:T(8,128)S(1)} collective-permute-done((f32[2,8,128]{2,1,0:T(8,128)S(1)}, f32[2,8,128]{2,1,0:T(8,128)S(1)}, u32[]{:S(2)}, u32[]{:S(2)}) %collective-permute-start.12) | collective-permute-done | bytes 8224 | tf_op jit(solution)/shard_map/ppermute | solution.py:418
  75.2 1.6 %collective-permute-start.13 = (f32[4,8,128]{2,1,0:T(8,128)S(1)}, f32[4,8,128]{2,1,0:T(8,128)S(1)}, u32[]{:S(2)}, u32[]{:S(2)}) collective-permute-start(f32[4,8,128]{2,1,0:T(8,128)S(1)} %pad_maximum_fusion.1), channel_id=1, source_target_pairs={{0,2},{1,3},{2,0},{3,1},{4,6},{5,7},{6,4},{7,5},{8,10},{9,11},{10,... | collective-permute-start | bytes 49160 | tf_op jit(solution)/shard_map/ppermute | solution.py:418
  76.8 2.5 %collective-permute-done.13 = f32[4,8,128]{2,1,0:T(8,128)S(1)} collective-permute-done((f32[4,8,128]{2,1,0:T(8,128)S(1)}, f32[4,8,128]{2,1,0:T(8,128)S(1)}, u32[]{:S(2)}, u32[]{:S(2)}) %collective-permute-start.13) | collective-permute-done | bytes 16416 | tf_op jit(solution)/shard_map/ppermute | solution.py:418
  79.3 4.3 %collective-permute-start.14 = (f32[8,8,128]{2,1,0:T(8,128)S(1)}, f32[8,8,128]{2,1,0:T(8,128)S(1)}, u32[]{:S(2)}, u32[]{:S(2)}) collective-permute-start(f32[8,8,128]{2,1,0:T(8,128)S(1)} %pad_maximum_fusion), channel_id=1, source_target_pairs={{0,1},{1,0},{2,3},{3,2},{4,5},{5,4},{6,7},{7,6},{8,9},{9,8},{10,11... | collective-permute-start | bytes 98312 | tf_op jit(solution)/shard_map/ppermute | solution.py:418
  83.5 0.9 collective-permute-done.14
  84.4 2.1 %power.1 = (f32[16,8,128]{2,1,0:T(8,128)S(1)}, f32[2,8,128]{2,1,0:T(8,128)S(1)}, f32[2,8,128]{2,1,0:T(8,128)S(1)}) custom-call(s32[8,33]{1,0:T(8,128)S(1)} %pad_add_fusion.ints_ref, f32[16,8,128]{2,1,0:T(8,128)S(1)} %constant_dynamic-update-slice_fusion.weights_ref, bf16[8,2,560,128]{3,2,1,0:T(8,128)(2,1)S(1)} %get-tuple-element.33.snap_ref, ...), custom_call_target="tpu_custom_call" | custom-call | tf_op jit(solution)/shard_map/power/pallas_call | solution.py:537
  86.5 2.2 %collective-permute-start.15 = (f32[2,8,128]{2,1,0:T(8,128)S(1)}, f32[2,8,128]{2,1,0:T(8,128)S(1)}, u32[]{:S(2)}, u32[]{:S(2)}) collective-permute-start(f32[2,8,128]{2,1,0:T(8,128)S(1)} %get-tuple-element.51), channel_id=1, source_target_pairs={{0,32},{32,0},{64,96},{96,64},{128,160},{160,128},{192,224},{224,1... | collective-permute-start | bytes 24584 | tf_op jit(solution)/shard_map/ppermute | solution.py:546
  88.7 1.7 %collective-permute-start.16 = (f32[2,8,128]{2,1,0:T(8,128)S(1)}, f32[2,8,128]{2,1,0:T(8,128)S(1)}, u32[]{:S(2)}, u32[]{:S(2)}) collective-permute-start(f32[2,8,128]{2,1,0:T(8,128)S(1)} %get-tuple-element.52), channel_id=1, source_target_pairs={{0,224},{32,64},{64,32},{96,128},{128,96},{160,192},{192,160},{224... | collective-permute-start | bytes 24584 | tf_op jit(solution)/shard_map/ppermute | solution.py:546
  90.4 2.9 %collective-permute-done.16.second_ref = f32[2,8,128]{2,1,0:T(8,128)S(1)} collective-permute-done((f32[2,8,128]{2,1,0:T(8,128)S(1)}, f32[2,8,128]{2,1,0:T(8,128)S(1)}, u32[]{:S(2)}, u32[]{:S(2)}) %collective-permute-start.16) | collective-permute-done | bytes 8224 | tf_op jit(solution)/shard_map/ppermute | solution.py:546
  93.3 0.6 smooth.1
  (26 shorter events, 0.3 us)
Async XLA Ops:
  0.0 11.4 %copy-start = (f32[64,16]{0,1:T(8,128)S(1)}, f32[64,16]{0,1:T(8,128)}, u32[]{:S(2)}) copy-start(f32[64,16]{0,1:T(8,128)} %param.11) | copy-start | bytes 12292
  0.0 22.9 %collective-permute-start.1 = (bf16[2,32,32,128]{3,2,1,0:T(8,128)(2,1)}, bf16[2,32,32,128]{3,2,1,0:T(8,128)(2,1)S(1)}, u32[]{:S(2)}, u32[]{:S(2)}) collective-permute-start(bf16[2,32,32,128]{3,2,1,0:T(8,128)(2,1)} %own_ref.1), channel_id=1, source_target_pairs={{32,0},{64,32},{96,64},{128,96},{160,128},{192,160},{224,192},{0,2... | collective-permute-start | bytes 1572872 | tf_op jit(solution)/shard_map/ppermute | solution.py:424
  4.3 21.9 %collective-permute-start = (bf16[2,32,32,128]{3,2,1,0:T(8,128)(2,1)}, bf16[2,32,32,128]{3,2,1,0:T(8,128)(2,1)S(1)}, u32[]{:S(2)}, u32[]{:S(2)}) collective-permute-start(bf16[2,32,32,128]{3,2,1,0:T(8,128)(2,1)} %own_ref.1), channel_id=1, source_target_pairs={{0,32},{32,64},{64,96},{96,128},{128,160},{160,192},{192,224},{224... | collective-permute-start | bytes 1572872 | tf_op jit(solution)/shard_map/ppermute | solution.py:423
  5.1 10.8 %collective-permute-start.2 = (f32[8,128]{1,0:T(8,128)S(1)}, f32[8,128]{1,0:T(8,128)S(1)}, u32[]{:S(2)}, u32[]{:S(2)}) collective-permute-start(f32[8,128]{1,0:T(8,128)S(1)} %broadcast_in_dim.12), channel_id=1, source_target_pairs={{0,28},{1,29},{2,30},{3,31},{4,24},{5,25},{6,26},{7,27},{8,20},{9,... | collective-permute-start | bytes 12296 | tf_op jit(solution)/shard_map/ppermute | solution.py:418
  13.5 1.0 %copy-start.1 = (bf16[2,32,32,128]{3,2,1,0:T(8,128)(2,1)S(1)}, bf16[2,32,32,128]{3,2,1,0:T(8,128)(2,1)}, u32[]{:S(2)}) copy-start(bf16[2,32,32,128]{3,2,1,0:T(8,128)(2,1)} %own_ref.1) | copy-start | bytes 1572868
  14.5 0.7 copy-start.2
  34.1 2.2 %collective-permute-start.3 = (f32[8,48,384]{2,1,0:T(8,128)S(1)}, f32[8,48,384]{2,1,0:T(8,128)S(1)}, u32[]{:S(2)}, u32[]{:S(2)}) collective-permute-start(f32[8,48,384]{2,1,0:T(8,128)S(1)} %get-tuple-element.32), channel_id=1, source_target_pairs={{0,1},{1,0},{2,3},{3,2},{4,5},{5,4},{6,7},{7,6},{8,9},{9,8},{10,11... | collective-permute-start | bytes 1769480 | tf_op jit(solution)/shard_map/ppermute | solution.py:418
  36.5 12.1 %collective-permute-start.6 = (f32[2,48,384]{2,1,0:T(8,128)S(1)}, f32[2,48,384]{2,1,0:T(8,128)S(1)}, u32[]{:S(2)}, u32[]{:S(2)}) collective-permute-start(f32[2,48,384]{2,1,0:T(8,128)S(1)} %get-tuple-element.53), channel_id=1, source_target_pairs={{0,6},{1,7},{2,4},{3,5},{4,2},{5,3},{6,0},{7,1},{8,14},{9,15},{10,... | collective-permute-start | bytes 442376 | tf_op jit(solution)/shard_map/ppermute | solution.py:418
  40.7 7.9 %collective-permute-start.5 = (f32[2,48,384]{2,1,0:T(8,128)S(1)}, f32[2,48,384]{2,1,0:T(8,128)S(1)}, u32[]{:S(2)}, u32[]{:S(2)}) collective-permute-start(f32[2,48,384]{2,1,0:T(8,128)S(1)} %get-tuple-element.54), channel_id=1, source_target_pairs={{0,2},{1,3},{2,0},{3,1},{4,6},{5,7},{6,4},{7,5},{8,10},{9,11},{10,... | collective-permute-start | bytes 442376 | tf_op jit(solution)/shard_map/ppermute | solution.py:418
  40.9 7.7 %collective-permute-start.4 = (f32[2,48,384]{2,1,0:T(8,128)S(1)}, f32[2,48,384]{2,1,0:T(8,128)S(1)}, u32[]{:S(2)}, u32[]{:S(2)}) collective-permute-start(f32[2,48,384]{2,1,0:T(8,128)S(1)} %get-tuple-element.55), channel_id=1, source_target_pairs={{0,4},{1,5},{2,6},{3,7},{4,0},{5,1},{6,2},{7,3},{8,12},{9,13},{10,... | collective-permute-start | bytes 442376 | tf_op jit(solution)/shard_map/ppermute | solution.py:418
  41.1 5.4 %collective-permute-start.7 = (bf16[64,128]{1,0:T(8,128)(2,1)S(1)}, bf16[64,128]{1,0:T(8,128)(2,1)S(1)}, u32[]{:S(2)}, u32[]{:S(2)}) collective-permute-start(bf16[64,128]{1,0:T(8,128)(2,1)S(1)} %get-tuple-element.37), channel_id=1, source_target_pairs={{0,1},{1,0},{2,3},{3,2},{4,5},{5,4},{6,7},{7,6},{8,9},{9,8},{10,11... | collective-permute-start | bytes 49160 | tf_op jit(solution)/shard_map/ppermute | solution.py:507
  42.0 6.5 %collective-permute-start.8 = (bf16[64,128]{1,0:T(8,128)(2,1)S(1)}, bf16[64,128]{1,0:T(8,128)(2,1)S(1)}, u32[]{:S(2)}, u32[]{:S(2)}) collective-permute-start(bf16[64,128]{1,0:T(8,128)(2,1)S(1)} %get-tuple-element.38), channel_id=1, source_target_pairs={{1,2},{2,1},{3,4},{4,3},{5,6},{6,5},{7,8},{8,7},{9,10},{10,9},{11,... | collective-permute-start | bytes 49160 | tf_op jit(solution)/shard_map/ppermute | solution.py:507
  48.7 5.1 %collective-permute-start.9 = (f32[48,384]{1,0:T(8,128)S(1)}, f32[48,384]{1,0:T(8,128)S(1)}, u32[]{:S(2)}, u32[]{:S(2)}) collective-permute-start(f32[48,384]{1,0:T(8,128)S(1)} %slice_bitcast_fusion), channel_id=1, source_target_pairs={{0,8},{1,9},{2,10},{3,11},{4,12},{5,13},{6,14},{7,15},{8,0},{9,1},... | collective-permute-start | bytes 221192 | tf_op jit(solution)/shard_map/ppermute | solution.py:418
  53.8 10.2 %collective-permute-start.10 = (f32[48,384]{1,0:T(8,128)S(1)}, f32[48,384]{1,0:T(8,128)S(1)}, u32[]{:S(2)}, u32[]{:S(2)}) collective-permute-start(f32[48,384]{1,0:T(8,128)S(1)} %fusion.2.first_ref), channel_id=1, source_target_pairs={{0,28},{1,29},{2,30},{3,31},{4,24},{5,25},{6,26},{7,27},{8,20},{9,... | collective-permute-start | bytes 221192 | tf_op jit(solution)/shard_map/ppermute | solution.py:418
  69.0 3.6 %collective-permute-start.11 = (f32[1,8,128]{2,1,0:T(8,128)S(1)}, f32[1,8,128]{2,1,0:T(8,128)S(1)}, u32[]{:S(2)}, u32[]{:S(2)}) collective-permute-start(f32[1,8,128]{2,1,0:T(8,128)S(1)} %bitcast.11), channel_id=1, source_target_pairs={{0,8},{1,9},{2,10},{3,11},{4,12},{5,13},{6,14},{7,15},{8,0},{9,1},... | collective-permute-start | bytes 12296 | tf_op jit(solution)/shard_map/ppermute | solution.py:418
  72.6 2.5 %collective-permute-start.12 = (f32[2,8,128]{2,1,0:T(8,128)S(1)}, f32[2,8,128]{2,1,0:T(8,128)S(1)}, u32[]{:S(2)}, u32[]{:S(2)}) collective-permute-start(f32[2,8,128]{2,1,0:T(8,128)S(1)} %pad_maximum_fusion.2), channel_id=1, source_target_pairs={{0,4},{1,5},{2,6},{3,7},{4,0},{5,1},{6,2},{7,3},{8,12},{9,13},{10,... | collective-permute-start | bytes 24584 | tf_op jit(solution)/shard_map/ppermute | solution.py:418
  75.2 4.1 %collective-permute-start.13 = (f32[4,8,128]{2,1,0:T(8,128)S(1)}, f32[4,8,128]{2,1,0:T(8,128)S(1)}, u32[]{:S(2)}, u32[]{:S(2)}) collective-permute-start(f32[4,8,128]{2,1,0:T(8,128)S(1)} %pad_maximum_fusion.1), channel_id=1, source_target_pairs={{0,2},{1,3},{2,0},{3,1},{4,6},{5,7},{6,4},{7,5},{8,10},{9,11},{10,... | collective-permute-start | bytes 49160 | tf_op jit(solution)/shard_map/ppermute | solution.py:418
  79.3 5.1 %collective-permute-start.14 = (f32[8,8,128]{2,1,0:T(8,128)S(1)}, f32[8,8,128]{2,1,0:T(8,128)S(1)}, u32[]{:S(2)}, u32[]{:S(2)}) collective-permute-start(f32[8,8,128]{2,1,0:T(8,128)S(1)} %pad_maximum_fusion), channel_id=1, source_target_pairs={{0,1},{1,0},{2,3},{3,2},{4,5},{5,4},{6,7},{7,6},{8,9},{9,8},{10,11... | collective-permute-start | bytes 98312 | tf_op jit(solution)/shard_map/ppermute | solution.py:418
  86.5 3.9 %collective-permute-start.15 = (f32[2,8,128]{2,1,0:T(8,128)S(1)}, f32[2,8,128]{2,1,0:T(8,128)S(1)}, u32[]{:S(2)}, u32[]{:S(2)}) collective-permute-start(f32[2,8,128]{2,1,0:T(8,128)S(1)} %get-tuple-element.51), channel_id=1, source_target_pairs={{0,32},{32,0},{64,96},{96,64},{128,160},{160,128},{192,224},{224,1... | collective-permute-start | bytes 24584 | tf_op jit(solution)/shard_map/ppermute | solution.py:546
  88.7 4.6 %collective-permute-start.16 = (f32[2,8,128]{2,1,0:T(8,128)S(1)}, f32[2,8,128]{2,1,0:T(8,128)S(1)}, u32[]{:S(2)}, u32[]{:S(2)}) collective-permute-start(f32[2,8,128]{2,1,0:T(8,128)S(1)} %get-tuple-element.52), channel_id=1, source_target_pairs={{0,224},{32,64},{64,32},{96,128},{128,96},{160,192},{192,160},{224... | collective-permute-start | bytes 24584 | tf_op jit(solution)/shard_map/ppermute | solution.py:546

commit v5 on v4

--- a/solution.py
+++ b/solution.py
@@ -22,7 +22,7 @@
 CELLS = 128
 GROUPS = 16
 LANES = 128
-SLOTS = PULSES + 3
+SLOTS = PULSES + 8
 LOADING = 0.1
 F32 = jnp.float32
 BF16 = jnp.bfloat16
@@ -80,7 +80,7 @@
     ints_ref, floats_ref,
     table_ref, low_ref, own_ref, high_ref, marks_ref,
     snap_ref, keep_ref, send_ref, passed_ref,
-    spec_ref, wide_ref,
+    spec_ref, wide_ref, even_ref, odd_ref,
 ):
     mine = own_group()
     table = table_ref[...]
@@ -89,9 +89,9 @@
     def transform(index, carry):
         for one in range(2):
             spectra(table, low_ref, 2 * index + one, spec_ref, 0)
-            spectra(table, high_ref, 2 * index + one, spec_ref, 2 * OWN_COLS)
         for one in range(4):
             spec_ref[OWN_COLS + 4 * index + one] = own_ref[4 * index + one]
+            spec_ref[2 * OWN_COLS + 4 * index + one] = high_ref[4 * index + one]
         return carry
 
     lax.fori_loop(0, OWN_COLS // 4, transform, 0)
@@ -105,7 +105,7 @@
     def first_group(step):
         return exclusive(exclusive(2 * step, 8), mine)
 
-    def turn(step):
+    def turn(step, work_ref):
         beam = lax.div(first_group(step), 2)
         for sel in range(SEL):
             column = ints_ref[beam, sel]
@@ -120,13 +120,16 @@
             for low, high, place in (
                 (SEL, SEL + last, SEL),
                 (last, last + SEL, 0),
-                (SEL, 3 * SEL, SEL + last),
+                (SEL, 2 * SEL, SEL + last),
             ):
-                snap_ref[beam, part, place : place + high - low, :] = wide_ref[
-                    part, low:high, :
-                ].astype(BF16)
-
-    def multiply(step, out_ref):
+                value = wide_ref[part, low:high, :].astype(BF16)
+                work_ref[part, place : place + high - low, :] = value
+                snap_ref[beam, part, place : place + high - low, :] = value
+            snap_ref[beam, part, last + 2 * SEL :, :] = jnp.zeros(
+                (SLOTS * SEL - last - 2 * SEL, CELLS), BF16
+            )
+
+    def multiply(step, work_ref, out_ref):
         group = first_group(step)
         beam = lax.div(group, 2)
         weight = ints_ref[beam, 2 * SEL].astype(F32)
@@ -138,8 +141,8 @@
                 for one in range(2):
                     centre = ints_ref[beam, SEL + base + pair * 2 + one]
                     rows = pl.ds(pl.multiple_of(centre * SEL, SEL), DOF)
-                    real = snap_ref[beam, 0, rows, :]
-                    imag = snap_ref[beam, 1, rows, :]
+                    real = work_ref[0, rows, :]
+                    imag = work_ref[1, rows, :]
                     same.append(jnp.concatenate([real, imag], 1))
                     turned.append(jnp.concatenate([imag, -real], 1))
                 left = jnp.concatenate([same[0], turned[0], same[1], turned[1]], 0)
@@ -171,20 +174,22 @@
                     out[part] * weight
                 )
 
-    def sending(step, carry):
-        turn(step + 1)
-        multiply(step, send_ref)
+    def sending(index, carry):
+        turn(2 * index + 1, odd_ref)
+        multiply(2 * index, even_ref, send_ref)
+        turn(2 * index + 2, even_ref)
+        multiply(2 * index + 1, odd_ref, send_ref)
         return carry
 
-    def keeping(step, carry):
-        turn(step + 1)
-        multiply(step, keep_ref)
-        return carry
-
-    turn(0)
-    lax.fori_loop(0, 4, sending, 0)
-    lax.fori_loop(4, 7, keeping, 0)
-    multiply(7, keep_ref)
+    turn(0, even_ref)
+    lax.fori_loop(0, 2, sending, 0)
+    turn(5, odd_ref)
+    multiply(4, even_ref, keep_ref)
+    turn(6, even_ref)
+    multiply(5, odd_ref, keep_ref)
+    turn(7, odd_ref)
+    multiply(6, even_ref, keep_ref)
+    multiply(7, odd_ref, keep_ref)
 
 
 def edge_out_kernel(snap_ref, first_ref, second_ref):
@@ -207,8 +212,9 @@
     second_ref[...] = jnp.where(even, ends[0], ends[1]).astype(BF16)
 
 
-def edge_in_kernel(first_ref, second_ref, direct_ref, turned_ref):
+def edge_in_kernel(first_ref, second_ref, out_ref):
     rows = 8 * 8
+    last = PULSES * SEL
     lane = lane_ids(rows)
     first = first_ref[...].astype(F32)
     second = second_ref[...].astype(F32)
@@ -220,13 +226,17 @@
         both = jnp.where(
             lane < 16, rolled(first, -16 * block), rolled(second, 16 - 16 * block)
         )
-        for ref, value in ((direct_ref, both), (turned_ref, rolled(both, -8))):
+        for part, value in enumerate((both, rolled(both, -8))):
             value = value.astype(BF16)
-            ref[SEL + rows * block : SEL + rows * (block + 1), :] = value
+            out_ref[part, SEL + rows * block : SEL + rows * (block + 1), :] = value
             if block == 0:
-                ref[PULSES * SEL + SEL :, :] = value[: 2 * SEL]
+                out_ref[part, last + SEL : last + 2 * SEL, :] = value[:SEL]
             if block == 7:
-                ref[:SEL, :] = value[rows - SEL :]
+                out_ref[part, :SEL, :] = value[rows - SEL :]
+    for part in range(2):
+        out_ref[part, last + 2 * SEL :, :] = jnp.zeros(
+            (SLOTS * SEL - last - 2 * SEL, CELLS), BF16
+        )
 
 
 def spread(value, index):
@@ -309,30 +319,75 @@
         real[group][3] = jnp.ones((8, LANES), F32)
         imag[group][3] = jnp.zeros((8, LANES), F32)
     inverse = [jnp.ones((8, LANES), F32)] * 6
-    for k in range(DOF):
+    for k in range(0, DOF, 2):
         group, inner, part = k // 8, k % 8, k // SEL
-        index = base + k % SEL
-        mult_re = [jnp.take_along_axis(real[i][part], index, axis=1) for i in range(6)]
-        mult_im = [jnp.take_along_axis(imag[i][part], index, axis=1) for i in range(6)]
-        pivot = jnp.broadcast_to(mult_re[group][inner : inner + 1], (8, LANES))
-        pivot = 1.0 / pivot
-        here = line == inner
-        mult_re[group] = jnp.where(here, 0.0, mult_re[group])
-        mult_im[group] = jnp.where(here, 0.0, mult_im[group])
-        inverse[group] = jnp.where(here, pivot, inverse[group])
+        columns = []
+        for step in range(2):
+            index = base + k % SEL + step
+            columns.append(
+                [
+                    [
+                        jnp.take_along_axis(half[i][part], index, axis=1)
+                        for i in range(6)
+                    ]
+                    for half in (real, imag)
+                ]
+            )
+        (zero_re, zero_im), (one_re, one_im) = columns
+
+        def line_of(value, offset):
+            return jnp.broadcast_to(
+                value[inner + offset : inner + offset + 1], (8, LANES)
+            )
+
+        side_re, side_im = line_of(one_re[group], 0), line_of(one_im[group], 0)
+        below_re, below_im = line_of(zero_re[group], 1), line_of(zero_im[group], 1)
+        first = 1.0 / line_of(zero_re[group], 0)
+        below_re, below_im = below_re * first, below_im * first
+        second = 1.0 / (
+            line_of(one_re[group], 1) - below_re * side_re + below_im * side_im
+        )
+        upper, under = line == inner, line == inner + 1
+        inverse[group] = jnp.where(
+            upper, first, jnp.where(under, second, inverse[group])
+        )
+        zero_re[group] = jnp.where(upper, 0.0, zero_re[group])
+        zero_im[group] = jnp.where(upper, 0.0, zero_im[group])
+        alpha_re = [value * first for value in zero_re]
+        alpha_im = [value * first for value in zero_im]
+        beta_re = [
+            (one_re[i] - alpha_re[i] * side_re + alpha_im[i] * side_im) * second
+            for i in range(6)
+        ]
+        beta_im = [
+            (one_im[i] - alpha_re[i] * side_im - alpha_im[i] * side_re) * second
+            for i in range(6)
+        ]
+        beta_re[group] = jnp.where(under, 0.0, beta_re[group])
+        beta_im[group] = jnp.where(under, 0.0, beta_im[group])
         for block in (*range(part, BINS), 3):
-            row_re = pivot * jnp.broadcast_to(
-                real[group][block][inner : inner + 1], (8, LANES)
-            )
-            row_im = pivot * jnp.broadcast_to(
-                imag[group][block][inner : inner + 1], (8, LANES)
+            row_re = line_of(real[group][block], 0)
+            row_im = line_of(imag[group][block], 0)
+            next_re = (
+                line_of(real[group][block], 1) - below_re * row_re + below_im * row_im
+            )
+            next_im = (
+                line_of(imag[group][block], 1) - below_re * row_im - below_im * row_re
             )
             for i in range(6):
                 real[i][block] = (
-                    real[i][block] - mult_re[i] * row_re + mult_im[i] * row_im
+                    real[i][block]
+                    - alpha_re[i] * row_re
+                    + alpha_im[i] * row_im
+                    - beta_re[i] * next_re
+                    + beta_im[i] * next_im
                 )
                 imag[i][block] = (
-                    imag[i][block] - mult_re[i] * row_im - mult_im[i] * row_re
+                    imag[i][block]
+                    - alpha_re[i] * row_im
+                    - alpha_im[i] * row_re
+                    - beta_re[i] * next_im
+                    - beta_im[i] * next_re
                 )
     gap = jnp.zeros((SEL, LANES), F32)
     found_re = [real[i][3] * inverse[i] for i in range(6)]
@@ -349,7 +404,7 @@
 
 
 def power_kernel(
-    ints_ref, weights_ref, snap_ref, direct_ref, turned_ref,
+    bins_ref, weights_ref, snap_ref, edge_ref,
     power_ref, first_ref, second_ref,
 ):
     mine = own_group()
@@ -359,40 +414,46 @@
     for place in range(GROUPS):
         counts = counts + weights_ref[place]
     counts = spread(counts, 120) * BLK
-    used = jnp.logical_or(
-        small < DOF, jnp.logical_and(small >= 64, small < 64 + DOF)
-    )
-    row = lax.broadcasted_iota(jnp.int32, (2 * 8, 2 * LANES), 0)
     low_lane = jnp.where(even, 16, 0)
-    for group in range(GROUPS):
-        beam = group // 2
-        scaled = weights_ref[exclusive(mine, group)] * counts[beam : beam + 1, :]
-        quiet = spread(scaled, 56)
-        direct = jnp.where(used, scaled, 0.0)
-        turned = pltpu.roll(direct, 64, 1)
-        turned = jnp.where(small < 64, -turned, turned)
-        left = jnp.concatenate([direct, turned], 0).astype(BF16)
-        found = jnp.zeros((16, 2 * LANES), F32)
-        for one in range(8):
-            centre = ints_ref[beam, SEL + (group % 2) * 8 + one]
-            rows = pl.ds(pl.multiple_of(centre * SEL, SEL), 64)
-            right = jnp.concatenate(
-                [
-                    jnp.concatenate([snap_ref[beam, 0, rows, :], direct_ref[rows, :]], 1),
-                    jnp.concatenate([snap_ref[beam, 1, rows, :], turned_ref[rows, :]], 1),
-                ],
-                0,
-            )
-            product = jnp.dot(left, right, preferred_element_type=F32)
-            found = jnp.where(lax.rem(row, 8) == one, product, found)
-        power = found[:8] * found[:8] + found[8:] * found[8:]
-        inner = power[:, :LANES] / quiet
-        outer = power[:, LANES:] / quiet
-        low = spread(outer, beam + low_lane)
-        high = spread(outer, beam + 16 - low_lane)
-        below = jnp.where(small == 0, low, pltpu.roll(inner, 1, 1))
-        above = jnp.where(small == LANES - 1, high, pltpu.roll(inner, LANES - 1, 1))
-        power_ref[group] = below + inner + above
+    rows = SLOTS * SEL
+    edge = edge_ref[...].reshape(2 * rows, LANES)
+    for beam in range(OWN_BEAMS):
+        lefts, quiets = [], []
+        for group in (2 * beam, 2 * beam + 1):
+            scaled = weights_ref[exclusive(mine, group)] * counts[beam : beam + 1, :]
+            quiets.append(spread(scaled, 56))
+            away = small - bins_ref[group] * SEL
+            left = [[], []]
+            for tile in range(rows // LANES):
+                index = away + LANES * tile
+                inside = jnp.logical_and(index >= 0, index < DOF)
+                direct = jnp.take_along_axis(
+                    scaled, lax.bitwise_and(index, LANES - 1), axis=1
+                )
+                crossed = jnp.take_along_axis(
+                    scaled, lax.bitwise_and(index + 64, LANES - 1), axis=1
+                )
+                direct = jnp.where(inside, direct, 0.0)
+                crossed = jnp.where(inside, crossed, 0.0)
+                left[0].append(jnp.concatenate([direct, -crossed], 0).astype(BF16))
+                left[1].append(jnp.concatenate([crossed, direct], 0).astype(BF16))
+            lefts.append(jnp.concatenate(left[0] + left[1], 1))
+        right = jnp.concatenate([snap_ref[beam].reshape(2 * rows, LANES), edge], 1)
+        found = jnp.dot(
+            jnp.concatenate(lefts, 0), right, preferred_element_type=F32
+        )
+        found = found * found
+        for half in range(2):
+            power = found[16 * half : 16 * half + 8] + found[16 * half + 8 : 16 * half + 16]
+            inner = power[:, :LANES] / quiets[half]
+            outer = power[:, LANES:] / quiets[half]
+            low = spread(outer, beam + low_lane)
+            high = spread(outer, beam + 16 - low_lane)
+            below = jnp.where(small == 0, low, pltpu.roll(inner, 1, 1))
+            above = jnp.where(
+                small == LANES - 1, high, pltpu.roll(inner, LANES - 1, 1)
+            )
+            power_ref[2 * beam + half] = below + inner + above
     even = lax.rem(lax.axis_index("az"), 2) == 0
     for half in range(2):
         bottom, top = power_ref[half], power_ref[GROUPS - 2 + half]
@@ -462,7 +523,10 @@
     )
     angles = own(steer_angles)
     floats = jnp.concatenate([jnp.cos(angles), jnp.sin(angles)], 1)
-    spec, table = pl.pallas_call(
+    centres = jnp.broadcast_to(
+        own(doppler_bins).reshape(GROUPS, 8, 1), (GROUPS, 8, LANES)
+    )
+    transform = pl.pallas_call(
         own_kernel,
         out_shape=(
             shape(OWN_COLS, 2 * PULSES, CELLS),
@@ -472,7 +536,9 @@
         out_specs=(VMEM, VMEM),
         compiler_params=limit(8),
         name="spectra",
-    )(jnp.asarray(table_array()), echoes)
+    )
+    spec, table = transform(jnp.asarray(table_array()), echoes)
+    high, table = transform(table, high)
     half = shape(8, DOF, 8 * DOF)
     snaps, keep, send, marks = pl.pallas_call(
         gram_kernel,
@@ -486,7 +552,9 @@
         out_specs=(VMEM,) * 4,
         scratch_shapes=[
             pltpu.VMEM((3 * OWN_COLS, 2 * PULSES, CELLS), F32),
-            pltpu.VMEM((2, SLOTS * SEL, CELLS), F32),
+            pltpu.VMEM((2, (PULSES + 1) * SEL, CELLS), F32),
+            pltpu.VMEM((2, (PULSES + 2) * SEL, CELLS), BF16),
+            pltpu.VMEM((2, (PULSES + 2) * SEL, CELLS), BF16),
         ],
         compiler_params=limit(16),
         name="grams",
@@ -511,12 +579,11 @@
     part = part[:2] + moved[0] + moved[1] + moved[2]
     part = part[0] + swap(part[1], 8)
     other = swap(part, 28)
-    edge = shape(SLOTS * SEL, LANES, dtype=BF16)
     edges = pl.pallas_call(
         edge_in_kernel,
-        out_shape=(edge, edge),
+        out_shape=shape(2, SLOTS * SEL, LANES, dtype=BF16),
         in_specs=[VMEM, VMEM],
-        out_specs=(VMEM, VMEM),
+        out_specs=VMEM,
         compiler_params=limit(8),
         name="edges_in",
     )(*edges)
@@ -537,11 +604,11 @@
     power, *rims = pl.pallas_call(
         power_kernel,
         out_shape=(shape(GROUPS, 8, CELLS), rim, rim),
-        in_specs=[SMEM] + [VMEM] * 4,
+        in_specs=[VMEM] * 4,
         out_specs=(VMEM,) * 3,
-        compiler_params=limit(8),
+        compiler_params=limit(12),
         name="power",
-    )(ints, weights, snaps, *edges)
+    )(centres, weights, snaps, edges)
     rims = [
         lax.ppermute(value, "az", pairs)
         for value, pairs in zip(rims, neighbours(8, True))

time: 94.3 us -> 91.5 us (0.970)
  Pallas kernels: 17.7 us -> 15.2 us
  starting transfers between devices: 41 us -> 38.7 us
  waiting for transfers between devices: 29.5 us -> 31.3 us
    ppermute x11, starting transfers between devices: 27.4 us -> 25.3 us  [swap(): return lax.ppermute(value, 'rng', [(i, i ^ turn) for i in range(32)])]
    ppermute x11, waiting for transfers between devices: 14.3 us -> 16.4 us  [swap(): return lax.ppermute(value, 'rng', [(i, i ^ turn) for i in range(32)])]
    pallas_call x1, Pallas kernels: 5.01 us -> 3.85 us  [body(): pl.pallas_call(solve_kernel, out_shape=shape(8, LANES), in_specs=[VMEM] *...]
    pallas_call x1, Pallas kernels: 7.9 us -> 6.9 us  [body(): pl.pallas_call(gram_kernel, out_shape=(shape(OWN_BEAMS, 2, SLOTS * SEL, C...]
    pallas_call x1, Pallas kernels: 2.11 us -> 1.13 us  [body(): pl.pallas_call(power_kernel, out_shape=(shape(GROUPS, 8, CELLS), rim, rim...]
  transfers between devices with their start and end apart: 17 -> 17, of which waited for: 11 -> 11; matrix products, arithmetic and copies ran while one was open for 4% -> 4% of each run, Pallas kernels for 2% -> 3%
where the time goes in v5:
time: 91.5 us; the launch traced here: 91.1 us
  starting transfers between devices  38.7 us (42%)
  waiting for transfers between devices  31.3 us (34%)
  Pallas kernels  15.2 us (17%)
  local copies, waits for them, and re-layouts  3.87 us (4%)
  other arithmetic  1.84 us (2%)
    ppermute x11, starting transfers between devices, swap(): return lax.ppermute(value, 'rng', [(i, i ^ turn) for i in range(32)])  25.3 us
    ppermute x11, waiting for transfers between devices, swap(): return lax.ppermute(value, 'rng', [(i, i ^ turn) for i in range(32)])  16.4 us
    ppermute x1, waiting for transfers between devices, halo_columns(): high = lax.ppermute(echoes, 'az', [(b, a) for a, b in ring])  6.99 us
    pallas_call x1, Pallas kernels, body(): pl.pallas_call(gram_kernel, out_shape=(shape(OWN_BEAMS, 2, SLOTS * SEL, C...  6.9 us
    ppermute x2, starting transfers between devices, body(): lax.ppermute(value, 'rng', pairs)  5.52 us
    ppermute x1, starting transfers between devices, halo_columns(): high = lax.ppermute(echoes, 'az', [(b, a) for a, b in ring])  4.32 us
    pallas_call x1, Pallas kernels, body(): pl.pallas_call(solve_kernel, out_shape=shape(8, LANES), in_specs=[VMEM] *...  3.85 us
    ppermute x2, starting transfers between devices, body(): lax.ppermute(value, 'az', pairs)  3.58 us
  transfers between devices with their start and end apart: 17, of which 11 were waited for; matrix products, arithmetic and copies ran while one was open for 4% of the time, Pallas kernels for 3%

profile of v5, /device:TPU:1, one launch (start us, length us, event | category | flops | bytes accessed | tf_op | source)
XLA Modules:
  0.0 91.1 jit_solution(13733129496140224483)
XLA Ops:
  0.0 4.3 %collective-permute-start = (bf16[2,32,32,128]{3,2,1,0:T(8,128)(2,1)}, bf16[2,32,32,128]{3,2,1,0:T(8,128)(2,1)S(1)}, u32[]{:S(2)}, u32[]{:S(2)}) collective-permute-start(bf16[2,32,32,128]{3,2,1,0:T(8,128)(2,1)} %own_ref.1), channel_id=1, source_target_pairs={{32,0},{64,32},{96,64},{128,96},{160,128},{192,160},{224,192},{0,2... | collective-permute-start | bytes 1572872 | tf_op jit(solution)/shard_map/ppermute | solution.py:485
  4.3 0.7 convert_bitcast_fusion
  5.0 0.1 broadcast_in_dim.21
  5.1 5.6 %collective-permute-start.2 = (f32[8,128]{1,0:T(8,128)S(1)}, f32[8,128]{1,0:T(8,128)S(1)}, u32[]{:S(2)}, u32[]{:S(2)}) collective-permute-start(f32[8,128]{1,0:T(8,128)S(1)} %broadcast_in_dim.21), channel_id=1, source_target_pairs={{0,28},{1,29},{2,30},{3,31},{4,24},{5,25},{6,26},{7,27},{8,20},{9,... | collective-permute-start | bytes 12296 | tf_op jit(solution)/shard_map/ppermute | solution.py:479
  10.6 0.7 copy.14
  11.4 0.8 constant_dynamic-slice_fusion.1
  12.3 0.1 constant_dynamic-slice_fusion
  12.4 0.1 copy.18
  12.5 0.7 and_select_fusion
  13.2 0.1 pad_maximum_fusion.3.floats_ref
  13.3 0.1 broadcast_add_fusion.1
  13.4 0.1 pad_add_fusion.ints_ref
  13.5 1.0 %copy-done.1 = bf16[2,32,32,128]{3,2,1,0:T(8,128)(2,1)S(1)} copy-done((bf16[2,32,32,128]{3,2,1,0:T(8,128)(2,1)S(1)}, bf16[2,32,32,128]{3,2,1,0:T(8,128)(2,1)}, u32[]{:S(2)}) %copy-start.1) | copy-done | bytes 524312
  14.5 0.7 copy-done.2
  15.2 0.7 spectra.2
  15.9 0.1 broadcast_add_fusion.marks_ref
  16.0 7.0 %collective-permute-done.own_ref = bf16[2,32,32,128]{3,2,1,0:T(8,128)(2,1)S(1)} collective-permute-done((bf16[2,32,32,128]{3,2,1,0:T(8,128)(2,1)}, bf16[2,32,32,128]{3,2,1,0:T(8,128)(2,1)S(1)}, u32[]{:S(2)}, u32[]{:S(2)}) %collective-permute-start) | collective-permute-done | bytes 524320 | tf_op jit(solution)/shard_map/ppermute | solution.py:485
  23.0 0.7 spectra.3
  23.6 2.6 %collective-permute-done.1.low_ref = bf16[2,32,32,128]{3,2,1,0:T(8,128)(2,1)S(1)} collective-permute-done((bf16[2,32,32,128]{3,2,1,0:T(8,128)(2,1)}, bf16[2,32,32,128]{3,2,1,0:T(8,128)(2,1)S(1)}, u32[]{:S(2)}, u32[]{:S(2)}) %collective-permute-start.1) | collective-permute-done | bytes 524320 | tf_op jit(solution)/shard_map/ppermute | solution.py:484
  26.2 6.9 %grams.1 = (bf16[8,2,640,128]{3,2,1,0:T(8,128)(2,1)S(1)}, f32[8,48,384]{2,1,0:T(8,128)S(1)}, f32[8,48,384]{2,1,0:T(8,128)S(1)}, f32[8,128]{1,0:T(8,128)S(1)}) custom-call(s32[8,33]{1,0:T(8,128)S(1)} %pad_add_fusion.ints_ref, f32[8,32]{1,0:T(8,128)S(1)} %pad_maximum_fusion.3.floats_ref, bf16[64,64]{1,0:T(8,128)(2,1)S(1)} %get-tuple-element.29.table_ref, ...), custom_call_target="tpu_custom_call" | custom-call | tf_op jit(solution)/shard_map/grams/pallas_call | solution.py:543
  33.1 1.0 %collective-permute-start.3 = (f32[8,48,384]{2,1,0:T(8,128)S(1)}, f32[8,48,384]{2,1,0:T(8,128)S(1)}, u32[]{:S(2)}, u32[]{:S(2)}) collective-permute-start(f32[8,48,384]{2,1,0:T(8,128)S(1)} %get-tuple-element.33), channel_id=1, source_target_pairs={{0,1},{1,0},{2,3},{3,2},{4,5},{5,4},{6,7},{7,6},{8,9},{9,8},{10,11... | collective-permute-start | bytes 1769480 | tf_op jit(solution)/shard_map/ppermute | solution.py:479
  34.1 1.2 %edges_out.1 = (bf16[64,128]{1,0:T(8,128)(2,1)S(1)}, bf16[64,128]{1,0:T(8,128)(2,1)S(1)}) custom-call(bf16[8,2,640,128]{3,2,1,0:T(8,128)(2,1)S(1)} %get-tuple-element.34.snap_ref), custom_call_target="tpu_custom_call" | custom-call | tf_op jit(solution)/shard_map/edges_out/pallas_call | solution.py:563
  35.3 0.5 collective-permute-done.3
  35.7 0.1 add.48
  35.9 1.9 %collective-permute-start.4 = (f32[2,48,384]{2,1,0:T(8,128)S(1)}, f32[2,48,384]{2,1,0:T(8,128)S(1)}, u32[]{:S(2)}, u32[]{:S(2)}) collective-permute-start(f32[2,48,384]{2,1,0:T(8,128)S(1)} %get-tuple-element.53), channel_id=1, source_target_pairs={{0,4},{1,5},{2,6},{3,7},{4,0},{5,1},{6,2},{7,3},{8,12},{9,13},{10,... | collective-permute-start | bytes 442376 | tf_op jit(solution)/shard_map/ppermute | solution.py:479
  37.7 2.9 %collective-permute-start.5 = (f32[2,48,384]{2,1,0:T(8,128)S(1)}, f32[2,48,384]{2,1,0:T(8,128)S(1)}, u32[]{:S(2)}, u32[]{:S(2)}) collective-permute-start(f32[2,48,384]{2,1,0:T(8,128)S(1)} %get-tuple-element.52), channel_id=1, source_target_pairs={{0,2},{1,3},{2,0},{3,1},{4,6},{5,7},{6,4},{7,5},{8,10},{9,11},{10,... | collective-permute-start | bytes 442376 | tf_op jit(solution)/shard_map/ppermute | solution.py:479
  40.7 0.9 %collective-permute-start.7 = (bf16[64,128]{1,0:T(8,128)(2,1)S(1)}, bf16[64,128]{1,0:T(8,128)(2,1)S(1)}, u32[]{:S(2)}, u32[]{:S(2)}) collective-permute-start(bf16[64,128]{1,0:T(8,128)(2,1)S(1)} %get-tuple-element.38), channel_id=1, source_target_pairs={{0,1},{1,0},{2,3},{3,2},{4,5},{5,4},{6,7},{7,6},{8,9},{9,8},{10,11... | collective-permute-start | bytes 49160 | tf_op jit(solution)/shard_map/ppermute | solution.py:575
  41.6 4.6 %collective-permute-start.8 = (bf16[64,128]{1,0:T(8,128)(2,1)S(1)}, bf16[64,128]{1,0:T(8,128)(2,1)S(1)}, u32[]{:S(2)}, u32[]{:S(2)}) collective-permute-start(bf16[64,128]{1,0:T(8,128)(2,1)S(1)} %get-tuple-element.39), channel_id=1, source_target_pairs={{1,2},{2,1},{3,4},{4,3},{5,6},{6,5},{7,8},{8,7},{9,10},{10,9},{11,... | collective-permute-start | bytes 49160 | tf_op jit(solution)/shard_map/ppermute | solution.py:575
  46.2 2.7 %collective-permute-done.8.second_ref = bf16[64,128]{1,0:T(8,128)(2,1)S(1)} collective-permute-done((bf16[64,128]{1,0:T(8,128)(2,1)S(1)}, bf16[64,128]{1,0:T(8,128)(2,1)S(1)}, u32[]{:S(2)}, u32[]{:S(2)}) %collective-permute-start.8) | collective-permute-done | bytes 16416 | tf_op jit(solution)/shard_map/ppermute | solution.py:575
  49.0 3.2 %collective-permute-start.9 = (f32[48,384]{1,0:T(8,128)S(1)}, f32[48,384]{1,0:T(8,128)S(1)}, u32[]{:S(2)}, u32[]{:S(2)}) collective-permute-start(f32[48,384]{1,0:T(8,128)S(1)} %slice_bitcast_fusion), channel_id=1, source_target_pairs={{0,8},{1,9},{2,10},{3,11},{4,12},{5,13},{6,14},{7,15},{8,0},{9,1},... | collective-permute-start | bytes 221192 | tf_op jit(solution)/shard_map/ppermute | solution.py:479
  52.2 3.7 %collective-permute-done.9 = f32[48,384]{1,0:T(8,128)S(1)} collective-permute-done((f32[48,384]{1,0:T(8,128)S(1)}, f32[48,384]{1,0:T(8,128)S(1)}, u32[]{:S(2)}, u32[]{:S(2)}) %collective-permute-start.9) | collective-permute-done | bytes 73760 | tf_op jit(solution)/shard_map/ppermute | solution.py:479
  55.9 4.7 %collective-permute-start.10 = (f32[48,384]{1,0:T(8,128)S(1)}, f32[48,384]{1,0:T(8,128)S(1)}, u32[]{:S(2)}, u32[]{:S(2)}) collective-permute-start(f32[48,384]{1,0:T(8,128)S(1)} %fusion.2.first_ref), channel_id=1, source_target_pairs={{0,28},{1,29},{2,30},{3,31},{4,24},{5,25},{6,26},{7,27},{8,20},{9,... | collective-permute-start | bytes 221192 | tf_op jit(solution)/shard_map/ppermute | solution.py:479
  60.6 0.2 edges_in.1.edge_ref
  60.9 3.1 %collective-permute-done.10.second_ref = f32[48,384]{1,0:T(8,128)S(1)} collective-permute-done((f32[48,384]{1,0:T(8,128)S(1)}, f32[48,384]{1,0:T(8,128)S(1)}, u32[]{:S(2)}, u32[]{:S(2)}) %collective-permute-start.10) | collective-permute-done | bytes 73760 | tf_op jit(solution)/shard_map/ppermute | solution.py:479
  64.0 3.8 %solve.1 = f32[8,128]{1,0:T(8,128)S(1)} custom-call(f32[48,384]{1,0:T(8,128)S(1)} %fusion.2.first_ref, f32[48,384]{1,0:T(8,128)S(1)} %collective-permute-done.10.second_ref, f32[8,128]{1,0:T(8,128)S(1)} %get-tuple-element.46.marks_ref), custom_call_target="tpu_custom_call" | custom-call | tf_op jit(solution)/shard_map/solve/pallas_call | solution.py:591
  67.9 0.1 collective-permute-start.11
  68.0 3.3 %collective-permute-done.11 = f32[1,8,128]{2,1,0:T(8,128)S(1)} collective-permute-done((f32[1,8,128]{2,1,0:T(8,128)S(1)}, f32[1,8,128]{2,1,0:T(8,128)S(1)}, u32[]{:S(2)}, u32[]{:S(2)}) %collective-permute-start.11) | collective-permute-done | bytes 4128 | tf_op jit(solution)/shard_map/ppermute | solution.py:479
  71.3 2.5 %collective-permute-done.12 = f32[2,8,128]{2,1,0:T(8,128)S(1)} collective-permute-done((f32[2,8,128]{2,1,0:T(8,128)S(1)}, f32[2,8,128]{2,1,0:T(8,128)S(1)}, u32[]{:S(2)}, u32[]{:S(2)}) %collective-permute-start.12) | collective-permute-done | bytes 8224 | tf_op jit(solution)/shard_map/ppermute | solution.py:479
  73.8 1.7 %collective-permute-start.13 = (f32[4,8,128]{2,1,0:T(8,128)S(1)}, f32[4,8,128]{2,1,0:T(8,128)S(1)}, u32[]{:S(2)}, u32[]{:S(2)}) collective-permute-start(f32[4,8,128]{2,1,0:T(8,128)S(1)} %pad_maximum_fusion.1), channel_id=1, source_target_pairs={{0,2},{1,3},{2,0},{3,1},{4,6},{5,7},{6,4},{7,5},{8,10},{9,11},{10,... | collective-permute-start | bytes 49160 | tf_op jit(solution)/shard_map/ppermute | solution.py:479
  75.6 2.4 %collective-permute-done.13 = f32[4,8,128]{2,1,0:T(8,128)S(1)} collective-permute-done((f32[4,8,128]{2,1,0:T(8,128)S(1)}, f32[4,8,128]{2,1,0:T(8,128)S(1)}, u32[]{:S(2)}, u32[]{:S(2)}) %collective-permute-start.13) | collective-permute-done | bytes 16416 | tf_op jit(solution)/shard_map/ppermute | solution.py:479
  77.9 4.3 %collective-permute-start.14 = (f32[8,8,128]{2,1,0:T(8,128)S(1)}, f32[8,8,128]{2,1,0:T(8,128)S(1)}, u32[]{:S(2)}, u32[]{:S(2)}) collective-permute-start(f32[8,8,128]{2,1,0:T(8,128)S(1)} %pad_maximum_fusion), channel_id=1, source_target_pairs={{0,1},{1,0},{2,3},{3,2},{4,5},{5,4},{6,7},{7,6},{8,9},{9,8},{10,11... | collective-permute-start | bytes 98312 | tf_op jit(solution)/shard_map/ppermute | solution.py:479
  82.2 0.9 collective-permute-done.14
  83.1 0.1 broadcast_in_dim.19.bins_ref
  83.1 1.1 %power.1 = (f32[16,8,128]{2,1,0:T(8,128)S(1)}, f32[2,8,128]{2,1,0:T(8,128)S(1)}, f32[2,8,128]{2,1,0:T(8,128)S(1)}) custom-call(s32[16,8,128]{2,1,0:T(8,128)S(1)} %broadcast_in_dim.19.bins_ref, f32[16,8,128]{2,1,0:T(8,128)S(1)} %constant_dynamic-update-slice_fusion.weights_ref, bf16[8,2,640,128]{3,2,1,0:T(8,128)(2,1)S(1)} %get-tuple-element.34.snap_ref, ...), custom_call_target="tpu_custom_call" | custom-call | tf_op jit(solution)/shard_map/power/pallas_call | solution.py:604
  84.3 1.6 %collective-permute-start.15 = (f32[2,8,128]{2,1,0:T(8,128)S(1)}, f32[2,8,128]{2,1,0:T(8,128)S(1)}, u32[]{:S(2)}, u32[]{:S(2)}) collective-permute-start(f32[2,8,128]{2,1,0:T(8,128)S(1)} %get-tuple-element.49), channel_id=1, source_target_pairs={{0,32},{32,0},{64,96},{96,64},{128,160},{160,128},{192,224},{224,1... | collective-permute-start | bytes 24584 | tf_op jit(solution)/shard_map/ppermute | solution.py:613
  85.8 2.0 %collective-permute-start.16 = (f32[2,8,128]{2,1,0:T(8,128)S(1)}, f32[2,8,128]{2,1,0:T(8,128)S(1)}, u32[]{:S(2)}, u32[]{:S(2)}) collective-permute-start(f32[2,8,128]{2,1,0:T(8,128)S(1)} %get-tuple-element.50), channel_id=1, source_target_pairs={{0,224},{32,64},{64,32},{96,128},{128,96},{160,192},{192,160},{224... | collective-permute-start | bytes 24584 | tf_op jit(solution)/shard_map/ppermute | solution.py:613
  87.9 2.6 %collective-permute-done.16.second_ref = f32[2,8,128]{2,1,0:T(8,128)S(1)} collective-permute-done((f32[2,8,128]{2,1,0:T(8,128)S(1)}, f32[2,8,128]{2,1,0:T(8,128)S(1)}, u32[]{:S(2)}, u32[]{:S(2)}) %collective-permute-start.16) | collective-permute-done | bytes 8224 | tf_op jit(solution)/shard_map/ppermute | solution.py:613
  90.4 0.6 smooth.1
  (29 shorter events, 0.4 us)
Async XLA Ops:
  0.0 12.3 %copy-start = (f32[64,16]{0,1:T(8,128)S(1)}, f32[64,16]{0,1:T(8,128)}, u32[]{:S(2)}) copy-start(f32[64,16]{0,1:T(8,128)} %param.11) | copy-start | bytes 12292
  0.0 22.9 %collective-permute-start = (bf16[2,32,32,128]{3,2,1,0:T(8,128)(2,1)}, bf16[2,32,32,128]{3,2,1,0:T(8,128)(2,1)S(1)}, u32[]{:S(2)}, u32[]{:S(2)}) collective-permute-start(bf16[2,32,32,128]{3,2,1,0:T(8,128)(2,1)} %own_ref.1), channel_id=1, source_target_pairs={{32,0},{64,32},{96,64},{128,96},{160,128},{192,160},{224,192},{0,2... | collective-permute-start | bytes 1572872 | tf_op jit(solution)/shard_map/ppermute | solution.py:485
  4.3 21.9 %collective-permute-start.1 = (bf16[2,32,32,128]{3,2,1,0:T(8,128)(2,1)}, bf16[2,32,32,128]{3,2,1,0:T(8,128)(2,1)S(1)}, u32[]{:S(2)}, u32[]{:S(2)}) collective-permute-start(bf16[2,32,32,128]{3,2,1,0:T(8,128)(2,1)} %own_ref.1), channel_id=1, source_target_pairs={{0,32},{32,64},{64,96},{96,128},{128,160},{160,192},{192,224},{224... | collective-permute-start | bytes 1572872 | tf_op jit(solution)/shard_map/ppermute | solution.py:484
  5.1 10.8 %collective-permute-start.2 = (f32[8,128]{1,0:T(8,128)S(1)}, f32[8,128]{1,0:T(8,128)S(1)}, u32[]{:S(2)}, u32[]{:S(2)}) collective-permute-start(f32[8,128]{1,0:T(8,128)S(1)} %broadcast_in_dim.21), channel_id=1, source_target_pairs={{0,28},{1,29},{2,30},{3,31},{4,24},{5,25},{6,26},{7,27},{8,20},{9,... | collective-permute-start | bytes 12296 | tf_op jit(solution)/shard_map/ppermute | solution.py:479
  13.5 1.0 %copy-start.1 = (bf16[2,32,32,128]{3,2,1,0:T(8,128)(2,1)S(1)}, bf16[2,32,32,128]{3,2,1,0:T(8,128)(2,1)}, u32[]{:S(2)}) copy-start(bf16[2,32,32,128]{3,2,1,0:T(8,128)(2,1)} %own_ref.1) | copy-start | bytes 1572868
  14.5 0.7 copy-start.2
  33.1 2.6 %collective-permute-start.3 = (f32[8,48,384]{2,1,0:T(8,128)S(1)}, f32[8,48,384]{2,1,0:T(8,128)S(1)}, u32[]{:S(2)}, u32[]{:S(2)}) collective-permute-start(f32[8,48,384]{2,1,0:T(8,128)S(1)} %get-tuple-element.33), channel_id=1, source_target_pairs={{0,1},{1,0},{2,3},{3,2},{4,5},{5,4},{6,7},{7,6},{8,9},{9,8},{10,11... | collective-permute-start | bytes 1769480 | tf_op jit(solution)/shard_map/ppermute | solution.py:479
  35.9 13.1 %collective-permute-start.4 = (f32[2,48,384]{2,1,0:T(8,128)S(1)}, f32[2,48,384]{2,1,0:T(8,128)S(1)}, u32[]{:S(2)}, u32[]{:S(2)}) collective-permute-start(f32[2,48,384]{2,1,0:T(8,128)S(1)} %get-tuple-element.53), channel_id=1, source_target_pairs={{0,4},{1,5},{2,6},{3,7},{4,0},{5,1},{6,2},{7,3},{8,12},{9,13},{10,... | collective-permute-start | bytes 442376 | tf_op jit(solution)/shard_map/ppermute | solution.py:479
  37.7 11.2 %collective-permute-start.5 = (f32[2,48,384]{2,1,0:T(8,128)S(1)}, f32[2,48,384]{2,1,0:T(8,128)S(1)}, u32[]{:S(2)}, u32[]{:S(2)}) collective-permute-start(f32[2,48,384]{2,1,0:T(8,128)S(1)} %get-tuple-element.52), channel_id=1, source_target_pairs={{0,2},{1,3},{2,0},{3,1},{4,6},{5,7},{6,4},{7,5},{8,10},{9,11},{10,... | collective-permute-start | bytes 442376 | tf_op jit(solution)/shard_map/ppermute | solution.py:479
  40.7 8.3 %collective-permute-start.6 = (f32[2,48,384]{2,1,0:T(8,128)S(1)}, f32[2,48,384]{2,1,0:T(8,128)S(1)}, u32[]{:S(2)}, u32[]{:S(2)}) collective-permute-start(f32[2,48,384]{2,1,0:T(8,128)S(1)} %get-tuple-element.51), channel_id=1, source_target_pairs={{0,6},{1,7},{2,4},{3,5},{4,2},{5,3},{6,0},{7,1},{8,14},{9,15},{10,... | collective-permute-start | bytes 442376 | tf_op jit(solution)/shard_map/ppermute | solution.py:479
  40.7 5.5 %collective-permute-start.7 = (bf16[64,128]{1,0:T(8,128)(2,1)S(1)}, bf16[64,128]{1,0:T(8,128)(2,1)S(1)}, u32[]{:S(2)}, u32[]{:S(2)}) collective-permute-start(bf16[64,128]{1,0:T(8,128)(2,1)S(1)} %get-tuple-element.38), channel_id=1, source_target_pairs={{0,1},{1,0},{2,3},{3,2},{4,5},{5,4},{6,7},{7,6},{8,9},{9,8},{10,11... | collective-permute-start | bytes 49160 | tf_op jit(solution)/shard_map/ppermute | solution.py:575
  41.6 7.3 %collective-permute-start.8 = (bf16[64,128]{1,0:T(8,128)(2,1)S(1)}, bf16[64,128]{1,0:T(8,128)(2,1)S(1)}, u32[]{:S(2)}, u32[]{:S(2)}) collective-permute-start(bf16[64,128]{1,0:T(8,128)(2,1)S(1)} %get-tuple-element.39), channel_id=1, source_target_pairs={{1,2},{2,1},{3,4},{4,3},{5,6},{6,5},{7,8},{8,7},{9,10},{10,9},{11,... | collective-permute-start | bytes 49160 | tf_op jit(solution)/shard_map/ppermute | solution.py:575
  49.0 6.8 %collective-permute-start.9 = (f32[48,384]{1,0:T(8,128)S(1)}, f32[48,384]{1,0:T(8,128)S(1)}, u32[]{:S(2)}, u32[]{:S(2)}) collective-permute-start(f32[48,384]{1,0:T(8,128)S(1)} %slice_bitcast_fusion), channel_id=1, source_target_pairs={{0,8},{1,9},{2,10},{3,11},{4,12},{5,13},{6,14},{7,15},{8,0},{9,1},... | collective-permute-start | bytes 221192 | tf_op jit(solution)/shard_map/ppermute | solution.py:479
  55.9 8.2 %collective-permute-start.10 = (f32[48,384]{1,0:T(8,128)S(1)}, f32[48,384]{1,0:T(8,128)S(1)}, u32[]{:S(2)}, u32[]{:S(2)}) collective-permute-start(f32[48,384]{1,0:T(8,128)S(1)} %fusion.2.first_ref), channel_id=1, source_target_pairs={{0,28},{1,29},{2,30},{3,31},{4,24},{5,25},{6,26},{7,27},{8,20},{9,... | collective-permute-start | bytes 221192 | tf_op jit(solution)/shard_map/ppermute | solution.py:479
  67.9 3.4 %collective-permute-start.11 = (f32[1,8,128]{2,1,0:T(8,128)S(1)}, f32[1,8,128]{2,1,0:T(8,128)S(1)}, u32[]{:S(2)}, u32[]{:S(2)}) collective-permute-start(f32[1,8,128]{2,1,0:T(8,128)S(1)} %bitcast.11), channel_id=1, source_target_pairs={{0,8},{1,9},{2,10},{3,11},{4,12},{5,13},{6,14},{7,15},{8,0},{9,1},... | collective-permute-start | bytes 12296 | tf_op jit(solution)/shard_map/ppermute | solution.py:479
  71.3 2.5 %collective-permute-start.12 = (f32[2,8,128]{2,1,0:T(8,128)S(1)}, f32[2,8,128]{2,1,0:T(8,128)S(1)}, u32[]{:S(2)}, u32[]{:S(2)}) collective-permute-start(f32[2,8,128]{2,1,0:T(8,128)S(1)} %pad_maximum_fusion.2), channel_id=1, source_target_pairs={{0,4},{1,5},{2,6},{3,7},{4,0},{5,1},{6,2},{7,3},{8,12},{9,13},{10,... | collective-permute-start | bytes 24584 | tf_op jit(solution)/shard_map/ppermute | solution.py:479
  73.8 4.1 %collective-permute-start.13 = (f32[4,8,128]{2,1,0:T(8,128)S(1)}, f32[4,8,128]{2,1,0:T(8,128)S(1)}, u32[]{:S(2)}, u32[]{:S(2)}) collective-permute-start(f32[4,8,128]{2,1,0:T(8,128)S(1)} %pad_maximum_fusion.1), channel_id=1, source_target_pairs={{0,2},{1,3},{2,0},{3,1},{4,6},{5,7},{6,4},{7,5},{8,10},{9,11},{10,... | collective-permute-start | bytes 49160 | tf_op jit(solution)/shard_map/ppermute | solution.py:479
  77.9 5.1 %collective-permute-start.14 = (f32[8,8,128]{2,1,0:T(8,128)S(1)}, f32[8,8,128]{2,1,0:T(8,128)S(1)}, u32[]{:S(2)}, u32[]{:S(2)}) collective-permute-start(f32[8,8,128]{2,1,0:T(8,128)S(1)} %pad_maximum_fusion), channel_id=1, source_target_pairs={{0,1},{1,0},{2,3},{3,2},{4,5},{5,4},{6,7},{7,6},{8,9},{9,8},{10,11... | collective-permute-start | bytes 98312 | tf_op jit(solution)/shard_map/ppermute | solution.py:479
  84.3 3.6 %collective-permute-start.15 = (f32[2,8,128]{2,1,0:T(8,128)S(1)}, f32[2,8,128]{2,1,0:T(8,128)S(1)}, u32[]{:S(2)}, u32[]{:S(2)}) collective-permute-start(f32[2,8,128]{2,1,0:T(8,128)S(1)} %get-tuple-element.49), channel_id=1, source_target_pairs={{0,32},{32,0},{64,96},{96,64},{128,160},{160,128},{192,224},{224,1... | collective-permute-start | bytes 24584 | tf_op jit(solution)/shard_map/ppermute | solution.py:613
  85.8 4.6 %collective-permute-start.16 = (f32[2,8,128]{2,1,0:T(8,128)S(1)}, f32[2,8,128]{2,1,0:T(8,128)S(1)}, u32[]{:S(2)}, u32[]{:S(2)}) collective-permute-start(f32[2,8,128]{2,1,0:T(8,128)S(1)} %get-tuple-element.50), channel_id=1, source_target_pairs={{0,224},{32,64},{64,32},{96,128},{128,96},{160,192},{192,160},{224... | collective-permute-start | bytes 24584 | tf_op jit(solution)/shard_map/ppermute | solution.py:613

commit v6 on v5

--- a/solution.py
+++ b/solution.py
@@ -1,4 +1,4 @@
-import functools
+import itertools
 
 import jax
 import jax.numpy as jnp
@@ -86,15 +86,11 @@
     table = table_ref[...]
     passed_ref[...] = marks_ref[...]
 
-    def transform(index, carry):
-        for one in range(2):
-            spectra(table, low_ref, 2 * index + one, spec_ref, 0)
-        for one in range(4):
-            spec_ref[OWN_COLS + 4 * index + one] = own_ref[4 * index + one]
-            spec_ref[2 * OWN_COLS + 4 * index + one] = high_ref[4 * index + one]
-        return carry
-
-    lax.fori_loop(0, OWN_COLS // 4, transform, 0)
+    for pair in range(OWN_COLS // 2):
+        spectra(table, low_ref, pair, spec_ref, 0)
+        for column in (2 * pair, 2 * pair + 1):
+            spec_ref[OWN_COLS + column] = own_ref[column]
+            spec_ref[2 * OWN_COLS + column] = high_ref[column]
 
     lane = lane_ids(DOF)
     row = lax.broadcasted_iota(jnp.int32, (DOF, LANES), 0)
@@ -116,15 +112,20 @@
             rows = pl.ds(SEL + sel, PULSES, stride=SEL)
             wide_ref[0, rows, :] = cosine * real - sine * imag
             wide_ref[1, rows, :] = sine * real + cosine * imag
+            if sel % 4 == 3:
+                yield
         for part in range(2):
             for low, high, place in (
-                (SEL, SEL + last, SEL),
+                (SEL, SEL + last // 2, SEL),
+                (SEL + last // 2, SEL + last, SEL + last // 2),
                 (last, last + SEL, 0),
                 (SEL, 2 * SEL, SEL + last),
             ):
                 value = wide_ref[part, low:high, :].astype(BF16)
                 work_ref[part, place : place + high - low, :] = value
                 snap_ref[beam, part, place : place + high - low, :] = value
+                if place in (SEL, SEL + last // 2):
+                    yield
             snap_ref[beam, part, last + 2 * SEL :, :] = jnp.zeros(
                 (SLOTS * SEL - last - 2 * SEL, CELLS), BF16
             )
@@ -168,28 +169,28 @@
                     out[2] = packed
                 else:
                     out[2] = jnp.where(lane >= 32, packed, out[2])
+                yield
             place = lax.rem(2 * step, 8) + half
             for part in range(3):
                 out_ref[place, :, LANES * part : LANES * (part + 1)] = (
                     out[part] * weight
                 )
 
+    def run(*works):
+        for _ in itertools.zip_longest(*works):
+            pass
+
     def sending(index, carry):
-        turn(2 * index + 1, odd_ref)
-        multiply(2 * index, even_ref, send_ref)
-        turn(2 * index + 2, even_ref)
-        multiply(2 * index + 1, odd_ref, send_ref)
+        run(turn(2 * index + 1, odd_ref), multiply(2 * index, even_ref, send_ref))
+        run(turn(2 * index + 2, even_ref), multiply(2 * index + 1, odd_ref, send_ref))
         return carry
 
-    turn(0, even_ref)
+    run(turn(0, even_ref))
     lax.fori_loop(0, 2, sending, 0)
-    turn(5, odd_ref)
-    multiply(4, even_ref, keep_ref)
-    turn(6, even_ref)
-    multiply(5, odd_ref, keep_ref)
-    turn(7, odd_ref)
-    multiply(6, even_ref, keep_ref)
-    multiply(7, odd_ref, keep_ref)
+    run(turn(5, odd_ref), multiply(4, even_ref, keep_ref))
+    run(turn(6, even_ref), multiply(5, odd_ref, keep_ref))
+    run(turn(7, odd_ref), multiply(6, even_ref, keep_ref))
+    run(multiply(7, odd_ref, keep_ref))
 
 
 def edge_out_kernel(snap_ref, first_ref, second_ref):
@@ -575,10 +576,11 @@
         lax.ppermute(value, "rng", pairs)
         for value, pairs in zip(edges, neighbours(32, False))
     ]
-    moved, edges = lax.optimization_barrier((moved, edges))
+    moved, edges[0] = lax.optimization_barrier((moved, edges[0]))
     part = part[:2] + moved[0] + moved[1] + moved[2]
     part = part[0] + swap(part[1], 8)
     other = swap(part, 28)
+    other, edges = lax.optimization_barrier((other, edges))
     edges = pl.pallas_call(
         edge_in_kernel,
         out_shape=shape(2, SLOTS * SEL, LANES, dtype=BF16),
@@ -587,7 +589,6 @@
         compiler_params=limit(8),
         name="edges_in",
     )(*edges)
-    other, edges = lax.optimization_barrier((other, edges))
     weights = pl.pallas_call(
         solve_kernel,
         out_shape=shape(8, LANES),

time: 91.5 us -> 92.5 us (1.011)
  starting transfers between devices: 38.7 us -> 44.3 us
  waiting for transfers between devices: 31.3 us -> 27.5 us
  Pallas kernels: 15.2 us -> 14.1 us
    ppermute x2, starting transfers between devices: 5.52 us -> 8.54 us  [body(): lax.ppermute(value, 'rng', pairs)]
    ppermute x11, starting transfers between devices: 25.3 us -> 27.7 us  [swap(): return lax.ppermute(value, 'rng', [(i, i ^ turn) for i in range(32)])]
    ppermute x11, waiting for transfers between devices: 16.4 us -> 14.1 us  [swap(): return lax.ppermute(value, 'rng', [(i, i ^ turn) for i in range(32)])]
    pallas_call x1, Pallas kernels: 6.9 us -> 5.8 us  [body(): pl.pallas_call(gram_kernel, out_shape=(shape(OWN_BEAMS, 2, SLOTS * SEL, C...]
  transfers between devices with their start and end apart: 17 -> 17, of which waited for: 11 -> 13; matrix products, arithmetic and copies ran while one was open for 4% -> 4% of each run, Pallas kernels for 3% -> 3%
where the time goes in v6:
time: 92.5 us; the launch traced here: 91.8 us
  starting transfers between devices  44.3 us (48%)
  waiting for transfers between devices  27.5 us (30%)
  Pallas kernels  14.1 us (15%)
  local copies, waits for them, and re-layouts  3.87 us (4%)
  other arithmetic  1.83 us (2%)
    ppermute x11, starting transfers between devices, swap(): return lax.ppermute(value, 'rng', [(i, i ^ turn) for i in range(32)])  27.7 us
    ppermute x11, waiting for transfers between devices, swap(): return lax.ppermute(value, 'rng', [(i, i ^ turn) for i in range(32)])  14.1 us
    ppermute x2, starting transfers between devices, body(): lax.ppermute(value, 'rng', pairs)  8.54 us
    ppermute x1, waiting for transfers between devices, halo_columns(): high = lax.ppermute(echoes, 'az', [(b, a) for a, b in ring])  6.99 us
    pallas_call x1, Pallas kernels, body(): pl.pallas_call(gram_kernel, out_shape=(shape(OWN_BEAMS, 2, SLOTS * SEL, C...  5.8 us
    ppermute x1, starting transfers between devices, halo_columns(): high = lax.ppermute(echoes, 'az', [(b, a) for a, b in ring])  4.32 us
    pallas_call x1, Pallas kernels, body(): pl.pallas_call(solve_kernel, out_shape=shape(8, LANES), in_specs=[VMEM] *...  3.85 us
    ppermute x2, starting transfers between devices, body(): lax.ppermute(value, 'az', pairs)  3.73 us
  transfers between devices with their start and end apart: 17, of which 13 were waited for; matrix products, arithmetic and copies ran while one was open for 4% of the time, Pallas kernels for 3%

profile of v6, /device:TPU:1, one launch (start us, length us, event | category | flops | bytes accessed | tf_op | source)
XLA Modules:
  0.0 91.8 jit_solution(10889775680659095221)
XLA Ops:
  0.0 4.3 %collective-permute-start = (bf16[2,32,32,128]{3,2,1,0:T(8,128)(2,1)}, bf16[2,32,32,128]{3,2,1,0:T(8,128)(2,1)S(1)}, u32[]{:S(2)}, u32[]{:S(2)}) collective-permute-start(bf16[2,32,32,128]{3,2,1,0:T(8,128)(2,1)} %own_ref.1), channel_id=1, source_target_pairs={{32,0},{64,32},{96,64},{128,96},{160,128},{192,160},{224,192},{0,2... | collective-permute-start | bytes 1572872 | tf_op jit(solution)/shard_map/ppermute | solution.py:486
  4.3 0.7 convert_bitcast_fusion
  5.0 0.1 broadcast_in_dim.21
  5.1 5.6 %collective-permute-start.2 = (f32[8,128]{1,0:T(8,128)S(1)}, f32[8,128]{1,0:T(8,128)S(1)}, u32[]{:S(2)}, u32[]{:S(2)}) collective-permute-start(f32[8,128]{1,0:T(8,128)S(1)} %broadcast_in_dim.21), channel_id=1, source_target_pairs={{0,28},{1,29},{2,30},{3,31},{4,24},{5,25},{6,26},{7,27},{8,20},{9,... | collective-permute-start | bytes 12296 | tf_op jit(solution)/shard_map/ppermute | solution.py:480
  10.6 0.7 copy.14
  11.4 0.8 constant_dynamic-slice_fusion.1
  12.3 0.1 constant_dynamic-slice_fusion
  12.5 0.7 and_select_fusion
  13.2 0.1 pad_maximum_fusion.3.floats_ref
  13.4 0.1 pad_add_fusion.ints_ref
  13.5 1.0 %copy-done.1 = bf16[2,32,32,128]{3,2,1,0:T(8,128)(2,1)S(1)} copy-done((bf16[2,32,32,128]{3,2,1,0:T(8,128)(2,1)S(1)}, bf16[2,32,32,128]{3,2,1,0:T(8,128)(2,1)}, u32[]{:S(2)}) %copy-start.1) | copy-done | bytes 524312
  14.5 0.7 copy-done.2
  15.2 0.7 spectra.2
  16.0 7.0 %collective-permute-done.own_ref = bf16[2,32,32,128]{3,2,1,0:T(8,128)(2,1)S(1)} collective-permute-done((bf16[2,32,32,128]{3,2,1,0:T(8,128)(2,1)}, bf16[2,32,32,128]{3,2,1,0:T(8,128)(2,1)S(1)}, u32[]{:S(2)}, u32[]{:S(2)}) %collective-permute-start) | collective-permute-done | bytes 524320 | tf_op jit(solution)/shard_map/ppermute | solution.py:486
  23.0 0.7 spectra.3
  23.6 2.6 %collective-permute-done.1.low_ref = bf16[2,32,32,128]{3,2,1,0:T(8,128)(2,1)S(1)} collective-permute-done((bf16[2,32,32,128]{3,2,1,0:T(8,128)(2,1)}, bf16[2,32,32,128]{3,2,1,0:T(8,128)(2,1)S(1)}, u32[]{:S(2)}, u32[]{:S(2)}) %collective-permute-start.1) | collective-permute-done | bytes 524320 | tf_op jit(solution)/shard_map/ppermute | solution.py:485
  26.2 5.8 %grams.1 = (bf16[8,2,640,128]{3,2,1,0:T(8,128)(2,1)S(1)}, f32[8,48,384]{2,1,0:T(8,128)S(1)}, f32[8,48,384]{2,1,0:T(8,128)S(1)}, f32[8,128]{1,0:T(8,128)S(1)}) custom-call(s32[8,33]{1,0:T(8,128)S(1)} %pad_add_fusion.ints_ref, f32[8,32]{1,0:T(8,128)S(1)} %pad_maximum_fusion.3.floats_ref, bf16[64,64]{1,0:T(8,128)(2,1)S(1)} %get-tuple-element.29.table_ref, ...), custom_call_target="tpu_custom_call" | custom-call | tf_op jit(solution)/shard_map/grams/pallas_call | solution.py:544
  32.0 1.0 %collective-permute-start.3 = (f32[8,48,384]{2,1,0:T(8,128)S(1)}, f32[8,48,384]{2,1,0:T(8,128)S(1)}, u32[]{:S(2)}, u32[]{:S(2)}) collective-permute-start(f32[8,48,384]{2,1,0:T(8,128)S(1)} %get-tuple-element.33), channel_id=1, source_target_pairs={{0,1},{1,0},{2,3},{3,2},{4,5},{5,4},{6,7},{7,6},{8,9},{9,8},{10,11... | collective-permute-start | bytes 1769480 | tf_op jit(solution)/shard_map/ppermute | solution.py:480
  33.0 1.2 %edges_out.1 = (bf16[64,128]{1,0:T(8,128)(2,1)S(1)}, bf16[64,128]{1,0:T(8,128)(2,1)S(1)}) custom-call(bf16[8,2,640,128]{3,2,1,0:T(8,128)(2,1)S(1)} %get-tuple-element.34.snap_ref), custom_call_target="tpu_custom_call" | custom-call | tf_op jit(solution)/shard_map/edges_out/pallas_call | solution.py:564
  34.2 0.5 collective-permute-done.3
  34.7 0.1 add.48
  34.8 1.9 %collective-permute-start.4 = (f32[2,48,384]{2,1,0:T(8,128)S(1)}, f32[2,48,384]{2,1,0:T(8,128)S(1)}, u32[]{:S(2)}, u32[]{:S(2)}) collective-permute-start(f32[2,48,384]{2,1,0:T(8,128)S(1)} %get-tuple-element.53), channel_id=1, source_target_pairs={{0,4},{1,5},{2,6},{3,7},{4,0},{5,1},{6,2},{7,3},{8,12},{9,13},{10,... | collective-permute-start | bytes 442376 | tf_op jit(solution)/shard_map/ppermute | solution.py:480
  36.7 2.9 %collective-permute-start.5 = (f32[2,48,384]{2,1,0:T(8,128)S(1)}, f32[2,48,384]{2,1,0:T(8,128)S(1)}, u32[]{:S(2)}, u32[]{:S(2)}) collective-permute-start(f32[2,48,384]{2,1,0:T(8,128)S(1)} %get-tuple-element.52), channel_id=1, source_target_pairs={{0,2},{1,3},{2,0},{3,1},{4,6},{5,7},{6,4},{7,5},{8,10},{9,11},{10,... | collective-permute-start | bytes 442376 | tf_op jit(solution)/shard_map/ppermute | solution.py:480
  39.6 0.9 %collective-permute-start.7 = (bf16[64,128]{1,0:T(8,128)(2,1)S(1)}, bf16[64,128]{1,0:T(8,128)(2,1)S(1)}, u32[]{:S(2)}, u32[]{:S(2)}) collective-permute-start(bf16[64,128]{1,0:T(8,128)(2,1)S(1)} %get-tuple-element.38), channel_id=1, source_target_pairs={{0,1},{1,0},{2,3},{3,2},{4,5},{5,4},{6,7},{7,6},{8,9},{9,8},{10,11... | collective-permute-start | bytes 49160 | tf_op jit(solution)/shard_map/ppermute | solution.py:576
  40.5 0.8 collective-permute-done.7.first_ref
  41.4 4.0 %collective-permute-done.5 = f32[2,48,384]{2,1,0:T(8,128)S(1)} collective-permute-done((f32[2,48,384]{2,1,0:T(8,128)S(1)}, f32[2,48,384]{2,1,0:T(8,128)S(1)}, u32[]{:S(2)}, u32[]{:S(2)}) %collective-permute-start.5) | collective-permute-done | bytes 147488 | tf_op jit(solution)/shard_map/ppermute | solution.py:480
  45.4 1.0 %collective-permute-done.6 = f32[2,48,384]{2,1,0:T(8,128)S(1)} collective-permute-done((f32[2,48,384]{2,1,0:T(8,128)S(1)}, f32[2,48,384]{2,1,0:T(8,128)S(1)}, u32[]{:S(2)}, u32[]{:S(2)}) %collective-permute-start.6) | collective-permute-done | bytes 147488 | tf_op jit(solution)/shard_map/ppermute | solution.py:480
  46.5 3.1 %collective-permute-start.8 = (f32[48,384]{1,0:T(8,128)S(1)}, f32[48,384]{1,0:T(8,128)S(1)}, u32[]{:S(2)}, u32[]{:S(2)}) collective-permute-start(f32[48,384]{1,0:T(8,128)S(1)} %slice_bitcast_fusion), channel_id=1, source_target_pairs={{0,8},{1,9},{2,10},{3,11},{4,12},{5,13},{6,14},{7,15},{8,0},{9,1},... | collective-permute-start | bytes 221192 | tf_op jit(solution)/shard_map/ppermute | solution.py:480
  49.5 1.7 %collective-permute-done.8 = f32[48,384]{1,0:T(8,128)S(1)} collective-permute-done((f32[48,384]{1,0:T(8,128)S(1)}, f32[48,384]{1,0:T(8,128)S(1)}, u32[]{:S(2)}, u32[]{:S(2)}) %collective-permute-start.8) | collective-permute-done | bytes 73760 | tf_op jit(solution)/shard_map/ppermute | solution.py:480
  51.3 4.9 %collective-permute-start.9 = (f32[48,384]{1,0:T(8,128)S(1)}, f32[48,384]{1,0:T(8,128)S(1)}, u32[]{:S(2)}, u32[]{:S(2)}) collective-permute-start(f32[48,384]{1,0:T(8,128)S(1)} %fusion.2.first_ref), channel_id=1, source_target_pairs={{0,28},{1,29},{2,30},{3,31},{4,24},{5,25},{6,26},{7,27},{8,20},{9,... | collective-permute-start | bytes 221192 | tf_op jit(solution)/shard_map/ppermute | solution.py:480
  56.2 7.6 %collective-permute-start.10 = (bf16[64,128]{1,0:T(8,128)(2,1)S(1)}, bf16[64,128]{1,0:T(8,128)(2,1)S(1)}, u32[]{:S(2)}, u32[]{:S(2)}) collective-permute-start(bf16[64,128]{1,0:T(8,128)(2,1)S(1)} %get-tuple-element.43), channel_id=1, source_target_pairs={{1,2},{2,1},{3,4},{4,3},{5,6},{6,5},{7,8},{8,7},{9,10},{10,9},{11,... | collective-permute-start | bytes 49160 | tf_op jit(solution)/shard_map/ppermute | solution.py:576
  63.9 1.2 %collective-permute-done.10.second_ref = bf16[64,128]{1,0:T(8,128)(2,1)S(1)} collective-permute-done((bf16[64,128]{1,0:T(8,128)(2,1)S(1)}, bf16[64,128]{1,0:T(8,128)(2,1)S(1)}, u32[]{:S(2)}, u32[]{:S(2)}) %collective-permute-start.10) | collective-permute-done | bytes 16416 | tf_op jit(solution)/shard_map/ppermute | solution.py:576
  65.1 3.8 %solve.1 = f32[8,128]{1,0:T(8,128)S(1)} custom-call(f32[48,384]{1,0:T(8,128)S(1)} %fusion.2.first_ref, f32[48,384]{1,0:T(8,128)S(1)} %collective-permute-done.9.second_ref, f32[8,128]{1,0:T(8,128)S(1)} %get-tuple-element.45.marks_ref), custom_call_target="tpu_custom_call" | custom-call | tf_op jit(solution)/shard_map/solve/pallas_call | solution.py:592
  68.9 1.4 %collective-permute-start.11 = (f32[1,8,128]{2,1,0:T(8,128)S(1)}, f32[1,8,128]{2,1,0:T(8,128)S(1)}, u32[]{:S(2)}, u32[]{:S(2)}) collective-permute-start(f32[1,8,128]{2,1,0:T(8,128)S(1)} %bitcast.11), channel_id=1, source_target_pairs={{0,8},{1,9},{2,10},{3,11},{4,12},{5,13},{6,14},{7,15},{8,0},{9,1},... | collective-permute-start | bytes 12296 | tf_op jit(solution)/shard_map/ppermute | solution.py:480
  70.3 0.2 edges_in.1.edge_ref
  70.5 1.8 %collective-permute-done.11 = f32[1,8,128]{2,1,0:T(8,128)S(1)} collective-permute-done((f32[1,8,128]{2,1,0:T(8,128)S(1)}, f32[1,8,128]{2,1,0:T(8,128)S(1)}, u32[]{:S(2)}, u32[]{:S(2)}) %collective-permute-start.11) | collective-permute-done | bytes 4128 | tf_op jit(solution)/shard_map/ppermute | solution.py:480
  72.4 0.9 collective-permute-start.12
  73.2 1.6 %collective-permute-done.12 = f32[2,8,128]{2,1,0:T(8,128)S(1)} collective-permute-done((f32[2,8,128]{2,1,0:T(8,128)S(1)}, f32[2,8,128]{2,1,0:T(8,128)S(1)}, u32[]{:S(2)}, u32[]{:S(2)}) %collective-permute-start.12) | collective-permute-done | bytes 8224 | tf_op jit(solution)/shard_map/ppermute | solution.py:480
  74.9 1.6 %collective-permute-start.13 = (f32[4,8,128]{2,1,0:T(8,128)S(1)}, f32[4,8,128]{2,1,0:T(8,128)S(1)}, u32[]{:S(2)}, u32[]{:S(2)}) collective-permute-start(f32[4,8,128]{2,1,0:T(8,128)S(1)} %pad_maximum_fusion.1), channel_id=1, source_target_pairs={{0,2},{1,3},{2,0},{3,1},{4,6},{5,7},{6,4},{7,5},{8,10},{9,11},{10,... | collective-permute-start | bytes 49160 | tf_op jit(solution)/shard_map/ppermute | solution.py:480
  76.5 2.5 %collective-permute-done.13 = f32[4,8,128]{2,1,0:T(8,128)S(1)} collective-permute-done((f32[4,8,128]{2,1,0:T(8,128)S(1)}, f32[4,8,128]{2,1,0:T(8,128)S(1)}, u32[]{:S(2)}, u32[]{:S(2)}) %collective-permute-start.13) | collective-permute-done | bytes 16416 | tf_op jit(solution)/shard_map/ppermute | solution.py:480
  79.0 4.6 %collective-permute-start.14 = (f32[8,8,128]{2,1,0:T(8,128)S(1)}, f32[8,8,128]{2,1,0:T(8,128)S(1)}, u32[]{:S(2)}, u32[]{:S(2)}) collective-permute-start(f32[8,8,128]{2,1,0:T(8,128)S(1)} %pad_maximum_fusion), channel_id=1, source_target_pairs={{0,1},{1,0},{2,3},{3,2},{4,5},{5,4},{6,7},{7,6},{8,9},{9,8},{10,11... | collective-permute-start | bytes 98312 | tf_op jit(solution)/shard_map/ppermute | solution.py:480
  83.5 0.9 collective-permute-done.14
  84.4 0.1 broadcast_in_dim.19.bins_ref
  84.5 1.1 %power.1 = (f32[16,8,128]{2,1,0:T(8,128)S(1)}, f32[2,8,128]{2,1,0:T(8,128)S(1)}, f32[2,8,128]{2,1,0:T(8,128)S(1)}) custom-call(s32[16,8,128]{2,1,0:T(8,128)S(1)} %broadcast_in_dim.19.bins_ref, f32[16,8,128]{2,1,0:T(8,128)S(1)} %constant_dynamic-update-slice_fusion.weights_ref, bf16[8,2,640,128]{3,2,1,0:T(8,128)(2,1)S(1)} %get-tuple-element.34.snap_ref, ...), custom_call_target="tpu_custom_call" | custom-call | tf_op jit(solution)/shard_map/power/pallas_call | solution.py:605
  85.6 0.9 %collective-permute-start.15 = (f32[2,8,128]{2,1,0:T(8,128)S(1)}, f32[2,8,128]{2,1,0:T(8,128)S(1)}, u32[]{:S(2)}, u32[]{:S(2)}) collective-permute-start(f32[2,8,128]{2,1,0:T(8,128)S(1)} %get-tuple-element.49), channel_id=1, source_target_pairs={{0,32},{32,0},{64,96},{96,64},{128,160},{160,128},{192,224},{224,1... | collective-permute-start | bytes 24584 | tf_op jit(solution)/shard_map/ppermute | solution.py:614
  86.5 2.8 %collective-permute-start.16 = (f32[2,8,128]{2,1,0:T(8,128)S(1)}, f32[2,8,128]{2,1,0:T(8,128)S(1)}, u32[]{:S(2)}, u32[]{:S(2)}) collective-permute-start(f32[2,8,128]{2,1,0:T(8,128)S(1)} %get-tuple-element.50), channel_id=1, source_target_pairs={{0,224},{32,64},{64,32},{96,128},{128,96},{160,192},{192,160},{224... | collective-permute-start | bytes 24584 | tf_op jit(solution)/shard_map/ppermute | solution.py:614
  89.3 1.8 %collective-permute-done.16.second_ref = f32[2,8,128]{2,1,0:T(8,128)S(1)} collective-permute-done((f32[2,8,128]{2,1,0:T(8,128)S(1)}, f32[2,8,128]{2,1,0:T(8,128)S(1)}, u32[]{:S(2)}, u32[]{:S(2)}) %collective-permute-start.16) | collective-permute-done | bytes 8224 | tf_op jit(solution)/shard_map/ppermute | solution.py:614
  91.1 0.6 smooth.1
  (29 shorter events, 0.6 us)
Async XLA Ops:
  0.0 12.3 %copy-start = (f32[64,16]{0,1:T(8,128)S(1)}, f32[64,16]{0,1:T(8,128)}, u32[]{:S(2)}) copy-start(f32[64,16]{0,1:T(8,128)} %param.11) | copy-start | bytes 12292
  0.0 22.9 %collective-permute-start = (bf16[2,32,32,128]{3,2,1,0:T(8,128)(2,1)}, bf16[2,32,32,128]{3,2,1,0:T(8,128)(2,1)S(1)}, u32[]{:S(2)}, u32[]{:S(2)}) collective-permute-start(bf16[2,32,32,128]{3,2,1,0:T(8,128)(2,1)} %own_ref.1), channel_id=1, source_target_pairs={{32,0},{64,32},{96,64},{128,96},{160,128},{192,160},{224,192},{0,2... | collective-permute-start | bytes 1572872 | tf_op jit(solution)/shard_map/ppermute | solution.py:486
  4.3 21.9 %collective-permute-start.1 = (bf16[2,32,32,128]{3,2,1,0:T(8,128)(2,1)}, bf16[2,32,32,128]{3,2,1,0:T(8,128)(2,1)S(1)}, u32[]{:S(2)}, u32[]{:S(2)}) collective-permute-start(bf16[2,32,32,128]{3,2,1,0:T(8,128)(2,1)} %own_ref.1), channel_id=1, source_target_pairs={{0,32},{32,64},{64,96},{96,128},{128,160},{160,192},{192,224},{224... | collective-permute-start | bytes 1572872 | tf_op jit(solution)/shard_map/ppermute | solution.py:485
  5.1 10.8 %collective-permute-start.2 = (f32[8,128]{1,0:T(8,128)S(1)}, f32[8,128]{1,0:T(8,128)S(1)}, u32[]{:S(2)}, u32[]{:S(2)}) collective-permute-start(f32[8,128]{1,0:T(8,128)S(1)} %broadcast_in_dim.21), channel_id=1, source_target_pairs={{0,28},{1,29},{2,30},{3,31},{4,24},{5,25},{6,26},{7,27},{8,20},{9,... | collective-permute-start | bytes 12296 | tf_op jit(solution)/shard_map/ppermute | solution.py:480
  13.5 1.0 %copy-start.1 = (bf16[2,32,32,128]{3,2,1,0:T(8,128)(2,1)S(1)}, bf16[2,32,32,128]{3,2,1,0:T(8,128)(2,1)}, u32[]{:S(2)}) copy-start(bf16[2,32,32,128]{3,2,1,0:T(8,128)(2,1)} %own_ref.1) | copy-start | bytes 1572868
  14.5 0.7 copy-start.2
  32.0 2.6 %collective-permute-start.3 = (f32[8,48,384]{2,1,0:T(8,128)S(1)}, f32[8,48,384]{2,1,0:T(8,128)S(1)}, u32[]{:S(2)}, u32[]{:S(2)}) collective-permute-start(f32[8,48,384]{2,1,0:T(8,128)S(1)} %get-tuple-element.33), channel_id=1, source_target_pairs={{0,1},{1,0},{2,3},{3,2},{4,5},{5,4},{6,7},{7,6},{8,9},{9,8},{10,11... | collective-permute-start | bytes 1769480 | tf_op jit(solution)/shard_map/ppermute | solution.py:480
  34.8 6.6 %collective-permute-start.4 = (f32[2,48,384]{2,1,0:T(8,128)S(1)}, f32[2,48,384]{2,1,0:T(8,128)S(1)}, u32[]{:S(2)}, u32[]{:S(2)}) collective-permute-start(f32[2,48,384]{2,1,0:T(8,128)S(1)} %get-tuple-element.53), channel_id=1, source_target_pairs={{0,4},{1,5},{2,6},{3,7},{4,0},{5,1},{6,2},{7,3},{8,12},{9,13},{10,... | collective-permute-start | bytes 442376 | tf_op jit(solution)/shard_map/ppermute | solution.py:480
  36.7 8.7 %collective-permute-start.5 = (f32[2,48,384]{2,1,0:T(8,128)S(1)}, f32[2,48,384]{2,1,0:T(8,128)S(1)}, u32[]{:S(2)}, u32[]{:S(2)}) collective-permute-start(f32[2,48,384]{2,1,0:T(8,128)S(1)} %get-tuple-element.52), channel_id=1, source_target_pairs={{0,2},{1,3},{2,0},{3,1},{4,6},{5,7},{6,4},{7,5},{8,10},{9,11},{10,... | collective-permute-start | bytes 442376 | tf_op jit(solution)/shard_map/ppermute | solution.py:480
  39.6 6.8 %collective-permute-start.6 = (f32[2,48,384]{2,1,0:T(8,128)S(1)}, f32[2,48,384]{2,1,0:T(8,128)S(1)}, u32[]{:S(2)}, u32[]{:S(2)}) collective-permute-start(f32[2,48,384]{2,1,0:T(8,128)S(1)} %get-tuple-element.51), channel_id=1, source_target_pairs={{0,6},{1,7},{2,4},{3,5},{4,2},{5,3},{6,0},{7,1},{8,14},{9,15},{10,... | collective-permute-start | bytes 442376 | tf_op jit(solution)/shard_map/ppermute | solution.py:480
  39.6 1.8 %collective-permute-start.7 = (bf16[64,128]{1,0:T(8,128)(2,1)S(1)}, bf16[64,128]{1,0:T(8,128)(2,1)S(1)}, u32[]{:S(2)}, u32[]{:S(2)}) collective-permute-start(bf16[64,128]{1,0:T(8,128)(2,1)S(1)} %get-tuple-element.38), channel_id=1, source_target_pairs={{0,1},{1,0},{2,3},{3,2},{4,5},{5,4},{6,7},{7,6},{8,9},{9,8},{10,11... | collective-permute-start | bytes 49160 | tf_op jit(solution)/shard_map/ppermute | solution.py:576
  46.5 4.8 %collective-permute-start.8 = (f32[48,384]{1,0:T(8,128)S(1)}, f32[48,384]{1,0:T(8,128)S(1)}, u32[]{:S(2)}, u32[]{:S(2)}) collective-permute-start(f32[48,384]{1,0:T(8,128)S(1)} %slice_bitcast_fusion), channel_id=1, source_target_pairs={{0,8},{1,9},{2,10},{3,11},{4,12},{5,13},{6,14},{7,15},{8,0},{9,1},... | collective-permute-start | bytes 221192 | tf_op jit(solution)/shard_map/ppermute | solution.py:480
  51.3 13.8 %collective-permute-start.9 = (f32[48,384]{1,0:T(8,128)S(1)}, f32[48,384]{1,0:T(8,128)S(1)}, u32[]{:S(2)}, u32[]{:S(2)}) collective-permute-start(f32[48,384]{1,0:T(8,128)S(1)} %fusion.2.first_ref), channel_id=1, source_target_pairs={{0,28},{1,29},{2,30},{3,31},{4,24},{5,25},{6,26},{7,27},{8,20},{9,... | collective-permute-start | bytes 221192 | tf_op jit(solution)/shard_map/ppermute | solution.py:480
  56.2 8.8 %collective-permute-start.10 = (bf16[64,128]{1,0:T(8,128)(2,1)S(1)}, bf16[64,128]{1,0:T(8,128)(2,1)S(1)}, u32[]{:S(2)}, u32[]{:S(2)}) collective-permute-start(bf16[64,128]{1,0:T(8,128)(2,1)S(1)} %get-tuple-element.43), channel_id=1, source_target_pairs={{1,2},{2,1},{3,4},{4,3},{5,6},{6,5},{7,8},{8,7},{9,10},{10,9},{11,... | collective-permute-start | bytes 49160 | tf_op jit(solution)/shard_map/ppermute | solution.py:576
  68.9 3.4 %collective-permute-start.11 = (f32[1,8,128]{2,1,0:T(8,128)S(1)}, f32[1,8,128]{2,1,0:T(8,128)S(1)}, u32[]{:S(2)}, u32[]{:S(2)}) collective-permute-start(f32[1,8,128]{2,1,0:T(8,128)S(1)} %bitcast.11), channel_id=1, source_target_pairs={{0,8},{1,9},{2,10},{3,11},{4,12},{5,13},{6,14},{7,15},{8,0},{9,1},... | collective-permute-start | bytes 12296 | tf_op jit(solution)/shard_map/ppermute | solution.py:480
  72.4 2.5 %collective-permute-start.12 = (f32[2,8,128]{2,1,0:T(8,128)S(1)}, f32[2,8,128]{2,1,0:T(8,128)S(1)}, u32[]{:S(2)}, u32[]{:S(2)}) collective-permute-start(f32[2,8,128]{2,1,0:T(8,128)S(1)} %pad_maximum_fusion.2), channel_id=1, source_target_pairs={{0,4},{1,5},{2,6},{3,7},{4,0},{5,1},{6,2},{7,3},{8,12},{9,13},{10,... | collective-permute-start | bytes 24584 | tf_op jit(solution)/shard_map/ppermute | solution.py:480
  74.9 4.1 %collective-permute-start.13 = (f32[4,8,128]{2,1,0:T(8,128)S(1)}, f32[4,8,128]{2,1,0:T(8,128)S(1)}, u32[]{:S(2)}, u32[]{:S(2)}) collective-permute-start(f32[4,8,128]{2,1,0:T(8,128)S(1)} %pad_maximum_fusion.1), channel_id=1, source_target_pairs={{0,2},{1,3},{2,0},{3,1},{4,6},{5,7},{6,4},{7,5},{8,10},{9,11},{10,... | collective-permute-start | bytes 49160 | tf_op jit(solution)/shard_map/ppermute | solution.py:480
  79.0 5.4 %collective-permute-start.14 = (f32[8,8,128]{2,1,0:T(8,128)S(1)}, f32[8,8,128]{2,1,0:T(8,128)S(1)}, u32[]{:S(2)}, u32[]{:S(2)}) collective-permute-start(f32[8,8,128]{2,1,0:T(8,128)S(1)} %pad_maximum_fusion), channel_id=1, source_target_pairs={{0,1},{1,0},{2,3},{3,2},{4,5},{5,4},{6,7},{7,6},{8,9},{9,8},{10,11... | collective-permute-start | bytes 98312 | tf_op jit(solution)/shard_map/ppermute | solution.py:480
  85.6 3.7 %collective-permute-start.15 = (f32[2,8,128]{2,1,0:T(8,128)S(1)}, f32[2,8,128]{2,1,0:T(8,128)S(1)}, u32[]{:S(2)}, u32[]{:S(2)}) collective-permute-start(f32[2,8,128]{2,1,0:T(8,128)S(1)} %get-tuple-element.49), channel_id=1, source_target_pairs={{0,32},{32,0},{64,96},{96,64},{128,160},{160,128},{192,224},{224,1... | collective-permute-start | bytes 24584 | tf_op jit(solution)/shard_map/ppermute | solution.py:614
  86.5 4.6 %collective-permute-start.16 = (f32[2,8,128]{2,1,0:T(8,128)S(1)}, f32[2,8,128]{2,1,0:T(8,128)S(1)}, u32[]{:S(2)}, u32[]{:S(2)}) collective-permute-start(f32[2,8,128]{2,1,0:T(8,128)S(1)} %get-tuple-element.50), channel_id=1, source_target_pairs={{0,224},{32,64},{64,32},{96,128},{128,96},{160,192},{192,160},{224... | collective-permute-start | bytes 24584 | tf_op jit(solution)/shard_map/ppermute | solution.py:614

commit v7 on v6

--- a/solution.py
+++ b/solution.py
@@ -193,50 +193,79 @@
     run(multiply(7, odd_ref, keep_ref))
 
 
-def edge_out_kernel(snap_ref, first_ref, second_ref):
-    rows = 8 * 8
-    lane = lane_ids(rows)
-    ends = [jnp.zeros((rows, LANES), F32) for _ in range(2)]
-    for beam in range(OWN_BEAMS):
+def edge_kernel(
+    table_ref, low_ref, own_ref, high_ref, ints_ref, floats_ref,
+    out_ref, wide_ref,
+):
+    last = PULSES * SEL
+    blank = jnp.zeros((LANES - 3 * OWN_COLS, PULSES), BF16)
+    small = lane_ids(8)
+    sides = []
+    for side in range(2):
+        total = None
         for part in range(2):
-            for block in range(8):
-                low = SEL + rows * block
-                value = snap_ref[beam, part, low : low + rows, :].astype(F32)
-                target = 16 * block + 8 * part + beam
-                here = lane == target
-                for end in range(2):
-                    shift = (target + end) % LANES
-                    moved = pltpu.roll(value, shift, 1) if shift else value
-                    ends[end] = jnp.where(here, moved, ends[end])
-    even = lax.rem(lax.axis_index("rng"), 2) == 0
-    first_ref[...] = jnp.where(even, ends[1], ends[0]).astype(BF16)
-    second_ref[...] = jnp.where(even, ends[0], ends[1]).astype(BF16)
-
-
-def edge_in_kernel(first_ref, second_ref, out_ref):
-    rows = 8 * 8
-    last = PULSES * SEL
-    lane = lane_ids(rows)
-    first = first_ref[...].astype(F32)
-    second = second_ref[...].astype(F32)
-
-    def rolled(value, shift):
-        return pltpu.roll(value, shift % LANES, 1) if shift % LANES else value
-
-    for block in range(8):
-        both = jnp.where(
-            lane < 16, rolled(first, -16 * block), rolled(second, 16 - 16 * block)
-        )
-        for part, value in enumerate((both, rolled(both, -8))):
-            value = value.astype(BF16)
-            out_ref[part, SEL + rows * block : SEL + rows * (block + 1), :] = value
-            if block == 0:
-                out_ref[part, last + SEL : last + 2 * SEL, :] = value[:SEL]
-            if block == 7:
-                out_ref[part, :SEL, :] = value[rows - SEL :]
+            columns = jnp.concatenate(
+                [low_ref[side, part], own_ref[side, part], high_ref[side, part], blank],
+                0,
+            )
+            product = lax.dot_general(
+                table_ref[:, PULSES * part : PULSES * (part + 1)],
+                columns,
+                TRANSPOSED,
+                preferred_element_type=F32,
+            )
+            total = product if total is None else total + product
+        sides.append(total)
+    first_part = lax.rem(small, 16) < 8
+    turned = jnp.transpose(
+        jnp.concatenate(
+            [
+                ints_ref[...].astype(F32),
+                floats_ref[...],
+                jnp.zeros((LANES - 16, LANES), F32),
+            ],
+            0,
+        )
+    )
+    nearest = lax.rem(small, 8)
+
+    def row_of(index, start):
+        value = jnp.broadcast_to(turned[index : index + 1, :], (8, LANES))
+        return jnp.take_along_axis(value, nearest + start, axis=1)
+
+    for sel in range(SEL):
+        index = row_of(sel, 0).astype(jnp.int32)
+        cosine = row_of(sel, 8)
+        sine = row_of(SEL + sel, 8)
+
+        def chosen(row):
+            picked = [
+                jnp.take_along_axis(value[row : row + 8], index, axis=1)
+                for value in sides
+            ]
+            return jnp.where(small < 16, picked[0], picked[1])
+
+        values = []
+        for row in range(0, PULSES, 8):
+            real, imag = chosen(row), chosen(PULSES + row)
+            values.append(
+                jnp.where(
+                    first_part,
+                    cosine * real - sine * imag,
+                    sine * real + cosine * imag,
+                )
+            )
+        wide_ref[pl.ds(sel, PULSES, stride=SEL), :] = jnp.concatenate(values, 0)
+    value = wide_ref[...]
     for part in range(2):
+        if part == 1:
+            value = pltpu.roll(value, LANES - 8, 1)
+        short = value.astype(BF16)
+        out_ref[part, SEL : SEL + last, :] = short
+        out_ref[part, :SEL, :] = short[last - SEL :]
+        out_ref[part, SEL + last : 2 * SEL + last, :] = short[:SEL]
         out_ref[part, last + 2 * SEL :, :] = jnp.zeros(
-            (SLOTS * SEL - last - 2 * SEL, CELLS), BF16
+            (SLOTS * SEL - last - 2 * SEL, LANES), BF16
         )
 
 
@@ -409,13 +438,11 @@
     power_ref, first_ref, second_ref,
 ):
     mine = own_group()
-    even = lax.rem(lax.axis_index("rng"), 2) == 0
     small = lane_ids(8)
     counts = jnp.zeros((8, LANES), F32)
     for place in range(GROUPS):
         counts = counts + weights_ref[place]
     counts = spread(counts, 120) * BLK
-    low_lane = jnp.where(even, 16, 0)
     rows = SLOTS * SEL
     edge = edge_ref[...].reshape(2 * rows, LANES)
     for beam in range(OWN_BEAMS):
@@ -448,8 +475,8 @@
             power = found[16 * half : 16 * half + 8] + found[16 * half + 8 : 16 * half + 16]
             inner = power[:, :LANES] / quiets[half]
             outer = power[:, LANES:] / quiets[half]
-            low = spread(outer, beam + low_lane)
-            high = spread(outer, beam + 16 - low_lane)
+            low = spread(outer, beam)
+            high = spread(outer, 16 + beam)
             below = jnp.where(small == 0, low, pltpu.roll(inner, 1, 1))
             above = jnp.where(
                 small == LANES - 1, high, pltpu.roll(inner, LANES - 1, 1)
@@ -516,14 +543,25 @@
     def own(value):
         return lax.dynamic_slice_in_dim(value, az * OWN_BEAMS, OWN_BEAMS, 0)
 
+    ends = [echoes[..., CELLS - 1], echoes[..., 0]]
+    ahead = [(i, i + 1) for i in range(31)]
+    ends = jnp.stack(
+        [
+            lax.ppermute(ends[0], "rng", ahead),
+            lax.ppermute(ends[1], "rng", [(b, a) for a, b in ahead]),
+        ]
+    )
+    low_ends, high_ends = halo_columns(ends)
     marks = jnp.broadcast_to(train_mask.astype(F32), (OWN_BEAMS, LANES))
     marks = marks + swap(marks, 28)
     first = (own(arc_start) - az * OWN_COLS + ARC // 2) % COLS
-    ints = jnp.concatenate(
-        [first[:, None] + own(arc_offsets), own(doppler_bins), train_mask], 1
-    )
+    columns = first[:, None] + own(arc_offsets)
+    ints = jnp.concatenate([columns, own(doppler_bins), train_mask], 1)
+    ints = jnp.pad(ints, ((0, 0), (0, LANES - ints.shape[1])))
     angles = own(steer_angles)
-    floats = jnp.concatenate([jnp.cos(angles), jnp.sin(angles)], 1)
+    cosine, sine = jnp.cos(angles), jnp.sin(angles)
+    floats = jnp.concatenate([cosine, sine], 1)
+    floats = jnp.pad(floats, ((0, 0), (0, LANES - floats.shape[1])))
     centres = jnp.broadcast_to(
         own(doppler_bins).reshape(GROUPS, 8, 1), (GROUPS, 8, LANES)
     )
@@ -539,6 +577,16 @@
         name="spectra",
     )
     spec, table = transform(jnp.asarray(table_array()), echoes)
+    edges = pl.pallas_call(
+        edge_kernel,
+        out_shape=shape(2, SLOTS * SEL, LANES, dtype=BF16),
+        in_specs=[VMEM] * 6,
+        out_specs=VMEM,
+        scratch_shapes=[pltpu.VMEM((PULSES * SEL, LANES), F32)],
+        compiler_params=limit(8),
+        name="edges",
+    )(table, low_ends, ends, high_ends, ints, floats)
+    high, edges, centres = lax.optimization_barrier((high, edges, centres))
     high, table = transform(table, high)
     half = shape(8, DOF, 8 * DOF)
     snaps, keep, send, marks = pl.pallas_call(
@@ -560,35 +608,10 @@
         compiler_params=limit(16),
         name="grams",
     )(ints, floats, table, low, spec, high, marks)
-    edge = shape(64, LANES, dtype=BF16)
-    edges = pl.pallas_call(
-        edge_out_kernel,
-        out_shape=(edge, edge),
-        in_specs=[VMEM],
-        out_specs=(VMEM, VMEM),
-        compiler_params=limit(8),
-        name="edges_out",
-    )(snaps)
-    moved, edges = lax.optimization_barrier((swap(send, 1), edges))
-    part = keep + moved
-    moved = [swap(part[2:4], 4), swap(part[4:6], 2), swap(part[6:], 6)]
-    edges = [
-        lax.ppermute(value, "rng", pairs)
-        for value, pairs in zip(edges, neighbours(32, False))
-    ]
-    moved, edges[0] = lax.optimization_barrier((moved, edges[0]))
-    part = part[:2] + moved[0] + moved[1] + moved[2]
+    part = keep + swap(send, 1)
+    part = part[:2] + swap(part[2:4], 4) + swap(part[4:6], 2) + swap(part[6:], 6)
     part = part[0] + swap(part[1], 8)
     other = swap(part, 28)
-    other, edges = lax.optimization_barrier((other, edges))
-    edges = pl.pallas_call(
-        edge_in_kernel,
-        out_shape=shape(2, SLOTS * SEL, LANES, dtype=BF16),
-        in_specs=[VMEM, VMEM],
-        out_specs=VMEM,
-        compiler_params=limit(8),
-        name="edges_in",
-    )(*edges)
     weights = pl.pallas_call(
         solve_kernel,
         out_shape=shape(8, LANES),

time: 92.5 us -> 100 us (1.081)
  waiting for transfers between devices: 27.5 us -> 37.7 us
    ppermute x11, waiting for transfers between devices: 14.1 us -> 21.2 us  [swap(): return lax.ppermute(value, 'rng', [(i, i ^ turn) for i in range(32)])]
    ppermute x2, waiting for transfers between devices: 2 us -> 7.84 us  [the longest x1 7.84 us: body(): lax.ppermute(ends[1], 'rng', [(b, a) for a, b in ahead])]
    ppermute x1 -> x2, waiting for transfers between devices: 6.99 us -> 1.23 us  [halo_columns(): high = lax.ppermute(echoes, 'az', [(b, a) for a, b in ring])]
    ppermute x2, starting transfers between devices: 3.73 us -> 0.62 us  [body(): lax.ppermute(value, 'az', pairs)]
    ppermute x2, waiting for transfers between devices: 1.82 us -> 4.17 us  [body(): lax.ppermute(value, 'az', pairs)]
    ppermute x11, starting transfers between devices: 27.7 us -> 29.7 us  [swap(): return lax.ppermute(value, 'rng', [(i, i ^ turn) for i in range(32)])]
    slice x1 -> x2, local copies, waits for them, and re-layouts: 0.03 us -> 1.56 us  [the longest x1 1.53 us: body(): ends = [echoes[..., CELLS - 1], echoes[..., 0]]]
    unnamed x14 -> x24, local copies, waits for them, and re-layouts: 2.71 us -> 1.24 us
  transfers between devices with their start and end apart: 17 -> 19, of which waited for: 13 -> 15; matrix products, arithmetic and copies ran while one was open for 4% -> 4% of each run, Pallas kernels for 3% -> 3%
where the time goes in v7:
time: 100 us
  starting transfers between devices  43.8 us (44%)
  waiting for transfers between devices  37.7 us (38%)
  Pallas kernels  14 us (14%)
  local copies, waits for them, and re-layouts  3.22 us (3%)
  other arithmetic  1.17 us (1%)
    ppermute x11, starting transfers between devices, swap(): return lax.ppermute(value, 'rng', [(i, i ^ turn) for i in range(32)])  29.7 us
    ppermute x11, waiting for transfers between devices, swap(): return lax.ppermute(value, 'rng', [(i, i ^ turn) for i in range(32)])  21.2 us
    ppermute x1, waiting for transfers between devices, body(): lax.ppermute(ends[1], 'rng', [(b, a) for a, b in ahead])  7.84 us
    pallas_call x1, Pallas kernels, body(): pl.pallas_call(gram_kernel, out_shape=(shape(OWN_BEAMS, 2, SLOTS * SEL, C...  5.81 us
    ppermute x2, starting transfers between devices, halo_columns(): high = lax.ppermute(echoes, 'az', [(b, a) for a, b in ring])  5.69 us
    ppermute x1, starting transfers between devices, body(): lax.ppermute(ends[0], 'rng', ahead)  4.43 us
    ppermute x2, waiting for transfers between devices, body(): lax.ppermute(value, 'az', pairs)  4.17 us
    pallas_call x1, Pallas kernels, body(): pl.pallas_call(solve_kernel, out_shape=shape(8, LANES), in_specs=[VMEM] *...  3.85 us
  transfers between devices with their start and end apart: 19, of which 15 were waited for; matrix products, arithmetic and copies ran while one was open for 4% of the time, Pallas kernels for 3%

profile of v7, /device:TPU:1, one launch (start us, length us, event | category | flops | bytes accessed | tf_op | source)
XLA Modules:
  0.0 100.2 jit_solution(14768810367324702684)
XLA Ops:
  0.1 4.4 %collective-permute-start = (bf16[2,32,32,128]{3,2,1,0:T(8,128)(2,1)}, bf16[2,32,32,128]{3,2,1,0:T(8,128)(2,1)S(1)}, u32[]{:S(2)}, u32[]{:S(2)}) collective-permute-start(bf16[2,32,32,128]{3,2,1,0:T(8,128)(2,1)} %own_ref.1), channel_id=1, source_target_pairs={{32,0},{64,32},{96,64},{128,96},{160,128},{192,160},{224,192},{0,2... | collective-permute-start | bytes 1572872 | tf_op jit(solution)/shard_map/ppermute | solution.py:513
  4.5 0.7 convert_bitcast_fusion
  5.2 5.6 %collective-permute-start.6 = (f32[8,128]{1,0:T(8,128)S(1)}, f32[8,128]{1,0:T(8,128)S(1)}, u32[]{:S(2)}, u32[]{:S(2)}) collective-permute-start(f32[8,128]{1,0:T(8,128)S(1)} %broadcast_in_dim.21), channel_id=1, source_target_pairs={{0,28},{1,29},{2,30},{3,31},{4,24},{5,25},{6,26},{7,27},{8,20},{9,... | collective-permute-start | bytes 12296 | tf_op jit(solution)/shard_map/ppermute | solution.py:507
  10.8 1.5 %fusion.5 = (bf16[2,32,32,1]{3,2,1,0:T(8,128)(2,1)S(1)}, bf16[2,32,32,1]{3,2,1,0:T(8,128)(2,1)S(1)}) fusion(bf16[2,32,32,128]{3,2,1,0:T(8,128)(2,1)} %own_ref.1), kind=kLoop, calls=%fused_computation.29 | loop fusion | bytes 16384 | tf_op jit(solution)/shard_map/slice | solution.py:546
  12.3 0.5 copy.21
  12.8 3.1 %collective-permute-start.2 = (bf16[2,32,32]{2,1,0:T(8,128)(2,1)S(1)}, bf16[2,32,32]{2,1,0:T(8,128)(2,1)S(1)}, u32[]{:S(2)}, u32[]{:S(2)}) collective-permute-start(bf16[2,32,32]{2,1,0:T(8,128)(2,1)S(1)} %bitcast.19), channel_id=1, source_target_pairs={{1,0},{2,1},{3,2},{4,3},{5,4},{6,5},{7,6},{8,7},{9,8},{10,9},{11,1... | collective-permute-start | bytes 12296 | tf_op jit(solution)/shard_map/ppermute | solution.py:551
  15.9 0.5 copy.20
  16.4 4.4 %collective-permute-start.1 = (bf16[2,32,32]{2,1,0:T(8,128)(2,1)S(1)}, bf16[2,32,32]{2,1,0:T(8,128)(2,1)S(1)}, u32[]{:S(2)}, u32[]{:S(2)}) collective-permute-start(bf16[2,32,32]{2,1,0:T(8,128)(2,1)S(1)} %bitcast.20), channel_id=1, source_target_pairs={{0,1},{1,2},{2,3},{3,4},{4,5},{5,6},{6,7},{7,8},{8,9},{9,10},{10,1... | collective-permute-start | bytes 12296 | tf_op jit(solution)/shard_map/ppermute | solution.py:550
  20.8 0.1 copy.18
  21.1 0.1 constant_dynamic-slice_fusion.1
  21.3 0.1 and_select_fusion
  21.7 0.7 spectra.2
  22.4 7.8 %collective-permute-done.2 = bf16[2,32,32]{2,1,0:T(8,128)(2,1)S(1)} collective-permute-done((bf16[2,32,32]{2,1,0:T(8,128)(2,1)S(1)}, bf16[2,32,32]{2,1,0:T(8,128)(2,1)S(1)}, u32[]{:S(2)}, u32[]{:S(2)}) %collective-permute-start.2) | collective-permute-done | bytes 4128 | tf_op jit(solution)/shard_map/ppermute | solution.py:551
  30.2 1.3 %collective-permute-start.4 = (bf16[2,2,32,32]{3,2,1,0:T(8,128)(2,1)S(1)}, bf16[2,2,32,32]{3,2,1,0:T(8,128)(2,1)S(1)}, u32[]{:S(2)}, u32[]{:S(2)}) collective-permute-start(bf16[2,2,32,32]{3,2,1,0:T(8,128)(2,1)S(1)} %pad_maximum_fusion.own_ref), channel_id=1, source_target_pairs={{32,0},{64,32},{96,64},{128,96},{160,128},{192,160},{224,192},{0,2... | collective-permute-start | bytes 24584 | tf_op jit(solution)/shard_map/ppermute | solution.py:513
  31.5 0.3 collective-permute-start.3
  31.9 1.2 %collective-permute-done.4.high_ref = bf16[2,2,32,32]{3,2,1,0:T(8,128)(2,1)S(1)} collective-permute-done((bf16[2,2,32,32]{3,2,1,0:T(8,128)(2,1)S(1)}, bf16[2,2,32,32]{3,2,1,0:T(8,128)(2,1)S(1)}, u32[]{:S(2)}, u32[]{:S(2)}) %collective-permute-start.4) | collective-permute-done | bytes 8224 | tf_op jit(solution)/shard_map/ppermute | solution.py:513
  33.1 3.3 %collective-permute-done.3.low_ref = bf16[2,2,32,32]{3,2,1,0:T(8,128)(2,1)S(1)} collective-permute-done((bf16[2,2,32,32]{3,2,1,0:T(8,128)(2,1)S(1)}, bf16[2,2,32,32]{3,2,1,0:T(8,128)(2,1)S(1)}, u32[]{:S(2)}, u32[]{:S(2)}) %collective-permute-start.3) | collective-permute-done | bytes 8224 | tf_op jit(solution)/shard_map/ppermute | solution.py:512
  36.4 1.3 %edges.1.edge_ref = bf16[2,640,128]{2,1,0:T(8,128)(2,1)S(1)} custom-call(bf16[64,64]{1,0:T(8,128)(2,1)S(1)} %get-tuple-element.19.table_ref, bf16[2,2,32,32]{3,2,1,0:T(8,128)(2,1)S(1)} %collective-permute-done.3.low_ref, bf16[2,2,32,32]{3,2,1,0:T(8,128)(2,1)S(1)} %pad_maximum_fusion.own_ref, bf16[2,2,32,32]{3,2,1,0:T(8,128)(2,1)S(1)} %collective-permute-done.4.high_ref, ...), custom_call_target="tpu_custom_call" | custom-call | tf_op jit(solution)/shard_map/edges/pallas_call | solution.py:580
  37.8 0.7 spectra.3
  38.5 5.8 %grams.1 = (bf16[8,2,640,128]{3,2,1,0:T(8,128)(2,1)S(1)}, f32[8,48,384]{2,1,0:T(8,128)S(1)}, f32[8,48,384]{2,1,0:T(8,128)S(1)}, f32[8,128]{1,0:T(8,128)S(1)}) custom-call(s32[8,128]{1,0:T(8,128)S(1)} %pad.8.ints_ref, f32[8,128]{1,0:T(8,128)S(1)} %select_maximum_fusion.floats_ref, bf16[64,64]{1,0:T(8,128)(2,1)S(1)} %get-tuple-element.22.table_ref, ...), custom_call_target="tpu_custom_call" | custom-call | tf_op jit(solution)/shard_map/grams/pallas_call | solution.py:592
  44.3 0.1 collective-permute-start.7
  44.4 2.0 %collective-permute-done.7 = f32[8,48,384]{2,1,0:T(8,128)S(1)} collective-permute-done((f32[8,48,384]{2,1,0:T(8,128)S(1)}, f32[8,48,384]{2,1,0:T(8,128)S(1)}, u32[]{:S(2)}, u32[]{:S(2)}) %collective-permute-start.7) | collective-permute-done | bytes 589856 | tf_op jit(solution)/shard_map/ppermute | solution.py:507
  46.4 0.1 add.52
  46.5 1.9 %collective-permute-start.8 = (f32[2,48,384]{2,1,0:T(8,128)S(1)}, f32[2,48,384]{2,1,0:T(8,128)S(1)}, u32[]{:S(2)}, u32[]{:S(2)}) collective-permute-start(f32[2,48,384]{2,1,0:T(8,128)S(1)} %get-tuple-element.33), channel_id=1, source_target_pairs={{0,4},{1,5},{2,6},{3,7},{4,0},{5,1},{6,2},{7,3},{8,12},{9,13},{10,... | collective-permute-start | bytes 442376 | tf_op jit(solution)/shard_map/ppermute | solution.py:507
  48.4 1.5 %collective-permute-start.10 = (f32[2,48,384]{2,1,0:T(8,128)S(1)}, f32[2,48,384]{2,1,0:T(8,128)S(1)}, u32[]{:S(2)}, u32[]{:S(2)}) collective-permute-start(f32[2,48,384]{2,1,0:T(8,128)S(1)} %get-tuple-element.34), channel_id=1, source_target_pairs={{0,6},{1,7},{2,4},{3,5},{4,2},{5,3},{6,0},{7,1},{8,14},{9,15},{10,... | collective-permute-start | bytes 442376 | tf_op jit(solution)/shard_map/ppermute | solution.py:507
  49.8 1.3 %collective-permute-start.9 = (f32[2,48,384]{2,1,0:T(8,128)S(1)}, f32[2,48,384]{2,1,0:T(8,128)S(1)}, u32[]{:S(2)}, u32[]{:S(2)}) collective-permute-start(f32[2,48,384]{2,1,0:T(8,128)S(1)} %get-tuple-element.35), channel_id=1, source_target_pairs={{0,2},{1,3},{2,0},{3,1},{4,6},{5,7},{6,4},{7,5},{8,10},{9,11},{10,... | collective-permute-start | bytes 442376 | tf_op jit(solution)/shard_map/ppermute | solution.py:507
  51.2 1.3 %collective-permute-done.8 = f32[2,48,384]{2,1,0:T(8,128)S(1)} collective-permute-done((f32[2,48,384]{2,1,0:T(8,128)S(1)}, f32[2,48,384]{2,1,0:T(8,128)S(1)}, u32[]{:S(2)}, u32[]{:S(2)}) %collective-permute-start.8) | collective-permute-done | bytes 147488 | tf_op jit(solution)/shard_map/ppermute | solution.py:507
  52.5 4.3 %collective-permute-done.10 = f32[2,48,384]{2,1,0:T(8,128)S(1)} collective-permute-done((f32[2,48,384]{2,1,0:T(8,128)S(1)}, f32[2,48,384]{2,1,0:T(8,128)S(1)}, u32[]{:S(2)}, u32[]{:S(2)}) %collective-permute-start.10) | collective-permute-done | bytes 147488 | tf_op jit(solution)/shard_map/ppermute | solution.py:507
  56.8 2.9 %collective-permute-done.9 = f32[2,48,384]{2,1,0:T(8,128)S(1)} collective-permute-done((f32[2,48,384]{2,1,0:T(8,128)S(1)}, f32[2,48,384]{2,1,0:T(8,128)S(1)}, u32[]{:S(2)}, u32[]{:S(2)}) %collective-permute-start.9) | collective-permute-done | bytes 147488 | tf_op jit(solution)/shard_map/ppermute | solution.py:507
  59.7 3.1 %collective-permute-start.11 = (f32[48,384]{1,0:T(8,128)S(1)}, f32[48,384]{1,0:T(8,128)S(1)}, u32[]{:S(2)}, u32[]{:S(2)}) collective-permute-start(f32[48,384]{1,0:T(8,128)S(1)} %slice_bitcast_fusion), channel_id=1, source_target_pairs={{0,8},{1,9},{2,10},{3,11},{4,12},{5,13},{6,14},{7,15},{8,0},{9,1},... | collective-permute-start | bytes 221192 | tf_op jit(solution)/shard_map/ppermute | solution.py:507
  62.8 1.7 %collective-permute-done.11 = f32[48,384]{1,0:T(8,128)S(1)} collective-permute-done((f32[48,384]{1,0:T(8,128)S(1)}, f32[48,384]{1,0:T(8,128)S(1)}, u32[]{:S(2)}, u32[]{:S(2)}) %collective-permute-start.11) | collective-permute-done | bytes 73760 | tf_op jit(solution)/shard_map/ppermute | solution.py:507
  64.6 5.7 %collective-permute-start.12 = (f32[48,384]{1,0:T(8,128)S(1)}, f32[48,384]{1,0:T(8,128)S(1)}, u32[]{:S(2)}, u32[]{:S(2)}) collective-permute-start(f32[48,384]{1,0:T(8,128)S(1)} %fusion.2.first_ref), channel_id=1, source_target_pairs={{0,28},{1,29},{2,30},{3,31},{4,24},{5,25},{6,26},{7,27},{8,20},{9,... | collective-permute-start | bytes 221192 | tf_op jit(solution)/shard_map/ppermute | solution.py:507
  70.3 2.3 %collective-permute-done.12.second_ref = f32[48,384]{1,0:T(8,128)S(1)} collective-permute-done((f32[48,384]{1,0:T(8,128)S(1)}, f32[48,384]{1,0:T(8,128)S(1)}, u32[]{:S(2)}, u32[]{:S(2)}) %collective-permute-start.12) | collective-permute-done | bytes 73760 | tf_op jit(solution)/shard_map/ppermute | solution.py:507
  72.6 3.8 %solve.1 = f32[8,128]{1,0:T(8,128)S(1)} custom-call(f32[48,384]{1,0:T(8,128)S(1)} %fusion.2.first_ref, f32[48,384]{1,0:T(8,128)S(1)} %collective-permute-done.12.second_ref, f32[8,128]{1,0:T(8,128)S(1)} %get-tuple-element.27.marks_ref), custom_call_target="tpu_custom_call" | custom-call | tf_op jit(solution)/shard_map/solve/pallas_call | solution.py:615
  76.5 1.0 collective-permute-start.13
  77.4 2.5 %collective-permute-done.13 = f32[1,8,128]{2,1,0:T(8,128)S(1)} collective-permute-done((f32[1,8,128]{2,1,0:T(8,128)S(1)}, f32[1,8,128]{2,1,0:T(8,128)S(1)}, u32[]{:S(2)}, u32[]{:S(2)}) %collective-permute-start.13) | collective-permute-done | bytes 4128 | tf_op jit(solution)/shard_map/ppermute | solution.py:507
  79.9 0.4 collective-permute-start.14
  80.4 2.1 %collective-permute-done.14 = f32[2,8,128]{2,1,0:T(8,128)S(1)} collective-permute-done((f32[2,8,128]{2,1,0:T(8,128)S(1)}, f32[2,8,128]{2,1,0:T(8,128)S(1)}, u32[]{:S(2)}, u32[]{:S(2)}) %collective-permute-start.14) | collective-permute-done | bytes 8224 | tf_op jit(solution)/shard_map/ppermute | solution.py:507
  82.4 2.8 %collective-permute-start.15 = (f32[4,8,128]{2,1,0:T(8,128)S(1)}, f32[4,8,128]{2,1,0:T(8,128)S(1)}, u32[]{:S(2)}, u32[]{:S(2)}) collective-permute-start(f32[4,8,128]{2,1,0:T(8,128)S(1)} %pad_maximum_fusion.2), channel_id=1, source_target_pairs={{0,2},{1,3},{2,0},{3,1},{4,6},{5,7},{6,4},{7,5},{8,10},{9,11},{10,... | collective-permute-start | bytes 49160 | tf_op jit(solution)/shard_map/ppermute | solution.py:507
  85.2 1.3 %collective-permute-done.15 = f32[4,8,128]{2,1,0:T(8,128)S(1)} collective-permute-done((f32[4,8,128]{2,1,0:T(8,128)S(1)}, f32[4,8,128]{2,1,0:T(8,128)S(1)}, u32[]{:S(2)}, u32[]{:S(2)}) %collective-permute-start.15) | collective-permute-done | bytes 16416 | tf_op jit(solution)/shard_map/ppermute | solution.py:507
  86.5 6.3 %collective-permute-start.16 = (f32[8,8,128]{2,1,0:T(8,128)S(1)}, f32[8,8,128]{2,1,0:T(8,128)S(1)}, u32[]{:S(2)}, u32[]{:S(2)}) collective-permute-start(f32[8,8,128]{2,1,0:T(8,128)S(1)} %pad_maximum_fusion.1), channel_id=1, source_target_pairs={{0,1},{1,0},{2,3},{3,2},{4,5},{5,4},{6,7},{7,6},{8,9},{9,8},{10,11... | collective-permute-start | bytes 98312 | tf_op jit(solution)/shard_map/ppermute | solution.py:507
  92.8 0.9 collective-permute-done.16
  93.6 1.1 %power.1 = (f32[16,8,128]{2,1,0:T(8,128)S(1)}, f32[2,8,128]{2,1,0:T(8,128)S(1)}, f32[2,8,128]{2,1,0:T(8,128)S(1)}) custom-call(s32[16,8,128]{2,1,0:T(8,128)S(1)} %broadcast_in_dim.19.bins_ref, f32[16,8,128]{2,1,0:T(8,128)S(1)} %constant_dynamic-update-slice_fusion.weights_ref, bf16[8,2,640,128]{3,2,1,0:T(8,128)(2,1)S(1)} %get-tuple-element.28.snap_ref, ...), custom_call_target="tpu_custom_call" | custom-call | tf_op jit(solution)/shard_map/power/pallas_call | solution.py:628
  94.8 0.1 collective-permute-start.17
  94.9 0.5 collective-permute-start.18
  95.4 2.0 %collective-permute-done.17.first_ref = f32[2,8,128]{2,1,0:T(8,128)S(1)} collective-permute-done((f32[2,8,128]{2,1,0:T(8,128)S(1)}, f32[2,8,128]{2,1,0:T(8,128)S(1)}, u32[]{:S(2)}, u32[]{:S(2)}) %collective-permute-start.17) | collective-permute-done | bytes 8224 | tf_op jit(solution)/shard_map/ppermute | solution.py:637
  97.3 2.2 %collective-permute-done.18.second_ref = f32[2,8,128]{2,1,0:T(8,128)S(1)} collective-permute-done((f32[2,8,128]{2,1,0:T(8,128)S(1)}, f32[2,8,128]{2,1,0:T(8,128)S(1)}, u32[]{:S(2)}, u32[]{:S(2)}) %collective-permute-start.18) | collective-permute-done | bytes 8224 | tf_op jit(solution)/shard_map/ppermute | solution.py:637
  99.6 0.6 smooth.1
  (45 shorter events, 1.0 us)
Async XLA Ops:
  0.0 20.9 %copy-start = (f32[64,16]{0,1:T(8,128)S(1)}, f32[64,16]{0,1:T(8,128)}, u32[]{:S(2)}) copy-start(f32[64,16]{0,1:T(8,128)} %param.11) | copy-start | bytes 12292
  0.0 21.7 %copy-start.2 = (bf16[64,64]{1,0:T(8,128)(2,1)S(1)}, bf16[64,64]{1,0:T(8,128)(2,1)}, u32[]{:S(2)}) copy-start(bf16[64,64]{1,0:T(8,128)(2,1)} %constant.33.clone.table_ref) | copy-start | bytes 24580
  0.0 21.7 %copy-start.1 = (bf16[2,32,32,128]{3,2,1,0:T(8,128)(2,1)S(1)}, bf16[2,32,32,128]{3,2,1,0:T(8,128)(2,1)}, u32[]{:S(2)}) copy-start(bf16[2,32,32,128]{3,2,1,0:T(8,128)(2,1)} %own_ref.1) | copy-start | bytes 1572868
  0.0 20.8 %copy-start.5 = (s32[8,1]{0,1:T(1,128)S(1)}, s32[8,1]{0,1:T(1,128)}, u32[]{:S(2)}) copy-start(s32[8,1]{0,1:T(1,128)} %param.12) | copy-start | bytes 100
  0.0 21.1 %copy-start.3 = (s32[64,16]{0,1:T(8,128)S(1)}, s32[64,16]{0,1:T(8,128)}, u32[]{:S(2)}) copy-start(s32[64,16]{0,1:T(8,128)} %param.10) | copy-start | bytes 12292
  0.0 21.1 %copy-start.4 = (s32[64,16]{0,1:T(8,128)S(1)}, s32[64,16]{0,1:T(8,128)}, u32[]{:S(2)}) copy-start(s32[64,16]{0,1:T(8,128)} %param.9) | copy-start | bytes 12292
  0.0 21.3 %copy-start.6 = (s32[64]{0:T(128)S(1)}, s32[64]{0:T(128)}, u32[]{:S(2)}) copy-start(s32[64]{0:T(128)} %param.8) | copy-start | bytes 772
  0.1 37.6 %collective-permute-start = (bf16[2,32,32,128]{3,2,1,0:T(8,128)(2,1)}, bf16[2,32,32,128]{3,2,1,0:T(8,128)(2,1)S(1)}, u32[]{:S(2)}, u32[]{:S(2)}) collective-permute-start(bf16[2,32,32,128]{3,2,1,0:T(8,128)(2,1)} %own_ref.1), channel_id=1, source_target_pairs={{32,0},{64,32},{96,64},{128,96},{160,128},{192,160},{224,192},{0,2... | collective-permute-start | bytes 1572872 | tf_op jit(solution)/shard_map/ppermute | solution.py:513
  4.5 34.0 %collective-permute-start.5 = (bf16[2,32,32,128]{3,2,1,0:T(8,128)(2,1)}, bf16[2,32,32,128]{3,2,1,0:T(8,128)(2,1)S(1)}, u32[]{:S(2)}, u32[]{:S(2)}) collective-permute-start(bf16[2,32,32,128]{3,2,1,0:T(8,128)(2,1)} %own_ref.1), channel_id=1, source_target_pairs={{0,32},{32,64},{64,96},{96,128},{128,160},{160,192},{192,224},{224... | collective-permute-start | bytes 1572872 | tf_op jit(solution)/shard_map/ppermute | solution.py:512
  5.2 26.6 %collective-permute-start.6 = (f32[8,128]{1,0:T(8,128)S(1)}, f32[8,128]{1,0:T(8,128)S(1)}, u32[]{:S(2)}, u32[]{:S(2)}) collective-permute-start(f32[8,128]{1,0:T(8,128)S(1)} %broadcast_in_dim.21), channel_id=1, source_target_pairs={{0,28},{1,29},{2,30},{3,31},{4,24},{5,25},{6,26},{7,27},{8,20},{9,... | collective-permute-start | bytes 12296 | tf_op jit(solution)/shard_map/ppermute | solution.py:507
  12.8 17.5 %collective-permute-start.2 = (bf16[2,32,32]{2,1,0:T(8,128)(2,1)S(1)}, bf16[2,32,32]{2,1,0:T(8,128)(2,1)S(1)}, u32[]{:S(2)}, u32[]{:S(2)}) collective-permute-start(bf16[2,32,32]{2,1,0:T(8,128)(2,1)S(1)} %bitcast.19), channel_id=1, source_target_pairs={{1,0},{2,1},{3,2},{4,3},{5,4},{6,5},{7,6},{8,7},{9,8},{10,9},{11,1... | collective-permute-start | bytes 12296 | tf_op jit(solution)/shard_map/ppermute | solution.py:551
  16.4 13.9 %collective-permute-start.1 = (bf16[2,32,32]{2,1,0:T(8,128)(2,1)S(1)}, bf16[2,32,32]{2,1,0:T(8,128)(2,1)S(1)}, u32[]{:S(2)}, u32[]{:S(2)}) collective-permute-start(bf16[2,32,32]{2,1,0:T(8,128)(2,1)S(1)} %bitcast.20), channel_id=1, source_target_pairs={{0,1},{1,2},{2,3},{3,4},{4,5},{5,6},{6,7},{7,8},{8,9},{9,10},{10,1... | collective-permute-start | bytes 12296 | tf_op jit(solution)/shard_map/ppermute | solution.py:550
  30.2 2.8 %collective-permute-start.4 = (bf16[2,2,32,32]{3,2,1,0:T(8,128)(2,1)S(1)}, bf16[2,2,32,32]{3,2,1,0:T(8,128)(2,1)S(1)}, u32[]{:S(2)}, u32[]{:S(2)}) collective-permute-start(bf16[2,2,32,32]{3,2,1,0:T(8,128)(2,1)S(1)} %pad_maximum_fusion.own_ref), channel_id=1, source_target_pairs={{32,0},{64,32},{96,64},{128,96},{160,128},{192,160},{224,192},{0,2... | collective-permute-start | bytes 24584 | tf_op jit(solution)/shard_map/ppermute | solution.py:513
  31.5 4.9 %collective-permute-start.3 = (bf16[2,2,32,32]{3,2,1,0:T(8,128)(2,1)S(1)}, bf16[2,2,32,32]{3,2,1,0:T(8,128)(2,1)S(1)}, u32[]{:S(2)}, u32[]{:S(2)}) collective-permute-start(bf16[2,2,32,32]{3,2,1,0:T(8,128)(2,1)S(1)} %pad_maximum_fusion.own_ref), channel_id=1, source_target_pairs={{0,32},{32,64},{64,96},{96,128},{128,160},{160,192},{192,224},{224... | collective-permute-start | bytes 24584 | tf_op jit(solution)/shard_map/ppermute | solution.py:512
  44.3 2.1 %collective-permute-start.7 = (f32[8,48,384]{2,1,0:T(8,128)S(1)}, f32[8,48,384]{2,1,0:T(8,128)S(1)}, u32[]{:S(2)}, u32[]{:S(2)}) collective-permute-start(f32[8,48,384]{2,1,0:T(8,128)S(1)} %get-tuple-element.26), channel_id=1, source_target_pairs={{0,1},{1,0},{2,3},{3,2},{4,5},{5,4},{6,7},{7,6},{8,9},{9,8},{10,11... | collective-permute-start | bytes 1769480 | tf_op jit(solution)/shard_map/ppermute | solution.py:507
  46.5 6.0 %collective-permute-start.8 = (f32[2,48,384]{2,1,0:T(8,128)S(1)}, f32[2,48,384]{2,1,0:T(8,128)S(1)}, u32[]{:S(2)}, u32[]{:S(2)}) collective-permute-start(f32[2,48,384]{2,1,0:T(8,128)S(1)} %get-tuple-element.33), channel_id=1, source_target_pairs={{0,4},{1,5},{2,6},{3,7},{4,0},{5,1},{6,2},{7,3},{8,12},{9,13},{10,... | collective-permute-start | bytes 442376 | tf_op jit(solution)/shard_map/ppermute | solution.py:507
  48.4 8.4 %collective-permute-start.10 = (f32[2,48,384]{2,1,0:T(8,128)S(1)}, f32[2,48,384]{2,1,0:T(8,128)S(1)}, u32[]{:S(2)}, u32[]{:S(2)}) collective-permute-start(f32[2,48,384]{2,1,0:T(8,128)S(1)} %get-tuple-element.34), channel_id=1, source_target_pairs={{0,6},{1,7},{2,4},{3,5},{4,2},{5,3},{6,0},{7,1},{8,14},{9,15},{10,... | collective-permute-start | bytes 442376 | tf_op jit(solution)/shard_map/ppermute | solution.py:507
  49.8 9.8 %collective-permute-start.9 = (f32[2,48,384]{2,1,0:T(8,128)S(1)}, f32[2,48,384]{2,1,0:T(8,128)S(1)}, u32[]{:S(2)}, u32[]{:S(2)}) collective-permute-start(f32[2,48,384]{2,1,0:T(8,128)S(1)} %get-tuple-element.35), channel_id=1, source_target_pairs={{0,2},{1,3},{2,0},{3,1},{4,6},{5,7},{6,4},{7,5},{8,10},{9,11},{10,... | collective-permute-start | bytes 442376 | tf_op jit(solution)/shard_map/ppermute | solution.py:507
  59.7 4.8 %collective-permute-start.11 = (f32[48,384]{1,0:T(8,128)S(1)}, f32[48,384]{1,0:T(8,128)S(1)}, u32[]{:S(2)}, u32[]{:S(2)}) collective-permute-start(f32[48,384]{1,0:T(8,128)S(1)} %slice_bitcast_fusion), channel_id=1, source_target_pairs={{0,8},{1,9},{2,10},{3,11},{4,12},{5,13},{6,14},{7,15},{8,0},{9,1},... | collective-permute-start | bytes 221192 | tf_op jit(solution)/shard_map/ppermute | solution.py:507
  64.6 8.0 %collective-permute-start.12 = (f32[48,384]{1,0:T(8,128)S(1)}, f32[48,384]{1,0:T(8,128)S(1)}, u32[]{:S(2)}, u32[]{:S(2)}) collective-permute-start(f32[48,384]{1,0:T(8,128)S(1)} %fusion.2.first_ref), channel_id=1, source_target_pairs={{0,28},{1,29},{2,30},{3,31},{4,24},{5,25},{6,26},{7,27},{8,20},{9,... | collective-permute-start | bytes 221192 | tf_op jit(solution)/shard_map/ppermute | solution.py:507
  76.5 3.4 %collective-permute-start.13 = (f32[1,8,128]{2,1,0:T(8,128)S(1)}, f32[1,8,128]{2,1,0:T(8,128)S(1)}, u32[]{:S(2)}, u32[]{:S(2)}) collective-permute-start(f32[1,8,128]{2,1,0:T(8,128)S(1)} %bitcast.15), channel_id=1, source_target_pairs={{0,8},{1,9},{2,10},{3,11},{4,12},{5,13},{6,14},{7,15},{8,0},{9,1},... | collective-permute-start | bytes 12296 | tf_op jit(solution)/shard_map/ppermute | solution.py:507
  79.9 2.5 %collective-permute-start.14 = (f32[2,8,128]{2,1,0:T(8,128)S(1)}, f32[2,8,128]{2,1,0:T(8,128)S(1)}, u32[]{:S(2)}, u32[]{:S(2)}) collective-permute-start(f32[2,8,128]{2,1,0:T(8,128)S(1)} %pad_maximum_fusion.3), channel_id=1, source_target_pairs={{0,4},{1,5},{2,6},{3,7},{4,0},{5,1},{6,2},{7,3},{8,12},{9,13},{10,... | collective-permute-start | bytes 24584 | tf_op jit(solution)/shard_map/ppermute | solution.py:507
  82.4 4.1 %collective-permute-start.15 = (f32[4,8,128]{2,1,0:T(8,128)S(1)}, f32[4,8,128]{2,1,0:T(8,128)S(1)}, u32[]{:S(2)}, u32[]{:S(2)}) collective-permute-start(f32[4,8,128]{2,1,0:T(8,128)S(1)} %pad_maximum_fusion.2), channel_id=1, source_target_pairs={{0,2},{1,3},{2,0},{3,1},{4,6},{5,7},{6,4},{7,5},{8,10},{9,11},{10,... | collective-permute-start | bytes 49160 | tf_op jit(solution)/shard_map/ppermute | solution.py:507
  86.5 7.1 %collective-permute-start.16 = (f32[8,8,128]{2,1,0:T(8,128)S(1)}, f32[8,8,128]{2,1,0:T(8,128)S(1)}, u32[]{:S(2)}, u32[]{:S(2)}) collective-permute-start(f32[8,8,128]{2,1,0:T(8,128)S(1)} %pad_maximum_fusion.1), channel_id=1, source_target_pairs={{0,1},{1,0},{2,3},{3,2},{4,5},{5,4},{6,7},{7,6},{8,9},{9,8},{10,11... | collective-permute-start | bytes 98312 | tf_op jit(solution)/shard_map/ppermute | solution.py:507
  94.8 2.6 %collective-permute-start.17 = (f32[2,8,128]{2,1,0:T(8,128)S(1)}, f32[2,8,128]{2,1,0:T(8,128)S(1)}, u32[]{:S(2)}, u32[]{:S(2)}) collective-permute-start(f32[2,8,128]{2,1,0:T(8,128)S(1)} %get-tuple-element.31), channel_id=1, source_target_pairs={{0,32},{32,0},{64,96},{96,64},{128,160},{160,128},{192,224},{224,1... | collective-permute-start | bytes 24584 | tf_op jit(solution)/shard_map/ppermute | solution.py:637
  94.9 4.7 %collective-permute-start.18 = (f32[2,8,128]{2,1,0:T(8,128)S(1)}, f32[2,8,128]{2,1,0:T(8,128)S(1)}, u32[]{:S(2)}, u32[]{:S(2)}) collective-permute-start(f32[2,8,128]{2,1,0:T(8,128)S(1)} %get-tuple-element.32), channel_id=1, source_target_pairs={{0,224},{32,64},{64,32},{96,128},{128,96},{160,192},{192,160},{224... | collective-permute-start | bytes 24584 | tf_op jit(solution)/shard_map/ppermute | solution.py:637

commit v8 on v6

--- a/solution.py
+++ b/solution.py
@@ -580,15 +580,6 @@
     part = part[:2] + moved[0] + moved[1] + moved[2]
     part = part[0] + swap(part[1], 8)
     other = swap(part, 28)
-    other, edges = lax.optimization_barrier((other, edges))
-    edges = pl.pallas_call(
-        edge_in_kernel,
-        out_shape=shape(2, SLOTS * SEL, LANES, dtype=BF16),
-        in_specs=[VMEM, VMEM],
-        out_specs=VMEM,
-        compiler_params=limit(8),
-        name="edges_in",
-    )(*edges)
     weights = pl.pallas_call(
         solve_kernel,
         out_shape=shape(8, LANES),
@@ -598,9 +589,21 @@
         compiler_params=limit(8),
         name="solve",
     )(part, other, marks)
+    weights, edges[1] = lax.optimization_barrier((weights, edges[1]))
+    edges = pl.pallas_call(
+        edge_in_kernel,
+        out_shape=shape(2, SLOTS * SEL, LANES, dtype=BF16),
+        in_specs=[VMEM, VMEM],
+        out_specs=VMEM,
+        compiler_params=limit(8),
+        name="edges_in",
+    )(*edges)
     weights = weights[None]
     for turn in (8, 4, 2, 1):
-        weights = jnp.concatenate([weights, swap(weights, turn)], 0)
+        moved = swap(weights, turn)
+        if turn == 2:
+            moved, edges, centres = lax.optimization_barrier((moved, edges, centres))
+        weights = jnp.concatenate([weights, moved], 0)
     rim = shape(2, 8, CELLS)
     power, *rims = pl.pallas_call(
         power_kernel,

time: 92.5 us -> 88.7 us (0.959)
  starting transfers between devices: 44.3 us -> 41.8 us
  waiting for transfers between devices: 27.5 us -> 26.4 us
    ppermute x11, starting transfers between devices: 27.7 us -> 25.1 us  [swap(): return lax.ppermute(value, 'rng', [(i, i ^ turn) for i in range(32)])]
    ppermute x2, waiting for transfers between devices: 2 us -> 0.84 us  [body(): lax.ppermute(value, 'rng', pairs)]
  transfers between devices with their start and end apart: 17 -> 17, of which waited for: 13 -> 12; matrix products, arithmetic and copies ran while one was open for 4% -> 4% of each run, Pallas kernels for 3% -> 7%
where the time goes in v8:
time: 88.7 us; the launch traced here: 88.1 us
  starting transfers between devices  41.8 us (47%)
  waiting for transfers between devices  26.4 us (30%)
  Pallas kernels  14.1 us (16%)
  local copies, waits for them, and re-layouts  3.87 us (4%)
  other arithmetic  1.83 us (2%)
    ppermute x11, starting transfers between devices, swap(): return lax.ppermute(value, 'rng', [(i, i ^ turn) for i in range(32)])  25.1 us
    ppermute x11, waiting for transfers between devices, swap(): return lax.ppermute(value, 'rng', [(i, i ^ turn) for i in range(32)])  14.1 us
    ppermute x2, starting transfers between devices, body(): lax.ppermute(value, 'rng', pairs)  8.54 us
    ppermute x1, waiting for transfers between devices, halo_columns(): high = lax.ppermute(echoes, 'az', [(b, a) for a, b in ring])  6.98 us
    pallas_call x1, Pallas kernels, body(): pl.pallas_call(gram_kernel, out_shape=(shape(OWN_BEAMS, 2, SLOTS * SEL, C...  5.79 us
    ppermute x1, starting transfers between devices, halo_columns(): high = lax.ppermute(echoes, 'az', [(b, a) for a, b in ring])  4.32 us
    pallas_call x1, Pallas kernels, body(): pl.pallas_call(solve_kernel, out_shape=shape(8, LANES), in_specs=[VMEM] *...  3.85 us
    ppermute x2, starting transfers between devices, body(): lax.ppermute(value, 'az', pairs)  3.76 us
  transfers between devices with their start and end apart: 17, of which 12 were waited for; matrix products, arithmetic and copies ran while one was open for 4% of the time, Pallas kernels for 7%

profile of v8, /device:TPU:1, one launch (start us, length us, event | category | flops | bytes accessed | tf_op | source)
XLA Modules:
  0.0 88.1 jit_solution(10102708287133420571)
XLA Ops:
  0.0 4.3 %collective-permute-start = (bf16[2,32,32,128]{3,2,1,0:T(8,128)(2,1)}, bf16[2,32,32,128]{3,2,1,0:T(8,128)(2,1)S(1)}, u32[]{:S(2)}, u32[]{:S(2)}) collective-permute-start(bf16[2,32,32,128]{3,2,1,0:T(8,128)(2,1)} %own_ref.1), channel_id=1, source_target_pairs={{32,0},{64,32},{96,64},{128,96},{160,128},{192,160},{224,192},{0,2... | collective-permute-start | bytes 1572872 | tf_op jit(solution)/shard_map/ppermute | solution.py:486
  4.3 0.7 convert_bitcast_fusion
  5.0 0.1 broadcast_in_dim.19
  5.1 5.6 %collective-permute-start.2 = (f32[8,128]{1,0:T(8,128)S(1)}, f32[8,128]{1,0:T(8,128)S(1)}, u32[]{:S(2)}, u32[]{:S(2)}) collective-permute-start(f32[8,128]{1,0:T(8,128)S(1)} %broadcast_in_dim.19), channel_id=1, source_target_pairs={{0,28},{1,29},{2,30},{3,31},{4,24},{5,25},{6,26},{7,27},{8,20},{9,... | collective-permute-start | bytes 12296 | tf_op jit(solution)/shard_map/ppermute | solution.py:480
  10.6 0.7 copy.14
  11.4 0.8 constant_dynamic-slice_fusion.1
  12.3 0.1 constant_dynamic-slice_fusion
  12.5 0.7 and_select_fusion
  13.2 0.1 pad_maximum_fusion.3.floats_ref
  13.4 0.1 pad_add_fusion.ints_ref
  13.5 1.0 %copy-done.1 = bf16[2,32,32,128]{3,2,1,0:T(8,128)(2,1)S(1)} copy-done((bf16[2,32,32,128]{3,2,1,0:T(8,128)(2,1)S(1)}, bf16[2,32,32,128]{3,2,1,0:T(8,128)(2,1)}, u32[]{:S(2)}) %copy-start.1) | copy-done | bytes 524312
  14.5 0.7 copy-done.2
  15.2 0.7 spectra.2
  15.9 0.1 broadcast_add_fusion.marks_ref
  16.0 7.0 %collective-permute-done.own_ref = bf16[2,32,32,128]{3,2,1,0:T(8,128)(2,1)S(1)} collective-permute-done((bf16[2,32,32,128]{3,2,1,0:T(8,128)(2,1)}, bf16[2,32,32,128]{3,2,1,0:T(8,128)(2,1)S(1)}, u32[]{:S(2)}, u32[]{:S(2)}) %collective-permute-start) | collective-permute-done | bytes 524320 | tf_op jit(solution)/shard_map/ppermute | solution.py:486
  23.0 0.7 spectra.3
  23.6 2.6 %collective-permute-done.1.low_ref = bf16[2,32,32,128]{3,2,1,0:T(8,128)(2,1)S(1)} collective-permute-done((bf16[2,32,32,128]{3,2,1,0:T(8,128)(2,1)}, bf16[2,32,32,128]{3,2,1,0:T(8,128)(2,1)S(1)}, u32[]{:S(2)}, u32[]{:S(2)}) %collective-permute-start.1) | collective-permute-done | bytes 524320 | tf_op jit(solution)/shard_map/ppermute | solution.py:485
  26.2 5.8 %grams.1 = (bf16[8,2,640,128]{3,2,1,0:T(8,128)(2,1)S(1)}, f32[8,48,384]{2,1,0:T(8,128)S(1)}, f32[8,48,384]{2,1,0:T(8,128)S(1)}, f32[8,128]{1,0:T(8,128)S(1)}) custom-call(s32[8,33]{1,0:T(8,128)S(1)} %pad_add_fusion.ints_ref, f32[8,32]{1,0:T(8,128)S(1)} %pad_maximum_fusion.3.floats_ref, bf16[64,64]{1,0:T(8,128)(2,1)S(1)} %get-tuple-element.31.table_ref, ...), custom_call_target="tpu_custom_call" | custom-call | tf_op jit(solution)/shard_map/grams/pallas_call | solution.py:544
  32.0 1.0 %collective-permute-start.3 = (f32[8,48,384]{2,1,0:T(8,128)S(1)}, f32[8,48,384]{2,1,0:T(8,128)S(1)}, u32[]{:S(2)}, u32[]{:S(2)}) collective-permute-start(f32[8,48,384]{2,1,0:T(8,128)S(1)} %get-tuple-element.35), channel_id=1, source_target_pairs={{0,1},{1,0},{2,3},{3,2},{4,5},{5,4},{6,7},{7,6},{8,9},{9,8},{10,11... | collective-permute-start | bytes 1769480 | tf_op jit(solution)/shard_map/ppermute | solution.py:480
  33.0 1.2 %edges_out.1 = (bf16[64,128]{1,0:T(8,128)(2,1)S(1)}, bf16[64,128]{1,0:T(8,128)(2,1)S(1)}) custom-call(bf16[8,2,640,128]{3,2,1,0:T(8,128)(2,1)S(1)} %get-tuple-element.36.snap_ref), custom_call_target="tpu_custom_call" | custom-call | tf_op jit(solution)/shard_map/edges_out/pallas_call | solution.py:564
  34.2 0.5 collective-permute-done.3
  34.7 0.1 add.48
  34.8 1.9 %collective-permute-start.4 = (f32[2,48,384]{2,1,0:T(8,128)S(1)}, f32[2,48,384]{2,1,0:T(8,128)S(1)}, u32[]{:S(2)}, u32[]{:S(2)}) collective-permute-start(f32[2,48,384]{2,1,0:T(8,128)S(1)} %get-tuple-element.57), channel_id=1, source_target_pairs={{0,4},{1,5},{2,6},{3,7},{4,0},{5,1},{6,2},{7,3},{8,12},{9,13},{10,... | collective-permute-start | bytes 442376 | tf_op jit(solution)/shard_map/ppermute | solution.py:480
  36.7 2.9 %collective-permute-start.5 = (f32[2,48,384]{2,1,0:T(8,128)S(1)}, f32[2,48,384]{2,1,0:T(8,128)S(1)}, u32[]{:S(2)}, u32[]{:S(2)}) collective-permute-start(f32[2,48,384]{2,1,0:T(8,128)S(1)} %get-tuple-element.56), channel_id=1, source_target_pairs={{0,2},{1,3},{2,0},{3,1},{4,6},{5,7},{6,4},{7,5},{8,10},{9,11},{10,... | collective-permute-start | bytes 442376 | tf_op jit(solution)/shard_map/ppermute | solution.py:480
  39.6 0.9 %collective-permute-start.7 = (bf16[64,128]{1,0:T(8,128)(2,1)S(1)}, bf16[64,128]{1,0:T(8,128)(2,1)S(1)}, u32[]{:S(2)}, u32[]{:S(2)}) collective-permute-start(bf16[64,128]{1,0:T(8,128)(2,1)S(1)} %get-tuple-element.40), channel_id=1, source_target_pairs={{0,1},{1,0},{2,3},{3,2},{4,5},{5,4},{6,7},{7,6},{8,9},{9,8},{10,11... | collective-permute-start | bytes 49160 | tf_op jit(solution)/shard_map/ppermute | solution.py:576
  40.5 0.8 collective-permute-done.7.first_ref
  41.4 4.0 %collective-permute-done.5 = f32[2,48,384]{2,1,0:T(8,128)S(1)} collective-permute-done((f32[2,48,384]{2,1,0:T(8,128)S(1)}, f32[2,48,384]{2,1,0:T(8,128)S(1)}, u32[]{:S(2)}, u32[]{:S(2)}) %collective-permute-start.5) | collective-permute-done | bytes 147488 | tf_op jit(solution)/shard_map/ppermute | solution.py:480
  45.3 1.1 %collective-permute-done.6 = f32[2,48,384]{2,1,0:T(8,128)S(1)} collective-permute-done((f32[2,48,384]{2,1,0:T(8,128)S(1)}, f32[2,48,384]{2,1,0:T(8,128)S(1)}, u32[]{:S(2)}, u32[]{:S(2)}) %collective-permute-start.6) | collective-permute-done | bytes 147488 | tf_op jit(solution)/shard_map/ppermute | solution.py:480
  46.5 3.1 %collective-permute-start.8 = (f32[48,384]{1,0:T(8,128)S(1)}, f32[48,384]{1,0:T(8,128)S(1)}, u32[]{:S(2)}, u32[]{:S(2)}) collective-permute-start(f32[48,384]{1,0:T(8,128)S(1)} %slice_bitcast_fusion), channel_id=1, source_target_pairs={{0,8},{1,9},{2,10},{3,11},{4,12},{5,13},{6,14},{7,15},{8,0},{9,1},... | collective-permute-start | bytes 221192 | tf_op jit(solution)/shard_map/ppermute | solution.py:480
  49.5 1.7 %collective-permute-done.8 = f32[48,384]{1,0:T(8,128)S(1)} collective-permute-done((f32[48,384]{1,0:T(8,128)S(1)}, f32[48,384]{1,0:T(8,128)S(1)}, u32[]{:S(2)}, u32[]{:S(2)}) %collective-permute-start.8) | collective-permute-done | bytes 73760 | tf_op jit(solution)/shard_map/ppermute | solution.py:480
  51.3 4.9 %collective-permute-start.9 = (f32[48,384]{1,0:T(8,128)S(1)}, f32[48,384]{1,0:T(8,128)S(1)}, u32[]{:S(2)}, u32[]{:S(2)}) collective-permute-start(f32[48,384]{1,0:T(8,128)S(1)} %fusion.2.first_ref), channel_id=1, source_target_pairs={{0,28},{1,29},{2,30},{3,31},{4,24},{5,25},{6,26},{7,27},{8,20},{9,... | collective-permute-start | bytes 221192 | tf_op jit(solution)/shard_map/ppermute | solution.py:480
  56.2 7.6 %collective-permute-start.10 = (bf16[64,128]{1,0:T(8,128)(2,1)S(1)}, bf16[64,128]{1,0:T(8,128)(2,1)S(1)}, u32[]{:S(2)}, u32[]{:S(2)}) collective-permute-start(bf16[64,128]{1,0:T(8,128)(2,1)S(1)} %get-tuple-element.45), channel_id=1, source_target_pairs={{1,2},{2,1},{3,4},{4,3},{5,6},{6,5},{7,8},{8,7},{9,10},{10,9},{11,... | collective-permute-start | bytes 49160 | tf_op jit(solution)/shard_map/ppermute | solution.py:576
  63.9 3.8 %solve.1 = f32[8,128]{1,0:T(8,128)S(1)} custom-call(f32[48,384]{1,0:T(8,128)S(1)} %fusion.2.first_ref, f32[48,384]{1,0:T(8,128)S(1)} %collective-permute-done.9.second_ref, f32[8,128]{1,0:T(8,128)S(1)} %get-tuple-element.44.marks_ref), custom_call_target="tpu_custom_call" | custom-call | tf_op jit(solution)/shard_map/solve/pallas_call | solution.py:583
  67.8 1.4 %collective-permute-start.11 = (f32[1,8,128]{2,1,0:T(8,128)S(1)}, f32[1,8,128]{2,1,0:T(8,128)S(1)}, u32[]{:S(2)}, u32[]{:S(2)}) collective-permute-start(f32[1,8,128]{2,1,0:T(8,128)S(1)} %bitcast.11), channel_id=1, source_target_pairs={{0,8},{1,9},{2,10},{3,11},{4,12},{5,13},{6,14},{7,15},{8,0},{9,1},... | collective-permute-start | bytes 12296 | tf_op jit(solution)/shard_map/ppermute | solution.py:480
  69.1 0.2 edges_in.1.edge_ref
  69.4 1.8 %collective-permute-done.11 = f32[1,8,128]{2,1,0:T(8,128)S(1)} collective-permute-done((f32[1,8,128]{2,1,0:T(8,128)S(1)}, f32[1,8,128]{2,1,0:T(8,128)S(1)}, u32[]{:S(2)}, u32[]{:S(2)}) %collective-permute-start.11) | collective-permute-done | bytes 4128 | tf_op jit(solution)/shard_map/ppermute | solution.py:480
  71.2 0.9 collective-permute-start.12
  72.1 1.6 %collective-permute-done.12 = f32[2,8,128]{2,1,0:T(8,128)S(1)} collective-permute-done((f32[2,8,128]{2,1,0:T(8,128)S(1)}, f32[2,8,128]{2,1,0:T(8,128)S(1)}, u32[]{:S(2)}, u32[]{:S(2)}) %collective-permute-start.12) | collective-permute-done | bytes 8224 | tf_op jit(solution)/shard_map/ppermute | solution.py:480
  73.7 1.5 %collective-permute-start.13 = (f32[4,8,128]{2,1,0:T(8,128)S(1)}, f32[4,8,128]{2,1,0:T(8,128)S(1)}, u32[]{:S(2)}, u32[]{:S(2)}) collective-permute-start(f32[4,8,128]{2,1,0:T(8,128)S(1)} %pad_maximum_fusion.1), channel_id=1, source_target_pairs={{0,2},{1,3},{2,0},{3,1},{4,6},{5,7},{6,4},{7,5},{8,10},{9,11},{10,... | collective-permute-start | bytes 49160 | tf_op jit(solution)/shard_map/ppermute | solution.py:480
  75.2 2.6 %collective-permute-done.13 = f32[4,8,128]{2,1,0:T(8,128)S(1)} collective-permute-done((f32[4,8,128]{2,1,0:T(8,128)S(1)}, f32[4,8,128]{2,1,0:T(8,128)S(1)}, u32[]{:S(2)}, u32[]{:S(2)}) %collective-permute-start.13) | collective-permute-done | bytes 16416 | tf_op jit(solution)/shard_map/ppermute | solution.py:480
  77.8 0.1 broadcast_in_dim.22.bins_ref
  77.9 2.0 %collective-permute-start.14 = (f32[8,8,128]{2,1,0:T(8,128)S(1)}, f32[8,8,128]{2,1,0:T(8,128)S(1)}, u32[]{:S(2)}, u32[]{:S(2)}) collective-permute-start(f32[8,8,128]{2,1,0:T(8,128)S(1)} %pad_maximum_fusion), channel_id=1, source_target_pairs={{0,1},{1,0},{2,3},{3,2},{4,5},{5,4},{6,7},{7,6},{8,9},{9,8},{10,11... | collective-permute-start | bytes 98312 | tf_op jit(solution)/shard_map/ppermute | solution.py:480
  79.9 0.9 collective-permute-done.14
  80.8 1.1 %power.1 = (f32[16,8,128]{2,1,0:T(8,128)S(1)}, f32[2,8,128]{2,1,0:T(8,128)S(1)}, f32[2,8,128]{2,1,0:T(8,128)S(1)}) custom-call(s32[16,8,128]{2,1,0:T(8,128)S(1)} %broadcast_in_dim.22.bins_ref, f32[16,8,128]{2,1,0:T(8,128)S(1)} %constant_dynamic-update-slice_fusion.weights_ref, bf16[8,2,640,128]{3,2,1,0:T(8,128)(2,1)S(1)} %get-tuple-element.36.snap_ref, ...), custom_call_target="tpu_custom_call" | custom-call | tf_op jit(solution)/shard_map/power/pallas_call | solution.py:608
  81.9 0.9 %collective-permute-start.15 = (f32[2,8,128]{2,1,0:T(8,128)S(1)}, f32[2,8,128]{2,1,0:T(8,128)S(1)}, u32[]{:S(2)}, u32[]{:S(2)}) collective-permute-start(f32[2,8,128]{2,1,0:T(8,128)S(1)} %get-tuple-element.53), channel_id=1, source_target_pairs={{0,32},{32,0},{64,96},{96,64},{128,160},{160,128},{192,224},{224,1... | collective-permute-start | bytes 24584 | tf_op jit(solution)/shard_map/ppermute | solution.py:617
  82.9 2.8 %collective-permute-start.16 = (f32[2,8,128]{2,1,0:T(8,128)S(1)}, f32[2,8,128]{2,1,0:T(8,128)S(1)}, u32[]{:S(2)}, u32[]{:S(2)}) collective-permute-start(f32[2,8,128]{2,1,0:T(8,128)S(1)} %get-tuple-element.54), channel_id=1, source_target_pairs={{0,224},{32,64},{64,32},{96,128},{128,96},{160,192},{192,160},{224... | collective-permute-start | bytes 24584 | tf_op jit(solution)/shard_map/ppermute | solution.py:617
  85.7 1.8 %collective-permute-done.16.second_ref = f32[2,8,128]{2,1,0:T(8,128)S(1)} collective-permute-done((f32[2,8,128]{2,1,0:T(8,128)S(1)}, f32[2,8,128]{2,1,0:T(8,128)S(1)}, u32[]{:S(2)}, u32[]{:S(2)}) %collective-permute-start.16) | collective-permute-done | bytes 8224 | tf_op jit(solution)/shard_map/ppermute | solution.py:617
  87.5 0.6 smooth.1
  (29 shorter events, 0.5 us)
Async XLA Ops:
  0.0 12.3 %copy-start = (f32[64,16]{0,1:T(8,128)S(1)}, f32[64,16]{0,1:T(8,128)}, u32[]{:S(2)}) copy-start(f32[64,16]{0,1:T(8,128)} %param.11) | copy-start | bytes 12292
  0.0 22.9 %collective-permute-start = (bf16[2,32,32,128]{3,2,1,0:T(8,128)(2,1)}, bf16[2,32,32,128]{3,2,1,0:T(8,128)(2,1)S(1)}, u32[]{:S(2)}, u32[]{:S(2)}) collective-permute-start(bf16[2,32,32,128]{3,2,1,0:T(8,128)(2,1)} %own_ref.1), channel_id=1, source_target_pairs={{32,0},{64,32},{96,64},{128,96},{160,128},{192,160},{224,192},{0,2... | collective-permute-start | bytes 1572872 | tf_op jit(solution)/shard_map/ppermute | solution.py:486
  4.3 21.9 %collective-permute-start.1 = (bf16[2,32,32,128]{3,2,1,0:T(8,128)(2,1)}, bf16[2,32,32,128]{3,2,1,0:T(8,128)(2,1)S(1)}, u32[]{:S(2)}, u32[]{:S(2)}) collective-permute-start(bf16[2,32,32,128]{3,2,1,0:T(8,128)(2,1)} %own_ref.1), channel_id=1, source_target_pairs={{0,32},{32,64},{64,96},{96,128},{128,160},{160,192},{192,224},{224... | collective-permute-start | bytes 1572872 | tf_op jit(solution)/shard_map/ppermute | solution.py:485
  5.1 10.8 %collective-permute-start.2 = (f32[8,128]{1,0:T(8,128)S(1)}, f32[8,128]{1,0:T(8,128)S(1)}, u32[]{:S(2)}, u32[]{:S(2)}) collective-permute-start(f32[8,128]{1,0:T(8,128)S(1)} %broadcast_in_dim.19), channel_id=1, source_target_pairs={{0,28},{1,29},{2,30},{3,31},{4,24},{5,25},{6,26},{7,27},{8,20},{9,... | collective-permute-start | bytes 12296 | tf_op jit(solution)/shard_map/ppermute | solution.py:480
  13.5 1.0 %copy-start.1 = (bf16[2,32,32,128]{3,2,1,0:T(8,128)(2,1)S(1)}, bf16[2,32,32,128]{3,2,1,0:T(8,128)(2,1)}, u32[]{:S(2)}) copy-start(bf16[2,32,32,128]{3,2,1,0:T(8,128)(2,1)} %own_ref.1) | copy-start | bytes 1572868
  14.5 0.7 copy-start.2
  32.0 2.6 %collective-permute-start.3 = (f32[8,48,384]{2,1,0:T(8,128)S(1)}, f32[8,48,384]{2,1,0:T(8,128)S(1)}, u32[]{:S(2)}, u32[]{:S(2)}) collective-permute-start(f32[8,48,384]{2,1,0:T(8,128)S(1)} %get-tuple-element.35), channel_id=1, source_target_pairs={{0,1},{1,0},{2,3},{3,2},{4,5},{5,4},{6,7},{7,6},{8,9},{9,8},{10,11... | collective-permute-start | bytes 1769480 | tf_op jit(solution)/shard_map/ppermute | solution.py:480
  34.8 6.6 %collective-permute-start.4 = (f32[2,48,384]{2,1,0:T(8,128)S(1)}, f32[2,48,384]{2,1,0:T(8,128)S(1)}, u32[]{:S(2)}, u32[]{:S(2)}) collective-permute-start(f32[2,48,384]{2,1,0:T(8,128)S(1)} %get-tuple-element.57), channel_id=1, source_target_pairs={{0,4},{1,5},{2,6},{3,7},{4,0},{5,1},{6,2},{7,3},{8,12},{9,13},{10,... | collective-permute-start | bytes 442376 | tf_op jit(solution)/shard_map/ppermute | solution.py:480
  36.7 8.7 %collective-permute-start.5 = (f32[2,48,384]{2,1,0:T(8,128)S(1)}, f32[2,48,384]{2,1,0:T(8,128)S(1)}, u32[]{:S(2)}, u32[]{:S(2)}) collective-permute-start(f32[2,48,384]{2,1,0:T(8,128)S(1)} %get-tuple-element.56), channel_id=1, source_target_pairs={{0,2},{1,3},{2,0},{3,1},{4,6},{5,7},{6,4},{7,5},{8,10},{9,11},{10,... | collective-permute-start | bytes 442376 | tf_op jit(solution)/shard_map/ppermute | solution.py:480
  39.6 6.8 %collective-permute-start.6 = (f32[2,48,384]{2,1,0:T(8,128)S(1)}, f32[2,48,384]{2,1,0:T(8,128)S(1)}, u32[]{:S(2)}, u32[]{:S(2)}) collective-permute-start(f32[2,48,384]{2,1,0:T(8,128)S(1)} %get-tuple-element.55), channel_id=1, source_target_pairs={{0,6},{1,7},{2,4},{3,5},{4,2},{5,3},{6,0},{7,1},{8,14},{9,15},{10,... | collective-permute-start | bytes 442376 | tf_op jit(solution)/shard_map/ppermute | solution.py:480
  39.6 1.8 %collective-permute-start.7 = (bf16[64,128]{1,0:T(8,128)(2,1)S(1)}, bf16[64,128]{1,0:T(8,128)(2,1)S(1)}, u32[]{:S(2)}, u32[]{:S(2)}) collective-permute-start(bf16[64,128]{1,0:T(8,128)(2,1)S(1)} %get-tuple-element.40), channel_id=1, source_target_pairs={{0,1},{1,0},{2,3},{3,2},{4,5},{5,4},{6,7},{7,6},{8,9},{9,8},{10,11... | collective-permute-start | bytes 49160 | tf_op jit(solution)/shard_map/ppermute | solution.py:576
  46.5 4.8 %collective-permute-start.8 = (f32[48,384]{1,0:T(8,128)S(1)}, f32[48,384]{1,0:T(8,128)S(1)}, u32[]{:S(2)}, u32[]{:S(2)}) collective-permute-start(f32[48,384]{1,0:T(8,128)S(1)} %slice_bitcast_fusion), channel_id=1, source_target_pairs={{0,8},{1,9},{2,10},{3,11},{4,12},{5,13},{6,14},{7,15},{8,0},{9,1},... | collective-permute-start | bytes 221192 | tf_op jit(solution)/shard_map/ppermute | solution.py:480
  51.3 12.6 %collective-permute-start.9 = (f32[48,384]{1,0:T(8,128)S(1)}, f32[48,384]{1,0:T(8,128)S(1)}, u32[]{:S(2)}, u32[]{:S(2)}) collective-permute-start(f32[48,384]{1,0:T(8,128)S(1)} %fusion.2.first_ref), channel_id=1, source_target_pairs={{0,28},{1,29},{2,30},{3,31},{4,24},{5,25},{6,26},{7,27},{8,20},{9,... | collective-permute-start | bytes 221192 | tf_op jit(solution)/shard_map/ppermute | solution.py:480
  56.2 11.5 %collective-permute-start.10 = (bf16[64,128]{1,0:T(8,128)(2,1)S(1)}, bf16[64,128]{1,0:T(8,128)(2,1)S(1)}, u32[]{:S(2)}, u32[]{:S(2)}) collective-permute-start(bf16[64,128]{1,0:T(8,128)(2,1)S(1)} %get-tuple-element.45), channel_id=1, source_target_pairs={{1,2},{2,1},{3,4},{4,3},{5,6},{6,5},{7,8},{8,7},{9,10},{10,9},{11,... | collective-permute-start | bytes 49160 | tf_op jit(solution)/shard_map/ppermute | solution.py:576
  67.8 3.4 %collective-permute-start.11 = (f32[1,8,128]{2,1,0:T(8,128)S(1)}, f32[1,8,128]{2,1,0:T(8,128)S(1)}, u32[]{:S(2)}, u32[]{:S(2)}) collective-permute-start(f32[1,8,128]{2,1,0:T(8,128)S(1)} %bitcast.11), channel_id=1, source_target_pairs={{0,8},{1,9},{2,10},{3,11},{4,12},{5,13},{6,14},{7,15},{8,0},{9,1},... | collective-permute-start | bytes 12296 | tf_op jit(solution)/shard_map/ppermute | solution.py:480
  71.2 2.5 %collective-permute-start.12 = (f32[2,8,128]{2,1,0:T(8,128)S(1)}, f32[2,8,128]{2,1,0:T(8,128)S(1)}, u32[]{:S(2)}, u32[]{:S(2)}) collective-permute-start(f32[2,8,128]{2,1,0:T(8,128)S(1)} %pad_maximum_fusion.2), channel_id=1, source_target_pairs={{0,4},{1,5},{2,6},{3,7},{4,0},{5,1},{6,2},{7,3},{8,12},{9,13},{10,... | collective-permute-start | bytes 24584 | tf_op jit(solution)/shard_map/ppermute | solution.py:480
  73.7 4.1 %collective-permute-start.13 = (f32[4,8,128]{2,1,0:T(8,128)S(1)}, f32[4,8,128]{2,1,0:T(8,128)S(1)}, u32[]{:S(2)}, u32[]{:S(2)}) collective-permute-start(f32[4,8,128]{2,1,0:T(8,128)S(1)} %pad_maximum_fusion.1), channel_id=1, source_target_pairs={{0,2},{1,3},{2,0},{3,1},{4,6},{5,7},{6,4},{7,5},{8,10},{9,11},{10,... | collective-permute-start | bytes 49160 | tf_op jit(solution)/shard_map/ppermute | solution.py:480
  77.9 2.9 %collective-permute-start.14 = (f32[8,8,128]{2,1,0:T(8,128)S(1)}, f32[8,8,128]{2,1,0:T(8,128)S(1)}, u32[]{:S(2)}, u32[]{:S(2)}) collective-permute-start(f32[8,8,128]{2,1,0:T(8,128)S(1)} %pad_maximum_fusion), channel_id=1, source_target_pairs={{0,1},{1,0},{2,3},{3,2},{4,5},{5,4},{6,7},{7,6},{8,9},{9,8},{10,11... | collective-permute-start | bytes 98312 | tf_op jit(solution)/shard_map/ppermute | solution.py:480
  81.9 3.8 %collective-permute-start.15 = (f32[2,8,128]{2,1,0:T(8,128)S(1)}, f32[2,8,128]{2,1,0:T(8,128)S(1)}, u32[]{:S(2)}, u32[]{:S(2)}) collective-permute-start(f32[2,8,128]{2,1,0:T(8,128)S(1)} %get-tuple-element.53), channel_id=1, source_target_pairs={{0,32},{32,0},{64,96},{96,64},{128,160},{160,128},{192,224},{224,1... | collective-permute-start | bytes 24584 | tf_op jit(solution)/shard_map/ppermute | solution.py:617
  82.9 4.6 %collective-permute-start.16 = (f32[2,8,128]{2,1,0:T(8,128)S(1)}, f32[2,8,128]{2,1,0:T(8,128)S(1)}, u32[]{:S(2)}, u32[]{:S(2)}) collective-permute-start(f32[2,8,128]{2,1,0:T(8,128)S(1)} %get-tuple-element.54), channel_id=1, source_target_pairs={{0,224},{32,64},{64,32},{96,128},{128,96},{160,192},{192,160},{224... | collective-permute-start | bytes 24584 | tf_op jit(solution)/shard_map/ppermute | solution.py:617

commit v9 on v8

--- a/solution.py
+++ b/solution.py
@@ -76,13 +76,16 @@
     lax.fori_loop(0, OWN_COLS // 8, step, 0)
 
 
-def gram_kernel(
+def first_group(step):
+    return exclusive(exclusive(2 * step, 8), own_group())
+
+
+def send_kernel(
     ints_ref, floats_ref,
     table_ref, low_ref, own_ref, high_ref, marks_ref,
-    snap_ref, keep_ref, send_ref, passed_ref,
-    spec_ref, wide_ref, even_ref, odd_ref,
+    snap_ref, send_ref, passed_ref, spec_ref,
+    wide_ref, even_ref, odd_ref,
 ):
-    mine = own_group()
     table = table_ref[...]
     passed_ref[...] = marks_ref[...]
 
@@ -91,15 +94,29 @@
         for column in (2 * pair, 2 * pair + 1):
             spec_ref[OWN_COLS + column] = own_ref[column]
             spec_ref[2 * OWN_COLS + column] = high_ref[column]
-
+    four_beams(
+        0, ints_ref, floats_ref, spec_ref, snap_ref, send_ref, wide_ref, even_ref, odd_ref
+    )
+
+
+def keep_kernel(
+    ints_ref, floats_ref, spec_ref,
+    snap_ref, keep_ref,
+    wide_ref, even_ref, odd_ref,
+):
+    four_beams(
+        4, ints_ref, floats_ref, spec_ref, snap_ref, keep_ref, wide_ref, even_ref, odd_ref
+    )
+
+
+def four_beams(
+    start, ints_ref, floats_ref, spec_ref, snap_ref, out_ref, wide_ref, even_ref, odd_ref
+):
     lane = lane_ids(DOF)
     row = lax.broadcasted_iota(jnp.int32, (DOF, LANES), 0)
     lower = row >= lane - jnp.where(lane < DOF, 0, DOF)
     blank = jnp.zeros((LANES - 2 * DOF, 2 * CELLS), BF16)
     last = PULSES * SEL
-
-    def first_group(step):
-        return exclusive(exclusive(2 * step, 8), mine)
 
     def turn(step, work_ref):
         beam = lax.div(first_group(step), 2)
@@ -123,14 +140,14 @@
             ):
                 value = wide_ref[part, low:high, :].astype(BF16)
                 work_ref[part, place : place + high - low, :] = value
-                snap_ref[beam, part, place : place + high - low, :] = value
+                snap_ref[step - start, part, place : place + high - low, :] = value
                 if place in (SEL, SEL + last // 2):
                     yield
-            snap_ref[beam, part, last + 2 * SEL :, :] = jnp.zeros(
+            snap_ref[step - start, part, last + 2 * SEL :, :] = jnp.zeros(
                 (SLOTS * SEL - last - 2 * SEL, CELLS), BF16
             )
 
-    def multiply(step, work_ref, out_ref):
+    def multiply(step, work_ref):
         group = first_group(step)
         beam = lax.div(group, 2)
         weight = ints_ref[beam, 2 * SEL].astype(F32)
@@ -170,7 +187,7 @@
                 else:
                     out[2] = jnp.where(lane >= 32, packed, out[2])
                 yield
-            place = lax.rem(2 * step, 8) + half
+            place = 2 * step % 8 + half
             for part in range(3):
                 out_ref[place, :, LANES * part : LANES * (part + 1)] = (
                     out[part] * weight
@@ -180,33 +197,30 @@
         for _ in itertools.zip_longest(*works):
             pass
 
-    def sending(index, carry):
-        run(turn(2 * index + 1, odd_ref), multiply(2 * index, even_ref, send_ref))
-        run(turn(2 * index + 2, even_ref), multiply(2 * index + 1, odd_ref, send_ref))
-        return carry
-
-    run(turn(0, even_ref))
-    lax.fori_loop(0, 2, sending, 0)
-    run(turn(5, odd_ref), multiply(4, even_ref, keep_ref))
-    run(turn(6, even_ref), multiply(5, odd_ref, keep_ref))
-    run(turn(7, odd_ref), multiply(6, even_ref, keep_ref))
-    run(multiply(7, odd_ref, keep_ref))
-
-
-def edge_out_kernel(snap_ref, first_ref, second_ref):
+    works = (even_ref, odd_ref)
+    run(turn(start, even_ref))
+    for step in range(start, start + 3):
+        run(
+            turn(step + 1, works[(step + 1) % 2]), multiply(step, works[step % 2])
+        )
+    run(multiply(start + 3, odd_ref))
+
+
+def edge_out_kernel(sent_ref, kept_ref, first_ref, second_ref):
     rows = 8 * 8
     lane = lane_ids(rows)
     ends = [jnp.zeros((rows, LANES), F32) for _ in range(2)]
-    for beam in range(OWN_BEAMS):
+    for step in range(OWN_BEAMS):
+        snap_ref = sent_ref if step < 4 else kept_ref
+        beam = lax.div(first_group(step), 2)
         for part in range(2):
             for block in range(8):
                 low = SEL + rows * block
-                value = snap_ref[beam, part, low : low + rows, :].astype(F32)
+                value = snap_ref[step % 4, part, low : low + rows, :].astype(F32)
                 target = 16 * block + 8 * part + beam
                 here = lane == target
                 for end in range(2):
-                    shift = (target + end) % LANES
-                    moved = pltpu.roll(value, shift, 1) if shift else value
+                    moved = pltpu.roll(value, lax.rem(target + end, LANES), 1)
                     ends[end] = jnp.where(here, moved, ends[end])
     even = lax.rem(lax.axis_index("rng"), 2) == 0
     first_ref[...] = jnp.where(even, ends[1], ends[0]).astype(BF16)
@@ -405,8 +419,9 @@
 
 
 def power_kernel(
-    bins_ref, weights_ref, snap_ref, edge_ref,
+    bins_ref, weights_ref, sent_ref, kept_ref, edge_ref,
     power_ref, first_ref, second_ref,
+    count_ref,
 ):
     mine = own_group()
     even = lax.rem(lax.axis_index("rng"), 2) == 0
@@ -414,14 +429,17 @@
     counts = jnp.zeros((8, LANES), F32)
     for place in range(GROUPS):
         counts = counts + weights_ref[place]
-    counts = spread(counts, 120) * BLK
+    count_ref[...] = spread(counts, 120) * BLK
     low_lane = jnp.where(even, 16, 0)
     rows = SLOTS * SEL
     edge = edge_ref[...].reshape(2 * rows, LANES)
-    for beam in range(OWN_BEAMS):
+    for step in range(OWN_BEAMS):
+        snap_ref = sent_ref if step < 4 else kept_ref
+        beam = lax.div(first_group(step), 2)
+        count = jnp.broadcast_to(count_ref[pl.ds(beam, 1), :], (8, LANES))
         lefts, quiets = [], []
         for group in (2 * beam, 2 * beam + 1):
-            scaled = weights_ref[exclusive(mine, group)] * counts[beam : beam + 1, :]
+            scaled = weights_ref[exclusive(mine, group)] * count
             quiets.append(spread(scaled, 56))
             away = small - bins_ref[group] * SEL
             left = [[], []]
@@ -439,7 +457,7 @@
                 left[0].append(jnp.concatenate([direct, -crossed], 0).astype(BF16))
                 left[1].append(jnp.concatenate([crossed, direct], 0).astype(BF16))
             lefts.append(jnp.concatenate(left[0] + left[1], 1))
-        right = jnp.concatenate([snap_ref[beam].reshape(2 * rows, LANES), edge], 1)
+        right = jnp.concatenate([snap_ref[step % 4].reshape(2 * rows, LANES), edge], 1)
         found = jnp.dot(
             jnp.concatenate(lefts, 0), right, preferred_element_type=F32
         )
@@ -541,36 +559,48 @@
     spec, table = transform(jnp.asarray(table_array()), echoes)
     high, table = transform(table, high)
     half = shape(8, DOF, 8 * DOF)
-    snaps, keep, send, marks = pl.pallas_call(
-        gram_kernel,
+    some = shape(OWN_BEAMS // 2, 2, SLOTS * SEL, CELLS, dtype=BF16)
+    scratch = [
+        pltpu.VMEM((2, (PULSES + 1) * SEL, CELLS), F32),
+        pltpu.VMEM((2, (PULSES + 2) * SEL, CELLS), BF16),
+        pltpu.VMEM((2, (PULSES + 2) * SEL, CELLS), BF16),
+    ]
+    sent, send, marks, spectrum = pl.pallas_call(
+        send_kernel,
         out_shape=(
-            shape(OWN_BEAMS, 2, SLOTS * SEL, CELLS, dtype=BF16),
-            half,
+            some,
             half,
             shape(OWN_BEAMS, LANES),
+            shape(3 * OWN_COLS, 2 * PULSES, CELLS),
         ),
         in_specs=[SMEM] * 2 + [VMEM] * 5,
         out_specs=(VMEM,) * 4,
-        scratch_shapes=[
-            pltpu.VMEM((3 * OWN_COLS, 2 * PULSES, CELLS), F32),
-            pltpu.VMEM((2, (PULSES + 1) * SEL, CELLS), F32),
-            pltpu.VMEM((2, (PULSES + 2) * SEL, CELLS), BF16),
-            pltpu.VMEM((2, (PULSES + 2) * SEL, CELLS), BF16),
-        ],
+        scratch_shapes=scratch,
         compiler_params=limit(16),
-        name="grams",
+        name="grams_sent",
     )(ints, floats, table, low, spec, high, marks)
+    moved = swap(send, 1)
+    kept, keep = pl.pallas_call(
+        keep_kernel,
+        out_shape=(some, half),
+        in_specs=[SMEM] * 2 + [VMEM],
+        out_specs=(VMEM,) * 2,
+        scratch_shapes=scratch,
+        compiler_params=limit(16),
+        name="grams_kept",
+    )(ints, floats, spectrum)
+    moved, keep, kept = lax.optimization_barrier((moved, keep, kept))
+    part = keep + moved
+    part, kept = lax.optimization_barrier((part, kept))
     edge = shape(64, LANES, dtype=BF16)
     edges = pl.pallas_call(
         edge_out_kernel,
         out_shape=(edge, edge),
-        in_specs=[VMEM],
+        in_specs=[VMEM, VMEM],
         out_specs=(VMEM, VMEM),
         compiler_params=limit(8),
         name="edges_out",
-    )(snaps)
-    moved, edges = lax.optimization_barrier((swap(send, 1), edges))
-    part = keep + moved
+    )(sent, kept)
     moved = [swap(part[2:4], 4), swap(part[4:6], 2), swap(part[6:], 6)]
     edges = [
         lax.ppermute(value, "rng", pairs)
@@ -608,11 +638,12 @@
     power, *rims = pl.pallas_call(
         power_kernel,
         out_shape=(shape(GROUPS, 8, CELLS), rim, rim),
-        in_specs=[VMEM] * 4,
+        in_specs=[VMEM] * 5,
         out_specs=(VMEM,) * 3,
+        scratch_shapes=[pltpu.VMEM((8, LANES), F32)],
         compiler_params=limit(12),
         name="power",
-    )(centres, weights, snaps, edges)
+    )(centres, weights, sent, kept, edges)
     rims = [
         lax.ppermute(value, "az", pairs)
         for value, pairs in zip(rims, neighbours(8, True))

time: 88.7 us -> 87.6 us (0.988)
  waiting for transfers between devices: 26.4 us -> 25.4 us
    ppermute x11, waiting for transfers between devices: 14.1 us -> 13.2 us  [swap(): return lax.ppermute(value, 'rng', [(i, i ^ turn) for i in range(32)])]
    pallas_call x2 -> x3, Pallas kernels: 6.95 us -> 7.45 us  [the longest x1 3.3 us: body(): pl.pallas_call(send_kernel, out_shape=(some, half, shape(OWN_BEAMS, LANES...]
  transfers between devices with their start and end apart: 17 -> 17, of which waited for: 12 -> 11; matrix products, arithmetic and copies ran while one was open for 4% -> 4% of each run, Pallas kernels for 7% -> 11%
where the time goes in v9:
time: 87.6 us; the launch traced here: 87 us
  starting transfers between devices  41.1 us (47%)
  waiting for transfers between devices  25.4 us (29%)
  Pallas kernels  14.7 us (17%)
  local copies, waits for them, and re-layouts  3.87 us (4%)
  other arithmetic  1.81 us (2%)
    ppermute x11, starting transfers between devices, swap(): return lax.ppermute(value, 'rng', [(i, i ^ turn) for i in range(32)])  25.1 us
    ppermute x11, waiting for transfers between devices, swap(): return lax.ppermute(value, 'rng', [(i, i ^ turn) for i in range(32)])  13.2 us
    ppermute x2, starting transfers between devices, body(): lax.ppermute(value, 'rng', pairs)  7.88 us
    ppermute x1, waiting for transfers between devices, halo_columns(): high = lax.ppermute(echoes, 'az', [(b, a) for a, b in ring])  6.98 us
    ppermute x1, starting transfers between devices, halo_columns(): high = lax.ppermute(echoes, 'az', [(b, a) for a, b in ring])  4.32 us
    pallas_call x1, Pallas kernels, body(): pl.pallas_call(solve_kernel, out_shape=shape(8, LANES), in_specs=[VMEM] *...  3.85 us
    ppermute x2, starting transfers between devices, body(): lax.ppermute(value, 'az', pairs)  3.76 us
    pallas_call x1, Pallas kernels, body(): pl.pallas_call(send_kernel, out_shape=(some, half, shape(OWN_BEAMS, LANES...  3.3 us
  transfers between devices with their start and end apart: 17, of which 11 were waited for; matrix products, arithmetic and copies ran while one was open for 4% of the time, Pallas kernels for 11%

profile of v9, /device:TPU:1, one launch (start us, length us, event | category | flops | bytes accessed | tf_op | source)
XLA Modules:
  0.0 87.0 jit_solution(11398856114484896180)
XLA Ops:
  0.0 4.3 %collective-permute-start = (bf16[2,32,32,128]{3,2,1,0:T(8,128)(2,1)}, bf16[2,32,32,128]{3,2,1,0:T(8,128)(2,1)S(1)}, u32[]{:S(2)}, u32[]{:S(2)}) collective-permute-start(bf16[2,32,32,128]{3,2,1,0:T(8,128)(2,1)} %own_ref.1), channel_id=1, source_target_pairs={{32,0},{64,32},{96,64},{128,96},{160,128},{192,160},{224,192},{0,2... | collective-permute-start | bytes 1572872 | tf_op jit(solution)/shard_map/ppermute | solution.py:504
  4.3 0.7 convert_bitcast_fusion
  5.0 0.1 broadcast_in_dim.19
  5.1 5.6 %collective-permute-start.2 = (f32[8,128]{1,0:T(8,128)S(1)}, f32[8,128]{1,0:T(8,128)S(1)}, u32[]{:S(2)}, u32[]{:S(2)}) collective-permute-start(f32[8,128]{1,0:T(8,128)S(1)} %broadcast_in_dim.19), channel_id=1, source_target_pairs={{0,28},{1,29},{2,30},{3,31},{4,24},{5,25},{6,26},{7,27},{8,20},{9,... | collective-permute-start | bytes 12296 | tf_op jit(solution)/shard_map/ppermute | solution.py:498
  10.6 0.7 copy.14
  11.4 0.8 constant_dynamic-slice_fusion.1
  12.3 0.1 constant_dynamic-slice_fusion
  12.4 0.1 copy.18
  12.5 0.7 and_select_fusion
  13.2 0.1 pad_maximum_fusion.3.floats_ref
  13.4 0.1 pad_add_fusion.ints_ref
  13.5 1.0 %copy-done.1 = bf16[2,32,32,128]{3,2,1,0:T(8,128)(2,1)S(1)} copy-done((bf16[2,32,32,128]{3,2,1,0:T(8,128)(2,1)S(1)}, bf16[2,32,32,128]{3,2,1,0:T(8,128)(2,1)}, u32[]{:S(2)}) %copy-start.1) | copy-done | bytes 524312
  14.5 0.7 copy-done.2
  15.2 0.7 spectra.2
  15.9 0.1 broadcast_add_fusion.marks_ref
  16.0 7.0 %collective-permute-done.own_ref = bf16[2,32,32,128]{3,2,1,0:T(8,128)(2,1)S(1)} collective-permute-done((bf16[2,32,32,128]{3,2,1,0:T(8,128)(2,1)}, bf16[2,32,32,128]{3,2,1,0:T(8,128)(2,1)S(1)}, u32[]{:S(2)}, u32[]{:S(2)}) %collective-permute-start) | collective-permute-done | bytes 524320 | tf_op jit(solution)/shard_map/ppermute | solution.py:504
  23.0 0.7 spectra.3
  23.6 2.6 %collective-permute-done.1.low_ref = bf16[2,32,32,128]{3,2,1,0:T(8,128)(2,1)S(1)} collective-permute-done((bf16[2,32,32,128]{3,2,1,0:T(8,128)(2,1)}, bf16[2,32,32,128]{3,2,1,0:T(8,128)(2,1)S(1)}, u32[]{:S(2)}, u32[]{:S(2)}) %collective-permute-start.1) | collective-permute-done | bytes 524320 | tf_op jit(solution)/shard_map/ppermute | solution.py:503
  26.2 3.3 %grams_sent.1 = (bf16[4,2,640,128]{3,2,1,0:T(8,128)(2,1)S(1)}, f32[8,48,384]{2,1,0:T(8,128)S(1)}, f32[8,128]{1,0:T(8,128)S(1)}, f32[96,64,128]{2,1,0:T(8,128)S(1)}) custom-call(s32[8,33]{1,0:T(8,128)S(1)} %pad_add_fusion.ints_ref, f32[8,32]{1,0:T(8,128)S(1)} %pad_maximum_fusion.3.floats_ref, bf16[64,64]{1,0:T(8,128)(2,1)S(1)} %get-tuple-element.35.table_ref, ...), custom_call_target="tpu_custom_call" | custom-call | tf_op jit(solution)/shard_map/grams_sent/pallas_call | solution.py:568
  29.5 1.0 %collective-permute-start.3 = (f32[8,48,384]{2,1,0:T(8,128)S(1)}, f32[8,48,384]{2,1,0:T(8,128)S(1)}, u32[]{:S(2)}, u32[]{:S(2)}) collective-permute-start(f32[8,48,384]{2,1,0:T(8,128)S(1)} %get-tuple-element.38), channel_id=1, source_target_pairs={{0,1},{1,0},{2,3},{3,2},{4,5},{5,4},{6,7},{7,6},{8,9},{9,8},{10,11... | collective-permute-start | bytes 1769480 | tf_op jit(solution)/shard_map/ppermute | solution.py:498
  30.5 3.0 %grams_kept.1 = (bf16[4,2,640,128]{3,2,1,0:T(8,128)(2,1)S(1)}, f32[8,48,384]{2,1,0:T(8,128)S(1)}) custom-call(s32[8,33]{1,0:T(8,128)S(1)} %pad_add_fusion.ints_ref, f32[8,32]{1,0:T(8,128)S(1)} %pad_maximum_fusion.3.floats_ref, f32[96,64,128]{2,1,0:T(8,128)S(1)} %get-tuple-element.39.spec_ref), custom_call_target="tpu_custom_call" | custom-call | tf_op jit(solution)/shard_map/grams_kept/pallas_call | solution.py:583
  33.7 1.9 %collective-permute-start.4 = (f32[2,48,384]{2,1,0:T(8,128)S(1)}, f32[2,48,384]{2,1,0:T(8,128)S(1)}, u32[]{:S(2)}, u32[]{:S(2)}) collective-permute-start(f32[2,48,384]{2,1,0:T(8,128)S(1)} %get-tuple-element.65), channel_id=1, source_target_pairs={{0,4},{1,5},{2,6},{3,7},{4,0},{5,1},{6,2},{7,3},{8,12},{9,13},{10,... | collective-permute-start | bytes 442376 | tf_op jit(solution)/shard_map/ppermute | solution.py:498
  35.5 2.9 %collective-permute-start.5 = (f32[2,48,384]{2,1,0:T(8,128)S(1)}, f32[2,48,384]{2,1,0:T(8,128)S(1)}, u32[]{:S(2)}, u32[]{:S(2)}) collective-permute-start(f32[2,48,384]{2,1,0:T(8,128)S(1)} %get-tuple-element.64), channel_id=1, source_target_pairs={{0,2},{1,3},{2,0},{3,1},{4,6},{5,7},{6,4},{7,5},{8,10},{9,11},{10,... | collective-permute-start | bytes 442376 | tf_op jit(solution)/shard_map/ppermute | solution.py:498
  38.4 1.2 %edges_out.1 = (bf16[64,128]{1,0:T(8,128)(2,1)S(1)}, bf16[64,128]{1,0:T(8,128)(2,1)S(1)}) custom-call(bf16[4,2,640,128]{3,2,1,0:T(8,128)(2,1)S(1)} %get-tuple-element.46.sent_ref, bf16[4,2,640,128]{3,2,1,0:T(8,128)(2,1)S(1)} %get-tuple-element.47.kept_ref), custom_call_target="tpu_custom_call" | custom-call | tf_op jit(solution)/shard_map/edges_out/pallas_call | solution.py:596
  39.6 0.7 collective-permute-start.7
  40.3 0.8 collective-permute-done.7.first_ref
  41.1 3.4 %collective-permute-done.5 = f32[2,48,384]{2,1,0:T(8,128)S(1)} collective-permute-done((f32[2,48,384]{2,1,0:T(8,128)S(1)}, f32[2,48,384]{2,1,0:T(8,128)S(1)}, u32[]{:S(2)}, u32[]{:S(2)}) %collective-permute-start.5) | collective-permute-done | bytes 147488 | tf_op jit(solution)/shard_map/ppermute | solution.py:498
  44.5 1.1 %collective-permute-done.6 = f32[2,48,384]{2,1,0:T(8,128)S(1)} collective-permute-done((f32[2,48,384]{2,1,0:T(8,128)S(1)}, f32[2,48,384]{2,1,0:T(8,128)S(1)}, u32[]{:S(2)}, u32[]{:S(2)}) %collective-permute-start.6) | collective-permute-done | bytes 147488 | tf_op jit(solution)/shard_map/ppermute | solution.py:498
  45.7 3.1 %collective-permute-start.8 = (f32[48,384]{1,0:T(8,128)S(1)}, f32[48,384]{1,0:T(8,128)S(1)}, u32[]{:S(2)}, u32[]{:S(2)}) collective-permute-start(f32[48,384]{1,0:T(8,128)S(1)} %slice_bitcast_fusion), channel_id=1, source_target_pairs={{0,8},{1,9},{2,10},{3,11},{4,12},{5,13},{6,14},{7,15},{8,0},{9,1},... | collective-permute-start | bytes 221192 | tf_op jit(solution)/shard_map/ppermute | solution.py:498
  48.8 1.7 %collective-permute-done.8 = f32[48,384]{1,0:T(8,128)S(1)} collective-permute-done((f32[48,384]{1,0:T(8,128)S(1)}, f32[48,384]{1,0:T(8,128)S(1)}, u32[]{:S(2)}, u32[]{:S(2)}) %collective-permute-start.8) | collective-permute-done | bytes 73760 | tf_op jit(solution)/shard_map/ppermute | solution.py:498
  50.6 4.9 %collective-permute-start.9 = (f32[48,384]{1,0:T(8,128)S(1)}, f32[48,384]{1,0:T(8,128)S(1)}, u32[]{:S(2)}, u32[]{:S(2)}) collective-permute-start(f32[48,384]{1,0:T(8,128)S(1)} %fusion.first_ref), channel_id=1, source_target_pairs={{0,28},{1,29},{2,30},{3,31},{4,24},{5,25},{6,26},{7,27},{8,20},{9,... | collective-permute-start | bytes 221192 | tf_op jit(solution)/shard_map/ppermute | solution.py:498
  55.4 7.2 %collective-permute-start.10 = (bf16[64,128]{1,0:T(8,128)(2,1)S(1)}, bf16[64,128]{1,0:T(8,128)(2,1)S(1)}, u32[]{:S(2)}, u32[]{:S(2)}) collective-permute-start(bf16[64,128]{1,0:T(8,128)(2,1)S(1)} %get-tuple-element.53), channel_id=1, source_target_pairs={{1,2},{2,1},{3,4},{4,3},{5,6},{6,5},{7,8},{8,7},{9,10},{10,9},{11,... | collective-permute-start | bytes 49160 | tf_op jit(solution)/shard_map/ppermute | solution.py:606
  62.7 3.8 %solve.1 = f32[8,128]{1,0:T(8,128)S(1)} custom-call(f32[48,384]{1,0:T(8,128)S(1)} %fusion.first_ref, f32[48,384]{1,0:T(8,128)S(1)} %collective-permute-done.9.second_ref, f32[8,128]{1,0:T(8,128)S(1)} %get-tuple-element.52.marks_ref), custom_call_target="tpu_custom_call" | custom-call | tf_op jit(solution)/shard_map/solve/pallas_call | solution.py:613
  66.6 1.4 %collective-permute-start.11 = (f32[1,8,128]{2,1,0:T(8,128)S(1)}, f32[1,8,128]{2,1,0:T(8,128)S(1)}, u32[]{:S(2)}, u32[]{:S(2)}) collective-permute-start(f32[1,8,128]{2,1,0:T(8,128)S(1)} %bitcast.11), channel_id=1, source_target_pairs={{0,8},{1,9},{2,10},{3,11},{4,12},{5,13},{6,14},{7,15},{8,0},{9,1},... | collective-permute-start | bytes 12296 | tf_op jit(solution)/shard_map/ppermute | solution.py:498
  68.0 0.2 edges_in.1.edge_ref
  68.2 1.8 %collective-permute-done.11 = f32[1,8,128]{2,1,0:T(8,128)S(1)} collective-permute-done((f32[1,8,128]{2,1,0:T(8,128)S(1)}, f32[1,8,128]{2,1,0:T(8,128)S(1)}, u32[]{:S(2)}, u32[]{:S(2)}) %collective-permute-start.11) | collective-permute-done | bytes 4128 | tf_op jit(solution)/shard_map/ppermute | solution.py:498
  70.0 0.9 collective-permute-start.12
  70.9 1.6 %collective-permute-done.12 = f32[2,8,128]{2,1,0:T(8,128)S(1)} collective-permute-done((f32[2,8,128]{2,1,0:T(8,128)S(1)}, f32[2,8,128]{2,1,0:T(8,128)S(1)}, u32[]{:S(2)}, u32[]{:S(2)}) %collective-permute-start.12) | collective-permute-done | bytes 8224 | tf_op jit(solution)/shard_map/ppermute | solution.py:498
  72.5 1.5 %collective-permute-start.13 = (f32[4,8,128]{2,1,0:T(8,128)S(1)}, f32[4,8,128]{2,1,0:T(8,128)S(1)}, u32[]{:S(2)}, u32[]{:S(2)}) collective-permute-start(f32[4,8,128]{2,1,0:T(8,128)S(1)} %pad_maximum_fusion.1), channel_id=1, source_target_pairs={{0,2},{1,3},{2,0},{3,1},{4,6},{5,7},{6,4},{7,5},{8,10},{9,11},{10,... | collective-permute-start | bytes 49160 | tf_op jit(solution)/shard_map/ppermute | solution.py:498
  74.1 2.6 %collective-permute-done.13 = f32[4,8,128]{2,1,0:T(8,128)S(1)} collective-permute-done((f32[4,8,128]{2,1,0:T(8,128)S(1)}, f32[4,8,128]{2,1,0:T(8,128)S(1)}, u32[]{:S(2)}, u32[]{:S(2)}) %collective-permute-start.13) | collective-permute-done | bytes 16416 | tf_op jit(solution)/shard_map/ppermute | solution.py:498
  76.6 0.1 broadcast_in_dim.22.bins_ref
  76.7 2.0 %collective-permute-start.14 = (f32[8,8,128]{2,1,0:T(8,128)S(1)}, f32[8,8,128]{2,1,0:T(8,128)S(1)}, u32[]{:S(2)}, u32[]{:S(2)}) collective-permute-start(f32[8,8,128]{2,1,0:T(8,128)S(1)} %pad_maximum_fusion), channel_id=1, source_target_pairs={{0,1},{1,0},{2,3},{3,2},{4,5},{5,4},{6,7},{7,6},{8,9},{9,8},{10,11... | collective-permute-start | bytes 98312 | tf_op jit(solution)/shard_map/ppermute | solution.py:498
  78.8 0.9 collective-permute-done.14
  79.6 1.2 %power.1 = (f32[16,8,128]{2,1,0:T(8,128)S(1)}, f32[2,8,128]{2,1,0:T(8,128)S(1)}, f32[2,8,128]{2,1,0:T(8,128)S(1)}) custom-call(s32[16,8,128]{2,1,0:T(8,128)S(1)} %broadcast_in_dim.22.bins_ref, f32[16,8,128]{2,1,0:T(8,128)S(1)} %constant_dynamic-update-slice_fusion.weights_ref, bf16[4,2,640,128]{3,2,1,0:T(8,128)(2,1)S(1)} %get-tuple-element.46.sent_ref, ...), custom_call_target="tpu_custom_call" | custom-call | tf_op jit(solution)/shard_map/power/pallas_call | solution.py:638
  80.8 1.0 %collective-permute-start.15 = (f32[2,8,128]{2,1,0:T(8,128)S(1)}, f32[2,8,128]{2,1,0:T(8,128)S(1)}, u32[]{:S(2)}, u32[]{:S(2)}) collective-permute-start(f32[2,8,128]{2,1,0:T(8,128)S(1)} %get-tuple-element.61), channel_id=1, source_target_pairs={{0,32},{32,0},{64,96},{96,64},{128,160},{160,128},{192,224},{224,1... | collective-permute-start | bytes 24584 | tf_op jit(solution)/shard_map/ppermute | solution.py:648
  81.8 2.8 %collective-permute-start.16 = (f32[2,8,128]{2,1,0:T(8,128)S(1)}, f32[2,8,128]{2,1,0:T(8,128)S(1)}, u32[]{:S(2)}, u32[]{:S(2)}) collective-permute-start(f32[2,8,128]{2,1,0:T(8,128)S(1)} %get-tuple-element.62), channel_id=1, source_target_pairs={{0,224},{32,64},{64,32},{96,128},{128,96},{160,192},{192,160},{224... | collective-permute-start | bytes 24584 | tf_op jit(solution)/shard_map/ppermute | solution.py:648
  84.6 1.8 %collective-permute-done.16.second_ref = f32[2,8,128]{2,1,0:T(8,128)S(1)} collective-permute-done((f32[2,8,128]{2,1,0:T(8,128)S(1)}, f32[2,8,128]{2,1,0:T(8,128)S(1)}, u32[]{:S(2)}, u32[]{:S(2)}) %collective-permute-start.16) | collective-permute-done | bytes 8224 | tf_op jit(solution)/shard_map/ppermute | solution.py:648
  86.4 0.6 smooth.1
  (30 shorter events, 0.5 us)
Async XLA Ops:
  0.0 12.3 %copy-start = (f32[64,16]{0,1:T(8,128)S(1)}, f32[64,16]{0,1:T(8,128)}, u32[]{:S(2)}) copy-start(f32[64,16]{0,1:T(8,128)} %param.11) | copy-start | bytes 12292
  0.0 22.9 %collective-permute-start = (bf16[2,32,32,128]{3,2,1,0:T(8,128)(2,1)}, bf16[2,32,32,128]{3,2,1,0:T(8,128)(2,1)S(1)}, u32[]{:S(2)}, u32[]{:S(2)}) collective-permute-start(bf16[2,32,32,128]{3,2,1,0:T(8,128)(2,1)} %own_ref.1), channel_id=1, source_target_pairs={{32,0},{64,32},{96,64},{128,96},{160,128},{192,160},{224,192},{0,2... | collective-permute-start | bytes 1572872 | tf_op jit(solution)/shard_map/ppermute | solution.py:504
  4.3 21.9 %collective-permute-start.1 = (bf16[2,32,32,128]{3,2,1,0:T(8,128)(2,1)}, bf16[2,32,32,128]{3,2,1,0:T(8,128)(2,1)S(1)}, u32[]{:S(2)}, u32[]{:S(2)}) collective-permute-start(bf16[2,32,32,128]{3,2,1,0:T(8,128)(2,1)} %own_ref.1), channel_id=1, source_target_pairs={{0,32},{32,64},{64,96},{96,128},{128,160},{160,192},{192,224},{224... | collective-permute-start | bytes 1572872 | tf_op jit(solution)/shard_map/ppermute | solution.py:503
  5.1 10.8 %collective-permute-start.2 = (f32[8,128]{1,0:T(8,128)S(1)}, f32[8,128]{1,0:T(8,128)S(1)}, u32[]{:S(2)}, u32[]{:S(2)}) collective-permute-start(f32[8,128]{1,0:T(8,128)S(1)} %broadcast_in_dim.19), channel_id=1, source_target_pairs={{0,28},{1,29},{2,30},{3,31},{4,24},{5,25},{6,26},{7,27},{8,20},{9,... | collective-permute-start | bytes 12296 | tf_op jit(solution)/shard_map/ppermute | solution.py:498
  13.5 1.0 %copy-start.1 = (bf16[2,32,32,128]{3,2,1,0:T(8,128)(2,1)S(1)}, bf16[2,32,32,128]{3,2,1,0:T(8,128)(2,1)}, u32[]{:S(2)}) copy-start(bf16[2,32,32,128]{3,2,1,0:T(8,128)(2,1)} %own_ref.1) | copy-start | bytes 1572868
  14.5 0.7 copy-start.2
  29.5 4.0 %collective-permute-start.3 = (f32[8,48,384]{2,1,0:T(8,128)S(1)}, f32[8,48,384]{2,1,0:T(8,128)S(1)}, u32[]{:S(2)}, u32[]{:S(2)}) collective-permute-start(f32[8,48,384]{2,1,0:T(8,128)S(1)} %get-tuple-element.38), channel_id=1, source_target_pairs={{0,1},{1,0},{2,3},{3,2},{4,5},{5,4},{6,7},{7,6},{8,9},{9,8},{10,11... | collective-permute-start | bytes 1769480 | tf_op jit(solution)/shard_map/ppermute | solution.py:498
  33.7 7.5 %collective-permute-start.4 = (f32[2,48,384]{2,1,0:T(8,128)S(1)}, f32[2,48,384]{2,1,0:T(8,128)S(1)}, u32[]{:S(2)}, u32[]{:S(2)}) collective-permute-start(f32[2,48,384]{2,1,0:T(8,128)S(1)} %get-tuple-element.65), channel_id=1, source_target_pairs={{0,4},{1,5},{2,6},{3,7},{4,0},{5,1},{6,2},{7,3},{8,12},{9,13},{10,... | collective-permute-start | bytes 442376 | tf_op jit(solution)/shard_map/ppermute | solution.py:498
  35.5 9.0 %collective-permute-start.5 = (f32[2,48,384]{2,1,0:T(8,128)S(1)}, f32[2,48,384]{2,1,0:T(8,128)S(1)}, u32[]{:S(2)}, u32[]{:S(2)}) collective-permute-start(f32[2,48,384]{2,1,0:T(8,128)S(1)} %get-tuple-element.64), channel_id=1, source_target_pairs={{0,2},{1,3},{2,0},{3,1},{4,6},{5,7},{6,4},{7,5},{8,10},{9,11},{10,... | collective-permute-start | bytes 442376 | tf_op jit(solution)/shard_map/ppermute | solution.py:498
  38.4 7.2 %collective-permute-start.6 = (f32[2,48,384]{2,1,0:T(8,128)S(1)}, f32[2,48,384]{2,1,0:T(8,128)S(1)}, u32[]{:S(2)}, u32[]{:S(2)}) collective-permute-start(f32[2,48,384]{2,1,0:T(8,128)S(1)} %get-tuple-element.63), channel_id=1, source_target_pairs={{0,6},{1,7},{2,4},{3,5},{4,2},{5,3},{6,0},{7,1},{8,14},{9,15},{10,... | collective-permute-start | bytes 442376 | tf_op jit(solution)/shard_map/ppermute | solution.py:498
  39.6 1.5 %collective-permute-start.7 = (bf16[64,128]{1,0:T(8,128)(2,1)S(1)}, bf16[64,128]{1,0:T(8,128)(2,1)S(1)}, u32[]{:S(2)}, u32[]{:S(2)}) collective-permute-start(bf16[64,128]{1,0:T(8,128)(2,1)S(1)} %get-tuple-element.48), channel_id=1, source_target_pairs={{0,1},{1,0},{2,3},{3,2},{4,5},{5,4},{6,7},{7,6},{8,9},{9,8},{10,11... | collective-permute-start | bytes 49160 | tf_op jit(solution)/shard_map/ppermute | solution.py:606
  45.7 4.8 %collective-permute-start.8 = (f32[48,384]{1,0:T(8,128)S(1)}, f32[48,384]{1,0:T(8,128)S(1)}, u32[]{:S(2)}, u32[]{:S(2)}) collective-permute-start(f32[48,384]{1,0:T(8,128)S(1)} %slice_bitcast_fusion), channel_id=1, source_target_pairs={{0,8},{1,9},{2,10},{3,11},{4,12},{5,13},{6,14},{7,15},{8,0},{9,1},... | collective-permute-start | bytes 221192 | tf_op jit(solution)/shard_map/ppermute | solution.py:498
  50.6 12.2 %collective-permute-start.9 = (f32[48,384]{1,0:T(8,128)S(1)}, f32[48,384]{1,0:T(8,128)S(1)}, u32[]{:S(2)}, u32[]{:S(2)}) collective-permute-start(f32[48,384]{1,0:T(8,128)S(1)} %fusion.first_ref), channel_id=1, source_target_pairs={{0,28},{1,29},{2,30},{3,31},{4,24},{5,25},{6,26},{7,27},{8,20},{9,... | collective-permute-start | bytes 221192 | tf_op jit(solution)/shard_map/ppermute | solution.py:498
  55.4 11.1 %collective-permute-start.10 = (bf16[64,128]{1,0:T(8,128)(2,1)S(1)}, bf16[64,128]{1,0:T(8,128)(2,1)S(1)}, u32[]{:S(2)}, u32[]{:S(2)}) collective-permute-start(bf16[64,128]{1,0:T(8,128)(2,1)S(1)} %get-tuple-element.53), channel_id=1, source_target_pairs={{1,2},{2,1},{3,4},{4,3},{5,6},{6,5},{7,8},{8,7},{9,10},{10,9},{11,... | collective-permute-start | bytes 49160 | tf_op jit(solution)/shard_map/ppermute | solution.py:606
  66.6 3.4 %collective-permute-start.11 = (f32[1,8,128]{2,1,0:T(8,128)S(1)}, f32[1,8,128]{2,1,0:T(8,128)S(1)}, u32[]{:S(2)}, u32[]{:S(2)}) collective-permute-start(f32[1,8,128]{2,1,0:T(8,128)S(1)} %bitcast.11), channel_id=1, source_target_pairs={{0,8},{1,9},{2,10},{3,11},{4,12},{5,13},{6,14},{7,15},{8,0},{9,1},... | collective-permute-start | bytes 12296 | tf_op jit(solution)/shard_map/ppermute | solution.py:498
  70.0 2.5 %collective-permute-start.12 = (f32[2,8,128]{2,1,0:T(8,128)S(1)}, f32[2,8,128]{2,1,0:T(8,128)S(1)}, u32[]{:S(2)}, u32[]{:S(2)}) collective-permute-start(f32[2,8,128]{2,1,0:T(8,128)S(1)} %pad_maximum_fusion.2), channel_id=1, source_target_pairs={{0,4},{1,5},{2,6},{3,7},{4,0},{5,1},{6,2},{7,3},{8,12},{9,13},{10,... | collective-permute-start | bytes 24584 | tf_op jit(solution)/shard_map/ppermute | solution.py:498
  72.5 4.1 %collective-permute-start.13 = (f32[4,8,128]{2,1,0:T(8,128)S(1)}, f32[4,8,128]{2,1,0:T(8,128)S(1)}, u32[]{:S(2)}, u32[]{:S(2)}) collective-permute-start(f32[4,8,128]{2,1,0:T(8,128)S(1)} %pad_maximum_fusion.1), channel_id=1, source_target_pairs={{0,2},{1,3},{2,0},{3,1},{4,6},{5,7},{6,4},{7,5},{8,10},{9,11},{10,... | collective-permute-start | bytes 49160 | tf_op jit(solution)/shard_map/ppermute | solution.py:498
  76.7 2.9 %collective-permute-start.14 = (f32[8,8,128]{2,1,0:T(8,128)S(1)}, f32[8,8,128]{2,1,0:T(8,128)S(1)}, u32[]{:S(2)}, u32[]{:S(2)}) collective-permute-start(f32[8,8,128]{2,1,0:T(8,128)S(1)} %pad_maximum_fusion), channel_id=1, source_target_pairs={{0,1},{1,0},{2,3},{3,2},{4,5},{5,4},{6,7},{7,6},{8,9},{9,8},{10,11... | collective-permute-start | bytes 98312 | tf_op jit(solution)/shard_map/ppermute | solution.py:498
  80.8 3.8 %collective-permute-start.15 = (f32[2,8,128]{2,1,0:T(8,128)S(1)}, f32[2,8,128]{2,1,0:T(8,128)S(1)}, u32[]{:S(2)}, u32[]{:S(2)}) collective-permute-start(f32[2,8,128]{2,1,0:T(8,128)S(1)} %get-tuple-element.61), channel_id=1, source_target_pairs={{0,32},{32,0},{64,96},{96,64},{128,160},{160,128},{192,224},{224,1... | collective-permute-start | bytes 24584 | tf_op jit(solution)/shard_map/ppermute | solution.py:648
  81.8 4.6 %collective-permute-start.16 = (f32[2,8,128]{2,1,0:T(8,128)S(1)}, f32[2,8,128]{2,1,0:T(8,128)S(1)}, u32[]{:S(2)}, u32[]{:S(2)}) collective-permute-start(f32[2,8,128]{2,1,0:T(8,128)S(1)} %get-tuple-element.62), channel_id=1, source_target_pairs={{0,224},{32,64},{64,32},{96,128},{128,96},{160,192},{192,160},{224... | collective-permute-start | bytes 24584 | tf_op jit(solution)/shard_map/ppermute | solution.py:648

commit v10 on v9

--- a/solution.py
+++ b/solution.py
@@ -602,10 +602,8 @@
         name="edges_out",
     )(sent, kept)
     moved = [swap(part[2:4], 4), swap(part[4:6], 2), swap(part[6:], 6)]
-    edges = [
-        lax.ppermute(value, "rng", pairs)
-        for value, pairs in zip(edges, neighbours(32, False))
-    ]
+    nearest, across = neighbours(32, False)
+    edges = [lax.ppermute(edges[0], "rng", nearest), edges[1]]
     moved, edges[0] = lax.optimization_barrier((moved, edges[0]))
     part = part[:2] + moved[0] + moved[1] + moved[2]
     part = part[0] + swap(part[1], 8)
@@ -620,6 +618,7 @@
         name="solve",
     )(part, other, marks)
     weights, edges[1] = lax.optimization_barrier((weights, edges[1]))
+    edges[1] = lax.ppermute(edges[1], "rng", across)
     edges = pl.pallas_call(
         edge_in_kernel,
         out_shape=shape(2, SLOTS * SEL, LANES, dtype=BF16),

time: 87.6 us -> 87.6 us (level)
  waiting for transfers between devices: 25.4 us -> 26.8 us
  starting transfers between devices: 41.1 us -> 39.9 us
    ppermute x11, starting transfers between devices: 25.1 us -> 23.1 us  [swap(): return lax.ppermute(value, 'rng', [(i, i ^ turn) for i in range(32)])]
    ppermute x11, waiting for transfers between devices: 13.2 us -> 14.5 us  [swap(): return lax.ppermute(value, 'rng', [(i, i ^ turn) for i in range(32)])]
  transfers between devices with their start and end apart: 17 -> 17, of which waited for: 11 -> 11; matrix products, arithmetic and copies ran while one was open for 4% -> 4% of each run, Pallas kernels for 11% -> 7%
where the time goes in v10:
time: 87.6 us; the launch traced here: 87.3 us
  starting transfers between devices  39.9 us (46%)
  waiting for transfers between devices  26.8 us (31%)
  Pallas kernels  14.7 us (17%)
  local copies, waits for them, and re-layouts  3.87 us (4%)
  other arithmetic  1.82 us (2%)
    ppermute x11, starting transfers between devices, swap(): return lax.ppermute(value, 'rng', [(i, i ^ turn) for i in range(32)])  23.1 us
    ppermute x11, waiting for transfers between devices, swap(): return lax.ppermute(value, 'rng', [(i, i ^ turn) for i in range(32)])  14.5 us
    ppermute x1, starting transfers between devices, body(): edges[1] = lax.ppermute(edges[1], 'rng', across)  8.05 us
    ppermute x1, waiting for transfers between devices, halo_columns(): high = lax.ppermute(echoes, 'az', [(b, a) for a, b in ring])  6.98 us
    ppermute x1, starting transfers between devices, halo_columns(): high = lax.ppermute(echoes, 'az', [(b, a) for a, b in ring])  4.32 us
    pallas_call x1, Pallas kernels, body(): pl.pallas_call(solve_kernel, out_shape=shape(8, LANES), in_specs=[VMEM] *...  3.85 us
    ppermute x2, starting transfers between devices, body(): lax.ppermute(value, 'az', pairs)  3.75 us
    pallas_call x1, Pallas kernels, body(): pl.pallas_call(send_kernel, out_shape=(some, half, shape(OWN_BEAMS, LANES...  3.3 us
  transfers between devices with their start and end apart: 17, of which 11 were waited for; matrix products, arithmetic and copies ran while one was open for 4% of the time, Pallas kernels for 7%

profile of v10, /device:TPU:1, one launch (start us, length us, event | category | flops | bytes accessed | tf_op | source)
XLA Modules:
  0.0 87.3 jit_solution(1317032489796849147)
XLA Ops:
  0.0 4.3 %collective-permute-start = (bf16[2,32,32,128]{3,2,1,0:T(8,128)(2,1)}, bf16[2,32,32,128]{3,2,1,0:T(8,128)(2,1)S(1)}, u32[]{:S(2)}, u32[]{:S(2)}) collective-permute-start(bf16[2,32,32,128]{3,2,1,0:T(8,128)(2,1)} %own_ref.1), channel_id=1, source_target_pairs={{32,0},{64,32},{96,64},{128,96},{160,128},{192,160},{224,192},{0,2... | collective-permute-start | bytes 1572872 | tf_op jit(solution)/shard_map/ppermute | solution.py:504
  4.3 0.7 convert_bitcast_fusion
  5.0 0.1 broadcast_in_dim.19
  5.1 5.6 %collective-permute-start.2 = (f32[8,128]{1,0:T(8,128)S(1)}, f32[8,128]{1,0:T(8,128)S(1)}, u32[]{:S(2)}, u32[]{:S(2)}) collective-permute-start(f32[8,128]{1,0:T(8,128)S(1)} %broadcast_in_dim.19), channel_id=1, source_target_pairs={{0,28},{1,29},{2,30},{3,31},{4,24},{5,25},{6,26},{7,27},{8,20},{9,... | collective-permute-start | bytes 12296 | tf_op jit(solution)/shard_map/ppermute | solution.py:498
  10.6 0.7 copy.14
  11.4 0.8 constant_dynamic-slice_fusion.1
  12.3 0.1 constant_dynamic-slice_fusion
  12.4 0.1 copy.18
  12.5 0.7 and_select_fusion
  13.2 0.1 pad_maximum_fusion.3.floats_ref
  13.4 0.1 pad_add_fusion.ints_ref
  13.5 1.0 %copy-done.1 = bf16[2,32,32,128]{3,2,1,0:T(8,128)(2,1)S(1)} copy-done((bf16[2,32,32,128]{3,2,1,0:T(8,128)(2,1)S(1)}, bf16[2,32,32,128]{3,2,1,0:T(8,128)(2,1)}, u32[]{:S(2)}) %copy-start.1) | copy-done | bytes 524312
  14.5 0.7 copy-done.2
  15.2 0.7 spectra.2
  15.9 0.1 broadcast_add_fusion.marks_ref
  16.0 7.0 %collective-permute-done.own_ref = bf16[2,32,32,128]{3,2,1,0:T(8,128)(2,1)S(1)} collective-permute-done((bf16[2,32,32,128]{3,2,1,0:T(8,128)(2,1)}, bf16[2,32,32,128]{3,2,1,0:T(8,128)(2,1)S(1)}, u32[]{:S(2)}, u32[]{:S(2)}) %collective-permute-start) | collective-permute-done | bytes 524320 | tf_op jit(solution)/shard_map/ppermute | solution.py:504
  23.0 0.7 spectra.3
  23.6 2.6 %collective-permute-done.1.low_ref = bf16[2,32,32,128]{3,2,1,0:T(8,128)(2,1)S(1)} collective-permute-done((bf16[2,32,32,128]{3,2,1,0:T(8,128)(2,1)}, bf16[2,32,32,128]{3,2,1,0:T(8,128)(2,1)S(1)}, u32[]{:S(2)}, u32[]{:S(2)}) %collective-permute-start.1) | collective-permute-done | bytes 524320 | tf_op jit(solution)/shard_map/ppermute | solution.py:503
  26.2 3.3 %grams_sent.1 = (bf16[4,2,640,128]{3,2,1,0:T(8,128)(2,1)S(1)}, f32[8,48,384]{2,1,0:T(8,128)S(1)}, f32[8,128]{1,0:T(8,128)S(1)}, f32[96,64,128]{2,1,0:T(8,128)S(1)}) custom-call(s32[8,33]{1,0:T(8,128)S(1)} %pad_add_fusion.ints_ref, f32[8,32]{1,0:T(8,128)S(1)} %pad_maximum_fusion.3.floats_ref, bf16[64,64]{1,0:T(8,128)(2,1)S(1)} %get-tuple-element.35.table_ref, ...), custom_call_target="tpu_custom_call" | custom-call | tf_op jit(solution)/shard_map/grams_sent/pallas_call | solution.py:568
  29.5 1.0 %collective-permute-start.3 = (f32[8,48,384]{2,1,0:T(8,128)S(1)}, f32[8,48,384]{2,1,0:T(8,128)S(1)}, u32[]{:S(2)}, u32[]{:S(2)}) collective-permute-start(f32[8,48,384]{2,1,0:T(8,128)S(1)} %get-tuple-element.38), channel_id=1, source_target_pairs={{0,1},{1,0},{2,3},{3,2},{4,5},{5,4},{6,7},{7,6},{8,9},{9,8},{10,11... | collective-permute-start | bytes 1769480 | tf_op jit(solution)/shard_map/ppermute | solution.py:498
  30.5 3.0 %grams_kept.1 = (bf16[4,2,640,128]{3,2,1,0:T(8,128)(2,1)S(1)}, f32[8,48,384]{2,1,0:T(8,128)S(1)}) custom-call(s32[8,33]{1,0:T(8,128)S(1)} %pad_add_fusion.ints_ref, f32[8,32]{1,0:T(8,128)S(1)} %pad_maximum_fusion.3.floats_ref, f32[96,64,128]{2,1,0:T(8,128)S(1)} %get-tuple-element.39.spec_ref), custom_call_target="tpu_custom_call" | custom-call | tf_op jit(solution)/shard_map/grams_kept/pallas_call | solution.py:583
  33.6 1.9 %collective-permute-start.4 = (f32[2,48,384]{2,1,0:T(8,128)S(1)}, f32[2,48,384]{2,1,0:T(8,128)S(1)}, u32[]{:S(2)}, u32[]{:S(2)}) collective-permute-start(f32[2,48,384]{2,1,0:T(8,128)S(1)} %get-tuple-element.65), channel_id=1, source_target_pairs={{0,4},{1,5},{2,6},{3,7},{4,0},{5,1},{6,2},{7,3},{8,12},{9,13},{10,... | collective-permute-start | bytes 442376 | tf_op jit(solution)/shard_map/ppermute | solution.py:498
  35.5 2.9 %collective-permute-start.5 = (f32[2,48,384]{2,1,0:T(8,128)S(1)}, f32[2,48,384]{2,1,0:T(8,128)S(1)}, u32[]{:S(2)}, u32[]{:S(2)}) collective-permute-start(f32[2,48,384]{2,1,0:T(8,128)S(1)} %get-tuple-element.64), channel_id=1, source_target_pairs={{0,2},{1,3},{2,0},{3,1},{4,6},{5,7},{6,4},{7,5},{8,10},{9,11},{10,... | collective-permute-start | bytes 442376 | tf_op jit(solution)/shard_map/ppermute | solution.py:498
  38.4 1.2 %edges_out.1 = (bf16[64,128]{1,0:T(8,128)(2,1)S(1)}, bf16[64,128]{1,0:T(8,128)(2,1)S(1)}) custom-call(bf16[4,2,640,128]{3,2,1,0:T(8,128)(2,1)S(1)} %get-tuple-element.46.sent_ref, bf16[4,2,640,128]{3,2,1,0:T(8,128)(2,1)S(1)} %get-tuple-element.47.kept_ref), custom_call_target="tpu_custom_call" | custom-call | tf_op jit(solution)/shard_map/edges_out/pallas_call | solution.py:596
  39.6 0.7 collective-permute-start.7
  40.3 0.8 collective-permute-done.7.first_ref
  41.1 3.4 %collective-permute-done.5 = f32[2,48,384]{2,1,0:T(8,128)S(1)} collective-permute-done((f32[2,48,384]{2,1,0:T(8,128)S(1)}, f32[2,48,384]{2,1,0:T(8,128)S(1)}, u32[]{:S(2)}, u32[]{:S(2)}) %collective-permute-start.5) | collective-permute-done | bytes 147488 | tf_op jit(solution)/shard_map/ppermute | solution.py:498
  44.6 1.1 %collective-permute-done.6 = f32[2,48,384]{2,1,0:T(8,128)S(1)} collective-permute-done((f32[2,48,384]{2,1,0:T(8,128)S(1)}, f32[2,48,384]{2,1,0:T(8,128)S(1)}, u32[]{:S(2)}, u32[]{:S(2)}) %collective-permute-start.6) | collective-permute-done | bytes 147488 | tf_op jit(solution)/shard_map/ppermute | solution.py:498
  45.7 3.1 %collective-permute-start.8 = (f32[48,384]{1,0:T(8,128)S(1)}, f32[48,384]{1,0:T(8,128)S(1)}, u32[]{:S(2)}, u32[]{:S(2)}) collective-permute-start(f32[48,384]{1,0:T(8,128)S(1)} %slice_bitcast_fusion), channel_id=1, source_target_pairs={{0,8},{1,9},{2,10},{3,11},{4,12},{5,13},{6,14},{7,15},{8,0},{9,1},... | collective-permute-start | bytes 221192 | tf_op jit(solution)/shard_map/ppermute | solution.py:498
  48.8 1.7 %collective-permute-done.8 = f32[48,384]{1,0:T(8,128)S(1)} collective-permute-done((f32[48,384]{1,0:T(8,128)S(1)}, f32[48,384]{1,0:T(8,128)S(1)}, u32[]{:S(2)}, u32[]{:S(2)}) %collective-permute-start.8) | collective-permute-done | bytes 73760 | tf_op jit(solution)/shard_map/ppermute | solution.py:498
  50.6 5.1 %collective-permute-start.9 = (f32[48,384]{1,0:T(8,128)S(1)}, f32[48,384]{1,0:T(8,128)S(1)}, u32[]{:S(2)}, u32[]{:S(2)}) collective-permute-start(f32[48,384]{1,0:T(8,128)S(1)} %fusion.first_ref), channel_id=1, source_target_pairs={{0,28},{1,29},{2,30},{3,31},{4,24},{5,25},{6,26},{7,27},{8,20},{9,... | collective-permute-start | bytes 221192 | tf_op jit(solution)/shard_map/ppermute | solution.py:498
  55.7 2.5 %collective-permute-done.9.second_ref = f32[48,384]{1,0:T(8,128)S(1)} collective-permute-done((f32[48,384]{1,0:T(8,128)S(1)}, f32[48,384]{1,0:T(8,128)S(1)}, u32[]{:S(2)}, u32[]{:S(2)}) %collective-permute-start.9) | collective-permute-done | bytes 73760 | tf_op jit(solution)/shard_map/ppermute | solution.py:498
  58.2 3.8 %solve.1 = f32[8,128]{1,0:T(8,128)S(1)} custom-call(f32[48,384]{1,0:T(8,128)S(1)} %fusion.first_ref, f32[48,384]{1,0:T(8,128)S(1)} %collective-permute-done.9.second_ref, f32[8,128]{1,0:T(8,128)S(1)} %get-tuple-element.52.marks_ref), custom_call_target="tpu_custom_call" | custom-call | tf_op jit(solution)/shard_map/solve/pallas_call | solution.py:611
  62.1 1.4 %collective-permute-start.10 = (f32[1,8,128]{2,1,0:T(8,128)S(1)}, f32[1,8,128]{2,1,0:T(8,128)S(1)}, u32[]{:S(2)}, u32[]{:S(2)}) collective-permute-start(f32[1,8,128]{2,1,0:T(8,128)S(1)} %bitcast.11), channel_id=1, source_target_pairs={{0,8},{1,9},{2,10},{3,11},{4,12},{5,13},{6,14},{7,15},{8,0},{9,1},... | collective-permute-start | bytes 12296 | tf_op jit(solution)/shard_map/ppermute | solution.py:498
  63.5 8.1 %collective-permute-start.13 = (bf16[64,128]{1,0:T(8,128)(2,1)S(1)}, bf16[64,128]{1,0:T(8,128)(2,1)S(1)}, u32[]{:S(2)}, u32[]{:S(2)}) collective-permute-start(bf16[64,128]{1,0:T(8,128)(2,1)S(1)} %get-tuple-element.56), channel_id=1, source_target_pairs={{1,2},{2,1},{3,4},{4,3},{5,6},{6,5},{7,8},{8,7},{9,10},{10,9},{11,... | collective-permute-start | bytes 49160 | tf_op jit(solution)/shard_map/ppermute | solution.py:621
  71.6 0.4 collective-permute-start.11
  72.0 2.2 %collective-permute-done.11 = f32[2,8,128]{2,1,0:T(8,128)S(1)} collective-permute-done((f32[2,8,128]{2,1,0:T(8,128)S(1)}, f32[2,8,128]{2,1,0:T(8,128)S(1)}, u32[]{:S(2)}, u32[]{:S(2)}) %collective-permute-start.11) | collective-permute-done | bytes 8224 | tf_op jit(solution)/shard_map/ppermute | solution.py:498
  74.2 1.3 %collective-permute-start.12 = (f32[4,8,128]{2,1,0:T(8,128)S(1)}, f32[4,8,128]{2,1,0:T(8,128)S(1)}, u32[]{:S(2)}, u32[]{:S(2)}) collective-permute-start(f32[4,8,128]{2,1,0:T(8,128)S(1)} %pad_maximum_fusion.1), channel_id=1, source_target_pairs={{0,2},{1,3},{2,0},{3,1},{4,6},{5,7},{6,4},{7,5},{8,10},{9,11},{10,... | collective-permute-start | bytes 49160 | tf_op jit(solution)/shard_map/ppermute | solution.py:498
  75.4 0.3 edges_in.1.edge_ref
  75.7 2.7 %collective-permute-done.12 = f32[4,8,128]{2,1,0:T(8,128)S(1)} collective-permute-done((f32[4,8,128]{2,1,0:T(8,128)S(1)}, f32[4,8,128]{2,1,0:T(8,128)S(1)}, u32[]{:S(2)}, u32[]{:S(2)}) %collective-permute-start.12) | collective-permute-done | bytes 16416 | tf_op jit(solution)/shard_map/ppermute | solution.py:498
  78.4 0.1 broadcast_in_dim.22.bins_ref
  78.5 0.5 collective-permute-start.14
  78.9 0.9 collective-permute-done.14
  79.8 1.2 %power.1 = (f32[16,8,128]{2,1,0:T(8,128)S(1)}, f32[2,8,128]{2,1,0:T(8,128)S(1)}, f32[2,8,128]{2,1,0:T(8,128)S(1)}) custom-call(s32[16,8,128]{2,1,0:T(8,128)S(1)} %broadcast_in_dim.22.bins_ref, f32[16,8,128]{2,1,0:T(8,128)S(1)} %constant_dynamic-update-slice_fusion.weights_ref, bf16[4,2,640,128]{3,2,1,0:T(8,128)(2,1)S(1)} %get-tuple-element.46.sent_ref, ...), custom_call_target="tpu_custom_call" | custom-call | tf_op jit(solution)/shard_map/power/pallas_call | solution.py:637
  81.0 1.0 %collective-permute-start.15 = (f32[2,8,128]{2,1,0:T(8,128)S(1)}, f32[2,8,128]{2,1,0:T(8,128)S(1)}, u32[]{:S(2)}, u32[]{:S(2)}) collective-permute-start(f32[2,8,128]{2,1,0:T(8,128)S(1)} %get-tuple-element.61), channel_id=1, source_target_pairs={{0,32},{32,0},{64,96},{96,64},{128,160},{160,128},{192,224},{224,1... | collective-permute-start | bytes 24584 | tf_op jit(solution)/shard_map/ppermute | solution.py:647
  82.0 2.7 %collective-permute-start.16 = (f32[2,8,128]{2,1,0:T(8,128)S(1)}, f32[2,8,128]{2,1,0:T(8,128)S(1)}, u32[]{:S(2)}, u32[]{:S(2)}) collective-permute-start(f32[2,8,128]{2,1,0:T(8,128)S(1)} %get-tuple-element.62), channel_id=1, source_target_pairs={{0,224},{32,64},{64,32},{96,128},{128,96},{160,192},{192,160},{224... | collective-permute-start | bytes 24584 | tf_op jit(solution)/shard_map/ppermute | solution.py:647
  84.7 1.9 %collective-permute-done.16.second_ref = f32[2,8,128]{2,1,0:T(8,128)S(1)} collective-permute-done((f32[2,8,128]{2,1,0:T(8,128)S(1)}, f32[2,8,128]{2,1,0:T(8,128)S(1)}, u32[]{:S(2)}, u32[]{:S(2)}) %collective-permute-start.16) | collective-permute-done | bytes 8224 | tf_op jit(solution)/shard_map/ppermute | solution.py:647
  86.6 0.6 smooth.1
  (30 shorter events, 0.5 us)
Async XLA Ops:
  0.0 12.3 %copy-start = (f32[64,16]{0,1:T(8,128)S(1)}, f32[64,16]{0,1:T(8,128)}, u32[]{:S(2)}) copy-start(f32[64,16]{0,1:T(8,128)} %param.11) | copy-start | bytes 12292
  0.0 22.9 %collective-permute-start = (bf16[2,32,32,128]{3,2,1,0:T(8,128)(2,1)}, bf16[2,32,32,128]{3,2,1,0:T(8,128)(2,1)S(1)}, u32[]{:S(2)}, u32[]{:S(2)}) collective-permute-start(bf16[2,32,32,128]{3,2,1,0:T(8,128)(2,1)} %own_ref.1), channel_id=1, source_target_pairs={{32,0},{64,32},{96,64},{128,96},{160,128},{192,160},{224,192},{0,2... | collective-permute-start | bytes 1572872 | tf_op jit(solution)/shard_map/ppermute | solution.py:504
  4.3 21.9 %collective-permute-start.1 = (bf16[2,32,32,128]{3,2,1,0:T(8,128)(2,1)}, bf16[2,32,32,128]{3,2,1,0:T(8,128)(2,1)S(1)}, u32[]{:S(2)}, u32[]{:S(2)}) collective-permute-start(bf16[2,32,32,128]{3,2,1,0:T(8,128)(2,1)} %own_ref.1), channel_id=1, source_target_pairs={{0,32},{32,64},{64,96},{96,128},{128,160},{160,192},{192,224},{224... | collective-permute-start | bytes 1572872 | tf_op jit(solution)/shard_map/ppermute | solution.py:503
  5.1 10.8 %collective-permute-start.2 = (f32[8,128]{1,0:T(8,128)S(1)}, f32[8,128]{1,0:T(8,128)S(1)}, u32[]{:S(2)}, u32[]{:S(2)}) collective-permute-start(f32[8,128]{1,0:T(8,128)S(1)} %broadcast_in_dim.19), channel_id=1, source_target_pairs={{0,28},{1,29},{2,30},{3,31},{4,24},{5,25},{6,26},{7,27},{8,20},{9,... | collective-permute-start | bytes 12296 | tf_op jit(solution)/shard_map/ppermute | solution.py:498
  13.5 1.0 %copy-start.1 = (bf16[2,32,32,128]{3,2,1,0:T(8,128)(2,1)S(1)}, bf16[2,32,32,128]{3,2,1,0:T(8,128)(2,1)}, u32[]{:S(2)}) copy-start(bf16[2,32,32,128]{3,2,1,0:T(8,128)(2,1)} %own_ref.1) | copy-start | bytes 1572868
  14.5 0.7 copy-start.2
  29.5 4.0 %collective-permute-start.3 = (f32[8,48,384]{2,1,0:T(8,128)S(1)}, f32[8,48,384]{2,1,0:T(8,128)S(1)}, u32[]{:S(2)}, u32[]{:S(2)}) collective-permute-start(f32[8,48,384]{2,1,0:T(8,128)S(1)} %get-tuple-element.38), channel_id=1, source_target_pairs={{0,1},{1,0},{2,3},{3,2},{4,5},{5,4},{6,7},{7,6},{8,9},{9,8},{10,11... | collective-permute-start | bytes 1769480 | tf_op jit(solution)/shard_map/ppermute | solution.py:498
  33.6 7.5 %collective-permute-start.4 = (f32[2,48,384]{2,1,0:T(8,128)S(1)}, f32[2,48,384]{2,1,0:T(8,128)S(1)}, u32[]{:S(2)}, u32[]{:S(2)}) collective-permute-start(f32[2,48,384]{2,1,0:T(8,128)S(1)} %get-tuple-element.65), channel_id=1, source_target_pairs={{0,4},{1,5},{2,6},{3,7},{4,0},{5,1},{6,2},{7,3},{8,12},{9,13},{10,... | collective-permute-start | bytes 442376 | tf_op jit(solution)/shard_map/ppermute | solution.py:498
  35.5 9.1 %collective-permute-start.5 = (f32[2,48,384]{2,1,0:T(8,128)S(1)}, f32[2,48,384]{2,1,0:T(8,128)S(1)}, u32[]{:S(2)}, u32[]{:S(2)}) collective-permute-start(f32[2,48,384]{2,1,0:T(8,128)S(1)} %get-tuple-element.64), channel_id=1, source_target_pairs={{0,2},{1,3},{2,0},{3,1},{4,6},{5,7},{6,4},{7,5},{8,10},{9,11},{10,... | collective-permute-start | bytes 442376 | tf_op jit(solution)/shard_map/ppermute | solution.py:498
  38.4 7.2 %collective-permute-start.6 = (f32[2,48,384]{2,1,0:T(8,128)S(1)}, f32[2,48,384]{2,1,0:T(8,128)S(1)}, u32[]{:S(2)}, u32[]{:S(2)}) collective-permute-start(f32[2,48,384]{2,1,0:T(8,128)S(1)} %get-tuple-element.63), channel_id=1, source_target_pairs={{0,6},{1,7},{2,4},{3,5},{4,2},{5,3},{6,0},{7,1},{8,14},{9,15},{10,... | collective-permute-start | bytes 442376 | tf_op jit(solution)/shard_map/ppermute | solution.py:498
  39.6 1.5 %collective-permute-start.7 = (bf16[64,128]{1,0:T(8,128)(2,1)S(1)}, bf16[64,128]{1,0:T(8,128)(2,1)S(1)}, u32[]{:S(2)}, u32[]{:S(2)}) collective-permute-start(bf16[64,128]{1,0:T(8,128)(2,1)S(1)} %get-tuple-element.48), channel_id=1, source_target_pairs={{0,1},{1,0},{2,3},{3,2},{4,5},{5,4},{6,7},{7,6},{8,9},{9,8},{10,11... | collective-permute-start | bytes 49160 | tf_op jit(solution)/shard_map/ppermute | solution.py:606
  45.7 4.8 %collective-permute-start.8 = (f32[48,384]{1,0:T(8,128)S(1)}, f32[48,384]{1,0:T(8,128)S(1)}, u32[]{:S(2)}, u32[]{:S(2)}) collective-permute-start(f32[48,384]{1,0:T(8,128)S(1)} %slice_bitcast_fusion), channel_id=1, source_target_pairs={{0,8},{1,9},{2,10},{3,11},{4,12},{5,13},{6,14},{7,15},{8,0},{9,1},... | collective-permute-start | bytes 221192 | tf_op jit(solution)/shard_map/ppermute | solution.py:498
  50.6 7.6 %collective-permute-start.9 = (f32[48,384]{1,0:T(8,128)S(1)}, f32[48,384]{1,0:T(8,128)S(1)}, u32[]{:S(2)}, u32[]{:S(2)}) collective-permute-start(f32[48,384]{1,0:T(8,128)S(1)} %fusion.first_ref), channel_id=1, source_target_pairs={{0,28},{1,29},{2,30},{3,31},{4,24},{5,25},{6,26},{7,27},{8,20},{9,... | collective-permute-start | bytes 221192 | tf_op jit(solution)/shard_map/ppermute | solution.py:498
  62.1 9.5 %collective-permute-start.10 = (f32[1,8,128]{2,1,0:T(8,128)S(1)}, f32[1,8,128]{2,1,0:T(8,128)S(1)}, u32[]{:S(2)}, u32[]{:S(2)}) collective-permute-start(f32[1,8,128]{2,1,0:T(8,128)S(1)} %bitcast.11), channel_id=1, source_target_pairs={{0,8},{1,9},{2,10},{3,11},{4,12},{5,13},{6,14},{7,15},{8,0},{9,1},... | collective-permute-start | bytes 12296 | tf_op jit(solution)/shard_map/ppermute | solution.py:498
  63.5 11.9 %collective-permute-start.13 = (bf16[64,128]{1,0:T(8,128)(2,1)S(1)}, bf16[64,128]{1,0:T(8,128)(2,1)S(1)}, u32[]{:S(2)}, u32[]{:S(2)}) collective-permute-start(bf16[64,128]{1,0:T(8,128)(2,1)S(1)} %get-tuple-element.56), channel_id=1, source_target_pairs={{1,2},{2,1},{3,4},{4,3},{5,6},{6,5},{7,8},{8,7},{9,10},{10,9},{11,... | collective-permute-start | bytes 49160 | tf_op jit(solution)/shard_map/ppermute | solution.py:621
  71.6 2.6 %collective-permute-start.11 = (f32[2,8,128]{2,1,0:T(8,128)S(1)}, f32[2,8,128]{2,1,0:T(8,128)S(1)}, u32[]{:S(2)}, u32[]{:S(2)}) collective-permute-start(f32[2,8,128]{2,1,0:T(8,128)S(1)} %pad_maximum_fusion.2), channel_id=1, source_target_pairs={{0,4},{1,5},{2,6},{3,7},{4,0},{5,1},{6,2},{7,3},{8,12},{9,13},{10,... | collective-permute-start | bytes 24584 | tf_op jit(solution)/shard_map/ppermute | solution.py:498
  74.2 4.2 %collective-permute-start.12 = (f32[4,8,128]{2,1,0:T(8,128)S(1)}, f32[4,8,128]{2,1,0:T(8,128)S(1)}, u32[]{:S(2)}, u32[]{:S(2)}) collective-permute-start(f32[4,8,128]{2,1,0:T(8,128)S(1)} %pad_maximum_fusion.1), channel_id=1, source_target_pairs={{0,2},{1,3},{2,0},{3,1},{4,6},{5,7},{6,4},{7,5},{8,10},{9,11},{10,... | collective-permute-start | bytes 49160 | tf_op jit(solution)/shard_map/ppermute | solution.py:498
  78.5 1.3 %collective-permute-start.14 = (f32[8,8,128]{2,1,0:T(8,128)S(1)}, f32[8,8,128]{2,1,0:T(8,128)S(1)}, u32[]{:S(2)}, u32[]{:S(2)}) collective-permute-start(f32[8,8,128]{2,1,0:T(8,128)S(1)} %pad_maximum_fusion), channel_id=1, source_target_pairs={{0,1},{1,0},{2,3},{3,2},{4,5},{5,4},{6,7},{7,6},{8,9},{9,8},{10,11... | collective-permute-start | bytes 98312 | tf_op jit(solution)/shard_map/ppermute | solution.py:498
  81.0 3.7 %collective-permute-start.15 = (f32[2,8,128]{2,1,0:T(8,128)S(1)}, f32[2,8,128]{2,1,0:T(8,128)S(1)}, u32[]{:S(2)}, u32[]{:S(2)}) collective-permute-start(f32[2,8,128]{2,1,0:T(8,128)S(1)} %get-tuple-element.61), channel_id=1, source_target_pairs={{0,32},{32,0},{64,96},{96,64},{128,160},{160,128},{192,224},{224,1... | collective-permute-start | bytes 24584 | tf_op jit(solution)/shard_map/ppermute | solution.py:647
  82.0 4.6 %collective-permute-start.16 = (f32[2,8,128]{2,1,0:T(8,128)S(1)}, f32[2,8,128]{2,1,0:T(8,128)S(1)}, u32[]{:S(2)}, u32[]{:S(2)}) collective-permute-start(f32[2,8,128]{2,1,0:T(8,128)S(1)} %get-tuple-element.62), channel_id=1, source_target_pairs={{0,224},{32,64},{64,32},{96,128},{128,96},{160,192},{192,160},{224... | collective-permute-start | bytes 24584 | tf_op jit(solution)/shard_map/ppermute | solution.py:647

commit v11 on v9

--- a/solution.py
+++ b/solution.py
@@ -601,7 +601,7 @@
         compiler_params=limit(8),
         name="edges_out",
     )(sent, kept)
-    moved = [swap(part[2:4], 4), swap(part[4:6], 2), swap(part[6:], 6)]
+    moved = [swap(part[4:6], 2), swap(part[6:], 6), swap(part[2:4], 4)]
     edges = [
         lax.ppermute(value, "rng", pairs)
         for value, pairs in zip(edges, neighbours(32, False))

time: 87.6 us -> 88.1 us (level)
  waiting for transfers between devices: 25.4 us -> 26.7 us
    ppermute x11, starting transfers between devices: 25.1 us -> 24.2 us  [swap(): return lax.ppermute(value, 'rng', [(i, i ^ turn) for i in range(32)])]
  transfers between devices with their start and end apart: 17 -> 17, of which waited for: 11 -> 12; matrix products, arithmetic and copies ran while one was open for 4% -> 4% of each run, Pallas kernels for 11% -> 11%
where the time goes in v11:
time: 88.1 us; the launch traced here: 87.5 us
  starting transfers between devices  40.3 us (46%)
  waiting for transfers between devices  26.7 us (30%)
  Pallas kernels  14.7 us (17%)
  local copies, waits for them, and re-layouts  3.87 us (4%)
  other arithmetic  1.81 us (2%)
    ppermute x11, starting transfers between devices, swap(): return lax.ppermute(value, 'rng', [(i, i ^ turn) for i in range(32)])  24.2 us
    ppermute x11, waiting for transfers between devices, swap(): return lax.ppermute(value, 'rng', [(i, i ^ turn) for i in range(32)])  13.9 us
    ppermute x2, starting transfers between devices, body(): lax.ppermute(value, 'rng', pairs)  8.05 us
    ppermute x1, waiting for transfers between devices, halo_columns(): high = lax.ppermute(echoes, 'az', [(b, a) for a, b in ring])  6.98 us
    ppermute x1, starting transfers between devices, halo_columns(): high = lax.ppermute(echoes, 'az', [(b, a) for a, b in ring])  4.32 us
    pallas_call x1, Pallas kernels, body(): pl.pallas_call(solve_kernel, out_shape=shape(8, LANES), in_specs=[VMEM] *...  3.85 us
    ppermute x2, starting transfers between devices, body(): lax.ppermute(value, 'az', pairs)  3.77 us
    pallas_call x1, Pallas kernels, body(): pl.pallas_call(send_kernel, out_shape=(some, half, shape(OWN_BEAMS, LANES...  3.3 us
  transfers between devices with their start and end apart: 17, of which 12 were waited for; matrix products, arithmetic and copies ran while one was open for 4% of the time, Pallas kernels for 11%

profile of v11, /device:TPU:1, one launch (start us, length us, event | category | flops | bytes accessed | tf_op | source)
XLA Modules:
  0.0 87.5 jit_solution(18370843809987341046)
XLA Ops:
  0.0 4.3 %collective-permute-start = (bf16[2,32,32,128]{3,2,1,0:T(8,128)(2,1)}, bf16[2,32,32,128]{3,2,1,0:T(8,128)(2,1)S(1)}, u32[]{:S(2)}, u32[]{:S(2)}) collective-permute-start(bf16[2,32,32,128]{3,2,1,0:T(8,128)(2,1)} %own_ref.1), channel_id=1, source_target_pairs={{32,0},{64,32},{96,64},{128,96},{160,128},{192,160},{224,192},{0,2... | collective-permute-start | bytes 1572872 | tf_op jit(solution)/shard_map/ppermute | solution.py:504
  4.3 0.7 convert_bitcast_fusion
  5.0 0.1 broadcast_in_dim.19
  5.1 5.6 %collective-permute-start.2 = (f32[8,128]{1,0:T(8,128)S(1)}, f32[8,128]{1,0:T(8,128)S(1)}, u32[]{:S(2)}, u32[]{:S(2)}) collective-permute-start(f32[8,128]{1,0:T(8,128)S(1)} %broadcast_in_dim.19), channel_id=1, source_target_pairs={{0,28},{1,29},{2,30},{3,31},{4,24},{5,25},{6,26},{7,27},{8,20},{9,... | collective-permute-start | bytes 12296 | tf_op jit(solution)/shard_map/ppermute | solution.py:498
  10.6 0.7 copy.14
  11.4 0.8 constant_dynamic-slice_fusion.1
  12.3 0.1 constant_dynamic-slice_fusion
  12.5 0.7 and_select_fusion
  13.2 0.1 pad_maximum_fusion.3.floats_ref
  13.4 0.1 pad_add_fusion.ints_ref
  13.5 1.0 %copy-done.1 = bf16[2,32,32,128]{3,2,1,0:T(8,128)(2,1)S(1)} copy-done((bf16[2,32,32,128]{3,2,1,0:T(8,128)(2,1)S(1)}, bf16[2,32,32,128]{3,2,1,0:T(8,128)(2,1)}, u32[]{:S(2)}) %copy-start.1) | copy-done | bytes 524312
  14.5 0.7 copy-done.2
  15.2 0.7 spectra.2
  16.0 7.0 %collective-permute-done.own_ref = bf16[2,32,32,128]{3,2,1,0:T(8,128)(2,1)S(1)} collective-permute-done((bf16[2,32,32,128]{3,2,1,0:T(8,128)(2,1)}, bf16[2,32,32,128]{3,2,1,0:T(8,128)(2,1)S(1)}, u32[]{:S(2)}, u32[]{:S(2)}) %collective-permute-start) | collective-permute-done | bytes 524320 | tf_op jit(solution)/shard_map/ppermute | solution.py:504
  23.0 0.7 spectra.3
  23.6 2.6 %collective-permute-done.1.low_ref = bf16[2,32,32,128]{3,2,1,0:T(8,128)(2,1)S(1)} collective-permute-done((bf16[2,32,32,128]{3,2,1,0:T(8,128)(2,1)}, bf16[2,32,32,128]{3,2,1,0:T(8,128)(2,1)S(1)}, u32[]{:S(2)}, u32[]{:S(2)}) %collective-permute-start.1) | collective-permute-done | bytes 524320 | tf_op jit(solution)/shard_map/ppermute | solution.py:503
  26.2 3.3 %grams_sent.1 = (bf16[4,2,640,128]{3,2,1,0:T(8,128)(2,1)S(1)}, f32[8,48,384]{2,1,0:T(8,128)S(1)}, f32[8,128]{1,0:T(8,128)S(1)}, f32[96,64,128]{2,1,0:T(8,128)S(1)}) custom-call(s32[8,33]{1,0:T(8,128)S(1)} %pad_add_fusion.ints_ref, f32[8,32]{1,0:T(8,128)S(1)} %pad_maximum_fusion.3.floats_ref, bf16[64,64]{1,0:T(8,128)(2,1)S(1)} %get-tuple-element.35.table_ref, ...), custom_call_target="tpu_custom_call" | custom-call | tf_op jit(solution)/shard_map/grams_sent/pallas_call | solution.py:568
  29.5 1.0 %collective-permute-start.3 = (f32[8,48,384]{2,1,0:T(8,128)S(1)}, f32[8,48,384]{2,1,0:T(8,128)S(1)}, u32[]{:S(2)}, u32[]{:S(2)}) collective-permute-start(f32[8,48,384]{2,1,0:T(8,128)S(1)} %get-tuple-element.38), channel_id=1, source_target_pairs={{0,1},{1,0},{2,3},{3,2},{4,5},{5,4},{6,7},{7,6},{8,9},{9,8},{10,11... | collective-permute-start | bytes 1769480 | tf_op jit(solution)/shard_map/ppermute | solution.py:498
  30.5 3.0 %grams_kept.1 = (bf16[4,2,640,128]{3,2,1,0:T(8,128)(2,1)S(1)}, f32[8,48,384]{2,1,0:T(8,128)S(1)}) custom-call(s32[8,33]{1,0:T(8,128)S(1)} %pad_add_fusion.ints_ref, f32[8,32]{1,0:T(8,128)S(1)} %pad_maximum_fusion.3.floats_ref, f32[96,64,128]{2,1,0:T(8,128)S(1)} %get-tuple-element.39.spec_ref), custom_call_target="tpu_custom_call" | custom-call | tf_op jit(solution)/shard_map/grams_kept/pallas_call | solution.py:583
  33.6 3.2 %collective-permute-start.4 = (f32[2,48,384]{2,1,0:T(8,128)S(1)}, f32[2,48,384]{2,1,0:T(8,128)S(1)}, u32[]{:S(2)}, u32[]{:S(2)}) collective-permute-start(f32[2,48,384]{2,1,0:T(8,128)S(1)} %get-tuple-element.65), channel_id=1, source_target_pairs={{0,2},{1,3},{2,0},{3,1},{4,6},{5,7},{6,4},{7,5},{8,10},{9,11},{10,... | collective-permute-start | bytes 442376 | tf_op jit(solution)/shard_map/ppermute | solution.py:498
  36.8 1.4 %collective-permute-start.5 = (f32[2,48,384]{2,1,0:T(8,128)S(1)}, f32[2,48,384]{2,1,0:T(8,128)S(1)}, u32[]{:S(2)}, u32[]{:S(2)}) collective-permute-start(f32[2,48,384]{2,1,0:T(8,128)S(1)} %get-tuple-element.64), channel_id=1, source_target_pairs={{0,6},{1,7},{2,4},{3,5},{4,2},{5,3},{6,0},{7,1},{8,14},{9,15},{10,... | collective-permute-start | bytes 442376 | tf_op jit(solution)/shard_map/ppermute | solution.py:498
  38.2 0.2 collective-permute-start.6
  38.4 1.2 %edges_out.1 = (bf16[64,128]{1,0:T(8,128)(2,1)S(1)}, bf16[64,128]{1,0:T(8,128)(2,1)S(1)}) custom-call(bf16[4,2,640,128]{3,2,1,0:T(8,128)(2,1)S(1)} %get-tuple-element.46.sent_ref, bf16[4,2,640,128]{3,2,1,0:T(8,128)(2,1)S(1)} %get-tuple-element.47.kept_ref), custom_call_target="tpu_custom_call" | custom-call | tf_op jit(solution)/shard_map/edges_out/pallas_call | solution.py:596
  39.6 0.7 collective-permute-start.7
  40.3 0.8 collective-permute-done.7.first_ref
  41.1 2.1 %collective-permute-done.4 = f32[2,48,384]{2,1,0:T(8,128)S(1)} collective-permute-done((f32[2,48,384]{2,1,0:T(8,128)S(1)}, f32[2,48,384]{2,1,0:T(8,128)S(1)}, u32[]{:S(2)}, u32[]{:S(2)}) %collective-permute-start.4) | collective-permute-done | bytes 147488 | tf_op jit(solution)/shard_map/ppermute | solution.py:498
  43.2 1.1 %collective-permute-done.5 = f32[2,48,384]{2,1,0:T(8,128)S(1)} collective-permute-done((f32[2,48,384]{2,1,0:T(8,128)S(1)}, f32[2,48,384]{2,1,0:T(8,128)S(1)}, u32[]{:S(2)}, u32[]{:S(2)}) %collective-permute-start.5) | collective-permute-done | bytes 147488 | tf_op jit(solution)/shard_map/ppermute | solution.py:498
  44.4 1.3 %collective-permute-done.6 = f32[2,48,384]{2,1,0:T(8,128)S(1)} collective-permute-done((f32[2,48,384]{2,1,0:T(8,128)S(1)}, f32[2,48,384]{2,1,0:T(8,128)S(1)}, u32[]{:S(2)}, u32[]{:S(2)}) %collective-permute-start.6) | collective-permute-done | bytes 147488 | tf_op jit(solution)/shard_map/ppermute | solution.py:498
  45.7 3.1 %collective-permute-start.8 = (f32[48,384]{1,0:T(8,128)S(1)}, f32[48,384]{1,0:T(8,128)S(1)}, u32[]{:S(2)}, u32[]{:S(2)}) collective-permute-start(f32[48,384]{1,0:T(8,128)S(1)} %slice_bitcast_fusion), channel_id=1, source_target_pairs={{0,8},{1,9},{2,10},{3,11},{4,12},{5,13},{6,14},{7,15},{8,0},{9,1},... | collective-permute-start | bytes 221192 | tf_op jit(solution)/shard_map/ppermute | solution.py:498
  48.8 1.8 %collective-permute-done.8 = f32[48,384]{1,0:T(8,128)S(1)} collective-permute-done((f32[48,384]{1,0:T(8,128)S(1)}, f32[48,384]{1,0:T(8,128)S(1)}, u32[]{:S(2)}, u32[]{:S(2)}) %collective-permute-start.8) | collective-permute-done | bytes 73760 | tf_op jit(solution)/shard_map/ppermute | solution.py:498
  50.5 5.2 %collective-permute-start.9 = (f32[48,384]{1,0:T(8,128)S(1)}, f32[48,384]{1,0:T(8,128)S(1)}, u32[]{:S(2)}, u32[]{:S(2)}) collective-permute-start(f32[48,384]{1,0:T(8,128)S(1)} %fusion.first_ref), channel_id=1, source_target_pairs={{0,28},{1,29},{2,30},{3,31},{4,24},{5,25},{6,26},{7,27},{8,20},{9,... | collective-permute-start | bytes 221192 | tf_op jit(solution)/shard_map/ppermute | solution.py:498
  55.7 7.4 %collective-permute-start.10 = (bf16[64,128]{1,0:T(8,128)(2,1)S(1)}, bf16[64,128]{1,0:T(8,128)(2,1)S(1)}, u32[]{:S(2)}, u32[]{:S(2)}) collective-permute-start(bf16[64,128]{1,0:T(8,128)(2,1)S(1)} %get-tuple-element.53), channel_id=1, source_target_pairs={{1,2},{2,1},{3,4},{4,3},{5,6},{6,5},{7,8},{8,7},{9,10},{10,9},{11,... | collective-permute-start | bytes 49160 | tf_op jit(solution)/shard_map/ppermute | solution.py:606
  63.2 3.8 %solve.1 = f32[8,128]{1,0:T(8,128)S(1)} custom-call(f32[48,384]{1,0:T(8,128)S(1)} %fusion.first_ref, f32[48,384]{1,0:T(8,128)S(1)} %collective-permute-done.9.second_ref, f32[8,128]{1,0:T(8,128)S(1)} %get-tuple-element.52.marks_ref), custom_call_target="tpu_custom_call" | custom-call | tf_op jit(solution)/shard_map/solve/pallas_call | solution.py:613
  67.1 1.4 %collective-permute-start.11 = (f32[1,8,128]{2,1,0:T(8,128)S(1)}, f32[1,8,128]{2,1,0:T(8,128)S(1)}, u32[]{:S(2)}, u32[]{:S(2)}) collective-permute-start(f32[1,8,128]{2,1,0:T(8,128)S(1)} %bitcast.11), channel_id=1, source_target_pairs={{0,8},{1,9},{2,10},{3,11},{4,12},{5,13},{6,14},{7,15},{8,0},{9,1},... | collective-permute-start | bytes 12296 | tf_op jit(solution)/shard_map/ppermute | solution.py:498
  68.4 0.2 edges_in.1.edge_ref
  68.7 1.8 %collective-permute-done.11 = f32[1,8,128]{2,1,0:T(8,128)S(1)} collective-permute-done((f32[1,8,128]{2,1,0:T(8,128)S(1)}, f32[1,8,128]{2,1,0:T(8,128)S(1)}, u32[]{:S(2)}, u32[]{:S(2)}) %collective-permute-start.11) | collective-permute-done | bytes 4128 | tf_op jit(solution)/shard_map/ppermute | solution.py:498
  70.5 0.8 collective-permute-start.12
  71.3 1.7 %collective-permute-done.12 = f32[2,8,128]{2,1,0:T(8,128)S(1)} collective-permute-done((f32[2,8,128]{2,1,0:T(8,128)S(1)}, f32[2,8,128]{2,1,0:T(8,128)S(1)}, u32[]{:S(2)}, u32[]{:S(2)}) %collective-permute-start.12) | collective-permute-done | bytes 8224 | tf_op jit(solution)/shard_map/ppermute | solution.py:498
  73.0 0.8 collective-permute-start.13
  73.8 3.3 %collective-permute-done.13 = f32[4,8,128]{2,1,0:T(8,128)S(1)} collective-permute-done((f32[4,8,128]{2,1,0:T(8,128)S(1)}, f32[4,8,128]{2,1,0:T(8,128)S(1)}, u32[]{:S(2)}, u32[]{:S(2)}) %collective-permute-start.13) | collective-permute-done | bytes 16416 | tf_op jit(solution)/shard_map/ppermute | solution.py:498
  77.1 0.1 broadcast_in_dim.22.bins_ref
  77.2 1.5 %collective-permute-start.14 = (f32[8,8,128]{2,1,0:T(8,128)S(1)}, f32[8,8,128]{2,1,0:T(8,128)S(1)}, u32[]{:S(2)}, u32[]{:S(2)}) collective-permute-start(f32[8,8,128]{2,1,0:T(8,128)S(1)} %pad_maximum_fusion), channel_id=1, source_target_pairs={{0,1},{1,0},{2,3},{3,2},{4,5},{5,4},{6,7},{7,6},{8,9},{9,8},{10,11... | collective-permute-start | bytes 98312 | tf_op jit(solution)/shard_map/ppermute | solution.py:498
  78.7 0.9 collective-permute-done.14
  79.6 1.2 %power.1 = (f32[16,8,128]{2,1,0:T(8,128)S(1)}, f32[2,8,128]{2,1,0:T(8,128)S(1)}, f32[2,8,128]{2,1,0:T(8,128)S(1)}) custom-call(s32[16,8,128]{2,1,0:T(8,128)S(1)} %broadcast_in_dim.22.bins_ref, f32[16,8,128]{2,1,0:T(8,128)S(1)} %constant_dynamic-update-slice_fusion.weights_ref, bf16[4,2,640,128]{3,2,1,0:T(8,128)(2,1)S(1)} %get-tuple-element.46.sent_ref, ...), custom_call_target="tpu_custom_call" | custom-call | tf_op jit(solution)/shard_map/power/pallas_call | solution.py:638
  80.8 1.5 %collective-permute-start.15 = (f32[2,8,128]{2,1,0:T(8,128)S(1)}, f32[2,8,128]{2,1,0:T(8,128)S(1)}, u32[]{:S(2)}, u32[]{:S(2)}) collective-permute-start(f32[2,8,128]{2,1,0:T(8,128)S(1)} %get-tuple-element.61), channel_id=1, source_target_pairs={{0,32},{32,0},{64,96},{96,64},{128,160},{160,128},{192,224},{224,1... | collective-permute-start | bytes 24584 | tf_op jit(solution)/shard_map/ppermute | solution.py:648
  82.2 2.3 %collective-permute-start.16 = (f32[2,8,128]{2,1,0:T(8,128)S(1)}, f32[2,8,128]{2,1,0:T(8,128)S(1)}, u32[]{:S(2)}, u32[]{:S(2)}) collective-permute-start(f32[2,8,128]{2,1,0:T(8,128)S(1)} %get-tuple-element.62), channel_id=1, source_target_pairs={{0,224},{32,64},{64,32},{96,128},{128,96},{160,192},{192,160},{224... | collective-permute-start | bytes 24584 | tf_op jit(solution)/shard_map/ppermute | solution.py:648
  84.5 2.3 %collective-permute-done.16.second_ref = f32[2,8,128]{2,1,0:T(8,128)S(1)} collective-permute-done((f32[2,8,128]{2,1,0:T(8,128)S(1)}, f32[2,8,128]{2,1,0:T(8,128)S(1)}, u32[]{:S(2)}, u32[]{:S(2)}) %collective-permute-start.16) | collective-permute-done | bytes 8224 | tf_op jit(solution)/shard_map/ppermute | solution.py:648
  86.9 0.6 smooth.1
  (30 shorter events, 0.7 us)
Async XLA Ops:
  0.0 12.3 %copy-start = (f32[64,16]{0,1:T(8,128)S(1)}, f32[64,16]{0,1:T(8,128)}, u32[]{:S(2)}) copy-start(f32[64,16]{0,1:T(8,128)} %param.11) | copy-start | bytes 12292
  0.0 22.9 %collective-permute-start = (bf16[2,32,32,128]{3,2,1,0:T(8,128)(2,1)}, bf16[2,32,32,128]{3,2,1,0:T(8,128)(2,1)S(1)}, u32[]{:S(2)}, u32[]{:S(2)}) collective-permute-start(bf16[2,32,32,128]{3,2,1,0:T(8,128)(2,1)} %own_ref.1), channel_id=1, source_target_pairs={{32,0},{64,32},{96,64},{128,96},{160,128},{192,160},{224,192},{0,2... | collective-permute-start | bytes 1572872 | tf_op jit(solution)/shard_map/ppermute | solution.py:504
  4.3 21.9 %collective-permute-start.1 = (bf16[2,32,32,128]{3,2,1,0:T(8,128)(2,1)}, bf16[2,32,32,128]{3,2,1,0:T(8,128)(2,1)S(1)}, u32[]{:S(2)}, u32[]{:S(2)}) collective-permute-start(bf16[2,32,32,128]{3,2,1,0:T(8,128)(2,1)} %own_ref.1), channel_id=1, source_target_pairs={{0,32},{32,64},{64,96},{96,128},{128,160},{160,192},{192,224},{224... | collective-permute-start | bytes 1572872 | tf_op jit(solution)/shard_map/ppermute | solution.py:503
  5.1 10.8 %collective-permute-start.2 = (f32[8,128]{1,0:T(8,128)S(1)}, f32[8,128]{1,0:T(8,128)S(1)}, u32[]{:S(2)}, u32[]{:S(2)}) collective-permute-start(f32[8,128]{1,0:T(8,128)S(1)} %broadcast_in_dim.19), channel_id=1, source_target_pairs={{0,28},{1,29},{2,30},{3,31},{4,24},{5,25},{6,26},{7,27},{8,20},{9,... | collective-permute-start | bytes 12296 | tf_op jit(solution)/shard_map/ppermute | solution.py:498
  13.5 1.0 %copy-start.1 = (bf16[2,32,32,128]{3,2,1,0:T(8,128)(2,1)S(1)}, bf16[2,32,32,128]{3,2,1,0:T(8,128)(2,1)}, u32[]{:S(2)}) copy-start(bf16[2,32,32,128]{3,2,1,0:T(8,128)(2,1)} %own_ref.1) | copy-start | bytes 1572868
  14.5 0.7 copy-start.2
  29.5 4.0 %collective-permute-start.3 = (f32[8,48,384]{2,1,0:T(8,128)S(1)}, f32[8,48,384]{2,1,0:T(8,128)S(1)}, u32[]{:S(2)}, u32[]{:S(2)}) collective-permute-start(f32[8,48,384]{2,1,0:T(8,128)S(1)} %get-tuple-element.38), channel_id=1, source_target_pairs={{0,1},{1,0},{2,3},{3,2},{4,5},{5,4},{6,7},{7,6},{8,9},{9,8},{10,11... | collective-permute-start | bytes 1769480 | tf_op jit(solution)/shard_map/ppermute | solution.py:498
  33.6 9.6 %collective-permute-start.4 = (f32[2,48,384]{2,1,0:T(8,128)S(1)}, f32[2,48,384]{2,1,0:T(8,128)S(1)}, u32[]{:S(2)}, u32[]{:S(2)}) collective-permute-start(f32[2,48,384]{2,1,0:T(8,128)S(1)} %get-tuple-element.65), channel_id=1, source_target_pairs={{0,2},{1,3},{2,0},{3,1},{4,6},{5,7},{6,4},{7,5},{8,10},{9,11},{10,... | collective-permute-start | bytes 442376 | tf_op jit(solution)/shard_map/ppermute | solution.py:498
  36.8 7.6 %collective-permute-start.5 = (f32[2,48,384]{2,1,0:T(8,128)S(1)}, f32[2,48,384]{2,1,0:T(8,128)S(1)}, u32[]{:S(2)}, u32[]{:S(2)}) collective-permute-start(f32[2,48,384]{2,1,0:T(8,128)S(1)} %get-tuple-element.64), channel_id=1, source_target_pairs={{0,6},{1,7},{2,4},{3,5},{4,2},{5,3},{6,0},{7,1},{8,14},{9,15},{10,... | collective-permute-start | bytes 442376 | tf_op jit(solution)/shard_map/ppermute | solution.py:498
  38.2 7.4 %collective-permute-start.6 = (f32[2,48,384]{2,1,0:T(8,128)S(1)}, f32[2,48,384]{2,1,0:T(8,128)S(1)}, u32[]{:S(2)}, u32[]{:S(2)}) collective-permute-start(f32[2,48,384]{2,1,0:T(8,128)S(1)} %get-tuple-element.63), channel_id=1, source_target_pairs={{0,4},{1,5},{2,6},{3,7},{4,0},{5,1},{6,2},{7,3},{8,12},{9,13},{10,... | collective-permute-start | bytes 442376 | tf_op jit(solution)/shard_map/ppermute | solution.py:498
  39.6 1.5 %collective-permute-start.7 = (bf16[64,128]{1,0:T(8,128)(2,1)S(1)}, bf16[64,128]{1,0:T(8,128)(2,1)S(1)}, u32[]{:S(2)}, u32[]{:S(2)}) collective-permute-start(bf16[64,128]{1,0:T(8,128)(2,1)S(1)} %get-tuple-element.48), channel_id=1, source_target_pairs={{0,1},{1,0},{2,3},{3,2},{4,5},{5,4},{6,7},{7,6},{8,9},{9,8},{10,11... | collective-permute-start | bytes 49160 | tf_op jit(solution)/shard_map/ppermute | solution.py:606
  45.7 4.8 %collective-permute-start.8 = (f32[48,384]{1,0:T(8,128)S(1)}, f32[48,384]{1,0:T(8,128)S(1)}, u32[]{:S(2)}, u32[]{:S(2)}) collective-permute-start(f32[48,384]{1,0:T(8,128)S(1)} %slice_bitcast_fusion), channel_id=1, source_target_pairs={{0,8},{1,9},{2,10},{3,11},{4,12},{5,13},{6,14},{7,15},{8,0},{9,1},... | collective-permute-start | bytes 221192 | tf_op jit(solution)/shard_map/ppermute | solution.py:498
  50.5 12.7 %collective-permute-start.9 = (f32[48,384]{1,0:T(8,128)S(1)}, f32[48,384]{1,0:T(8,128)S(1)}, u32[]{:S(2)}, u32[]{:S(2)}) collective-permute-start(f32[48,384]{1,0:T(8,128)S(1)} %fusion.first_ref), channel_id=1, source_target_pairs={{0,28},{1,29},{2,30},{3,31},{4,24},{5,25},{6,26},{7,27},{8,20},{9,... | collective-permute-start | bytes 221192 | tf_op jit(solution)/shard_map/ppermute | solution.py:498
  55.7 11.3 %collective-permute-start.10 = (bf16[64,128]{1,0:T(8,128)(2,1)S(1)}, bf16[64,128]{1,0:T(8,128)(2,1)S(1)}, u32[]{:S(2)}, u32[]{:S(2)}) collective-permute-start(bf16[64,128]{1,0:T(8,128)(2,1)S(1)} %get-tuple-element.53), channel_id=1, source_target_pairs={{1,2},{2,1},{3,4},{4,3},{5,6},{6,5},{7,8},{8,7},{9,10},{10,9},{11,... | collective-permute-start | bytes 49160 | tf_op jit(solution)/shard_map/ppermute | solution.py:606
  67.1 3.4 %collective-permute-start.11 = (f32[1,8,128]{2,1,0:T(8,128)S(1)}, f32[1,8,128]{2,1,0:T(8,128)S(1)}, u32[]{:S(2)}, u32[]{:S(2)}) collective-permute-start(f32[1,8,128]{2,1,0:T(8,128)S(1)} %bitcast.11), channel_id=1, source_target_pairs={{0,8},{1,9},{2,10},{3,11},{4,12},{5,13},{6,14},{7,15},{8,0},{9,1},... | collective-permute-start | bytes 12296 | tf_op jit(solution)/shard_map/ppermute | solution.py:498
  70.5 2.5 %collective-permute-start.12 = (f32[2,8,128]{2,1,0:T(8,128)S(1)}, f32[2,8,128]{2,1,0:T(8,128)S(1)}, u32[]{:S(2)}, u32[]{:S(2)}) collective-permute-start(f32[2,8,128]{2,1,0:T(8,128)S(1)} %pad_maximum_fusion.2), channel_id=1, source_target_pairs={{0,4},{1,5},{2,6},{3,7},{4,0},{5,1},{6,2},{7,3},{8,12},{9,13},{10,... | collective-permute-start | bytes 24584 | tf_op jit(solution)/shard_map/ppermute | solution.py:498
  73.0 4.1 %collective-permute-start.13 = (f32[4,8,128]{2,1,0:T(8,128)S(1)}, f32[4,8,128]{2,1,0:T(8,128)S(1)}, u32[]{:S(2)}, u32[]{:S(2)}) collective-permute-start(f32[4,8,128]{2,1,0:T(8,128)S(1)} %pad_maximum_fusion.1), channel_id=1, source_target_pairs={{0,2},{1,3},{2,0},{3,1},{4,6},{5,7},{6,4},{7,5},{8,10},{9,11},{10,... | collective-permute-start | bytes 49160 | tf_op jit(solution)/shard_map/ppermute | solution.py:498
  77.2 2.4 %collective-permute-start.14 = (f32[8,8,128]{2,1,0:T(8,128)S(1)}, f32[8,8,128]{2,1,0:T(8,128)S(1)}, u32[]{:S(2)}, u32[]{:S(2)}) collective-permute-start(f32[8,8,128]{2,1,0:T(8,128)S(1)} %pad_maximum_fusion), channel_id=1, source_target_pairs={{0,1},{1,0},{2,3},{3,2},{4,5},{5,4},{6,7},{7,6},{8,9},{9,8},{10,11... | collective-permute-start | bytes 98312 | tf_op jit(solution)/shard_map/ppermute | solution.py:498
  80.8 3.8 %collective-permute-start.15 = (f32[2,8,128]{2,1,0:T(8,128)S(1)}, f32[2,8,128]{2,1,0:T(8,128)S(1)}, u32[]{:S(2)}, u32[]{:S(2)}) collective-permute-start(f32[2,8,128]{2,1,0:T(8,128)S(1)} %get-tuple-element.61), channel_id=1, source_target_pairs={{0,32},{32,0},{64,96},{96,64},{128,160},{160,128},{192,224},{224,1... | collective-permute-start | bytes 24584 | tf_op jit(solution)/shard_map/ppermute | solution.py:648
  82.2 4.6 %collective-permute-start.16 = (f32[2,8,128]{2,1,0:T(8,128)S(1)}, f32[2,8,128]{2,1,0:T(8,128)S(1)}, u32[]{:S(2)}, u32[]{:S(2)}) collective-permute-start(f32[2,8,128]{2,1,0:T(8,128)S(1)} %get-tuple-element.62), channel_id=1, source_target_pairs={{0,224},{32,64},{64,32},{96,128},{128,96},{160,192},{192,160},{224... | collective-permute-start | bytes 24584 | tf_op jit(solution)/shard_map/ppermute | solution.py:648

commit v12 on v9

--- a/solution.py
+++ b/solution.py
@@ -644,10 +644,11 @@
         compiler_params=limit(12),
         name="power",
     )(centres, weights, sent, kept, edges)
-    rims = [
-        lax.ppermute(value, "az", pairs)
-        for value, pairs in zip(rims, neighbours(8, True))
-    ]
+    nearest, across = neighbours(8, True)
+    second = lax.ppermute(rims[1], "az", across)
+    second, first = lax.optimization_barrier(
+        (second, lax.ppermute(rims[0], "az", nearest))
+    )
     smoothed = pl.pallas_call(
         smooth_kernel,
         out_shape=shape(GROUPS, 8, CELLS),
@@ -655,7 +656,7 @@
         out_specs=VMEM,
         compiler_params=limit(8),
         name="smooth",
-    )(power, *rims)
+    )(power, first, second)
     return smoothed.reshape(OWN_BEAMS, DBINS, CELLS)
 
 

time: 87.6 us -> 87.2 us (level)
  starting transfers between devices: 41.1 us -> 39.9 us
  waiting for transfers between devices: 25.4 us -> 26.4 us
    ppermute x2, starting transfers between devices: 3.76 us -> 2.54 us  [the longest x1 2.54 us: body(): second = lax.ppermute(rims[1], 'az', across)]
    ppermute x2, waiting for transfers between devices: 1.81 us -> 2.79 us  [the longest x1 2.15 us: body(): second = lax.ppermute(rims[1], 'az', across)]
  transfers between devices with their start and end apart: 17 -> 17, of which waited for: 11 -> 12; matrix products, arithmetic and copies ran while one was open for 4% -> 4% of each run, Pallas kernels for 11% -> 11%
where the time goes in v12:
time: 87.2 us; the launch traced here: 86.8 us
  starting transfers between devices  39.9 us (46%)
  waiting for transfers between devices  26.4 us (30%)
  Pallas kernels  14.7 us (17%)
  local copies, waits for them, and re-layouts  3.87 us (4%)
  other arithmetic  1.81 us (2%)
    ppermute x11, starting transfers between devices, swap(): return lax.ppermute(value, 'rng', [(i, i ^ turn) for i in range(32)])  25.1 us
    ppermute x11, waiting for transfers between devices, swap(): return lax.ppermute(value, 'rng', [(i, i ^ turn) for i in range(32)])  13.2 us
    ppermute x2, starting transfers between devices, body(): lax.ppermute(value, 'rng', pairs)  7.87 us
    ppermute x1, waiting for transfers between devices, halo_columns(): high = lax.ppermute(echoes, 'az', [(b, a) for a, b in ring])  6.98 us
    ppermute x1, starting transfers between devices, halo_columns(): high = lax.ppermute(echoes, 'az', [(b, a) for a, b in ring])  4.32 us
    pallas_call x1, Pallas kernels, body(): pl.pallas_call(solve_kernel, out_shape=shape(8, LANES), in_specs=[VMEM] *...  3.85 us
    pallas_call x1, Pallas kernels, body(): pl.pallas_call(send_kernel, out_shape=(some, half, shape(OWN_BEAMS, LANES...  3.31 us
    pallas_call x1, Pallas kernels, body(): pl.pallas_call(keep_kernel, out_shape=(some, half), in_specs=[SMEM] * 2 +...  2.96 us
  transfers between devices with their start and end apart: 17, of which 12 were waited for; matrix products, arithmetic and copies ran while one was open for 4% of the time, Pallas kernels for 11%

profile of v12, /device:TPU:1, one launch (start us, length us, event | category | flops | bytes accessed | tf_op | source)
XLA Modules:
  0.0 86.8 jit_solution(7334603907284157939)
XLA Ops:
  0.0 4.3 %collective-permute-start = (bf16[2,32,32,128]{3,2,1,0:T(8,128)(2,1)}, bf16[2,32,32,128]{3,2,1,0:T(8,128)(2,1)S(1)}, u32[]{:S(2)}, u32[]{:S(2)}) collective-permute-start(bf16[2,32,32,128]{3,2,1,0:T(8,128)(2,1)} %own_ref.1), channel_id=1, source_target_pairs={{32,0},{64,32},{96,64},{128,96},{160,128},{192,160},{224,192},{0,2... | collective-permute-start | bytes 1572872 | tf_op jit(solution)/shard_map/ppermute | solution.py:504
  4.3 0.7 convert_bitcast_fusion
  5.0 0.1 broadcast_in_dim.19
  5.1 5.6 %collective-permute-start.2 = (f32[8,128]{1,0:T(8,128)S(1)}, f32[8,128]{1,0:T(8,128)S(1)}, u32[]{:S(2)}, u32[]{:S(2)}) collective-permute-start(f32[8,128]{1,0:T(8,128)S(1)} %broadcast_in_dim.19), channel_id=1, source_target_pairs={{0,28},{1,29},{2,30},{3,31},{4,24},{5,25},{6,26},{7,27},{8,20},{9,... | collective-permute-start | bytes 12296 | tf_op jit(solution)/shard_map/ppermute | solution.py:498
  10.6 0.7 copy.14
  11.4 0.8 constant_dynamic-slice_fusion.1
  12.3 0.1 constant_dynamic-slice_fusion
  12.4 0.1 copy.18
  12.5 0.7 and_select_fusion
  13.2 0.1 pad_maximum_fusion.3.floats_ref
  13.4 0.1 pad_add_fusion.ints_ref
  13.5 1.0 %copy-done.1 = bf16[2,32,32,128]{3,2,1,0:T(8,128)(2,1)S(1)} copy-done((bf16[2,32,32,128]{3,2,1,0:T(8,128)(2,1)S(1)}, bf16[2,32,32,128]{3,2,1,0:T(8,128)(2,1)}, u32[]{:S(2)}) %copy-start.1) | copy-done | bytes 524312
  14.5 0.7 copy-done.2
  15.2 0.7 spectra.2
  15.9 0.1 broadcast_add_fusion.marks_ref
  16.0 7.0 %collective-permute-done.own_ref = bf16[2,32,32,128]{3,2,1,0:T(8,128)(2,1)S(1)} collective-permute-done((bf16[2,32,32,128]{3,2,1,0:T(8,128)(2,1)}, bf16[2,32,32,128]{3,2,1,0:T(8,128)(2,1)S(1)}, u32[]{:S(2)}, u32[]{:S(2)}) %collective-permute-start) | collective-permute-done | bytes 524320 | tf_op jit(solution)/shard_map/ppermute | solution.py:504
  23.0 0.7 spectra.3
  23.6 2.6 %collective-permute-done.1.low_ref = bf16[2,32,32,128]{3,2,1,0:T(8,128)(2,1)S(1)} collective-permute-done((bf16[2,32,32,128]{3,2,1,0:T(8,128)(2,1)}, bf16[2,32,32,128]{3,2,1,0:T(8,128)(2,1)S(1)}, u32[]{:S(2)}, u32[]{:S(2)}) %collective-permute-start.1) | collective-permute-done | bytes 524320 | tf_op jit(solution)/shard_map/ppermute | solution.py:503
  26.2 3.3 %grams_sent.1 = (bf16[4,2,640,128]{3,2,1,0:T(8,128)(2,1)S(1)}, f32[8,48,384]{2,1,0:T(8,128)S(1)}, f32[8,128]{1,0:T(8,128)S(1)}, f32[96,64,128]{2,1,0:T(8,128)S(1)}) custom-call(s32[8,33]{1,0:T(8,128)S(1)} %pad_add_fusion.ints_ref, f32[8,32]{1,0:T(8,128)S(1)} %pad_maximum_fusion.3.floats_ref, bf16[64,64]{1,0:T(8,128)(2,1)S(1)} %get-tuple-element.37.table_ref, ...), custom_call_target="tpu_custom_call" | custom-call | tf_op jit(solution)/shard_map/grams_sent/pallas_call | solution.py:568
  29.5 1.0 %collective-permute-start.3 = (f32[8,48,384]{2,1,0:T(8,128)S(1)}, f32[8,48,384]{2,1,0:T(8,128)S(1)}, u32[]{:S(2)}, u32[]{:S(2)}) collective-permute-start(f32[8,48,384]{2,1,0:T(8,128)S(1)} %get-tuple-element.40), channel_id=1, source_target_pairs={{0,1},{1,0},{2,3},{3,2},{4,5},{5,4},{6,7},{7,6},{8,9},{9,8},{10,11... | collective-permute-start | bytes 1769480 | tf_op jit(solution)/shard_map/ppermute | solution.py:498
  30.5 3.0 %grams_kept.1 = (bf16[4,2,640,128]{3,2,1,0:T(8,128)(2,1)S(1)}, f32[8,48,384]{2,1,0:T(8,128)S(1)}) custom-call(s32[8,33]{1,0:T(8,128)S(1)} %pad_add_fusion.ints_ref, f32[8,32]{1,0:T(8,128)S(1)} %pad_maximum_fusion.3.floats_ref, f32[96,64,128]{2,1,0:T(8,128)S(1)} %get-tuple-element.41.spec_ref), custom_call_target="tpu_custom_call" | custom-call | tf_op jit(solution)/shard_map/grams_kept/pallas_call | solution.py:583
  33.6 1.9 %collective-permute-start.4 = (f32[2,48,384]{2,1,0:T(8,128)S(1)}, f32[2,48,384]{2,1,0:T(8,128)S(1)}, u32[]{:S(2)}, u32[]{:S(2)}) collective-permute-start(f32[2,48,384]{2,1,0:T(8,128)S(1)} %get-tuple-element.69), channel_id=1, source_target_pairs={{0,4},{1,5},{2,6},{3,7},{4,0},{5,1},{6,2},{7,3},{8,12},{9,13},{10,... | collective-permute-start | bytes 442376 | tf_op jit(solution)/shard_map/ppermute | solution.py:498
  35.5 2.9 %collective-permute-start.5 = (f32[2,48,384]{2,1,0:T(8,128)S(1)}, f32[2,48,384]{2,1,0:T(8,128)S(1)}, u32[]{:S(2)}, u32[]{:S(2)}) collective-permute-start(f32[2,48,384]{2,1,0:T(8,128)S(1)} %get-tuple-element.68), channel_id=1, source_target_pairs={{0,2},{1,3},{2,0},{3,1},{4,6},{5,7},{6,4},{7,5},{8,10},{9,11},{10,... | collective-permute-start | bytes 442376 | tf_op jit(solution)/shard_map/ppermute | solution.py:498
  38.4 1.2 %edges_out.1 = (bf16[64,128]{1,0:T(8,128)(2,1)S(1)}, bf16[64,128]{1,0:T(8,128)(2,1)S(1)}) custom-call(bf16[4,2,640,128]{3,2,1,0:T(8,128)(2,1)S(1)} %get-tuple-element.48.sent_ref, bf16[4,2,640,128]{3,2,1,0:T(8,128)(2,1)S(1)} %get-tuple-element.49.kept_ref), custom_call_target="tpu_custom_call" | custom-call | tf_op jit(solution)/shard_map/edges_out/pallas_call | solution.py:596
  39.6 0.7 collective-permute-start.7
  40.3 0.8 collective-permute-done.7.first_ref
  41.1 3.4 %collective-permute-done.5 = f32[2,48,384]{2,1,0:T(8,128)S(1)} collective-permute-done((f32[2,48,384]{2,1,0:T(8,128)S(1)}, f32[2,48,384]{2,1,0:T(8,128)S(1)}, u32[]{:S(2)}, u32[]{:S(2)}) %collective-permute-start.5) | collective-permute-done | bytes 147488 | tf_op jit(solution)/shard_map/ppermute | solution.py:498
  44.5 1.1 %collective-permute-done.6 = f32[2,48,384]{2,1,0:T(8,128)S(1)} collective-permute-done((f32[2,48,384]{2,1,0:T(8,128)S(1)}, f32[2,48,384]{2,1,0:T(8,128)S(1)}, u32[]{:S(2)}, u32[]{:S(2)}) %collective-permute-start.6) | collective-permute-done | bytes 147488 | tf_op jit(solution)/shard_map/ppermute | solution.py:498
  45.7 3.1 %collective-permute-start.8 = (f32[48,384]{1,0:T(8,128)S(1)}, f32[48,384]{1,0:T(8,128)S(1)}, u32[]{:S(2)}, u32[]{:S(2)}) collective-permute-start(f32[48,384]{1,0:T(8,128)S(1)} %slice_bitcast_fusion), channel_id=1, source_target_pairs={{0,8},{1,9},{2,10},{3,11},{4,12},{5,13},{6,14},{7,15},{8,0},{9,1},... | collective-permute-start | bytes 221192 | tf_op jit(solution)/shard_map/ppermute | solution.py:498
  48.8 1.7 %collective-permute-done.8 = f32[48,384]{1,0:T(8,128)S(1)} collective-permute-done((f32[48,384]{1,0:T(8,128)S(1)}, f32[48,384]{1,0:T(8,128)S(1)}, u32[]{:S(2)}, u32[]{:S(2)}) %collective-permute-start.8) | collective-permute-done | bytes 73760 | tf_op jit(solution)/shard_map/ppermute | solution.py:498
  50.6 4.9 %collective-permute-start.9 = (f32[48,384]{1,0:T(8,128)S(1)}, f32[48,384]{1,0:T(8,128)S(1)}, u32[]{:S(2)}, u32[]{:S(2)}) collective-permute-start(f32[48,384]{1,0:T(8,128)S(1)} %fusion.first_ref), channel_id=1, source_target_pairs={{0,28},{1,29},{2,30},{3,31},{4,24},{5,25},{6,26},{7,27},{8,20},{9,... | collective-permute-start | bytes 221192 | tf_op jit(solution)/shard_map/ppermute | solution.py:498
  55.4 7.2 %collective-permute-start.10 = (bf16[64,128]{1,0:T(8,128)(2,1)S(1)}, bf16[64,128]{1,0:T(8,128)(2,1)S(1)}, u32[]{:S(2)}, u32[]{:S(2)}) collective-permute-start(bf16[64,128]{1,0:T(8,128)(2,1)S(1)} %get-tuple-element.55), channel_id=1, source_target_pairs={{1,2},{2,1},{3,4},{4,3},{5,6},{6,5},{7,8},{8,7},{9,10},{10,9},{11,... | collective-permute-start | bytes 49160 | tf_op jit(solution)/shard_map/ppermute | solution.py:606
  62.7 3.8 %solve.1 = f32[8,128]{1,0:T(8,128)S(1)} custom-call(f32[48,384]{1,0:T(8,128)S(1)} %fusion.first_ref, f32[48,384]{1,0:T(8,128)S(1)} %collective-permute-done.9.second_ref, f32[8,128]{1,0:T(8,128)S(1)} %get-tuple-element.54.marks_ref), custom_call_target="tpu_custom_call" | custom-call | tf_op jit(solution)/shard_map/solve/pallas_call | solution.py:613
  66.6 1.4 %collective-permute-start.11 = (f32[1,8,128]{2,1,0:T(8,128)S(1)}, f32[1,8,128]{2,1,0:T(8,128)S(1)}, u32[]{:S(2)}, u32[]{:S(2)}) collective-permute-start(f32[1,8,128]{2,1,0:T(8,128)S(1)} %bitcast.11), channel_id=1, source_target_pairs={{0,8},{1,9},{2,10},{3,11},{4,12},{5,13},{6,14},{7,15},{8,0},{9,1},... | collective-permute-start | bytes 12296 | tf_op jit(solution)/shard_map/ppermute | solution.py:498
  68.0 0.2 edges_in.1.edge_ref
  68.2 1.8 %collective-permute-done.11 = f32[1,8,128]{2,1,0:T(8,128)S(1)} collective-permute-done((f32[1,8,128]{2,1,0:T(8,128)S(1)}, f32[1,8,128]{2,1,0:T(8,128)S(1)}, u32[]{:S(2)}, u32[]{:S(2)}) %collective-permute-start.11) | collective-permute-done | bytes 4128 | tf_op jit(solution)/shard_map/ppermute | solution.py:498
  70.0 0.9 collective-permute-start.12
  70.9 1.6 %collective-permute-done.12 = f32[2,8,128]{2,1,0:T(8,128)S(1)} collective-permute-done((f32[2,8,128]{2,1,0:T(8,128)S(1)}, f32[2,8,128]{2,1,0:T(8,128)S(1)}, u32[]{:S(2)}, u32[]{:S(2)}) %collective-permute-start.12) | collective-permute-done | bytes 8224 | tf_op jit(solution)/shard_map/ppermute | solution.py:498
  72.5 1.5 %collective-permute-start.13 = (f32[4,8,128]{2,1,0:T(8,128)S(1)}, f32[4,8,128]{2,1,0:T(8,128)S(1)}, u32[]{:S(2)}, u32[]{:S(2)}) collective-permute-start(f32[4,8,128]{2,1,0:T(8,128)S(1)} %pad_maximum_fusion.1), channel_id=1, source_target_pairs={{0,2},{1,3},{2,0},{3,1},{4,6},{5,7},{6,4},{7,5},{8,10},{9,11},{10,... | collective-permute-start | bytes 49160 | tf_op jit(solution)/shard_map/ppermute | solution.py:498
  74.1 2.6 %collective-permute-done.13 = f32[4,8,128]{2,1,0:T(8,128)S(1)} collective-permute-done((f32[4,8,128]{2,1,0:T(8,128)S(1)}, f32[4,8,128]{2,1,0:T(8,128)S(1)}, u32[]{:S(2)}, u32[]{:S(2)}) %collective-permute-start.13) | collective-permute-done | bytes 16416 | tf_op jit(solution)/shard_map/ppermute | solution.py:498
  76.6 0.1 broadcast_in_dim.22.bins_ref
  76.7 2.0 %collective-permute-start.14 = (f32[8,8,128]{2,1,0:T(8,128)S(1)}, f32[8,8,128]{2,1,0:T(8,128)S(1)}, u32[]{:S(2)}, u32[]{:S(2)}) collective-permute-start(f32[8,8,128]{2,1,0:T(8,128)S(1)} %pad_maximum_fusion), channel_id=1, source_target_pairs={{0,1},{1,0},{2,3},{3,2},{4,5},{5,4},{6,7},{7,6},{8,9},{9,8},{10,11... | collective-permute-start | bytes 98312 | tf_op jit(solution)/shard_map/ppermute | solution.py:498
  78.8 0.9 collective-permute-done.14
  79.6 1.2 %power.1 = (f32[16,8,128]{2,1,0:T(8,128)S(1)}, f32[2,8,128]{2,1,0:T(8,128)S(1)}, f32[2,8,128]{2,1,0:T(8,128)S(1)}) custom-call(s32[16,8,128]{2,1,0:T(8,128)S(1)} %broadcast_in_dim.22.bins_ref, f32[16,8,128]{2,1,0:T(8,128)S(1)} %constant_dynamic-update-slice_fusion.weights_ref, bf16[4,2,640,128]{3,2,1,0:T(8,128)(2,1)S(1)} %get-tuple-element.48.sent_ref, ...), custom_call_target="tpu_custom_call" | custom-call | tf_op jit(solution)/shard_map/power/pallas_call | solution.py:638
  80.8 2.5 %collective-permute-start.15 = (f32[2,8,128]{2,1,0:T(8,128)S(1)}, f32[2,8,128]{2,1,0:T(8,128)S(1)}, u32[]{:S(2)}, u32[]{:S(2)}) collective-permute-start(f32[2,8,128]{2,1,0:T(8,128)S(1)} %get-tuple-element.63), channel_id=1, source_target_pairs={{0,224},{32,64},{64,32},{96,128},{128,96},{160,192},{192,160},{224... | collective-permute-start | bytes 24584 | tf_op jit(solution)/shard_map/ppermute | solution.py:648
  83.3 2.2 %collective-permute-done.15.second_ref = f32[2,8,128]{2,1,0:T(8,128)S(1)} collective-permute-done((f32[2,8,128]{2,1,0:T(8,128)S(1)}, f32[2,8,128]{2,1,0:T(8,128)S(1)}, u32[]{:S(2)}, u32[]{:S(2)}) %collective-permute-start.15) | collective-permute-done | bytes 8224 | tf_op jit(solution)/shard_map/ppermute | solution.py:648
  85.5 0.6 collective-permute-done.16.first_ref
  86.1 0.6 smooth.1
  (30 shorter events, 0.5 us)
Async XLA Ops:
  0.0 12.3 %copy-start = (f32[64,16]{0,1:T(8,128)S(1)}, f32[64,16]{0,1:T(8,128)}, u32[]{:S(2)}) copy-start(f32[64,16]{0,1:T(8,128)} %param.11) | copy-start | bytes 12292
  0.0 22.9 %collective-permute-start = (bf16[2,32,32,128]{3,2,1,0:T(8,128)(2,1)}, bf16[2,32,32,128]{3,2,1,0:T(8,128)(2,1)S(1)}, u32[]{:S(2)}, u32[]{:S(2)}) collective-permute-start(bf16[2,32,32,128]{3,2,1,0:T(8,128)(2,1)} %own_ref.1), channel_id=1, source_target_pairs={{32,0},{64,32},{96,64},{128,96},{160,128},{192,160},{224,192},{0,2... | collective-permute-start | bytes 1572872 | tf_op jit(solution)/shard_map/ppermute | solution.py:504
  4.3 21.9 %collective-permute-start.1 = (bf16[2,32,32,128]{3,2,1,0:T(8,128)(2,1)}, bf16[2,32,32,128]{3,2,1,0:T(8,128)(2,1)S(1)}, u32[]{:S(2)}, u32[]{:S(2)}) collective-permute-start(bf16[2,32,32,128]{3,2,1,0:T(8,128)(2,1)} %own_ref.1), channel_id=1, source_target_pairs={{0,32},{32,64},{64,96},{96,128},{128,160},{160,192},{192,224},{224... | collective-permute-start | bytes 1572872 | tf_op jit(solution)/shard_map/ppermute | solution.py:503
  5.1 10.8 %collective-permute-start.2 = (f32[8,128]{1,0:T(8,128)S(1)}, f32[8,128]{1,0:T(8,128)S(1)}, u32[]{:S(2)}, u32[]{:S(2)}) collective-permute-start(f32[8,128]{1,0:T(8,128)S(1)} %broadcast_in_dim.19), channel_id=1, source_target_pairs={{0,28},{1,29},{2,30},{3,31},{4,24},{5,25},{6,26},{7,27},{8,20},{9,... | collective-permute-start | bytes 12296 | tf_op jit(solution)/shard_map/ppermute | solution.py:498
  13.5 1.0 %copy-start.1 = (bf16[2,32,32,128]{3,2,1,0:T(8,128)(2,1)S(1)}, bf16[2,32,32,128]{3,2,1,0:T(8,128)(2,1)}, u32[]{:S(2)}) copy-start(bf16[2,32,32,128]{3,2,1,0:T(8,128)(2,1)} %own_ref.1) | copy-start | bytes 1572868
  14.5 0.7 copy-start.2
  29.5 3.9 %collective-permute-start.3 = (f32[8,48,384]{2,1,0:T(8,128)S(1)}, f32[8,48,384]{2,1,0:T(8,128)S(1)}, u32[]{:S(2)}, u32[]{:S(2)}) collective-permute-start(f32[8,48,384]{2,1,0:T(8,128)S(1)} %get-tuple-element.40), channel_id=1, source_target_pairs={{0,1},{1,0},{2,3},{3,2},{4,5},{5,4},{6,7},{7,6},{8,9},{9,8},{10,11... | collective-permute-start | bytes 1769480 | tf_op jit(solution)/shard_map/ppermute | solution.py:498
  33.6 7.5 %collective-permute-start.4 = (f32[2,48,384]{2,1,0:T(8,128)S(1)}, f32[2,48,384]{2,1,0:T(8,128)S(1)}, u32[]{:S(2)}, u32[]{:S(2)}) collective-permute-start(f32[2,48,384]{2,1,0:T(8,128)S(1)} %get-tuple-element.69), channel_id=1, source_target_pairs={{0,4},{1,5},{2,6},{3,7},{4,0},{5,1},{6,2},{7,3},{8,12},{9,13},{10,... | collective-permute-start | bytes 442376 | tf_op jit(solution)/shard_map/ppermute | solution.py:498
  35.5 9.0 %collective-permute-start.5 = (f32[2,48,384]{2,1,0:T(8,128)S(1)}, f32[2,48,384]{2,1,0:T(8,128)S(1)}, u32[]{:S(2)}, u32[]{:S(2)}) collective-permute-start(f32[2,48,384]{2,1,0:T(8,128)S(1)} %get-tuple-element.68), channel_id=1, source_target_pairs={{0,2},{1,3},{2,0},{3,1},{4,6},{5,7},{6,4},{7,5},{8,10},{9,11},{10,... | collective-permute-start | bytes 442376 | tf_op jit(solution)/shard_map/ppermute | solution.py:498
  38.4 7.2 %collective-permute-start.6 = (f32[2,48,384]{2,1,0:T(8,128)S(1)}, f32[2,48,384]{2,1,0:T(8,128)S(1)}, u32[]{:S(2)}, u32[]{:S(2)}) collective-permute-start(f32[2,48,384]{2,1,0:T(8,128)S(1)} %get-tuple-element.67), channel_id=1, source_target_pairs={{0,6},{1,7},{2,4},{3,5},{4,2},{5,3},{6,0},{7,1},{8,14},{9,15},{10,... | collective-permute-start | bytes 442376 | tf_op jit(solution)/shard_map/ppermute | solution.py:498
  39.6 1.5 %collective-permute-start.7 = (bf16[64,128]{1,0:T(8,128)(2,1)S(1)}, bf16[64,128]{1,0:T(8,128)(2,1)S(1)}, u32[]{:S(2)}, u32[]{:S(2)}) collective-permute-start(bf16[64,128]{1,0:T(8,128)(2,1)S(1)} %get-tuple-element.50), channel_id=1, source_target_pairs={{0,1},{1,0},{2,3},{3,2},{4,5},{5,4},{6,7},{7,6},{8,9},{9,8},{10,11... | collective-permute-start | bytes 49160 | tf_op jit(solution)/shard_map/ppermute | solution.py:606
  45.7 4.8 %collective-permute-start.8 = (f32[48,384]{1,0:T(8,128)S(1)}, f32[48,384]{1,0:T(8,128)S(1)}, u32[]{:S(2)}, u32[]{:S(2)}) collective-permute-start(f32[48,384]{1,0:T(8,128)S(1)} %slice_bitcast_fusion), channel_id=1, source_target_pairs={{0,8},{1,9},{2,10},{3,11},{4,12},{5,13},{6,14},{7,15},{8,0},{9,1},... | collective-permute-start | bytes 221192 | tf_op jit(solution)/shard_map/ppermute | solution.py:498
  50.6 12.2 %collective-permute-start.9 = (f32[48,384]{1,0:T(8,128)S(1)}, f32[48,384]{1,0:T(8,128)S(1)}, u32[]{:S(2)}, u32[]{:S(2)}) collective-permute-start(f32[48,384]{1,0:T(8,128)S(1)} %fusion.first_ref), channel_id=1, source_target_pairs={{0,28},{1,29},{2,30},{3,31},{4,24},{5,25},{6,26},{7,27},{8,20},{9,... | collective-permute-start | bytes 221192 | tf_op jit(solution)/shard_map/ppermute | solution.py:498
  55.4 11.1 %collective-permute-start.10 = (bf16[64,128]{1,0:T(8,128)(2,1)S(1)}, bf16[64,128]{1,0:T(8,128)(2,1)S(1)}, u32[]{:S(2)}, u32[]{:S(2)}) collective-permute-start(bf16[64,128]{1,0:T(8,128)(2,1)S(1)} %get-tuple-element.55), channel_id=1, source_target_pairs={{1,2},{2,1},{3,4},{4,3},{5,6},{6,5},{7,8},{8,7},{9,10},{10,9},{11,... | collective-permute-start | bytes 49160 | tf_op jit(solution)/shard_map/ppermute | solution.py:606
  66.6 3.4 %collective-permute-start.11 = (f32[1,8,128]{2,1,0:T(8,128)S(1)}, f32[1,8,128]{2,1,0:T(8,128)S(1)}, u32[]{:S(2)}, u32[]{:S(2)}) collective-permute-start(f32[1,8,128]{2,1,0:T(8,128)S(1)} %bitcast.11), channel_id=1, source_target_pairs={{0,8},{1,9},{2,10},{3,11},{4,12},{5,13},{6,14},{7,15},{8,0},{9,1},... | collective-permute-start | bytes 12296 | tf_op jit(solution)/shard_map/ppermute | solution.py:498
  70.0 2.5 %collective-permute-start.12 = (f32[2,8,128]{2,1,0:T(8,128)S(1)}, f32[2,8,128]{2,1,0:T(8,128)S(1)}, u32[]{:S(2)}, u32[]{:S(2)}) collective-permute-start(f32[2,8,128]{2,1,0:T(8,128)S(1)} %pad_maximum_fusion.2), channel_id=1, source_target_pairs={{0,4},{1,5},{2,6},{3,7},{4,0},{5,1},{6,2},{7,3},{8,12},{9,13},{10,... | collective-permute-start | bytes 24584 | tf_op jit(solution)/shard_map/ppermute | solution.py:498
  72.5 4.1 %collective-permute-start.13 = (f32[4,8,128]{2,1,0:T(8,128)S(1)}, f32[4,8,128]{2,1,0:T(8,128)S(1)}, u32[]{:S(2)}, u32[]{:S(2)}) collective-permute-start(f32[4,8,128]{2,1,0:T(8,128)S(1)} %pad_maximum_fusion.1), channel_id=1, source_target_pairs={{0,2},{1,3},{2,0},{3,1},{4,6},{5,7},{6,4},{7,5},{8,10},{9,11},{10,... | collective-permute-start | bytes 49160 | tf_op jit(solution)/shard_map/ppermute | solution.py:498
  76.7 2.9 %collective-permute-start.14 = (f32[8,8,128]{2,1,0:T(8,128)S(1)}, f32[8,8,128]{2,1,0:T(8,128)S(1)}, u32[]{:S(2)}, u32[]{:S(2)}) collective-permute-start(f32[8,8,128]{2,1,0:T(8,128)S(1)} %pad_maximum_fusion), channel_id=1, source_target_pairs={{0,1},{1,0},{2,3},{3,2},{4,5},{5,4},{6,7},{7,6},{8,9},{9,8},{10,11... | collective-permute-start | bytes 98312 | tf_op jit(solution)/shard_map/ppermute | solution.py:498
  80.8 4.7 %collective-permute-start.15 = (f32[2,8,128]{2,1,0:T(8,128)S(1)}, f32[2,8,128]{2,1,0:T(8,128)S(1)}, u32[]{:S(2)}, u32[]{:S(2)}) collective-permute-start(f32[2,8,128]{2,1,0:T(8,128)S(1)} %get-tuple-element.63), channel_id=1, source_target_pairs={{0,224},{32,64},{64,32},{96,128},{128,96},{160,192},{192,160},{224... | collective-permute-start | bytes 24584 | tf_op jit(solution)/shard_map/ppermute | solution.py:648
  83.3 2.8 %collective-permute-start.16 = (f32[2,8,128]{2,1,0:T(8,128)S(1)}, f32[2,8,128]{2,1,0:T(8,128)S(1)}, u32[]{:S(2)}, u32[]{:S(2)}) collective-permute-start(f32[2,8,128]{2,1,0:T(8,128)S(1)} %get-tuple-element.64), channel_id=1, source_target_pairs={{0,32},{32,0},{64,96},{96,64},{128,160},{160,128},{192,224},{224,1... | collective-permute-start | bytes 24584 | tf_op jit(solution)/shard_map/ppermute | solution.py:650

commit v13 on v12

--- a/solution.py
+++ b/solution.py
@@ -601,7 +601,7 @@
         compiler_params=limit(8),
         name="edges_out",
     )(sent, kept)
-    moved = [swap(part[2:4], 4), swap(part[4:6], 2), swap(part[6:], 6)]
+    moved = [swap(part[4:6], 2), swap(part[6:], 6), swap(part[2:4], 4)]
     edges = [
         lax.ppermute(value, "rng", pairs)
         for value, pairs in zip(edges, neighbours(32, False))

time: 87.2 us -> 87.6 us (level)
    ppermute x11, starting transfers between devices: 25.1 us -> 24.1 us  [swap(): return lax.ppermute(value, 'rng', [(i, i ^ turn) for i in range(32)])]
  transfers between devices with their start and end apart: 17 -> 17, of which waited for: 12 -> 13; matrix products, arithmetic and copies ran while one was open for 4% -> 4% of each run, Pallas kernels for 11% -> 11%
where the time goes in v13:
time: 87.6 us; the launch traced here: 87.2 us
  starting transfers between devices  39.5 us (45%)
  waiting for transfers between devices  27.2 us (31%)
  Pallas kernels  14.7 us (17%)
  local copies, waits for them, and re-layouts  3.87 us (4%)
  other arithmetic  1.81 us (2%)
    ppermute x11, starting transfers between devices, swap(): return lax.ppermute(value, 'rng', [(i, i ^ turn) for i in range(32)])  24.1 us
    ppermute x11, waiting for transfers between devices, swap(): return lax.ppermute(value, 'rng', [(i, i ^ turn) for i in range(32)])  14 us
    ppermute x2, starting transfers between devices, body(): lax.ppermute(value, 'rng', pairs)  8.03 us
    ppermute x1, waiting for transfers between devices, halo_columns(): high = lax.ppermute(echoes, 'az', [(b, a) for a, b in ring])  6.98 us
    ppermute x1, starting transfers between devices, halo_columns(): high = lax.ppermute(echoes, 'az', [(b, a) for a, b in ring])  4.32 us
    pallas_call x1, Pallas kernels, body(): pl.pallas_call(solve_kernel, out_shape=shape(8, LANES), in_specs=[VMEM] *...  3.85 us
    pallas_call x1, Pallas kernels, body(): pl.pallas_call(send_kernel, out_shape=(some, half, shape(OWN_BEAMS, LANES...  3.3 us
    ppermute x1, starting transfers between devices, body(): second = lax.ppermute(rims[1], 'az', across)  3.04 us
  transfers between devices with their start and end apart: 17, of which 13 were waited for; matrix products, arithmetic and copies ran while one was open for 4% of the time, Pallas kernels for 11%

profile of v13, /device:TPU:1, one launch (start us, length us, event | category | flops | bytes accessed | tf_op | source)
XLA Modules:
  0.0 87.2 jit_solution(12843082816786449633)
XLA Ops:
  0.0 4.3 %collective-permute-start = (bf16[2,32,32,128]{3,2,1,0:T(8,128)(2,1)}, bf16[2,32,32,128]{3,2,1,0:T(8,128)(2,1)S(1)}, u32[]{:S(2)}, u32[]{:S(2)}) collective-permute-start(bf16[2,32,32,128]{3,2,1,0:T(8,128)(2,1)} %own_ref.1), channel_id=1, source_target_pairs={{32,0},{64,32},{96,64},{128,96},{160,128},{192,160},{224,192},{0,2... | collective-permute-start | bytes 1572872 | tf_op jit(solution)/shard_map/ppermute | solution.py:504
  4.3 0.7 convert_bitcast_fusion
  5.0 0.1 broadcast_in_dim.19
  5.1 5.6 %collective-permute-start.2 = (f32[8,128]{1,0:T(8,128)S(1)}, f32[8,128]{1,0:T(8,128)S(1)}, u32[]{:S(2)}, u32[]{:S(2)}) collective-permute-start(f32[8,128]{1,0:T(8,128)S(1)} %broadcast_in_dim.19), channel_id=1, source_target_pairs={{0,28},{1,29},{2,30},{3,31},{4,24},{5,25},{6,26},{7,27},{8,20},{9,... | collective-permute-start | bytes 12296 | tf_op jit(solution)/shard_map/ppermute | solution.py:498
  10.6 0.7 copy.14
  11.4 0.8 constant_dynamic-slice_fusion.1
  12.3 0.1 constant_dynamic-slice_fusion
  12.5 0.7 and_select_fusion
  13.2 0.1 pad_maximum_fusion.3.floats_ref
  13.4 0.1 pad_add_fusion.ints_ref
  13.5 1.0 %copy-done.1 = bf16[2,32,32,128]{3,2,1,0:T(8,128)(2,1)S(1)} copy-done((bf16[2,32,32,128]{3,2,1,0:T(8,128)(2,1)S(1)}, bf16[2,32,32,128]{3,2,1,0:T(8,128)(2,1)}, u32[]{:S(2)}) %copy-start.1) | copy-done | bytes 524312
  14.5 0.7 copy-done.2
  15.2 0.7 spectra.2
  16.0 7.0 %collective-permute-done.own_ref = bf16[2,32,32,128]{3,2,1,0:T(8,128)(2,1)S(1)} collective-permute-done((bf16[2,32,32,128]{3,2,1,0:T(8,128)(2,1)}, bf16[2,32,32,128]{3,2,1,0:T(8,128)(2,1)S(1)}, u32[]{:S(2)}, u32[]{:S(2)}) %collective-permute-start) | collective-permute-done | bytes 524320 | tf_op jit(solution)/shard_map/ppermute | solution.py:504
  23.0 0.7 spectra.3
  23.6 2.6 %collective-permute-done.1.low_ref = bf16[2,32,32,128]{3,2,1,0:T(8,128)(2,1)S(1)} collective-permute-done((bf16[2,32,32,128]{3,2,1,0:T(8,128)(2,1)}, bf16[2,32,32,128]{3,2,1,0:T(8,128)(2,1)S(1)}, u32[]{:S(2)}, u32[]{:S(2)}) %collective-permute-start.1) | collective-permute-done | bytes 524320 | tf_op jit(solution)/shard_map/ppermute | solution.py:503
  26.2 3.3 %grams_sent.1 = (bf16[4,2,640,128]{3,2,1,0:T(8,128)(2,1)S(1)}, f32[8,48,384]{2,1,0:T(8,128)S(1)}, f32[8,128]{1,0:T(8,128)S(1)}, f32[96,64,128]{2,1,0:T(8,128)S(1)}) custom-call(s32[8,33]{1,0:T(8,128)S(1)} %pad_add_fusion.ints_ref, f32[8,32]{1,0:T(8,128)S(1)} %pad_maximum_fusion.3.floats_ref, bf16[64,64]{1,0:T(8,128)(2,1)S(1)} %get-tuple-element.37.table_ref, ...), custom_call_target="tpu_custom_call" | custom-call | tf_op jit(solution)/shard_map/grams_sent/pallas_call | solution.py:568
  29.5 1.0 %collective-permute-start.3 = (f32[8,48,384]{2,1,0:T(8,128)S(1)}, f32[8,48,384]{2,1,0:T(8,128)S(1)}, u32[]{:S(2)}, u32[]{:S(2)}) collective-permute-start(f32[8,48,384]{2,1,0:T(8,128)S(1)} %get-tuple-element.40), channel_id=1, source_target_pairs={{0,1},{1,0},{2,3},{3,2},{4,5},{5,4},{6,7},{7,6},{8,9},{9,8},{10,11... | collective-permute-start | bytes 1769480 | tf_op jit(solution)/shard_map/ppermute | solution.py:498
  30.5 3.0 %grams_kept.1 = (bf16[4,2,640,128]{3,2,1,0:T(8,128)(2,1)S(1)}, f32[8,48,384]{2,1,0:T(8,128)S(1)}) custom-call(s32[8,33]{1,0:T(8,128)S(1)} %pad_add_fusion.ints_ref, f32[8,32]{1,0:T(8,128)S(1)} %pad_maximum_fusion.3.floats_ref, f32[96,64,128]{2,1,0:T(8,128)S(1)} %get-tuple-element.41.spec_ref), custom_call_target="tpu_custom_call" | custom-call | tf_op jit(solution)/shard_map/grams_kept/pallas_call | solution.py:583
  33.6 3.2 %collective-permute-start.4 = (f32[2,48,384]{2,1,0:T(8,128)S(1)}, f32[2,48,384]{2,1,0:T(8,128)S(1)}, u32[]{:S(2)}, u32[]{:S(2)}) collective-permute-start(f32[2,48,384]{2,1,0:T(8,128)S(1)} %get-tuple-element.69), channel_id=1, source_target_pairs={{0,2},{1,3},{2,0},{3,1},{4,6},{5,7},{6,4},{7,5},{8,10},{9,11},{10,... | collective-permute-start | bytes 442376 | tf_op jit(solution)/shard_map/ppermute | solution.py:498
  36.8 1.5 %collective-permute-start.5 = (f32[2,48,384]{2,1,0:T(8,128)S(1)}, f32[2,48,384]{2,1,0:T(8,128)S(1)}, u32[]{:S(2)}, u32[]{:S(2)}) collective-permute-start(f32[2,48,384]{2,1,0:T(8,128)S(1)} %get-tuple-element.68), channel_id=1, source_target_pairs={{0,6},{1,7},{2,4},{3,5},{4,2},{5,3},{6,0},{7,1},{8,14},{9,15},{10,... | collective-permute-start | bytes 442376 | tf_op jit(solution)/shard_map/ppermute | solution.py:498
  38.3 0.2 collective-permute-start.6
  38.5 1.2 %edges_out.1 = (bf16[64,128]{1,0:T(8,128)(2,1)S(1)}, bf16[64,128]{1,0:T(8,128)(2,1)S(1)}) custom-call(bf16[4,2,640,128]{3,2,1,0:T(8,128)(2,1)S(1)} %get-tuple-element.48.sent_ref, bf16[4,2,640,128]{3,2,1,0:T(8,128)(2,1)S(1)} %get-tuple-element.49.kept_ref), custom_call_target="tpu_custom_call" | custom-call | tf_op jit(solution)/shard_map/edges_out/pallas_call | solution.py:596
  39.6 0.6 collective-permute-start.7
  40.3 0.8 collective-permute-done.7.first_ref
  41.1 2.1 %collective-permute-done.4 = f32[2,48,384]{2,1,0:T(8,128)S(1)} collective-permute-done((f32[2,48,384]{2,1,0:T(8,128)S(1)}, f32[2,48,384]{2,1,0:T(8,128)S(1)}, u32[]{:S(2)}, u32[]{:S(2)}) %collective-permute-start.4) | collective-permute-done | bytes 147488 | tf_op jit(solution)/shard_map/ppermute | solution.py:498
  43.2 1.1 %collective-permute-done.5 = f32[2,48,384]{2,1,0:T(8,128)S(1)} collective-permute-done((f32[2,48,384]{2,1,0:T(8,128)S(1)}, f32[2,48,384]{2,1,0:T(8,128)S(1)}, u32[]{:S(2)}, u32[]{:S(2)}) %collective-permute-start.5) | collective-permute-done | bytes 147488 | tf_op jit(solution)/shard_map/ppermute | solution.py:498
  44.4 1.3 %collective-permute-done.6 = f32[2,48,384]{2,1,0:T(8,128)S(1)} collective-permute-done((f32[2,48,384]{2,1,0:T(8,128)S(1)}, f32[2,48,384]{2,1,0:T(8,128)S(1)}, u32[]{:S(2)}, u32[]{:S(2)}) %collective-permute-start.6) | collective-permute-done | bytes 147488 | tf_op jit(solution)/shard_map/ppermute | solution.py:498
  45.7 3.1 %collective-permute-start.8 = (f32[48,384]{1,0:T(8,128)S(1)}, f32[48,384]{1,0:T(8,128)S(1)}, u32[]{:S(2)}, u32[]{:S(2)}) collective-permute-start(f32[48,384]{1,0:T(8,128)S(1)} %slice_bitcast_fusion), channel_id=1, source_target_pairs={{0,8},{1,9},{2,10},{3,11},{4,12},{5,13},{6,14},{7,15},{8,0},{9,1},... | collective-permute-start | bytes 221192 | tf_op jit(solution)/shard_map/ppermute | solution.py:498
  48.8 1.8 %collective-permute-done.8 = f32[48,384]{1,0:T(8,128)S(1)} collective-permute-done((f32[48,384]{1,0:T(8,128)S(1)}, f32[48,384]{1,0:T(8,128)S(1)}, u32[]{:S(2)}, u32[]{:S(2)}) %collective-permute-start.8) | collective-permute-done | bytes 73760 | tf_op jit(solution)/shard_map/ppermute | solution.py:498
  50.6 5.2 %collective-permute-start.9 = (f32[48,384]{1,0:T(8,128)S(1)}, f32[48,384]{1,0:T(8,128)S(1)}, u32[]{:S(2)}, u32[]{:S(2)}) collective-permute-start(f32[48,384]{1,0:T(8,128)S(1)} %fusion.first_ref), channel_id=1, source_target_pairs={{0,28},{1,29},{2,30},{3,31},{4,24},{5,25},{6,26},{7,27},{8,20},{9,... | collective-permute-start | bytes 221192 | tf_op jit(solution)/shard_map/ppermute | solution.py:498
  55.7 7.4 %collective-permute-start.10 = (bf16[64,128]{1,0:T(8,128)(2,1)S(1)}, bf16[64,128]{1,0:T(8,128)(2,1)S(1)}, u32[]{:S(2)}, u32[]{:S(2)}) collective-permute-start(bf16[64,128]{1,0:T(8,128)(2,1)S(1)} %get-tuple-element.55), channel_id=1, source_target_pairs={{1,2},{2,1},{3,4},{4,3},{5,6},{6,5},{7,8},{8,7},{9,10},{10,9},{11,... | collective-permute-start | bytes 49160 | tf_op jit(solution)/shard_map/ppermute | solution.py:606
  63.2 3.8 %solve.1 = f32[8,128]{1,0:T(8,128)S(1)} custom-call(f32[48,384]{1,0:T(8,128)S(1)} %fusion.first_ref, f32[48,384]{1,0:T(8,128)S(1)} %collective-permute-done.9.second_ref, f32[8,128]{1,0:T(8,128)S(1)} %get-tuple-element.54.marks_ref), custom_call_target="tpu_custom_call" | custom-call | tf_op jit(solution)/shard_map/solve/pallas_call | solution.py:613
  67.1 1.4 %collective-permute-start.11 = (f32[1,8,128]{2,1,0:T(8,128)S(1)}, f32[1,8,128]{2,1,0:T(8,128)S(1)}, u32[]{:S(2)}, u32[]{:S(2)}) collective-permute-start(f32[1,8,128]{2,1,0:T(8,128)S(1)} %bitcast.11), channel_id=1, source_target_pairs={{0,8},{1,9},{2,10},{3,11},{4,12},{5,13},{6,14},{7,15},{8,0},{9,1},... | collective-permute-start | bytes 12296 | tf_op jit(solution)/shard_map/ppermute | solution.py:498
  68.4 0.2 edges_in.1.edge_ref
  68.7 1.8 %collective-permute-done.11 = f32[1,8,128]{2,1,0:T(8,128)S(1)} collective-permute-done((f32[1,8,128]{2,1,0:T(8,128)S(1)}, f32[1,8,128]{2,1,0:T(8,128)S(1)}, u32[]{:S(2)}, u32[]{:S(2)}) %collective-permute-start.11) | collective-permute-done | bytes 4128 | tf_op jit(solution)/shard_map/ppermute | solution.py:498
  70.5 0.8 collective-permute-start.12
  71.4 1.7 %collective-permute-done.12 = f32[2,8,128]{2,1,0:T(8,128)S(1)} collective-permute-done((f32[2,8,128]{2,1,0:T(8,128)S(1)}, f32[2,8,128]{2,1,0:T(8,128)S(1)}, u32[]{:S(2)}, u32[]{:S(2)}) %collective-permute-start.12) | collective-permute-done | bytes 8224 | tf_op jit(solution)/shard_map/ppermute | solution.py:498
  73.0 0.8 collective-permute-start.13
  73.8 3.3 %collective-permute-done.13 = f32[4,8,128]{2,1,0:T(8,128)S(1)} collective-permute-done((f32[4,8,128]{2,1,0:T(8,128)S(1)}, f32[4,8,128]{2,1,0:T(8,128)S(1)}, u32[]{:S(2)}, u32[]{:S(2)}) %collective-permute-start.13) | collective-permute-done | bytes 16416 | tf_op jit(solution)/shard_map/ppermute | solution.py:498
  77.1 0.1 broadcast_in_dim.22.bins_ref
  77.2 1.5 %collective-permute-start.14 = (f32[8,8,128]{2,1,0:T(8,128)S(1)}, f32[8,8,128]{2,1,0:T(8,128)S(1)}, u32[]{:S(2)}, u32[]{:S(2)}) collective-permute-start(f32[8,8,128]{2,1,0:T(8,128)S(1)} %pad_maximum_fusion), channel_id=1, source_target_pairs={{0,1},{1,0},{2,3},{3,2},{4,5},{5,4},{6,7},{7,6},{8,9},{9,8},{10,11... | collective-permute-start | bytes 98312 | tf_op jit(solution)/shard_map/ppermute | solution.py:498
  78.7 0.9 collective-permute-done.14
  79.6 1.2 %power.1 = (f32[16,8,128]{2,1,0:T(8,128)S(1)}, f32[2,8,128]{2,1,0:T(8,128)S(1)}, f32[2,8,128]{2,1,0:T(8,128)S(1)}) custom-call(s32[16,8,128]{2,1,0:T(8,128)S(1)} %broadcast_in_dim.22.bins_ref, f32[16,8,128]{2,1,0:T(8,128)S(1)} %constant_dynamic-update-slice_fusion.weights_ref, bf16[4,2,640,128]{3,2,1,0:T(8,128)(2,1)S(1)} %get-tuple-element.48.sent_ref, ...), custom_call_target="tpu_custom_call" | custom-call | tf_op jit(solution)/shard_map/power/pallas_call | solution.py:638
  80.8 3.0 %collective-permute-start.15 = (f32[2,8,128]{2,1,0:T(8,128)S(1)}, f32[2,8,128]{2,1,0:T(8,128)S(1)}, u32[]{:S(2)}, u32[]{:S(2)}) collective-permute-start(f32[2,8,128]{2,1,0:T(8,128)S(1)} %get-tuple-element.63), channel_id=1, source_target_pairs={{0,224},{32,64},{64,32},{96,128},{128,96},{160,192},{192,160},{224... | collective-permute-start | bytes 24584 | tf_op jit(solution)/shard_map/ppermute | solution.py:648
  83.8 1.7 %collective-permute-done.15.second_ref = f32[2,8,128]{2,1,0:T(8,128)S(1)} collective-permute-done((f32[2,8,128]{2,1,0:T(8,128)S(1)}, f32[2,8,128]{2,1,0:T(8,128)S(1)}, u32[]{:S(2)}, u32[]{:S(2)}) %collective-permute-start.15) | collective-permute-done | bytes 8224 | tf_op jit(solution)/shard_map/ppermute | solution.py:648
  85.5 1.1 %collective-permute-done.16.first_ref = f32[2,8,128]{2,1,0:T(8,128)S(1)} collective-permute-done((f32[2,8,128]{2,1,0:T(8,128)S(1)}, f32[2,8,128]{2,1,0:T(8,128)S(1)}, u32[]{:S(2)}, u32[]{:S(2)}) %collective-permute-start.16) | collective-permute-done | bytes 8224 | tf_op jit(solution)/shard_map/ppermute | solution.py:650
  86.6 0.6 smooth.1
  (30 shorter events, 0.7 us)
Async XLA Ops:
  0.0 12.3 %copy-start = (f32[64,16]{0,1:T(8,128)S(1)}, f32[64,16]{0,1:T(8,128)}, u32[]{:S(2)}) copy-start(f32[64,16]{0,1:T(8,128)} %param.11) | copy-start | bytes 12292
  0.0 22.9 %collective-permute-start = (bf16[2,32,32,128]{3,2,1,0:T(8,128)(2,1)}, bf16[2,32,32,128]{3,2,1,0:T(8,128)(2,1)S(1)}, u32[]{:S(2)}, u32[]{:S(2)}) collective-permute-start(bf16[2,32,32,128]{3,2,1,0:T(8,128)(2,1)} %own_ref.1), channel_id=1, source_target_pairs={{32,0},{64,32},{96,64},{128,96},{160,128},{192,160},{224,192},{0,2... | collective-permute-start | bytes 1572872 | tf_op jit(solution)/shard_map/ppermute | solution.py:504
  4.3 21.9 %collective-permute-start.1 = (bf16[2,32,32,128]{3,2,1,0:T(8,128)(2,1)}, bf16[2,32,32,128]{3,2,1,0:T(8,128)(2,1)S(1)}, u32[]{:S(2)}, u32[]{:S(2)}) collective-permute-start(bf16[2,32,32,128]{3,2,1,0:T(8,128)(2,1)} %own_ref.1), channel_id=1, source_target_pairs={{0,32},{32,64},{64,96},{96,128},{128,160},{160,192},{192,224},{224... | collective-permute-start | bytes 1572872 | tf_op jit(solution)/shard_map/ppermute | solution.py:503
  5.1 10.8 %collective-permute-start.2 = (f32[8,128]{1,0:T(8,128)S(1)}, f32[8,128]{1,0:T(8,128)S(1)}, u32[]{:S(2)}, u32[]{:S(2)}) collective-permute-start(f32[8,128]{1,0:T(8,128)S(1)} %broadcast_in_dim.19), channel_id=1, source_target_pairs={{0,28},{1,29},{2,30},{3,31},{4,24},{5,25},{6,26},{7,27},{8,20},{9,... | collective-permute-start | bytes 12296 | tf_op jit(solution)/shard_map/ppermute | solution.py:498
  13.5 1.0 %copy-start.1 = (bf16[2,32,32,128]{3,2,1,0:T(8,128)(2,1)S(1)}, bf16[2,32,32,128]{3,2,1,0:T(8,128)(2,1)}, u32[]{:S(2)}) copy-start(bf16[2,32,32,128]{3,2,1,0:T(8,128)(2,1)} %own_ref.1) | copy-start | bytes 1572868
  14.5 0.7 copy-start.2
  29.5 4.0 %collective-permute-start.3 = (f32[8,48,384]{2,1,0:T(8,128)S(1)}, f32[8,48,384]{2,1,0:T(8,128)S(1)}, u32[]{:S(2)}, u32[]{:S(2)}) collective-permute-start(f32[8,48,384]{2,1,0:T(8,128)S(1)} %get-tuple-element.40), channel_id=1, source_target_pairs={{0,1},{1,0},{2,3},{3,2},{4,5},{5,4},{6,7},{7,6},{8,9},{9,8},{10,11... | collective-permute-start | bytes 1769480 | tf_op jit(solution)/shard_map/ppermute | solution.py:498
  33.6 9.6 %collective-permute-start.4 = (f32[2,48,384]{2,1,0:T(8,128)S(1)}, f32[2,48,384]{2,1,0:T(8,128)S(1)}, u32[]{:S(2)}, u32[]{:S(2)}) collective-permute-start(f32[2,48,384]{2,1,0:T(8,128)S(1)} %get-tuple-element.69), channel_id=1, source_target_pairs={{0,2},{1,3},{2,0},{3,1},{4,6},{5,7},{6,4},{7,5},{8,10},{9,11},{10,... | collective-permute-start | bytes 442376 | tf_op jit(solution)/shard_map/ppermute | solution.py:498
  36.8 7.6 %collective-permute-start.5 = (f32[2,48,384]{2,1,0:T(8,128)S(1)}, f32[2,48,384]{2,1,0:T(8,128)S(1)}, u32[]{:S(2)}, u32[]{:S(2)}) collective-permute-start(f32[2,48,384]{2,1,0:T(8,128)S(1)} %get-tuple-element.68), channel_id=1, source_target_pairs={{0,6},{1,7},{2,4},{3,5},{4,2},{5,3},{6,0},{7,1},{8,14},{9,15},{10,... | collective-permute-start | bytes 442376 | tf_op jit(solution)/shard_map/ppermute | solution.py:498
  38.3 7.4 %collective-permute-start.6 = (f32[2,48,384]{2,1,0:T(8,128)S(1)}, f32[2,48,384]{2,1,0:T(8,128)S(1)}, u32[]{:S(2)}, u32[]{:S(2)}) collective-permute-start(f32[2,48,384]{2,1,0:T(8,128)S(1)} %get-tuple-element.67), channel_id=1, source_target_pairs={{0,4},{1,5},{2,6},{3,7},{4,0},{5,1},{6,2},{7,3},{8,12},{9,13},{10,... | collective-permute-start | bytes 442376 | tf_op jit(solution)/shard_map/ppermute | solution.py:498
  39.6 1.5 %collective-permute-start.7 = (bf16[64,128]{1,0:T(8,128)(2,1)S(1)}, bf16[64,128]{1,0:T(8,128)(2,1)S(1)}, u32[]{:S(2)}, u32[]{:S(2)}) collective-permute-start(bf16[64,128]{1,0:T(8,128)(2,1)S(1)} %get-tuple-element.50), channel_id=1, source_target_pairs={{0,1},{1,0},{2,3},{3,2},{4,5},{5,4},{6,7},{7,6},{8,9},{9,8},{10,11... | collective-permute-start | bytes 49160 | tf_op jit(solution)/shard_map/ppermute | solution.py:606
  45.7 4.8 %collective-permute-start.8 = (f32[48,384]{1,0:T(8,128)S(1)}, f32[48,384]{1,0:T(8,128)S(1)}, u32[]{:S(2)}, u32[]{:S(2)}) collective-permute-start(f32[48,384]{1,0:T(8,128)S(1)} %slice_bitcast_fusion), channel_id=1, source_target_pairs={{0,8},{1,9},{2,10},{3,11},{4,12},{5,13},{6,14},{7,15},{8,0},{9,1},... | collective-permute-start | bytes 221192 | tf_op jit(solution)/shard_map/ppermute | solution.py:498
  50.6 12.7 %collective-permute-start.9 = (f32[48,384]{1,0:T(8,128)S(1)}, f32[48,384]{1,0:T(8,128)S(1)}, u32[]{:S(2)}, u32[]{:S(2)}) collective-permute-start(f32[48,384]{1,0:T(8,128)S(1)} %fusion.first_ref), channel_id=1, source_target_pairs={{0,28},{1,29},{2,30},{3,31},{4,24},{5,25},{6,26},{7,27},{8,20},{9,... | collective-permute-start | bytes 221192 | tf_op jit(solution)/shard_map/ppermute | solution.py:498
  55.7 11.3 %collective-permute-start.10 = (bf16[64,128]{1,0:T(8,128)(2,1)S(1)}, bf16[64,128]{1,0:T(8,128)(2,1)S(1)}, u32[]{:S(2)}, u32[]{:S(2)}) collective-permute-start(bf16[64,128]{1,0:T(8,128)(2,1)S(1)} %get-tuple-element.55), channel_id=1, source_target_pairs={{1,2},{2,1},{3,4},{4,3},{5,6},{6,5},{7,8},{8,7},{9,10},{10,9},{11,... | collective-permute-start | bytes 49160 | tf_op jit(solution)/shard_map/ppermute | solution.py:606
  67.1 3.4 %collective-permute-start.11 = (f32[1,8,128]{2,1,0:T(8,128)S(1)}, f32[1,8,128]{2,1,0:T(8,128)S(1)}, u32[]{:S(2)}, u32[]{:S(2)}) collective-permute-start(f32[1,8,128]{2,1,0:T(8,128)S(1)} %bitcast.11), channel_id=1, source_target_pairs={{0,8},{1,9},{2,10},{3,11},{4,12},{5,13},{6,14},{7,15},{8,0},{9,1},... | collective-permute-start | bytes 12296 | tf_op jit(solution)/shard_map/ppermute | solution.py:498
  70.5 2.5 %collective-permute-start.12 = (f32[2,8,128]{2,1,0:T(8,128)S(1)}, f32[2,8,128]{2,1,0:T(8,128)S(1)}, u32[]{:S(2)}, u32[]{:S(2)}) collective-permute-start(f32[2,8,128]{2,1,0:T(8,128)S(1)} %pad_maximum_fusion.2), channel_id=1, source_target_pairs={{0,4},{1,5},{2,6},{3,7},{4,0},{5,1},{6,2},{7,3},{8,12},{9,13},{10,... | collective-permute-start | bytes 24584 | tf_op jit(solution)/shard_map/ppermute | solution.py:498
  73.0 4.1 %collective-permute-start.13 = (f32[4,8,128]{2,1,0:T(8,128)S(1)}, f32[4,8,128]{2,1,0:T(8,128)S(1)}, u32[]{:S(2)}, u32[]{:S(2)}) collective-permute-start(f32[4,8,128]{2,1,0:T(8,128)S(1)} %pad_maximum_fusion.1), channel_id=1, source_target_pairs={{0,2},{1,3},{2,0},{3,1},{4,6},{5,7},{6,4},{7,5},{8,10},{9,11},{10,... | collective-permute-start | bytes 49160 | tf_op jit(solution)/shard_map/ppermute | solution.py:498
  77.2 2.4 %collective-permute-start.14 = (f32[8,8,128]{2,1,0:T(8,128)S(1)}, f32[8,8,128]{2,1,0:T(8,128)S(1)}, u32[]{:S(2)}, u32[]{:S(2)}) collective-permute-start(f32[8,8,128]{2,1,0:T(8,128)S(1)} %pad_maximum_fusion), channel_id=1, source_target_pairs={{0,1},{1,0},{2,3},{3,2},{4,5},{5,4},{6,7},{7,6},{8,9},{9,8},{10,11... | collective-permute-start | bytes 98312 | tf_op jit(solution)/shard_map/ppermute | solution.py:498
  80.8 4.7 %collective-permute-start.15 = (f32[2,8,128]{2,1,0:T(8,128)S(1)}, f32[2,8,128]{2,1,0:T(8,128)S(1)}, u32[]{:S(2)}, u32[]{:S(2)}) collective-permute-start(f32[2,8,128]{2,1,0:T(8,128)S(1)} %get-tuple-element.63), channel_id=1, source_target_pairs={{0,224},{32,64},{64,32},{96,128},{128,96},{160,192},{192,160},{224... | collective-permute-start | bytes 24584 | tf_op jit(solution)/shard_map/ppermute | solution.py:648
  83.8 2.8 %collective-permute-start.16 = (f32[2,8,128]{2,1,0:T(8,128)S(1)}, f32[2,8,128]{2,1,0:T(8,128)S(1)}, u32[]{:S(2)}, u32[]{:S(2)}) collective-permute-start(f32[2,8,128]{2,1,0:T(8,128)S(1)} %get-tuple-element.64), channel_id=1, source_target_pairs={{0,32},{32,0},{64,96},{96,64},{128,160},{160,128},{192,224},{224,1... | collective-permute-start | bytes 24584 | tf_op jit(solution)/shard_map/ppermute | solution.py:650
